TPU v7x, 32 devices: a whole 2x2x4 slice. The times are simulated.
32 devices in a mesh: obs: 4 (over z), cell: 8 (over y, x, core).
Axes of the slice: x: 2, y: 2, z: 4, core: 2. Of those that a mesh axis runs over, the one named last changes fastest.
Arguments:
- start: float32 [4, 384, 128], P('obs', 'cell'), may hold values from -6 to 6
- lat_mats: float32 [384, 128, 128], P('cell'), may hold values from -0.5 to 0.5
- footprints: bfloat16 [64, 128, 768], P(('obs', 'cell')), may hold values from -0.21875 to 0.21875
- blk_sub: int32 [64], P(('obs', 'cell')), may hold values from 0 to 7
- blk_off: int32 [64], P(('obs', 'cell')), may hold values from 0 to 31, as said below
- counts: int32 [32], P('obs'), may hold values from 64 to 128
- rinv: float32 [4096], P('obs'), may hold values from 0.25 to 4
Outputs:
- krylov: float32 [4, 4, 384, 128], P(None, 'obs', 'cell')
- coeffs: float32 [2, 3], replicated
Inputs may be any that keep to these rules, and one draw needn't show every extreme that they name: `blk_off`: of the 2 footprint blocks of one device, at most 1 read cell blocks in the periods of any one obs index (cell blocks k with the same k div (32 / 4)); on every device some obs index receives exactly 1.
All inputs are finite; a program needn't handle non-finite values.
Results may differ from a plain program's by a relative error of at most 0.009.
Values may be sent and summed in bfloat16 or wider, within the bound.
No kernel may reach another device: no remote copies, remote signals or barrier semaphores. Data moves between devices by JAX's collectives and lax.ppermute only.
A program may use at most 64 MiB of HBM per device.

v0:
```python
import math

import jax
import jax.numpy as jnp
from jax import lax
from jax.sharding import PartitionSpec as P

CR = 2
STEPS = 3


HIGH = lax.Precision.HIGHEST


def lon_table(order):
    index = jnp.arange(order, dtype=jnp.int32)
    mode = index[:, None]
    point = index[None, :]
    half = order // 2
    freq = jnp.where(mode <= half, mode, mode - half)
    phase = (freq * point % order).astype(jnp.float32) * (2.0 * math.pi / order)
    factor = jnp.where((mode == 0) | (mode == half), math.sqrt(1.0 / order), math.sqrt(2.0 / order))
    return jnp.where(mode <= half, jnp.cos(phase), jnp.sin(phase)) * factor


def body(start, lat_mats, footprints, blk_sub, blk_off, counts, rinv):
    per_dev, modes_dev, lat_rows = start.shape
    cell_count = lax.axis_size("cell")
    obs_count = lax.axis_size("obs")
    lon_cols = modes_dev * cell_count
    band = lat_rows // cell_count
    groups = band // CR
    width = CR * lon_cols
    sub_rows = counts.shape[0]
    obs_rows = footprints.shape[1]
    table = lon_table(lon_cols)
    valid = (jnp.arange(obs_rows, dtype=jnp.int32)[None, :] < counts[:, None]).astype(jnp.float32)
    weights = rinv.reshape(sub_rows, obs_rows) * valid
    sub_onehot = (blk_sub[:, None] == jnp.arange(sub_rows, dtype=jnp.int32)[None, :]).astype(
        jnp.float32
    )
    first = jnp.sqrt(lax.psum(jnp.sum(start * start), ("obs", "cell")))
    current = start / first
    previous = jnp.zeros_like(start)
    beta = jnp.float32(0.0)
    vectors = [current]
    alphas = []
    betas = []
    for step in range(STEPS):
        spread = jnp.einsum("mab,pmb->pma", lat_mats, current, precision=HIGH)
        grid = jnp.einsum(
            "pma,mn->pan",
            lax.all_to_all(spread, "cell", split_axis=2, concat_axis=1, tiled=True),
            table,
            precision=HIGH,
        ).astype(jnp.bfloat16)
        every = lax.all_gather(grid, "obs", axis=0, tiled=True)
        blocks = every.reshape(per_dev * obs_count * groups, width)
        picked = blocks[blk_off]
        prod = jnp.einsum("bok,bk->bo", footprints, picked, preferred_element_type=jnp.float32)
        partial_sim = jnp.einsum("bs,bo->so", sub_onehot, prod, precision=HIGH)
        sim = lax.psum(partial_sim, "cell")
        weighted = (weights * sim).astype(jnp.bfloat16)
        chosen = weighted[blk_sub]
        terms = jnp.einsum("bok,bo->bk", footprints, chosen, preferred_element_type=jnp.float32)
        count = lax.axis_size("obs") * per_dev
        onehot = (blk_off[:, None] == jnp.arange(count * groups, dtype=jnp.int32)[None, :]).astype(
            jnp.float32
        )
        placed = jnp.einsum("bc,bk->ck", onehot, terms, precision=HIGH)
        back = lax.psum_scatter(
            placed.reshape(count, band, lon_cols), "obs", scatter_dimension=0, tiled=True
        )
        hessian_coef = jnp.einsum("pan,mn->pam", back, table, precision=HIGH)
        image = (
            current
            + jnp.einsum(
                "mab,pam->pmb",
                lat_mats,
                lax.all_to_all(hessian_coef, "cell", split_axis=2, concat_axis=1, tiled=True),
                precision=HIGH,
            )
            - beta * previous
        )
        alpha = lax.psum(jnp.sum(current * image), ("obs", "cell"))
        direction = image - alpha * current
        beta = jnp.sqrt(lax.psum(jnp.sum(direction * direction), ("obs", "cell")))
        previous = current
        current = direction / beta
        vectors.append(current)
        alphas.append(alpha)
        betas.append(beta)
    factor = jnp.sqrt(jnp.float32(per_dev * obs_count * lon_cols * lat_rows))
    krylov = jnp.stack(vectors) * factor
    coeffs = jnp.stack([jnp.stack(alphas), jnp.stack(betas)])
    return (krylov, coeffs)


def solution(mesh):
    placed = (
        P("obs", "cell", None),
        P("cell", None, None),
        P(("obs", "cell"), None, None),
        P(("obs", "cell")),
        P(("obs", "cell")),
        P("obs"),
        P("obs"),
    )
    return jax.shard_map(
        body,
        mesh=mesh,
        in_specs=placed,
        out_specs=(P(None, "obs", "cell", None), P()),
        check_vma=False,
    )
```

profile of v0, /device:TPU:0, one launch (start us, length us, event | category | flops | bytes accessed | tf_op | source)
XLA Modules:
  0.0 637.9 jit_solution(2310644867710698100)
XLA Ops:
  8.7 42.2 %psum.70 = f32[]{:T(128)} all-reduce(f32[]{:T(128)} %multiply_reduce_fusion.6), channel_id=1, replica_groups=mesh['obs'=4,'cell'=8] {'obs','cell'}, use_global_device_ids=true, to_apply=%region_1.2 | all-reduce | flops 1 | bytes 8 | tf_op jit(solution)/shard_map/psum | solution.py:42
  52.3 5.6 fusion.63
  60.0 2.3 reduce
  63.9 4.0 all-to-all-start
  69.8 2.9 all-to-all-done
  72.6 2.1 reduce.1
  79.2 3.7 convolution_convert_fusion.2
  82.9 13.8 %all-gather = bf16[64,384]{1,0:T(8,128)(2,1)} all-gather(bf16[16,384]{1,0:T(8,128)(2,1)S(1)} %convolution_convert_fusion.2), channel_id=2, replica_groups=mesh['obs'=4,'cell'=8] {'obs'}, dimensions={0}, use_global_device_ids=true | all-gather | bytes 61440 | tf_op jit(solution)/shard_map/all_gather | solution.py:57
  100.7 11.8 %psum.71 = f32[8,128]{1,0:T(8,128)S(1)} all-reduce(f32[8,128]{1,0:T(8,128)S(1)} %fusion.38), channel_id=1, replica_groups=mesh['obs'=4,'cell'=8] {'cell'}, use_global_device_ids=true, to_apply=%region_2.3 | all-reduce | flops 1024 | bytes 8192 | tf_op jit(solution)/shard_map/psum | solution.py:62
  117.3 17.3 %reduce-scatter.4.cloned.1.call-done = f32[1,16,384]{2,1,0:T(8,128)} async-done(((f32[4,16,384]{2,1,0:T(8,128)}), f32[1,16,384]{2,1,0:T(8,128)}) %reduce-scatter.4.cloned.1.call-update) | async-done | bytes 24592 | tf_op jit(solution)/shard_map/reduce_scatter | solution.py:71
  134.6 5.7 fusion.7
  140.3 2.8 reduce.2
  144.7 8.9 %all_to_all.90 = f32[8,1,768]{2,1,0:T(1,128)} all-to-all(f32[8,1,768]{2,1,0:T(1,128)} %reshape.291), channel_id=1, replica_groups=mesh['obs'=4,'cell'=8] {'cell'}, dimensions={0} | all-to-all | bytes 49152 | tf_op jit(solution)/shard_map/all_to_all | solution.py:80
  153.6 2.1 reduce.3
  160.6 3.5 fusion.64
  165.4 37.7 %psum.72 = f32[]{:T(128)} all-reduce(f32[]{:T(128)} %multiply_reduce_fusion.5), channel_id=1, replica_groups=mesh['obs'=4,'cell'=8] {'obs','cell'}, use_global_device_ids=true, to_apply=%region_5.6 | all-reduce | flops 1 | bytes 8 | tf_op jit(solution)/shard_map/psum | solution.py:85
  205.1 41.2 %psum.73 = f32[]{:T(128)} all-reduce(f32[]{:T(128)} %multiply_reduce_fusion.4), channel_id=1, replica_groups=mesh['obs'=4,'cell'=8] {'obs','cell'}, use_global_device_ids=true, to_apply=%region_7.8 | all-reduce | flops 1 | bytes 8 | tf_op jit(solution)/shard_map/psum | solution.py:87
  249.0 5.6 fusion.65
  256.0 2.3 reduce.4
  259.9 9.6 %all_to_all.91 = f32[8,1,768]{2,1,0:T(1,128)} all-to-all(f32[8,1,768]{2,1,0:T(1,128)} %reshape.293), channel_id=1, replica_groups=mesh['obs'=4,'cell'=8] {'cell'}, dimensions={0} | all-to-all | bytes 49152 | tf_op jit(solution)/shard_map/all_to_all | solution.py:53
  269.5 2.1 reduce.5
  276.1 3.7 convolution_convert_fusion.1
  279.8 13.8 %all-gather.1 = bf16[64,384]{1,0:T(8,128)(2,1)} all-gather(bf16[16,384]{1,0:T(8,128)(2,1)S(1)} %convolution_convert_fusion.1), channel_id=3, replica_groups=mesh['obs'=4,'cell'=8] {'obs'}, dimensions={0}, use_global_device_ids=true | all-gather | bytes 61440 | tf_op jit(solution)/shard_map/all_gather | solution.py:57
  297.5 12.0 %psum.74 = f32[8,128]{1,0:T(8,128)S(1)} all-reduce(f32[8,128]{1,0:T(8,128)S(1)} %fusion.37), channel_id=1, replica_groups=mesh['obs'=4,'cell'=8] {'cell'}, use_global_device_ids=true, to_apply=%region_8.9 | all-reduce | flops 1024 | bytes 8192 | tf_op jit(solution)/shard_map/psum | solution.py:62
  314.4 16.5 %reduce-scatter.6.cloned.1.call-done = f32[1,16,384]{2,1,0:T(8,128)} async-done(((f32[4,16,384]{2,1,0:T(8,128)}), f32[1,16,384]{2,1,0:T(8,128)}) %reduce-scatter.6.cloned.1.call-update) | async-done | bytes 24592 | tf_op jit(solution)/shard_map/reduce_scatter | solution.py:71
  330.9 5.7 fusion.6
  336.6 2.8 reduce.6
  341.0 8.7 %all_to_all.92 = f32[8,1,768]{2,1,0:T(1,128)} all-to-all(f32[8,1,768]{2,1,0:T(1,128)} %reshape.295), channel_id=1, replica_groups=mesh['obs'=4,'cell'=8] {'cell'}, dimensions={0} | all-to-all | bytes 49152 | tf_op jit(solution)/shard_map/all_to_all | solution.py:80
  349.7 2.1 reduce.7
  356.7 3.5 fusion.66
  361.6 37.7 %psum.75 = f32[]{:T(128)} all-reduce(f32[]{:T(128)} %multiply_reduce_fusion.3), channel_id=1, replica_groups=mesh['obs'=4,'cell'=8] {'obs','cell'}, use_global_device_ids=true, to_apply=%region_11.12 | all-reduce | flops 1 | bytes 8 | tf_op jit(solution)/shard_map/psum | solution.py:85
  399.3 2.7 multiply_reduce_fusion.2
  402.0 41.2 %psum.76 = f32[]{:T(128)} all-reduce(f32[]{:T(128)} %get-tuple-element.4), channel_id=1, replica_groups=mesh['obs'=4,'cell'=8] {'obs','cell'}, use_global_device_ids=true, to_apply=%region_13.14 | all-reduce | flops 1 | bytes 8 | tf_op jit(solution)/shard_map/psum | solution.py:87
  444.6 5.6 fusion.67
  451.7 2.3 reduce.8
  455.6 9.8 %all_to_all.93 = f32[8,1,768]{2,1,0:T(1,128)} all-to-all(f32[8,1,768]{2,1,0:T(1,128)} %reshape.297), channel_id=1, replica_groups=mesh['obs'=4,'cell'=8] {'cell'}, dimensions={0} | all-to-all | bytes 49152 | tf_op jit(solution)/shard_map/all_to_all | solution.py:53
  465.3 2.1 reduce.9
  472.0 3.7 convolution_convert_fusion
  475.6 13.8 %all-gather.2 = bf16[64,384]{1,0:T(8,128)(2,1)} all-gather(bf16[16,384]{1,0:T(8,128)(2,1)S(1)} %convolution_convert_fusion), channel_id=4, replica_groups=mesh['obs'=4,'cell'=8] {'obs'}, dimensions={0}, use_global_device_ids=true | all-gather | bytes 61440 | tf_op jit(solution)/shard_map/all_gather | solution.py:57
  493.4 11.9 %psum.77 = f32[8,128]{1,0:T(8,128)S(1)} all-reduce(f32[8,128]{1,0:T(8,128)S(1)} %fusion.36), channel_id=1, replica_groups=mesh['obs'=4,'cell'=8] {'cell'}, use_global_device_ids=true, to_apply=%region_14.15 | all-reduce | flops 1024 | bytes 8192 | tf_op jit(solution)/shard_map/psum | solution.py:62
  508.5 16.6 %reduce-scatter.8.cloned.1.call-done = f32[1,16,384]{2,1,0:T(8,128)} async-done(((f32[4,16,384]{2,1,0:T(8,128)}), f32[1,16,384]{2,1,0:T(8,128)}) %reduce-scatter.8.cloned.1.call-update) | async-done | bytes 24592 | tf_op jit(solution)/shard_map/reduce_scatter | solution.py:71
  525.1 5.7 fusion.5
  530.7 2.1 reduce.10
  533.6 3.7 all-to-all-start.5
  537.3 4.8 all-to-all-done.5
  543.3 2.8 fusion.68
  546.7 37.7 %psum.78 = f32[]{:T(128)} all-reduce(f32[]{:T(128)} %multiply_reduce_fusion.1), channel_id=1, replica_groups=mesh['obs'=4,'cell'=8] {'obs','cell'}, use_global_device_ids=true, to_apply=%region_17.18 | all-reduce | flops 1 | bytes 8 | tf_op jit(solution)/shard_map/psum | solution.py:85
  585.7 41.2 %psum.79 = f32[]{:T(128)} all-reduce(f32[]{:T(128)} %get-tuple-element.2), channel_id=1, replica_groups=mesh['obs'=4,'cell'=8] {'obs','cell'}, use_global_device_ids=true, to_apply=%region_19.20 | all-reduce | flops 1 | bytes 8 | tf_op jit(solution)/shard_map/psum | solution.py:87
  (123 shorter events, 79.8 us)
Async XLA Ops:
  7.2 45.2 %copy-start = (f32[48,128,128]{2,1,0:T(8,128)S(1)}, f32[48,128,128]{2,1,0:T(8,128)}, u32[]{:S(2)}) copy-start(f32[48,128,128]{2,1,0:T(8,128)} %param.8) | copy-start | bytes 9437188
  7.2 61.3 %copy-start.12 = (s32[2]{0:T(128)S(1)}, s32[2]{0:T(128)}, u32[]{:S(2)}) copy-start(s32[2]{0:T(128)} %param.11) | copy-start | bytes 28
  7.2 92.4 %copy-start.1 = (bf16[2,128,768]{2,1,0:T(8,128)(2,1)S(1)}, bf16[2,128,768]{2,1,0:T(8,128)(2,1)}, u32[]{:S(2)}) copy-start(bf16[2,128,768]{2,1,0:T(8,128)(2,1)} %param.9) | copy-start | bytes 1179652
  52.3 60.1 %copy-start.11 = (f32[1024]{0:T(1024)S(1)}, f32[1024]{0:T(1024)}, u32[]{:S(2)}) copy-start(f32[1024]{0:T(1024)} %param.13) | copy-start | bytes 12292
  63.9 8.8 %all-to-all-start = ((f32[8,1,768]{2,1,0:T(1,128)}), f32[8,1,768]{2,1,0:T(1,128)}, u32[]{:S(2)}, u32[]{:S(2)}) async-start(f32[8,1,768]{2,1,0:T(1,128)} %reshape.289), calls=%async_computation | async-start | bytes 49152 | tf_op jit(solution)/shard_map/all_to_all | solution.py:53
  67.8 66.8 %reduce-scatter.4.cloned.1.call-start = ((), (), s32[]{:S(2)}) async-start(), calls=%async_computation.9 | async-start | bytes 122880 | tf_op jit(solution)/shard_map/reduce_scatter | solution.py:71
  67.9 31.9 %copy-start.13 = (s32[384]{0:T(512)}, s32[384]{0:T(512)S(1)}, u32[]{:S(2)}) copy-start(s32[384]{0:T(512)S(1)} %add_select_fusion.1) | copy-start | bytes 4612
  69.8 27.0 %copy-start.18 = (pred[384]{0:T(512)(128)(4,1)}, pred[384]{0:T(512)(128)(4,1)S(1)}, u32[]{:S(2)}) copy-start(pred[384]{0:T(512)(128)(4,1)S(1)} %iota_compare_fusion.3) | copy-start | bytes 1156
  117.2 213.6 %reduce-scatter.6.cloned.1.call-start = ((), (), s32[]{:S(2)}) async-start(), calls=%async_computation.10 | async-start | bytes 122880 | tf_op jit(solution)/shard_map/reduce_scatter | solution.py:71
  160.6 4.1 copy-start.2
  160.6 115.5 %copy-start.14 = (s32[384]{0:T(512)S(1)}, s32[384]{0:T(512)}, u32[]{:S(2)}) copy-start(s32[384]{0:T(512)} %copy-done.13) | copy-start | bytes 4612
  160.6 115.5 %copy-start.16 = (f32[384]{0:T(512)S(1)}, f32[384]{0:T(512)}, u32[]{:S(2)}) copy-start(f32[384]{0:T(512)} %fusion.29) | copy-start | bytes 4612
  164.1 0.6 copy-start.9
  248.4 0.6 copy-start.5
  314.3 210.7 %reduce-scatter.8.cloned.1.call-start = ((), (), s32[]{:S(2)}) async-start(), calls=%async_computation.11 | async-start | bytes 122880 | tf_op jit(solution)/shard_map/reduce_scatter | solution.py:71
  356.7 4.1 copy-start.3
  356.7 4.1 copy-start.6
  356.7 115.2 %copy-start.15 = (s32[384]{0:T(512)S(1)}, s32[384]{0:T(512)}, u32[]{:S(2)}) copy-start(s32[384]{0:T(512)} %copy-done.13) | copy-start | bytes 4612
  356.7 115.2 %copy-start.17 = (f32[384]{0:T(512)S(1)}, f32[384]{0:T(512)}, u32[]{:S(2)}) copy-start(f32[384]{0:T(512)} %fusion.29) | copy-start | bytes 4612
  360.2 0.6 copy-start.10
  506.8 30.4 %copy-start.4 = (f32[1,48,128]{2,1,0:T(8,128)S(1)}, f32[1,48,128]{2,1,0:T(8,128)}, u32[]{:S(2)}) copy-start(f32[1,48,128]{2,1,0:T(8,128)} %param.7) | copy-start | bytes 73732
  508.5 37.6 %copy-start.7 = (f32[1,48,128]{2,1,0:T(8,128)S(1)}, f32[1,48,128]{2,1,0:T(8,128)}, u32[]{:S(2)}) copy-start(f32[1,48,128]{2,1,0:T(8,128)} %copy-done.5) | copy-start | bytes 73732
  508.5 37.6 %copy-start.8 = (f32[1,48,128]{2,1,0:T(8,128)S(1)}, f32[1,48,128]{2,1,0:T(8,128)}, u32[]{:S(2)}) copy-start(f32[1,48,128]{2,1,0:T(8,128)} %get-tuple-element.5) | copy-start | bytes 73732
  533.6 8.5 %all-to-all-start.5 = ((f32[8,1,768]{2,1,0:T(1,128)}), f32[8,1,768]{2,1,0:T(1,128)S(1)}, u32[]{:S(2)}, u32[]{:S(2)}) async-start(f32[8,1,768]{2,1,0:T(1,128)} %reshape.299), calls=%async_computation.8 | async-start | bytes 49152 | tf_op jit(solution)/shard_map/all_to_all | solution.py:80
Sparse Core Ops, SparseCore 0:
  117.3 17.2 reduce-scatter.3
  314.4 16.3 reduce-scatter.5
  508.6 16.4 reduce-scatter.7
where the time goes:
time: 650 us; the launch traced here: 638 us
  blocking collectives  393 us (60%)
  matrix products  62.7 us (10%)
  waiting for transfers between devices  58.1 us (9%)
  local copies, waits for them, and re-layouts  53.8 us (8%)
  other arithmetic  45.4 us (7%)
  between operations  17.1 us (3%)
  starting transfers between devices  7.74 us (1%)
    psum x3, blocking collectives, body(): beta = jnp.sqrt(lax.psum(jnp.sum(direction * direction), ('obs', 'cell')))  124 us
    psum x3, blocking collectives, body(): alpha = lax.psum(jnp.sum(current * image), ('obs', 'cell'))  113 us
    reduce_scatter x3, waiting for transfers between devices, body(): lax.psum_scatter(placed.reshape(count, band, lon_cols), 'obs', scatter_di...  50.4 us
    psum x1, blocking collectives, body(): first = jnp.sqrt(lax.psum(jnp.sum(start * start), ('obs', 'cell')))  42.2 us
    all_gather x3, blocking collectives, body(): every = lax.all_gather(grid, 'obs', axis=0, tiled=True)  41.4 us
    psum x3, blocking collectives, body(): sim = lax.psum(partial_sim, 'cell')  35.7 us
    unnamed x51, local copies, waits for them, and re-layouts  19.6 us
    all_to_all x2, blocking collectives, body(): lax.all_to_all(spread, 'cell', split_axis=2, concat_axis=1, tiled=True)  19.3 us
  transfers between devices with their start and end apart: 5, of which 5 were waited for; matrix products, arithmetic and copies ran while one was open for 0% of the time, Pallas kernels for 0%

commit v1 on v0

v1 whole, which is shorter than its diff:
```python
import functools
import math

import jax
import jax.numpy as jnp
import ml_dtypes
import numpy as np
from jax import lax
from jax.experimental import pallas as pl
from jax.experimental.pallas import tpu as pltpu
from jax.sharding import PartitionSpec as P

CR = 2
STEPS = 3
ROWS = 8
VMEM = pl.BlockSpec(memory_space=pltpu.VMEM)
SMEM = pl.BlockSpec(memory_space=pltpu.SMEM)
F32 = jnp.float32
BF16 = jnp.bfloat16


def lon_table(order, parts, padded):
    index = np.arange(order)
    half = order // 2
    freq = np.where(index <= half, index, index - half)[:, None]
    phase = (freq * index[None, :] % order) * (2.0 * math.pi / order)
    factor = np.where((index == 0) | (index == half), math.sqrt(1.0 / order), math.sqrt(2.0 / order))
    table = np.where(index[:, None] <= half, np.cos(phase), np.sin(phase)) * factor[:, None]
    table = table.reshape(parts, order // parts, order)
    table = np.pad(table, ((0, 0), (0, padded - order // parts), (0, 0))).reshape(parts * padded, order)
    high = table.astype(np.float32).astype(ml_dtypes.bfloat16)
    low = (table - high.astype(np.float64)).astype(np.float32).astype(ml_dtypes.bfloat16)
    return high, low


def call(kernel, outs, specs, *args, scratch=()):
    return pl.pallas_call(
        kernel,
        out_shape=outs,
        in_specs=specs,
        out_specs=jax.tree.map(lambda _: VMEM, outs),
        scratch_shapes=scratch,
        compiler_params=pltpu.CompilerParams(vmem_limit_bytes=16 * 1024 * 1024),
    )(*args)


def transform_kernel(dims, high_ref, low_ref, foot_ref, off_ref, sub_ref, out_ref):
    nc, nb, modes, groups, band = dims
    ob = foot_ref.shape[1]
    lon = high_ref.shape[1]
    contract = (((1,), (1,)), ((), ()))
    for b in range(nb):
        for r in range(CR):
            foot = foot_ref[b, :, r * lon:(r + 1) * lon]
            hat = lax.dot_general(high_ref[...], foot, contract, preferred_element_type=F32)
            hat += lax.dot_general(low_ref[...], foot, contract, preferred_element_type=F32)
            hat = hat.astype(BF16)
            at = (b * CR + r) * modes
            for c in range(nc):
                out_ref[c, at:at + modes, :] = hat[c * modes:(c + 1) * modes, :]
    lane = lax.broadcasted_iota(jnp.int32, (16, ob), 1)
    ids = jnp.zeros((16, ob), F32)
    for b in range(nb):
        ids = jnp.where(lane == b, off_ref[b].astype(F32), ids)
        ids = jnp.where(lane == nb + b, sub_ref[b].astype(F32), ids)
    ids = ids.astype(BF16)
    for c in range(nc):
        out_ref[c, nb * CR * modes:, :] = ids


def fold(ref):
    periods, modes, _ = ref.shape
    total = jnp.zeros((ROWS, ref.shape[2]), F32)
    for p in range(periods):
        for at in range(0, modes, ROWS):
            part = ref[p, at:at + ROWS, :]
            total += part * part
    return total


def forward(dims, field_ref, lat_ref, foot_ref, ids_ref, sim_ref, out_ref):
    nc, nb, modes, groups, band = dims
    subs = sim_ref.shape[0] - ROWS
    sim_ref[...] = jnp.zeros_like(sim_ref)
    for j in range(nc):
        for b in range(nb):
            off = ids_ref[j, b]
            sub = ids_ref[j, nb + b]
            period = off // groups
            row = j * band + off % groups * CR
            total = None
            for r in range(CR):
                column = jnp.sum(lat_ref[row + r] * field_ref[period], axis=1, keepdims=True)
                at = (b * CR + r) * modes
                term = foot_ref[j, at:at + modes, :].astype(F32) * column
                total = term if total is None else total + term
            sim_ref[pl.ds(sub, 1), :] += jnp.sum(total, axis=0, keepdims=True)
    sim_ref[subs:, :] = fold(field_ref)
    for c in range(nc):
        out_ref[c] = sim_ref[...]


def first_kernel(dims, near_ref, lat_ref, foot_ref, ids_ref, out_ref, field_ref, sim_ref):
    modes = dims[2]
    per_dev = field_ref.shape[0] // near_ref.shape[0]
    for i in range(near_ref.shape[0]):
        for l in range(per_dev):
            field_ref[i * per_dev + l] = near_ref[i, l * modes:(l + 1) * modes, :]
    forward(dims, field_ref, lat_ref, foot_ref, ids_ref, sim_ref, out_ref)


def adjoint_kernel(dims, sim_ref, weight_ref, foot_ref, ids_ref, out_ref, norm_ref, weighted_ref):
    nc, nb, modes, groups, band = dims
    subs = weight_ref.shape[0]
    mine = nc * nb
    total = sim_ref[0]
    for c in range(1, nc):
        total += sim_ref[c]
    norm = jnp.sqrt(jnp.sum(total[subs:], keepdims=True))
    norm_ref[...] = jnp.broadcast_to(norm, norm_ref.shape)
    sim = total[:subs] / norm
    weighted = sim * weight_ref[...]
    weighted_ref[...] = weighted
    lane = lax.broadcasted_iota(jnp.int32, (modes, 128), 1)
    parts = [jnp.zeros((modes, 128), F32) for _ in range(CR)]
    for j in range(nc):
        for b in range(nb):
            chosen = weighted_ref[pl.ds(ids_ref[j, nb + b], 1), :]
            for r in range(CR):
                at = (b * CR + r) * modes
                column = jnp.sum(foot_ref[j, at:at + modes, :].astype(F32) * chosen, axis=1, keepdims=True)
                parts[r] = jnp.where(lane == j * nb + b, column, parts[r])
    rest = 128 - CR * modes
    if rest:
        parts.append(jnp.zeros((rest, 128), F32))
    rows = jnp.concatenate(parts, axis=0).T
    power = sim * weighted
    for i in range(out_ref.shape[0]):
        out_ref[i, :mine, :] = rows[:mine]
        out_ref[i, mine:, :] = power


def image_kernel(dims, first, last, *refs):
    if first:
        coef_ref, norm_ref, field_ref, lat_ref, foot_ref, ids_ref, all_ref, *refs = refs
        prior_ref = None
    else:
        coef_ref, norm_ref, field_ref, prior_ref, lat_ref, foot_ref, ids_ref, all_ref, *refs = refs
    out_ref, vector_ref, next_ref, alpha_ref, sim_ref = refs
    nc, nb, modes, groups, band = dims
    mine = nc * nb
    no = coef_ref.shape[0]
    periods = field_ref.shape[0]
    power = coef_ref[0, mine:, :]
    for i in range(1, no):
        power += coef_ref[i, mine:, :]
    gain = jnp.sum(power, keepdims=True)
    alpha_ref[...] = jnp.broadcast_to(1.0 + gain, alpha_ref.shape)
    norm = norm_ref[0:1, :]
    for p in range(periods):
        vector = field_ref[p] / norm
        vector_ref[p] = vector
        rest = vector * -gain
        if not first:
            rest -= prior_ref[p] * norm
        next_ref[p] = rest

    def group(i, carry):
        coef = coef_ref[i, :mine, :].T
        for j in range(nc):
            for b in range(nb):
                off = all_ref[i, j * 2 * nb + b]
                period = off // groups
                row = j * band + off % groups * CR
                at = j * nb + b
                total = next_ref[period]
                for r in range(CR):
                    total += coef[r * modes:(r + 1) * modes, at:at + 1] * lat_ref[row + r]
                next_ref[period] = total
        return carry

    if no <= 4:
        for i in range(no):
            group(i, 0)
    else:
        lax.fori_loop(0, no, group, 0)
    if last:
        total = fold(next_ref)
        for c in range(nc):
            out_ref[c] = total
    else:
        forward(dims, next_ref, lat_ref, foot_ref, ids_ref, sim_ref, out_ref)


def finish_kernel(factor, own_ref, sum_ref, *refs):
    vectors, refs = refs[:STEPS], refs[STEPS:]
    field_ref, refs = refs[0], refs[1:]
    alphas, refs = refs[:STEPS], refs[STEPS:]
    norms, refs = refs[:STEPS - 1], refs[STEPS - 1:]
    out_ref, coef_ref = refs
    per_dev = out_ref.shape[1]
    total = sum_ref[0]
    for c in range(1, sum_ref.shape[0]):
        total += sum_ref[c]
    norm = jnp.sqrt(jnp.sum(total, keepdims=True))
    for l in range(per_dev):
        at = own_ref[0] * per_dev + l
        for k in range(STEPS):
            out_ref[k, l] = vectors[k][at] * factor
        out_ref[STEPS, l] = field_ref[at] / norm * factor
    row = lax.broadcasted_iota(jnp.int32, coef_ref.shape, 0)
    col = lax.broadcasted_iota(jnp.int32, coef_ref.shape, 1)
    coefs = jnp.zeros(coef_ref.shape, F32)
    for k in range(STEPS):
        beta = norms[k][0:1, 0:1] if k < STEPS - 1 else norm
        coefs = jnp.where((row == 0) & (col == k), alphas[k][0:1, 0:1], coefs)
        coefs = jnp.where((row == 1) & (col == k), beta, coefs)
    coef_ref[...] = coefs


def swap(array, axis):
    return lax.all_to_all(array, axis, split_axis=0, concat_axis=0, tiled=True)


def body(start, lat_mats, footprints, blk_sub, blk_off, counts, rinv):
    per_dev, held, lat_rows = start.shape
    nc = lax.axis_size("cell")
    no = lax.axis_size("obs")
    lon_cols = held * nc
    band = lat_rows // nc
    groups = band // CR
    nb, ob, _ = footprints.shape
    subs = counts.shape[0]
    modes = -(-held // 16) * 16
    mine = nc * nb
    periods = per_dev * no
    dims = (nc, nb, modes, groups, band)
    shape = functools.partial(jax.ShapeDtypeStruct, dtype=F32)

    valid = (jnp.arange(ob, dtype=jnp.int32)[None, :] < counts[:, None]).astype(F32)
    weights = rinv.reshape(subs, ob) * valid
    high, low = lon_table(lon_cols, nc, modes)
    if modes != held:
        start = jnp.pad(start, ((0, 0), (0, modes - held), (0, 0)))
        lat_mats = jnp.pad(lat_mats, ((0, modes - held), (0, 0), (0, 0)))
    lat = lat_mats.transpose(1, 0, 2)

    foot_rows = nb * CR * modes
    hats = call(
        functools.partial(transform_kernel, dims),
        jax.ShapeDtypeStruct((nc, foot_rows + 16, ob), BF16),
        [VMEM, VMEM, VMEM, SMEM, SMEM],
        jnp.asarray(high), jnp.asarray(low), footprints, blk_off, blk_sub,
    )
    foot = swap(hats, "cell")
    ids = foot[:, foot_rows, :2 * nb].astype(F32)
    tail = jnp.pad(ids.reshape(1, -1), ((0, ROWS - 1), (0, lat_rows - 2 * mine)))
    ids = ids.astype(jnp.int32)
    near = jnp.concatenate([start.reshape(per_dev * modes, lat_rows), tail], axis=0)
    near = swap(jnp.broadcast_to(near[None], (no,) + near.shape), "obs")
    every = near[:, per_dev * modes, :2 * mine].astype(jnp.int32)

    field_shape = shape((periods, modes, lat_rows))
    small = shape((ROWS, 128))
    sim_scratch = pltpu.VMEM((subs + ROWS, ob), F32)
    sims, field = call(
        functools.partial(first_kernel, dims),
        (shape((nc, subs + ROWS, ob)), field_shape),
        [VMEM, VMEM, VMEM, SMEM],
        near, lat, foot, ids,
        scratch=[sim_scratch],
    )
    vectors, alphas, norms = [], [], []
    for step in range(STEPS):
        last = step == STEPS - 1
        sims = swap(sims, "cell")
        coefs, norm = call(
            functools.partial(adjoint_kernel, dims),
            (shape((no, mine + subs, 128)), small),
            [VMEM, VMEM, VMEM, SMEM],
            sims, weights, foot, ids,
            scratch=[pltpu.VMEM((subs, ob), F32)],
        )
        coefs = swap(coefs, "obs")
        before = [vectors[-1]] if step else []
        sims, vector, field, alpha = call(
            functools.partial(image_kernel, dims, step == 0, last),
            (
                shape((nc, ROWS if last else subs + ROWS, 128)),
                field_shape,
                field_shape,
                small,
            ),
            [VMEM] * (5 + len(before)) + [SMEM, SMEM],
            coefs, norm, field, *before, lat, foot, ids, every,
            scratch=[sim_scratch],
        )
        vectors.append(vector)
        alphas.append(alpha)
        norms.append(norm)
    sums = swap(sims, "cell")
    factor = math.sqrt(periods * lon_cols * lat_rows)
    own = lax.axis_index("obs").astype(jnp.int32).reshape(1)
    krylov, coeffs = call(
        functools.partial(finish_kernel, factor),
        (shape((STEPS + 1, per_dev, modes, lat_rows)), shape((2, STEPS))),
        [SMEM] + [VMEM] * (1 + STEPS + 1 + STEPS + STEPS - 1),
        own, sums, *vectors, field, *alphas, *norms[1:],
    )
    return krylov[:, :, :held], coeffs


def solution(mesh):
    placed = (
        P("obs", "cell", None),
        P("cell", None, None),
        P(("obs", "cell"), None, None),
        P(("obs", "cell")),
        P(("obs", "cell")),
        P("obs"),
        P("obs"),
    )
    return jax.shard_map(
        body,
        mesh=mesh,
        in_specs=placed,
        out_specs=(P(None, "obs", "cell", None), P()),
        check_vma=False,
    )
```

time: 650 us -> 109 us (0.17); the launches traced: 638 us -> 108 us
  blocking collectives: 393 us -> 44.6 us
  matrix products: 62.7 us -> 0 us
  other arithmetic: 45.4 us -> 0.85 us
  waiting for transfers between devices: 58.1 us -> 17.4 us
  local copies, waits for them, and re-layouts: 53.8 us -> 16.4 us
  between operations: 17.1 us -> 0.78 us
  Pallas kernels: 0 us -> 13.5 us
  starting transfers between devices: 7.74 us -> 14.8 us
    psum x10 -> x0, blocking collectives: 315 us -> none  [the longest x3 124 us: body(): beta = jnp.sqrt(lax.psum(jnp.sum(direction * direction), ('obs', 'cell')))]
    dot_general x24 -> x0, matrix products: 62.7 us -> none  [the longest x3 17.1 us: body(): hessian_coef = jnp.einsum('pan,mn->pam', back, table, precision=HIGH)]
    reduce_scatter x3 -> x0, waiting for transfers between devices: 50.4 us -> none  [body(): lax.psum_scatter(placed.reshape(count, band, lon_cols), 'obs', scatter_di...]
    all_gather x3 -> x0, blocking collectives: 41.4 us -> none  [body(): every = lax.all_gather(grid, 'obs', axis=0, tiled=True)]
    unnamed x6 -> x0, other arithmetic: 14.6 us -> none
    pallas_call x0 -> x9, Pallas kernels: none -> 13.5 us  [call(): pl.pallas_call(kernel, out_shape=outs, in_specs=specs, out_specs=jax.tree...]
    all_to_all x6 -> x0, other arithmetic: 11.2 us -> none  [the longest x3 6.24 us: body(): lax.all_to_all(spread, 'cell', split_axis=2, concat_axis=1, tiled=True)]
    all_to_all x2 -> x4, waiting for transfers between devices: 7.65 us -> 17.4 us  [swap(): return lax.all_to_all(array, axis, split_axis=0, concat_axis=0, tiled=True)]
  transfers between devices with their start and end apart: 5 -> 4, of which waited for: 5 -> 4; matrix products, arithmetic and copies ran while one was open for 0% -> 3% of each run, Pallas kernels for 0% -> 0%
where the time goes in v1:
time: 109 us; the launch traced here: 108 us
  blocking collectives  44.6 us (41%)
  waiting for transfers between devices  17.4 us (16%)
  local copies, waits for them, and re-layouts  16.4 us (15%)
  starting transfers between devices  14.8 us (14%)
  Pallas kernels  13.5 us (12%)
    all_to_all x5, blocking collectives, swap(): return lax.all_to_all(array, axis, split_axis=0, concat_axis=0, tiled=True)  44.6 us
    all_to_all x4, waiting for transfers between devices, swap(): return lax.all_to_all(array, axis, split_axis=0, concat_axis=0, tiled=True)  17.4 us
    unnamed x41, local copies, waits for them, and re-layouts  15.6 us
    all_to_all x4, starting transfers between devices, swap(): return lax.all_to_all(array, axis, split_axis=0, concat_axis=0, tiled=True)  14.8 us
    pallas_call x9, Pallas kernels, call(): pl.pallas_call(kernel, out_shape=outs, in_specs=specs, out_specs=jax.tree...  13.5 us
  transfers between devices with their start and end apart: 4, of which 4 were waited for; matrix products, arithmetic and copies ran while one was open for 3% of the time, Pallas kernels for 0%

profile of v1, /device:TPU:0, one launch (start us, length us, event | category | flops | bytes accessed | tf_op | source)
XLA Modules:
  0.0 108.3 jit_solution(12039667017083999948)
XLA Ops:
  0.6 0.0 copy-start.4
  0.6 1.0 copy-done.4
  1.6 1.0 copy-done.5
  2.6 1.0 copy-done.6
  3.6 0.7 copy-done.16
  4.2 0.7 copy-done.17
  4.9 1.3 %shard_map.104 = bf16[8,208,128]{2,1,0:T(8,128)(2,1)S(1)} custom-call(bf16[384,384]{1,0:T(8,128)(2,1)S(1)} %copy-done.5, bf16[384,384]{1,0:T(8,128)(2,1)S(1)} %copy-done.6, bf16[2,128,768]{2,1,0:T(8,128)(2,1)S(1)} %copy-done.4, s32[2]{0:T(128)S(1)} %copy-done.16, s32[2]{0:T(128)S(1)} %copy-done.17), custom_call_target="tpu_custom_call" | custom-call | tf_op jit(solution)/shard_map/pallas_call | solution.py:37
  6.2 13.7 %all_to_all.45.foot_ref.refs_4_.refs_5_ = bf16[8,208,128]{2,1,0:T(8,128)(2,1)S(1)} all-to-all(bf16[8,208,128]{2,1,0:T(8,128)(2,1)S(1)} %shard_map.104), channel_id=1, replica_groups=mesh['obs'=4,'cell'=8] {'cell'}, dimensions={0} | all-to-all | bytes 851968 | tf_op jit(solution)/shard_map/all_to_all | solution.py:222
  19.9 0.8 copy-done
  20.6 0.1 convert_element_type.27
  20.7 0.7 pad_maximum_fusion
  21.5 0.7 broadcast_in_dim.2
  22.1 4.9 %all-to-all-start.1 = ((f32[4,56,128]{2,1,0:T(8,128)}), f32[4,56,128]{2,1,0:T(8,128)S(1)}, u32[]{:S(2)}, u32[]{:S(2)}) async-start(f32[4,56,128]{2,1,0:T(8,128)} %broadcast_in_dim.2), calls=%async_computation.1 | async-start | bytes 229376 | tf_op jit(solution)/shard_map/all_to_all | solution.py:222
  27.0 3.7 %copy.40 = f32[48,128,128]{2,0,1:T(8,128)S(1)} copy(f32[48,128,128]{2,1,0:T(8,128)} %param.10) | data formatting | bytes 6291456 | tf_op args[1]
  30.7 0.0 copy-start.18
  30.7 0.0 copy-start.19
  30.7 2.1 %all-to-all-done.1.near_ref = f32[4,56,128]{2,1,0:T(8,128)S(1)} async-done(((f32[4,56,128]{2,1,0:T(8,128)}), f32[4,56,128]{2,1,0:T(8,128)S(1)}, u32[]{:S(2)}, u32[]{:S(2)}) %all-to-all-start.1) | async-done | bytes 114720 | tf_op jit(solution)/shard_map/all_to_all | solution.py:222
  32.9 1.0 copy-done.1
  33.9 1.5 %shard_map.105 = (f32[8,16,128]{2,1,0:T(8,128)}, f32[4,48,128]{2,1,0:T(8,128)S(1)}) custom-call(f32[4,56,128]{2,1,0:T(8,128)S(1)} %all-to-all-done.1.near_ref, f32[128,48,128]{2,1,0:T(8,128)S(1)} %bitcast.9, bf16[8,208,128]{2,1,0:T(8,128)(2,1)S(1)} %copy-done.1, s32[8,4]{1,0:T(8,128)S(1)} %bitcast.13), custom_call_target="tpu_custom_call" | custom-call | tf_op jit(solution)/shard_map/pallas_call | solution.py:37
  35.4 3.4 %all-to-all-start.2 = ((f32[8,16,128]{2,1,0:T(8,128)}), f32[8,16,128]{2,1,0:T(8,128)S(1)}, u32[]{:S(2)}, u32[]{:S(2)}) async-start(f32[8,16,128]{2,1,0:T(8,128)} %get-tuple-element.22), calls=%async_computation.2 | async-start | bytes 131072 | tf_op jit(solution)/shard_map/all_to_all | solution.py:222
  38.8 0.0 copy-done.18
  38.8 0.0 copy-done.19
  38.8 0.1 bitcast_select_fusion.weight_ref
  38.9 4.9 %all-to-all-done.2.sim_ref = f32[8,16,128]{2,1,0:T(8,128)S(1)} async-done(((f32[8,16,128]{2,1,0:T(8,128)}), f32[8,16,128]{2,1,0:T(8,128)S(1)}, u32[]{:S(2)}, u32[]{:S(2)}) %all-to-all-start.2) | async-done | bytes 65568 | tf_op jit(solution)/shard_map/all_to_all | solution.py:222
  43.7 1.0 copy-done.2
  44.8 1.7 %shard_map.106 = (f32[4,24,128]{2,1,0:T(8,128)}, f32[8,128]{1,0:T(8,128)S(1)}) custom-call(f32[8,16,128]{2,1,0:T(8,128)S(1)} %all-to-all-done.2.sim_ref, f32[8,128]{1,0:T(8,128)S(1)} %bitcast_select_fusion.weight_ref, bf16[8,208,128]{2,1,0:T(8,128)(2,1)S(1)} %copy-done.2, s32[8,4]{1,0:T(8,128)S(1)} %bitcast.14), custom_call_target="tpu_custom_call" | custom-call | tf_op jit(solution)/shard_map/pallas_call | solution.py:37
  46.4 3.3 %all-to-all-start.3 = ((f32[4,24,128]{2,1,0:T(8,128)}), f32[4,24,128]{2,1,0:T(8,128)S(1)}, u32[]{:S(2)}, u32[]{:S(2)}) async-start(f32[4,24,128]{2,1,0:T(8,128)} %get-tuple-element.23), calls=%async_computation.3 | async-start | bytes 98304 | tf_op jit(solution)/shard_map/all_to_all | solution.py:222
  49.7 5.7 %all-to-all-done.3.refs_0_ = f32[4,24,128]{2,1,0:T(8,128)S(1)} async-done(((f32[4,24,128]{2,1,0:T(8,128)}), f32[4,24,128]{2,1,0:T(8,128)S(1)}, u32[]{:S(2)}, u32[]{:S(2)}) %all-to-all-start.3) | async-done | bytes 49184 | tf_op jit(solution)/shard_map/all_to_all | solution.py:222
  55.4 1.0 copy-done.3
  56.4 2.1 %shard_map.107 = (f32[8,16,128]{2,1,0:T(8,128)S(1)}, f32[4,48,128]{2,1,0:T(8,128)S(1)}, f32[4,48,128]{2,1,0:T(8,128)S(1)}, f32[8,128]{1,0:T(8,128)S(1)}) custom-call(f32[4,24,128]{2,1,0:T(8,128)S(1)} %all-to-all-done.3.refs_0_, f32[8,128]{1,0:T(8,128)S(1)} %get-tuple-element.24.refs_1_, f32[4,48,128]{2,1,0:T(8,128)S(1)} %get-tuple-element.25.refs_2_, ...), custom_call_target="tpu_custom_call" | custom-call | tf_op jit(solution)/shard_map/pallas_call | solution.py:37
  58.5 0.6 copy-done.10
  59.1 7.4 %all_to_all.46.sim_ref = f32[8,16,128]{2,1,0:T(8,128)S(1)} all-to-all(f32[8,16,128]{2,1,0:T(8,128)S(1)} %get-tuple-element.26), channel_id=1, replica_groups=mesh['obs'=4,'cell'=8] {'cell'}, dimensions={0} | all-to-all | bytes 131072 | tf_op jit(solution)/shard_map/all_to_all | solution.py:222
  66.5 1.1 shard_map.108
  67.6 8.1 %all_to_all.47.refs_0_ = f32[4,24,128]{2,1,0:T(8,128)S(1)} all-to-all(f32[4,24,128]{2,1,0:T(8,128)S(1)} %get-tuple-element.27), channel_id=1, replica_groups=mesh['obs'=4,'cell'=8] {'obs'}, dimensions={0} | all-to-all | bytes 98304 | tf_op jit(solution)/shard_map/all_to_all | solution.py:222
  75.6 2.1 %shard_map.109 = (f32[8,16,128]{2,1,0:T(8,128)S(1)}, f32[4,48,128]{2,1,0:T(8,128)S(1)}, f32[4,48,128]{2,1,0:T(8,128)S(1)}, f32[8,128]{1,0:T(8,128)S(1)}) custom-call(f32[4,24,128]{2,1,0:T(8,128)S(1)} %all_to_all.47.refs_0_, f32[8,128]{1,0:T(8,128)S(1)} %get-tuple-element.28.refs_1_.refs_7_, f32[4,48,128]{2,1,0:T(8,128)S(1)} %get-tuple-element.29.refs_2_, ...), custom_call_target="tpu_custom_call" | custom-call | tf_op jit(solution)/shard_map/pallas_call | solution.py:37
  77.8 7.4 %all_to_all.48.sim_ref = f32[8,16,128]{2,1,0:T(8,128)S(1)} all-to-all(f32[8,16,128]{2,1,0:T(8,128)S(1)} %get-tuple-element.31), channel_id=1, replica_groups=mesh['obs'=4,'cell'=8] {'cell'}, dimensions={0} | all-to-all | bytes 131072 | tf_op jit(solution)/shard_map/all_to_all | solution.py:222
  85.2 1.1 shard_map.110
  86.2 8.1 %all_to_all.49.refs_0_ = f32[4,24,128]{2,1,0:T(8,128)S(1)} all-to-all(f32[4,24,128]{2,1,0:T(8,128)S(1)} %get-tuple-element.32), channel_id=1, replica_groups=mesh['obs'=4,'cell'=8] {'obs'}, dimensions={0} | all-to-all | bytes 98304 | tf_op jit(solution)/shard_map/all_to_all | solution.py:222
  94.3 1.8 %shard_map.111 = (f32[8,8,128]{2,1,0:T(8,128)S(1)}, f32[4,48,128]{2,1,0:T(8,128)S(1)}, f32[4,48,128]{2,1,0:T(8,128)S(1)}, f32[8,128]{1,0:T(8,128)S(1)}) custom-call(f32[4,24,128]{2,1,0:T(8,128)S(1)} %all_to_all.49.refs_0_, f32[8,128]{1,0:T(8,128)S(1)} %get-tuple-element.33.refs_1_.refs_8_, f32[4,48,128]{2,1,0:T(8,128)S(1)} %get-tuple-element.34.refs_2_, ...), custom_call_target="tpu_custom_call" | custom-call | tf_op jit(solution)/shard_map/pallas_call | solution.py:37
  96.1 0.0 copy-start.7
  96.1 0.6 copy-done.7
  96.7 3.3 %all-to-all-start.8 = ((f32[8,8,128]{2,1,0:T(8,128)}), f32[8,8,128]{2,1,0:T(8,128)S(1)}, u32[]{:S(2)}, u32[]{:S(2)}) async-start(f32[8,8,128]{2,1,0:T(8,128)} %copy-done.7), calls=%async_computation.8 | async-start | bytes 65536 | tf_op jit(solution)/shard_map/all_to_all | solution.py:222
  100.0 4.8 %all-to-all-done.8.sum_ref = f32[8,8,128]{2,1,0:T(8,128)S(1)} async-done(((f32[8,8,128]{2,1,0:T(8,128)}), f32[8,8,128]{2,1,0:T(8,128)S(1)}, u32[]{:S(2)}, u32[]{:S(2)}) %all-to-all-start.8) | async-done | bytes 32800 | tf_op jit(solution)/shard_map/all_to_all | solution.py:222
  104.8 0.7 copy-done.9
  105.5 0.7 copy-done.11
  106.2 0.7 copy-done.13
  106.9 0.7 copy-done.15
  107.5 0.8 shard_map.112
  (22 shorter events, 0.1 us)
Async XLA Ops:
  0.6 1.0 copy-start.4
  1.6 1.0 copy-start.5
  2.6 1.0 copy-start.6
  3.6 0.7 copy-start.16
  4.2 0.7 copy-start.17
  19.9 0.8 copy-start
  22.1 10.7 %all-to-all-start.1 = ((f32[4,56,128]{2,1,0:T(8,128)}), f32[4,56,128]{2,1,0:T(8,128)S(1)}, u32[]{:S(2)}, u32[]{:S(2)}) async-start(f32[4,56,128]{2,1,0:T(8,128)} %broadcast_in_dim.2), calls=%async_computation.1 | async-start | bytes 229376 | tf_op jit(solution)/shard_map/all_to_all | solution.py:222
  30.7 8.1 %copy-start.18 = (f32[1024]{0:T(1024)S(1)}, f32[1024]{0:T(1024)}, u32[]{:S(2)}) copy-start(f32[1024]{0:T(1024)} %param.15) | copy-start | bytes 12292
  30.7 8.1 %copy-start.19 = (s32[8]{0:T(128)S(1)}, s32[8]{0:T(128)}, u32[]{:S(2)}) copy-start(s32[8]{0:T(128)} %param.14) | copy-start | bytes 100
  32.9 1.0 copy-start.1
  35.4 8.3 %all-to-all-start.2 = ((f32[8,16,128]{2,1,0:T(8,128)}), f32[8,16,128]{2,1,0:T(8,128)S(1)}, u32[]{:S(2)}, u32[]{:S(2)}) async-start(f32[8,16,128]{2,1,0:T(8,128)} %get-tuple-element.22), calls=%async_computation.2 | async-start | bytes 131072 | tf_op jit(solution)/shard_map/all_to_all | solution.py:222
  43.7 1.0 copy-start.2
  46.4 8.9 %all-to-all-start.3 = ((f32[4,24,128]{2,1,0:T(8,128)}), f32[4,24,128]{2,1,0:T(8,128)S(1)}, u32[]{:S(2)}, u32[]{:S(2)}) async-start(f32[4,24,128]{2,1,0:T(8,128)} %get-tuple-element.23), calls=%async_computation.3 | async-start | bytes 98304 | tf_op jit(solution)/shard_map/all_to_all | solution.py:222
  55.4 1.0 copy-start.3
  58.5 0.6 copy-start.10
  77.7 16.5 %copy-start.12 = (f32[8,128]{1,0:T(8,128)}, f32[8,128]{1,0:T(8,128)S(1)}, u32[]{:S(2)}) copy-start(f32[8,128]{1,0:T(8,128)S(1)} %get-tuple-element.40.refs_5_) | copy-start | bytes 12292
  86.2 9.8 %copy-start.8 = (f32[8,128]{1,0:T(8,128)}, f32[8,128]{1,0:T(8,128)S(1)}, u32[]{:S(2)}) copy-start(f32[8,128]{1,0:T(8,128)S(1)} %get-tuple-element.33.refs_1_.refs_8_) | copy-start | bytes 12292
  96.1 0.6 copy-start.7
  96.7 8.1 %copy-start.14 = (f32[8,128]{1,0:T(8,128)}, f32[8,128]{1,0:T(8,128)S(1)}, u32[]{:S(2)}) copy-start(f32[8,128]{1,0:T(8,128)S(1)} %get-tuple-element.41.refs_6_) | copy-start | bytes 12292
  96.7 8.1 %all-to-all-start.8 = ((f32[8,8,128]{2,1,0:T(8,128)}), f32[8,8,128]{2,1,0:T(8,128)S(1)}, u32[]{:S(2)}, u32[]{:S(2)}) async-start(f32[8,8,128]{2,1,0:T(8,128)} %copy-done.7), calls=%async_computation.8 | async-start | bytes 65536 | tf_op jit(solution)/shard_map/all_to_all | solution.py:222
  104.8 0.7 copy-start.9
  105.5 0.7 copy-start.11
  106.2 0.7 copy-start.13
  106.8 0.7 copy-start.15

commit v2 on v1

v2 whole, which is shorter than its diff:
```python
import functools
import math

import jax
import jax.numpy as jnp
import ml_dtypes
import numpy as np
from jax import lax
from jax.experimental import pallas as pl
from jax.experimental.pallas import tpu as pltpu
from jax.sharding import PartitionSpec as P

CR = 2
STEPS = 3
ROWS = 8
VMEM = pl.BlockSpec(memory_space=pltpu.VMEM)
ANY = pl.BlockSpec(memory_space=pl.ANY)
SMEM = pl.BlockSpec(memory_space=pltpu.SMEM)
F32 = jnp.float32
BF16 = jnp.bfloat16


def lon_table(order, parts, padded):
    index = np.arange(order)
    half = order // 2
    freq = np.where(index <= half, index, index - half)[:, None]
    phase = (freq * index[None, :] % order) * (2.0 * math.pi / order)
    factor = np.where((index == 0) | (index == half), math.sqrt(1.0 / order), math.sqrt(2.0 / order))
    table = np.where(index[:, None] <= half, np.cos(phase), np.sin(phase)) * factor[:, None]
    table = table.reshape(parts, order // parts, order)
    table = np.pad(table, ((0, 0), (0, padded - order // parts), (0, 0))).reshape(parts * padded, order)
    high = table.astype(np.float32).astype(ml_dtypes.bfloat16)
    low = (table - high.astype(np.float64)).astype(np.float32).astype(ml_dtypes.bfloat16)
    return high, low


def call(kernel, outs, specs, *args, scratch=()):
    return pl.pallas_call(
        kernel,
        out_shape=outs,
        in_specs=specs,
        out_specs=jax.tree.map(lambda _: VMEM, outs),
        scratch_shapes=scratch,
        compiler_params=pltpu.CompilerParams(vmem_limit_bytes=8 * 1024 * 1024),
    )(*args)


def tree_sum(parts):
    parts = list(parts)
    while len(parts) > 1:
        parts = [sum(parts[at:at + 2][1:], parts[at]) for at in range(0, len(parts), 2)]
    return parts[0]


def transform_kernel(dims, own_ref, high_any, low_any, foot_any, off_any, sub_any, *refs):
    nc, nb, modes, groups, band = dims
    outs, refs = refs[:nc], refs[nc:]
    high_ref, low_ref, foot_ref, off_ref, sub_ref, hats_ref, sems = refs
    copies = [
        pltpu.make_async_copy(source, target, sems.at[at])
        for at, (source, target) in enumerate(
            [
                (foot_any, foot_ref),
                (high_any, high_ref),
                (low_any, low_ref),
                (off_any, off_ref),
                (sub_any, sub_ref),
            ]
        )
    ]
    for copy in copies:
        copy.start()
    for copy in copies:
        copy.wait()
    ob = foot_ref.shape[1]
    lon = high_ref.shape[1]
    contract = (((1,), (1,)), ((), ()))
    for b in range(nb):
        for r in range(CR):
            foot = foot_ref[b, :, r * lon:(r + 1) * lon]
            hat = lax.dot_general(high_ref[...], foot, contract, preferred_element_type=F32)
            hat += lax.dot_general(low_ref[...], foot, contract, preferred_element_type=F32)
            hat = hat.astype(BF16)
            at = (b * CR + r) * modes
            for c in range(nc):
                hats_ref[c, at:at + modes, :] = hat[c * modes:(c + 1) * modes, :]
    lane = lax.broadcasted_iota(jnp.int32, (16, ob), 1)
    ids = jnp.zeros((16, ob), F32)
    for b in range(nb):
        ids = jnp.where(lane == b, off_ref[b].astype(F32), ids)
        ids = jnp.where(lane == nb + b, sub_ref[b].astype(F32), ids)
    ids = ids.astype(BF16)
    for s in range(nc):
        outs[s][:nb * CR * modes, :] = hats_ref[own_ref[1] ^ s]
        outs[s][nb * CR * modes:, :] = ids


def fold(ref):
    periods, modes, _ = ref.shape
    total = jnp.zeros((ROWS, ref.shape[2]), F32)
    for p in range(periods):
        for at in range(0, modes, ROWS):
            part = ref[p, at:at + ROWS, :]
            total += part * part
    return total


def forward(dims, own_ref, field_ref, lat_ref, foot_refs, ids_ref, out_ref):
    nc, nb, modes, groups, band = dims
    subs = out_ref.shape[0] - ROWS
    out_ref[:subs] = jnp.zeros((subs, out_ref.shape[1]), F32)
    for s in range(nc):
        for b in range(nb):
            off = ids_ref[s, b]
            sub = ids_ref[s, nb + b]
            period = off // groups
            row = (own_ref[1] ^ s) * band + off % groups * CR
            total = None
            for r in range(CR):
                column = jnp.sum(lat_ref[row + r] * field_ref[period], axis=1, keepdims=True)
                at = (b * CR + r) * modes
                term = foot_refs[s][at:at + modes, :].astype(F32) * column
                total = term if total is None else total + term
            out_ref[pl.ds(sub, 1), :] += jnp.sum(total, axis=0, keepdims=True)
    out_ref[subs:, :] = fold(field_ref)


def first_kernel(dims, no, own_ref, ids_ref, lat_ref, *refs):
    nc, _, modes, _, _ = dims
    near_refs, refs = refs[:no], refs[no:]
    foot_refs, refs = refs[:nc], refs[nc:]
    out_ref, field_ref = refs
    per_dev = field_ref.shape[0] // no
    for s in range(no):
        for l in range(per_dev):
            field_ref[(own_ref[0] ^ s) * per_dev + l] = near_refs[s][l]
    forward(dims, own_ref, field_ref, lat_ref, foot_refs, ids_ref, out_ref)


def adjoint_kernel(dims, tails, ids_ref, weight_ref, *refs):
    nc, nb, modes, groups, band = dims
    sim_refs, refs = refs[:nc], refs[nc:]
    foot_refs, refs = refs[:nc], refs[nc:]
    tail_refs, refs = refs[:tails], refs[tails:]
    out_ref, norm_ref, weighted_ref = refs
    subs = weight_ref.shape[0]
    mine = nc * nb
    total = tree_sum(ref[...] for ref in sim_refs)
    norm = jnp.sqrt(jnp.sum(total[subs:], keepdims=True))
    norm_ref[...] = jnp.broadcast_to(norm, norm_ref.shape)
    sim = total[:subs] / norm
    weighted = sim * weight_ref[...]
    weighted_ref[...] = weighted
    lane = lax.broadcasted_iota(jnp.int32, (modes, 128), 1)
    parts = [jnp.zeros((modes, 128), F32) for _ in range(CR)]
    for s in range(nc):
        for b in range(nb):
            chosen = weighted_ref[pl.ds(ids_ref[s, nb + b], 1), :]
            for r in range(CR):
                at = (b * CR + r) * modes
                column = jnp.sum(foot_refs[s][at:at + modes, :].astype(F32) * chosen, axis=1, keepdims=True)
                parts[r] = jnp.where(lane == s * nb + b, column, parts[r])
    rest = 128 - CR * modes
    if rest:
        parts.append(jnp.zeros((rest, 128), F32))
    rows = jnp.concatenate(parts, axis=0).T
    out_ref[:mine, :] = rows[:mine]
    out_ref[mine:mine + subs, :] = sim * weighted
    for tail_ref in tail_refs:
        out_ref[mine + subs:, :] = tail_ref[...]


def image_kernel(dims, no, first, last, own_ref, ids_ref, all_ref, lat_ref, norm_ref, field_ref, *refs):
    nc, nb, modes, groups, band = dims
    if not first:
        prior_ref, refs = refs[0], refs[1:]
    coef_refs, refs = refs[:no], refs[no:]
    foot_refs, refs = refs[:nc], refs[nc:]
    out_ref, vector_ref, next_ref, alpha_ref, held_ref = refs
    mine = nc * nb
    periods = field_ref.shape[0]
    subs = ROWS
    for s in range(no):
        held_ref[s] = coef_refs[s][:mine, :]
    gain = jnp.sum(tree_sum(ref[mine:mine + subs, :] for ref in coef_refs), keepdims=True)
    alpha_ref[...] = jnp.broadcast_to(1.0 + gain, alpha_ref.shape)
    norm = norm_ref[0:1, :]
    for p in range(periods):
        vector = field_ref[p] / norm
        vector_ref[p] = vector
        rest = vector * -gain
        if not first:
            rest -= prior_ref[p] * norm
        next_ref[p] = rest

    def group(i, carry):
        at_i = own_ref[0] ^ i
        coef = held_ref[at_i].T
        for s in range(nc):
            for b in range(nb):
                at = s * nb + b
                off = all_ref[at_i, s * 2 * nb + b]
                period = off // groups
                row = (own_ref[1] ^ s) * band + off % groups * CR
                total = next_ref[period]
                for r in range(CR):
                    total += coef[r * modes:(r + 1) * modes, at:at + 1] * lat_ref[row + r]
                next_ref[period] = total
        return carry

    if no <= 4:
        for i in range(no):
            group(i, 0)
    else:
        lax.fori_loop(0, no, group, 0)
    if last:
        out_ref[...] = fold(next_ref)
    else:
        forward(dims, own_ref, next_ref, lat_ref, foot_refs, ids_ref, out_ref)


def finish_kernel(factor, nc, own_ref, *refs):
    sum_refs, refs = refs[:nc], refs[nc:]
    vectors, refs = refs[:STEPS], refs[STEPS:]
    field_ref, refs = refs[0], refs[1:]
    alphas, refs = refs[:STEPS], refs[STEPS:]
    norms, refs = refs[:STEPS - 1], refs[STEPS - 1:]
    out_ref, coef_ref = refs
    per_dev = out_ref.shape[1]
    norm = jnp.sqrt(jnp.sum(tree_sum(ref[...] for ref in sum_refs), keepdims=True))
    for l in range(per_dev):
        at = own_ref[2] * per_dev + l
        for k in range(STEPS):
            out_ref[k, l] = vectors[k][at] * factor
        out_ref[STEPS, l] = field_ref[at] / norm * factor
    row = lax.broadcasted_iota(jnp.int32, coef_ref.shape, 0)
    col = lax.broadcasted_iota(jnp.int32, coef_ref.shape, 1)
    coefs = jnp.zeros(coef_ref.shape, F32)
    for k in range(STEPS):
        beta = norms[k][0:1, 0:1] if k < STEPS - 1 else norm
        coefs = jnp.where((row == 0) & (col == k), alphas[k][0:1, 0:1], coefs)
        coefs = jnp.where((row == 1) & (col == k), beta, coefs)
    coef_ref[...] = coefs


def permuted(size):
    return size <= 8 and size & (size - 1) == 0


def share(arrays, axis):
    size = lax.axis_size(axis)
    arrays = arrays if isinstance(arrays, (list, tuple)) else [arrays] * size
    if permuted(size):
        return [
            arrays[s] if s == 0 else lax.ppermute(arrays[s], axis, [(d, d ^ s) for d in range(size)])
            for s in range(size)
        ]
    swapped = lax.all_to_all(jnp.stack(arrays), axis, split_axis=0, concat_axis=0, tiled=True)
    return [swapped[s] for s in range(size)]


def body(start, lat_mats, footprints, blk_sub, blk_off, counts, rinv):
    per_dev, held, lat_rows = start.shape
    nc = lax.axis_size("cell")
    no = lax.axis_size("obs")
    lon_cols = held * nc
    band = lat_rows // nc
    groups = band // CR
    nb, ob, _ = footprints.shape
    subs = counts.shape[0]
    modes = -(-held // 16) * 16
    mine = nc * nb
    periods = per_dev * no
    dims = (nc, nb, modes, groups, band)
    shape = functools.partial(jax.ShapeDtypeStruct, dtype=F32)

    valid = (jnp.arange(ob, dtype=jnp.int32)[None, :] < counts[:, None]).astype(F32)
    weights = rinv.reshape(subs, ob) * valid
    high, low = lon_table(lon_cols, nc, modes)
    if modes != held:
        start = jnp.pad(start, ((0, 0), (0, modes - held), (0, 0)))
        lat_mats = jnp.pad(lat_mats, ((0, modes - held), (0, 0), (0, 0)))
    lat = lat_mats.transpose(1, 0, 2)
    at_obs = lax.axis_index("obs").astype(jnp.int32)
    at_cell = lax.axis_index("cell").astype(jnp.int32)
    own = jnp.stack([at_obs if permuted(no) else 0 * at_obs, at_cell if permuted(nc) else 0 * at_cell, at_obs])

    near = share(start, "obs")
    foot_rows = nb * CR * modes
    hats = call(
        functools.partial(transform_kernel, dims),
        [jax.ShapeDtypeStruct((foot_rows + 16, ob), BF16)] * nc,
        [SMEM] + [ANY] * 5,
        own, jnp.asarray(high), jnp.asarray(low), footprints, blk_off, blk_sub,
        scratch=[
            pltpu.VMEM(high.shape, BF16),
            pltpu.VMEM(low.shape, BF16),
            pltpu.VMEM(footprints.shape, BF16),
            pltpu.SMEM((nb,), jnp.int32),
            pltpu.SMEM((nb,), jnp.int32),
            pltpu.VMEM((nc, foot_rows, ob), BF16),
            pltpu.SemaphoreType.DMA((5,)),
        ],
    )
    foot = share(hats, "cell")
    ids = jnp.stack([part[foot_rows, :2 * nb] for part in foot]).astype(F32)
    tail = jnp.pad(ids.reshape(1, -1), ((0, ROWS - 1), (0, 128 - 2 * mine)))
    ids = ids.astype(jnp.int32)

    field_shape = shape((periods, modes, lat_rows))
    small = shape((ROWS, 128))
    sims, field = call(
        functools.partial(first_kernel, dims, no),
        (shape((subs + ROWS, ob)), field_shape),
        [SMEM, SMEM] + [VMEM] * (1 + no + nc),
        own, ids, lat, *near, *foot,
    )
    vectors, alphas, norms = [], [], []
    for step in range(STEPS):
        last = step == STEPS - 1
        tails = [] if step else [tail]
        coefs, norm = call(
            functools.partial(adjoint_kernel, dims, len(tails)),
            (shape((mine + subs + ROWS * len(tails), 128)), small),
            [SMEM] + [VMEM] * (1 + 2 * nc + len(tails)),
            ids, weights, *share(sims, "cell"), *foot, *tails,
            scratch=[pltpu.VMEM((subs, ob), F32)],
        )
        coefs = share(coefs, "obs")
        if step == 0:
            every = jnp.stack([part[mine + subs, :2 * mine] for part in coefs]).astype(jnp.int32)
        before = [vectors[-1]] if step else []
        sims, vector, field, alpha = call(
            functools.partial(image_kernel, dims, no, step == 0, last),
            (
                shape((ROWS if last else subs + ROWS, 128)),
                field_shape,
                field_shape,
                small,
            ),
            [SMEM] * 3 + [VMEM] * (3 + len(before) + no + nc),
            own, ids, every, lat, norm, field, *before, *coefs, *foot,
            scratch=[pltpu.VMEM((no, mine, 128), F32)],
        )
        vectors.append(vector)
        alphas.append(alpha)
        norms.append(norm)
    factor = math.sqrt(periods * lon_cols * lat_rows)
    krylov, coeffs = call(
        functools.partial(finish_kernel, factor, nc),
        (shape((STEPS + 1, per_dev, modes, lat_rows)), shape((2, STEPS))),
        [SMEM] + [VMEM] * (nc + STEPS + 1 + STEPS + STEPS - 1),
        own, *share(sims, "cell"), *vectors, field, *alphas, *norms[1:],
    )
    return krylov[:, :, :held], coeffs


def solution(mesh):
    placed = (
        P("obs", "cell", None),
        P("cell", None, None),
        P(("obs", "cell"), None, None),
        P(("obs", "cell")),
        P(("obs", "cell")),
        P("obs"),
        P("obs"),
    )
    return jax.shard_map(
        body,
        mesh=mesh,
        in_specs=placed,
        out_specs=(P(None, "obs", "cell", None), P()),
        check_vma=False,
    )
```

time: 109 us -> 104 us (0.954)
  blocking collectives: 44.6 us -> 0 us
  starting transfers between devices: 14.8 us -> 50.5 us
  local copies, waits for them, and re-layouts: 16.4 us -> 19.6 us
    ppermute x0 -> x47, starting transfers between devices: none -> 50.5 us  [share(): lax.ppermute(arrays[s], axis, [(d, d ^ s) for d in range(size)])]
    all_to_all x5 -> x0, blocking collectives: 44.6 us -> none  [swap(): return lax.all_to_all(array, axis, split_axis=0, concat_axis=0, tiled=True)]
    all_to_all x4 -> x0, waiting for transfers between devices: 17.4 us -> none  [swap(): return lax.all_to_all(array, axis, split_axis=0, concat_axis=0, tiled=True)]
    ppermute x0 -> x47, waiting for transfers between devices: none -> 16.6 us  [share(): lax.ppermute(arrays[s], axis, [(d, d ^ s) for d in range(size)])]
    all_to_all x4 -> x0, starting transfers between devices: 14.8 us -> none  [swap(): return lax.all_to_all(array, axis, split_axis=0, concat_axis=0, tiled=True)]
    slice x0 -> x12, local copies, waits for them, and re-layouts: none -> 3.72 us  [the longest x8 3.72 us: body(): ids = jnp.stack([part[foot_rows, :2 * nb] for part in foot]).astype(F32)]
    unnamed x41 -> x35, local copies, waits for them, and re-layouts: 15.6 us -> 15.1 us
  transfers between devices with their start and end apart: 4 -> 47, of which waited for: 4 -> 21; matrix products, arithmetic and copies ran while one was open for 3% -> 9% of each run, Pallas kernels for 0% -> 0%
where the time goes in v2:
time: 104 us; the launch traced here: 103 us
  starting transfers between devices  50.5 us (49%)
  local copies, waits for them, and re-layouts  19.6 us (19%)
  waiting for transfers between devices  16.6 us (16%)
  Pallas kernels  14.5 us (14%)
    ppermute x47, starting transfers between devices, share(): lax.ppermute(arrays[s], axis, [(d, d ^ s) for d in range(size)])  50.5 us
    ppermute x47, waiting for transfers between devices, share(): lax.ppermute(arrays[s], axis, [(d, d ^ s) for d in range(size)])  16.6 us
    unnamed x35, local copies, waits for them, and re-layouts  15.1 us
    pallas_call x9, Pallas kernels, call(): pl.pallas_call(kernel, out_shape=outs, in_specs=specs, out_specs=jax.tree...  14.5 us
    slice x8, local copies, waits for them, and re-layouts, body(): ids = jnp.stack([part[foot_rows, :2 * nb] for part in foot]).astype(F32)  3.72 us
  transfers between devices with their start and end apart: 47, of which 21 were waited for; matrix products, arithmetic and copies ran while one was open for 9% of the time, Pallas kernels for 0%

profile of v2, /device:TPU:0, one launch (start us, length us, event | category | flops | bytes accessed | tf_op | source)
XLA Modules:
  0.0 102.9 jit_solution(8904159650970367666)
XLA Ops:
  0.7 1.0 copy-done.5
  1.7 1.0 copy-done.6
  2.7 1.0 copy-done.7
  4.9 2.2 %shard_map.104 = (bf16[208,128]{1,0:T(8,128)(2,1)S(1)}, bf16[208,128]{1,0:T(8,128)(2,1)S(1)}, bf16[208,128]{1,0:T(8,128)(2,1)S(1)}, bf16[208,128]{1,0:T(8,128)(2...) custom-call(s32[3]{0:T(128)S(1)} %pad_add_fusion.own_ref, ...), custom_call_target="tpu_custom_call" | custom-call | tf_op jit(solution)/shard_map/pallas_call | solution.py:38
  7.7 2.6 %collective-permute-start.1 = (bf16[208,128]{1,0:T(8,128)(2,1)S(1)}, bf16[208,128]{1,0:T(8,128)(2,1)S(1)}, u32[]{:S(2)}, u32[]{:S(2)}) collective-permute-start(bf16[208,128]{1,0:T(8,128)(2,1)S(1)} %get-tuple-element.32), channel_id=1, source_target_pairs={{0,2},{1,3},{2,0},{3,1},{4,6},{5,7},{6,4},{7,5},{8,10},{9,11},{10,... | collective-permute-start | bytes 159752 | tf_op jit(solution)/shard_map/ppermute | solution.py:255
  10.3 1.8 %collective-permute-start.3 = (bf16[208,128]{1,0:T(8,128)(2,1)S(1)}, bf16[208,128]{1,0:T(8,128)(2,1)S(1)}, u32[]{:S(2)}, u32[]{:S(2)}) collective-permute-start(bf16[208,128]{1,0:T(8,128)(2,1)S(1)} %get-tuple-element.34), channel_id=1, source_target_pairs={{0,4},{1,5},{2,6},{3,7},{4,0},{5,1},{6,2},{7,3},{8,12},{9,13},{10,... | collective-permute-start | bytes 159752 | tf_op jit(solution)/shard_map/ppermute | solution.py:255
  12.1 2.6 %collective-permute-start.5 = (bf16[208,128]{1,0:T(8,128)(2,1)S(1)}, bf16[208,128]{1,0:T(8,128)(2,1)S(1)}, u32[]{:S(2)}, u32[]{:S(2)}) collective-permute-start(bf16[208,128]{1,0:T(8,128)(2,1)S(1)} %get-tuple-element.36), channel_id=1, source_target_pairs={{0,6},{1,7},{2,4},{3,5},{4,2},{5,3},{6,0},{7,1},{8,14},{9,15},{10,... | collective-permute-start | bytes 159752 | tf_op jit(solution)/shard_map/ppermute | solution.py:255
  14.9 3.7 %copy.14 = f32[48,128,128]{2,0,1:T(8,128)S(1)} copy(f32[48,128,128]{2,1,0:T(8,128)} %param.10) | data formatting | bytes 6291456 | tf_op args[1]
  19.6 2.7 %collective-permute-start.8 = (f32[1,48,128]{2,1,0:T(8,128)S(1)}, f32[1,48,128]{2,1,0:T(8,128)}, u32[]{:S(2)}, u32[]{:S(2)}) collective-permute-start(f32[1,48,128]{2,1,0:T(8,128)S(1)} %copy-done.10), channel_id=1, source_target_pairs={{0,16},{8,24},{16,0},{24,8},{1,17},{9,25},{17,1},{25,9},{2,18},{10... | collective-permute-start | bytes 73736 | tf_op jit(solution)/shard_map/ppermute | solution.py:255
  22.9 1.6 %collective-permute-start.7 = (f32[1,48,128]{2,1,0:T(8,128)S(1)}, f32[1,48,128]{2,1,0:T(8,128)}, u32[]{:S(2)}, u32[]{:S(2)}) collective-permute-start(f32[1,48,128]{2,1,0:T(8,128)S(1)} %copy-done.10), channel_id=1, source_target_pairs={{0,8},{8,0},{16,24},{24,16},{1,9},{9,1},{17,25},{25,17},{2,10},{10... | collective-permute-start | bytes 73736 | tf_op jit(solution)/shard_map/ppermute | solution.py:255
  28.1 2.6 %collective-permute-done.9.refs_3_ = f32[1,48,128]{2,1,0:T(8,128)} collective-permute-done((f32[1,48,128]{2,1,0:T(8,128)S(1)}, f32[1,48,128]{2,1,0:T(8,128)}, u32[]{:S(2)}, u32[]{:S(2)}) %collective-permute-start.9) | collective-permute-done | bytes 24608 | tf_op jit(solution)/shard_map/ppermute | solution.py:255
  31.5 1.7 %shard_map.105 = (f32[16,128]{1,0:T(8,128)}, f32[4,48,128]{2,1,0:T(8,128)S(1)}) custom-call(s32[3]{0:T(128)S(1)} %pad_add_fusion.own_ref, s32[8,4]{1,0:T(8,128)S(1)} %convert_convert_fusion.ids_ref, f32[128,48,128]{2,1,0:T(8,128)S(1)} %bitcast.7, f32[1,48,128]{2,1,0:T(8,128)S(1)} %copy-done.10, f32[1,48,128]{2,1,0:T(8,128)} %collective-permute-done.7.refs_1_, ...), custom_call_target="tpu_custom_call" | custom-call | tf_op jit(solution)/shard_map/pallas_call | solution.py:38
  34.6 1.8 %collective-permute-start.15 = (f32[16,128]{1,0:T(8,128)}, f32[16,128]{1,0:T(8,128)S(1)}, u32[]{:S(2)}, u32[]{:S(2)}) collective-permute-start(f32[16,128]{1,0:T(8,128)} %get-tuple-element.38.refs_0_), channel_id=1, source_target_pairs={{0,6},{1,7},{2,4},{3,5},{4,2},{5,3},{6,0},{7,1},{8,14},{9,15},{10,... | collective-permute-start | bytes 24584 | tf_op jit(solution)/shard_map/ppermute | solution.py:255
  37.2 1.4 %collective-permute-start.14 = (f32[16,128]{1,0:T(8,128)}, f32[16,128]{1,0:T(8,128)S(1)}, u32[]{:S(2)}, u32[]{:S(2)}) collective-permute-start(f32[16,128]{1,0:T(8,128)} %get-tuple-element.38.refs_0_), channel_id=1, source_target_pairs={{0,5},{1,4},{2,7},{3,6},{4,1},{5,0},{6,3},{7,2},{8,13},{9,12},{10,... | collective-permute-start | bytes 24584 | tf_op jit(solution)/shard_map/ppermute | solution.py:255
  42.5 1.9 %collective-permute-done.11.refs_2_ = f32[16,128]{1,0:T(8,128)S(1)} collective-permute-done((f32[16,128]{1,0:T(8,128)}, f32[16,128]{1,0:T(8,128)S(1)}, u32[]{:S(2)}, u32[]{:S(2)}) %collective-permute-start.11) | collective-permute-done | bytes 8224 | tf_op jit(solution)/shard_map/ppermute | solution.py:255
  46.6 1.2 %shard_map.106 = (f32[32,128]{1,0:T(8,128)S(1)}, f32[8,128]{1,0:T(8,128)S(1)}) custom-call(s32[8,4]{1,0:T(8,128)S(1)} %convert_convert_fusion.ids_ref, f32[8,128]{1,0:T(8,128)S(1)} %bitcast_select_fusion.weight_ref, f32[16,128]{1,0:T(8,128)} %get-tuple-element.38.refs_0_, f32[16,128]{1,0:T(8,128)S(1)} %collective-permute-done.10.refs_1_, ...), custom_call_target="tpu_custom_call" | custom-call | tf_op jit(solution)/shard_map/pallas_call | solution.py:38
  47.8 1.1 %collective-permute-start.19 = (f32[32,128]{1,0:T(8,128)S(1)}, f32[32,128]{1,0:T(8,128)S(1)}, u32[]{:S(2)}, u32[]{:S(2)}) collective-permute-start(f32[32,128]{1,0:T(8,128)S(1)} %get-tuple-element.39.refs_0_), channel_id=1, source_target_pairs={{0,24},{8,16},{16,8},{24,0},{1,25},{9,17},{17,9},{25,1},{2,26},{10... | collective-permute-start | bytes 49160 | tf_op jit(solution)/shard_map/ppermute | solution.py:255
  48.9 3.3 %collective-permute-start.17 = (f32[32,128]{1,0:T(8,128)S(1)}, f32[32,128]{1,0:T(8,128)S(1)}, u32[]{:S(2)}, u32[]{:S(2)}) collective-permute-start(f32[32,128]{1,0:T(8,128)S(1)} %get-tuple-element.39.refs_0_), channel_id=1, source_target_pairs={{0,8},{8,0},{16,24},{24,16},{1,9},{9,1},{17,25},{25,17},{2,10},{10... | collective-permute-start | bytes 49160 | tf_op jit(solution)/shard_map/ppermute | solution.py:255
  52.2 1.1 %collective-permute-done.19.refs_3_ = f32[32,128]{1,0:T(8,128)S(1)} collective-permute-done((f32[32,128]{1,0:T(8,128)S(1)}, f32[32,128]{1,0:T(8,128)S(1)}, u32[]{:S(2)}, u32[]{:S(2)}) %collective-permute-start.19) | collective-permute-done | bytes 16416 | tf_op jit(solution)/shard_map/ppermute | solution.py:255
  54.7 0.9 copy-done.9
  55.6 2.1 %shard_map.107 = (f32[16,128]{1,0:T(8,128)S(1)}, f32[4,48,128]{2,1,0:T(8,128)S(1)}, f32[4,48,128]{2,1,0:T(8,128)S(1)}, f32[8,128]{1,0:T(8,128)S(1)}) custom-call(s32[3]{0:T(128)S(1)} %pad_add_fusion.own_ref, s32[8,4]{1,0:T(8,128)S(1)} %convert_convert_fusion.ids_ref, s32[4,32]{1,0:T(4,128)S(1)} %maximum_convert_fusion.all_ref, f32[128,48,128]{2,1,0:T(8,128)S(1)} %bitcast.8, ...), custom_call_target="tpu_custom_call" | custom-call | tf_op jit(solution)/shard_map/pallas_call | solution.py:38
  57.9 1.6 %collective-permute-start.25 = (f32[16,128]{1,0:T(8,128)S(1)}, f32[16,128]{1,0:T(8,128)S(1)}, u32[]{:S(2)}, u32[]{:S(2)}) collective-permute-start(f32[16,128]{1,0:T(8,128)S(1)} %get-tuple-element.42.refs_0_), channel_id=1, source_target_pairs={{0,6},{1,7},{2,4},{3,5},{4,2},{5,3},{6,0},{7,1},{8,14},{9,15},{10,... | collective-permute-start | bytes 24584 | tf_op jit(solution)/shard_map/ppermute | solution.py:255
  59.5 1.6 %collective-permute-start.24 = (f32[16,128]{1,0:T(8,128)S(1)}, f32[16,128]{1,0:T(8,128)S(1)}, u32[]{:S(2)}, u32[]{:S(2)}) collective-permute-start(f32[16,128]{1,0:T(8,128)S(1)} %get-tuple-element.42.refs_0_), channel_id=1, source_target_pairs={{0,5},{1,4},{2,7},{3,6},{4,1},{5,0},{6,3},{7,2},{8,13},{9,12},{10,... | collective-permute-start | bytes 24584 | tf_op jit(solution)/shard_map/ppermute | solution.py:255
  61.2 1.0 collective-permute-start.23
  62.2 1.0 collective-permute-start.21
  63.1 0.9 collective-permute-start.20
  65.9 1.1 %shard_map.108 = (f32[24,128]{1,0:T(8,128)S(1)}, f32[8,128]{1,0:T(8,128)S(1)}) custom-call(s32[8,4]{1,0:T(8,128)S(1)} %convert_convert_fusion.ids_ref, f32[8,128]{1,0:T(8,128)S(1)} %bitcast_select_fusion.weight_ref, f32[16,128]{1,0:T(8,128)S(1)} %get-tuple-element.42.refs_0_, f32[16,128]{1,0:T(8,128)S(1)} %collective-permute-done.20.refs_1_, ...), custom_call_target="tpu_custom_call" | custom-call | tf_op jit(solution)/shard_map/pallas_call | solution.py:38
  67.0 2.4 %collective-permute-start.29 = (f32[24,128]{1,0:T(8,128)S(1)}, f32[24,128]{1,0:T(8,128)S(1)}, u32[]{:S(2)}, u32[]{:S(2)}) collective-permute-start(f32[24,128]{1,0:T(8,128)S(1)} %get-tuple-element.46.refs_1_), channel_id=1, source_target_pairs={{0,24},{8,16},{16,8},{24,0},{1,25},{9,17},{17,9},{25,1},{2,26},{10... | collective-permute-start | bytes 36872 | tf_op jit(solution)/shard_map/ppermute | solution.py:255
  69.3 1.1 %collective-permute-start.28 = (f32[24,128]{1,0:T(8,128)S(1)}, f32[24,128]{1,0:T(8,128)S(1)}, u32[]{:S(2)}, u32[]{:S(2)}) collective-permute-start(f32[24,128]{1,0:T(8,128)S(1)} %get-tuple-element.46.refs_1_), channel_id=1, source_target_pairs={{0,16},{8,24},{16,0},{24,8},{1,17},{9,25},{17,1},{25,9},{2,18},{10... | collective-permute-start | bytes 36872 | tf_op jit(solution)/shard_map/ppermute | solution.py:255
  70.5 0.9 collective-permute-start.27
  71.4 1.2 %collective-permute-done.29.refs_4_ = f32[24,128]{1,0:T(8,128)S(1)} collective-permute-done((f32[24,128]{1,0:T(8,128)S(1)}, f32[24,128]{1,0:T(8,128)S(1)}, u32[]{:S(2)}, u32[]{:S(2)}) %collective-permute-start.29) | collective-permute-done | bytes 12320 | tf_op jit(solution)/shard_map/ppermute | solution.py:255
  72.6 1.4 %collective-permute-done.28.refs_3_ = f32[24,128]{1,0:T(8,128)S(1)} collective-permute-done((f32[24,128]{1,0:T(8,128)S(1)}, f32[24,128]{1,0:T(8,128)S(1)}, u32[]{:S(2)}, u32[]{:S(2)}) %collective-permute-start.28) | collective-permute-done | bytes 12320 | tf_op jit(solution)/shard_map/ppermute | solution.py:255
  74.1 2.1 %shard_map.109 = (f32[16,128]{1,0:T(8,128)S(1)}, f32[4,48,128]{2,1,0:T(8,128)S(1)}, f32[4,48,128]{2,1,0:T(8,128)S(1)}, f32[8,128]{1,0:T(8,128)S(1)}) custom-call(s32[3]{0:T(128)S(1)} %pad_add_fusion.own_ref, s32[8,4]{1,0:T(8,128)S(1)} %convert_convert_fusion.ids_ref, s32[4,32]{1,0:T(4,128)S(1)} %maximum_convert_fusion.all_ref, f32[128,48,128]{2,1,0:T(8,128)S(1)} %bitcast.9, ...), custom_call_target="tpu_custom_call" | custom-call | tf_op jit(solution)/shard_map/pallas_call | solution.py:38
  76.3 1.7 %collective-permute-start.35 = (f32[16,128]{1,0:T(8,128)S(1)}, f32[16,128]{1,0:T(8,128)S(1)}, u32[]{:S(2)}, u32[]{:S(2)}) collective-permute-start(f32[16,128]{1,0:T(8,128)S(1)} %get-tuple-element.47.refs_0_), channel_id=1, source_target_pairs={{0,6},{1,7},{2,4},{3,5},{4,2},{5,3},{6,0},{7,1},{8,14},{9,15},{10,... | collective-permute-start | bytes 24584 | tf_op jit(solution)/shard_map/ppermute | solution.py:255
  78.1 1.4 %collective-permute-start.34 = (f32[16,128]{1,0:T(8,128)S(1)}, f32[16,128]{1,0:T(8,128)S(1)}, u32[]{:S(2)}, u32[]{:S(2)}) collective-permute-start(f32[16,128]{1,0:T(8,128)S(1)} %get-tuple-element.47.refs_0_), channel_id=1, source_target_pairs={{0,5},{1,4},{2,7},{3,6},{4,1},{5,0},{6,3},{7,2},{8,13},{9,12},{10,... | collective-permute-start | bytes 24584 | tf_op jit(solution)/shard_map/ppermute | solution.py:255
  79.4 1.3 %collective-permute-start.33 = (f32[16,128]{1,0:T(8,128)S(1)}, f32[16,128]{1,0:T(8,128)S(1)}, u32[]{:S(2)}, u32[]{:S(2)}) collective-permute-start(f32[16,128]{1,0:T(8,128)S(1)} %get-tuple-element.47.refs_0_), channel_id=1, source_target_pairs={{0,4},{1,5},{2,6},{3,7},{4,0},{5,1},{6,2},{7,3},{8,12},{9,13},{10,... | collective-permute-start | bytes 24584 | tf_op jit(solution)/shard_map/ppermute | solution.py:255
  81.6 1.0 collective-permute-start.30
  84.4 1.1 %shard_map.110 = (f32[24,128]{1,0:T(8,128)S(1)}, f32[8,128]{1,0:T(8,128)S(1)}) custom-call(s32[8,4]{1,0:T(8,128)S(1)} %convert_convert_fusion.ids_ref, f32[8,128]{1,0:T(8,128)S(1)} %bitcast_select_fusion.weight_ref, f32[16,128]{1,0:T(8,128)S(1)} %get-tuple-element.47.refs_0_, f32[16,128]{1,0:T(8,128)S(1)} %collective-permute-done.30.refs_1_, ...), custom_call_target="tpu_custom_call" | custom-call | tf_op jit(solution)/shard_map/pallas_call | solution.py:38
  85.5 1.5 %collective-permute-start.39 = (f32[24,128]{1,0:T(8,128)S(1)}, f32[24,128]{1,0:T(8,128)S(1)}, u32[]{:S(2)}, u32[]{:S(2)}) collective-permute-start(f32[24,128]{1,0:T(8,128)S(1)} %get-tuple-element.51.refs_1_), channel_id=1, source_target_pairs={{0,24},{8,16},{16,8},{24,0},{1,25},{9,17},{17,9},{25,1},{2,26},{10... | collective-permute-start | bytes 36872 | tf_op jit(solution)/shard_map/ppermute | solution.py:255
  86.9 1.0 %collective-permute-start.38 = (f32[24,128]{1,0:T(8,128)S(1)}, f32[24,128]{1,0:T(8,128)S(1)}, u32[]{:S(2)}, u32[]{:S(2)}) collective-permute-start(f32[24,128]{1,0:T(8,128)S(1)} %get-tuple-element.51.refs_1_), channel_id=1, source_target_pairs={{0,16},{8,24},{16,0},{24,8},{1,17},{9,25},{17,1},{25,9},{2,18},{10... | collective-permute-start | bytes 36872 | tf_op jit(solution)/shard_map/ppermute | solution.py:255
  88.0 1.9 %collective-permute-start.37 = (f32[24,128]{1,0:T(8,128)S(1)}, f32[24,128]{1,0:T(8,128)S(1)}, u32[]{:S(2)}, u32[]{:S(2)}) collective-permute-start(f32[24,128]{1,0:T(8,128)S(1)} %get-tuple-element.51.refs_1_), channel_id=1, source_target_pairs={{0,8},{8,0},{16,24},{24,16},{1,9},{9,1},{17,25},{25,17},{2,10},{10... | collective-permute-start | bytes 36872 | tf_op jit(solution)/shard_map/ppermute | solution.py:255
  89.9 1.1 %collective-permute-done.39.refs_4_ = f32[24,128]{1,0:T(8,128)S(1)} collective-permute-done((f32[24,128]{1,0:T(8,128)S(1)}, f32[24,128]{1,0:T(8,128)S(1)}, u32[]{:S(2)}, u32[]{:S(2)}) %collective-permute-start.39) | collective-permute-done | bytes 12320 | tf_op jit(solution)/shard_map/ppermute | solution.py:255
  91.7 1.8 %shard_map.111 = (f32[8,128]{1,0:T(8,128)S(1)}, f32[4,48,128]{2,1,0:T(8,128)S(1)}, f32[4,48,128]{2,1,0:T(8,128)S(1)}, f32[8,128]{1,0:T(8,128)S(1)}) custom-call(s32[3]{0:T(128)S(1)} %pad_add_fusion.own_ref, s32[8,4]{1,0:T(8,128)S(1)} %convert_convert_fusion.ids_ref, s32[4,32]{1,0:T(4,128)S(1)} %maximum_convert_fusion.all_ref, f32[128,48,128]{2,1,0:T(8,128)S(1)} %bitcast.10, ...), custom_call_target="tpu_custom_call" | custom-call | tf_op jit(solution)/shard_map/pallas_call | solution.py:38
  93.5 1.7 %collective-permute-start.45 = (f32[8,128]{1,0:T(8,128)S(1)}, f32[8,128]{1,0:T(8,128)S(1)}, u32[]{:S(2)}, u32[]{:S(2)}) collective-permute-start(f32[8,128]{1,0:T(8,128)S(1)} %get-tuple-element.52.refs_0_), channel_id=1, source_target_pairs={{0,6},{1,7},{2,4},{3,5},{4,2},{5,3},{6,0},{7,1},{8,14},{9,15},{10,... | collective-permute-start | bytes 12296 | tf_op jit(solution)/shard_map/ppermute | solution.py:255
  95.2 1.8 %collective-permute-start.44 = (f32[8,128]{1,0:T(8,128)S(1)}, f32[8,128]{1,0:T(8,128)S(1)}, u32[]{:S(2)}, u32[]{:S(2)}) collective-permute-start(f32[8,128]{1,0:T(8,128)S(1)} %get-tuple-element.52.refs_0_), channel_id=1, source_target_pairs={{0,5},{1,4},{2,7},{3,6},{4,1},{5,0},{6,3},{7,2},{8,13},{9,12},{10,... | collective-permute-start | bytes 12296 | tf_op jit(solution)/shard_map/ppermute | solution.py:255
  96.9 1.0 collective-permute-start.43
  98.8 1.0 collective-permute-start.40
  101.5 1.3 %shard_map.112 = (f32[4,1,48,128]{3,2,1,0:T(8,128)}, f32[2,3]{1,0:T(2,128)}) custom-call(s32[3]{0:T(128)S(1)} %pad_add_fusion.own_ref, f32[8,128]{1,0:T(8,128)S(1)} %get-tuple-element.52.refs_0_, f32[8,128]{1,0:T(8,128)S(1)} %collective-permute-done.40.refs_1_, f32[8,128]{1,0:T(8,128)S(1)} %collective-permute-done.41.refs_2_, ...), custom_call_target="tpu_custom_call" | custom-call | tf_op jit(solution)/shard_map/pallas_call | solution.py:38
  (109 shorter events, 26.2 us)
Async XLA Ops:
  7.2 4.9 %collective-permute-start = (bf16[208,128]{1,0:T(8,128)(2,1)S(1)}, bf16[208,128]{1,0:T(8,128)(2,1)S(1)}, u32[]{:S(2)}, u32[]{:S(2)}) collective-permute-start(bf16[208,128]{1,0:T(8,128)(2,1)S(1)} %get-tuple-element.31), channel_id=1, source_target_pairs={{0,1},{1,0},{2,3},{3,2},{4,5},{5,4},{6,7},{7,6},{8,9},{9,8},{10,11... | collective-permute-start | bytes 159752 | tf_op jit(solution)/shard_map/ppermute | solution.py:255
  7.7 7.0 %collective-permute-start.1 = (bf16[208,128]{1,0:T(8,128)(2,1)S(1)}, bf16[208,128]{1,0:T(8,128)(2,1)S(1)}, u32[]{:S(2)}, u32[]{:S(2)}) collective-permute-start(bf16[208,128]{1,0:T(8,128)(2,1)S(1)} %get-tuple-element.32), channel_id=1, source_target_pairs={{0,2},{1,3},{2,0},{3,1},{4,6},{5,7},{6,4},{7,5},{8,10},{9,11},{10,... | collective-permute-start | bytes 159752 | tf_op jit(solution)/shard_map/ppermute | solution.py:255
  10.3 9.3 %collective-permute-start.2 = (bf16[208,128]{1,0:T(8,128)(2,1)S(1)}, bf16[208,128]{1,0:T(8,128)(2,1)S(1)}, u32[]{:S(2)}, u32[]{:S(2)}) collective-permute-start(bf16[208,128]{1,0:T(8,128)(2,1)S(1)} %get-tuple-element.33), channel_id=1, source_target_pairs={{0,3},{1,2},{2,1},{3,0},{4,7},{5,6},{6,5},{7,4},{8,11},{9,10},{10,... | collective-permute-start | bytes 159752 | tf_op jit(solution)/shard_map/ppermute | solution.py:255
  10.3 12.6 %collective-permute-start.3 = (bf16[208,128]{1,0:T(8,128)(2,1)S(1)}, bf16[208,128]{1,0:T(8,128)(2,1)S(1)}, u32[]{:S(2)}, u32[]{:S(2)}) collective-permute-start(bf16[208,128]{1,0:T(8,128)(2,1)S(1)} %get-tuple-element.34), channel_id=1, source_target_pairs={{0,4},{1,5},{2,6},{3,7},{4,0},{5,1},{6,2},{7,3},{8,12},{9,13},{10,... | collective-permute-start | bytes 159752 | tf_op jit(solution)/shard_map/ppermute | solution.py:255
  12.1 12.9 %collective-permute-start.4 = (bf16[208,128]{1,0:T(8,128)(2,1)S(1)}, bf16[208,128]{1,0:T(8,128)(2,1)S(1)}, u32[]{:S(2)}, u32[]{:S(2)}) collective-permute-start(bf16[208,128]{1,0:T(8,128)(2,1)S(1)} %get-tuple-element.35), channel_id=1, source_target_pairs={{0,5},{1,4},{2,7},{3,6},{4,1},{5,0},{6,3},{7,2},{8,13},{9,12},{10,... | collective-permute-start | bytes 159752 | tf_op jit(solution)/shard_map/ppermute | solution.py:255
  12.1 13.5 %collective-permute-start.5 = (bf16[208,128]{1,0:T(8,128)(2,1)S(1)}, bf16[208,128]{1,0:T(8,128)(2,1)S(1)}, u32[]{:S(2)}, u32[]{:S(2)}) collective-permute-start(bf16[208,128]{1,0:T(8,128)(2,1)S(1)} %get-tuple-element.36), channel_id=1, source_target_pairs={{0,6},{1,7},{2,4},{3,5},{4,2},{5,3},{6,0},{7,1},{8,14},{9,15},{10,... | collective-permute-start | bytes 159752 | tf_op jit(solution)/shard_map/ppermute | solution.py:255
  14.7 11.5 %collective-permute-start.6 = (bf16[208,128]{1,0:T(8,128)(2,1)S(1)}, bf16[208,128]{1,0:T(8,128)(2,1)S(1)}, u32[]{:S(2)}, u32[]{:S(2)}) collective-permute-start(bf16[208,128]{1,0:T(8,128)(2,1)S(1)} %get-tuple-element.37), channel_id=1, source_target_pairs={{0,7},{1,6},{2,5},{3,4},{4,3},{5,2},{6,1},{7,0},{8,15},{9,14},{10,... | collective-permute-start | bytes 159752 | tf_op jit(solution)/shard_map/ppermute | solution.py:255
  19.6 8.5 %collective-permute-start.8 = (f32[1,48,128]{2,1,0:T(8,128)S(1)}, f32[1,48,128]{2,1,0:T(8,128)}, u32[]{:S(2)}, u32[]{:S(2)}) collective-permute-start(f32[1,48,128]{2,1,0:T(8,128)S(1)} %copy-done.10), channel_id=1, source_target_pairs={{0,16},{8,24},{16,0},{24,8},{1,17},{9,25},{17,1},{25,9},{2,18},{10... | collective-permute-start | bytes 73736 | tf_op jit(solution)/shard_map/ppermute | solution.py:255
  22.9 5.2 %collective-permute-start.7 = (f32[1,48,128]{2,1,0:T(8,128)S(1)}, f32[1,48,128]{2,1,0:T(8,128)}, u32[]{:S(2)}, u32[]{:S(2)}) collective-permute-start(f32[1,48,128]{2,1,0:T(8,128)S(1)} %copy-done.10), channel_id=1, source_target_pairs={{0,8},{8,0},{16,24},{24,16},{1,9},{9,1},{17,25},{25,17},{2,10},{10... | collective-permute-start | bytes 73736 | tf_op jit(solution)/shard_map/ppermute | solution.py:255
  25.0 5.7 %collective-permute-start.9 = (f32[1,48,128]{2,1,0:T(8,128)S(1)}, f32[1,48,128]{2,1,0:T(8,128)}, u32[]{:S(2)}, u32[]{:S(2)}) collective-permute-start(f32[1,48,128]{2,1,0:T(8,128)S(1)} %copy-done.10), channel_id=1, source_target_pairs={{0,24},{8,16},{16,8},{24,0},{1,25},{9,17},{17,9},{25,1},{2,26},{10... | collective-permute-start | bytes 73736 | tf_op jit(solution)/shard_map/ppermute | solution.py:255
  33.9 6.0 %collective-permute-start.16 = (f32[16,128]{1,0:T(8,128)}, f32[16,128]{1,0:T(8,128)S(1)}, u32[]{:S(2)}, u32[]{:S(2)}) collective-permute-start(f32[16,128]{1,0:T(8,128)} %get-tuple-element.38.refs_0_), channel_id=1, source_target_pairs={{0,7},{1,6},{2,5},{3,4},{4,3},{5,2},{6,1},{7,0},{8,15},{9,14},{10,... | collective-permute-start | bytes 24584 | tf_op jit(solution)/shard_map/ppermute | solution.py:255
  34.6 6.7 %collective-permute-start.15 = (f32[16,128]{1,0:T(8,128)}, f32[16,128]{1,0:T(8,128)S(1)}, u32[]{:S(2)}, u32[]{:S(2)}) collective-permute-start(f32[16,128]{1,0:T(8,128)} %get-tuple-element.38.refs_0_), channel_id=1, source_target_pairs={{0,6},{1,7},{2,4},{3,5},{4,2},{5,3},{6,0},{7,1},{8,14},{9,15},{10,... | collective-permute-start | bytes 24584 | tf_op jit(solution)/shard_map/ppermute | solution.py:255
  37.2 5.0 %collective-permute-start.14 = (f32[16,128]{1,0:T(8,128)}, f32[16,128]{1,0:T(8,128)S(1)}, u32[]{:S(2)}, u32[]{:S(2)}) collective-permute-start(f32[16,128]{1,0:T(8,128)} %get-tuple-element.38.refs_0_), channel_id=1, source_target_pairs={{0,5},{1,4},{2,7},{3,6},{4,1},{5,0},{6,3},{7,2},{8,13},{9,12},{10,... | collective-permute-start | bytes 24584 | tf_op jit(solution)/shard_map/ppermute | solution.py:255
  38.6 3.9 %collective-permute-start.13 = (f32[16,128]{1,0:T(8,128)}, f32[16,128]{1,0:T(8,128)S(1)}, u32[]{:S(2)}, u32[]{:S(2)}) collective-permute-start(f32[16,128]{1,0:T(8,128)} %get-tuple-element.38.refs_0_), channel_id=1, source_target_pairs={{0,4},{1,5},{2,6},{3,7},{4,0},{5,1},{6,2},{7,3},{8,12},{9,13},{10,... | collective-permute-start | bytes 24584 | tf_op jit(solution)/shard_map/ppermute | solution.py:255
  39.1 3.4 %collective-permute-start.12 = (f32[16,128]{1,0:T(8,128)}, f32[16,128]{1,0:T(8,128)S(1)}, u32[]{:S(2)}, u32[]{:S(2)}) collective-permute-start(f32[16,128]{1,0:T(8,128)} %get-tuple-element.38.refs_0_), channel_id=1, source_target_pairs={{0,3},{1,2},{2,1},{3,0},{4,7},{5,6},{6,5},{7,4},{8,11},{9,10},{10,... | collective-permute-start | bytes 24584 | tf_op jit(solution)/shard_map/ppermute | solution.py:255
  40.5 3.9 %collective-permute-start.11 = (f32[16,128]{1,0:T(8,128)}, f32[16,128]{1,0:T(8,128)S(1)}, u32[]{:S(2)}, u32[]{:S(2)}) collective-permute-start(f32[16,128]{1,0:T(8,128)} %get-tuple-element.38.refs_0_), channel_id=1, source_target_pairs={{0,2},{1,3},{2,0},{3,1},{4,6},{5,7},{6,4},{7,5},{8,10},{9,11},{10,... | collective-permute-start | bytes 24584 | tf_op jit(solution)/shard_map/ppermute | solution.py:255
  41.9 2.5 %collective-permute-start.10 = (f32[16,128]{1,0:T(8,128)}, f32[16,128]{1,0:T(8,128)S(1)}, u32[]{:S(2)}, u32[]{:S(2)}) collective-permute-start(f32[16,128]{1,0:T(8,128)} %get-tuple-element.38.refs_0_), channel_id=1, source_target_pairs={{0,1},{1,0},{2,3},{3,2},{4,5},{5,4},{6,7},{7,6},{8,9},{9,8},{10,11... | collective-permute-start | bytes 24584 | tf_op jit(solution)/shard_map/ppermute | solution.py:255
  46.6 19.3 %copy-start.4 = (bf16[208,128]{1,0:T(8,128)(2,1)S(1)}, bf16[208,128]{1,0:T(8,128)(2,1)}, u32[]{:S(2)}) copy-start(bf16[208,128]{1,0:T(8,128)(2,1)} %copy-done) | copy-start | bytes 159748
  47.8 5.6 %collective-permute-start.19 = (f32[32,128]{1,0:T(8,128)S(1)}, f32[32,128]{1,0:T(8,128)S(1)}, u32[]{:S(2)}, u32[]{:S(2)}) collective-permute-start(f32[32,128]{1,0:T(8,128)S(1)} %get-tuple-element.39.refs_0_), channel_id=1, source_target_pairs={{0,24},{8,16},{16,8},{24,0},{1,25},{9,17},{17,9},{25,1},{2,26},{10... | collective-permute-start | bytes 49160 | tf_op jit(solution)/shard_map/ppermute | solution.py:255
  48.9 4.8 %collective-permute-start.18 = (f32[32,128]{1,0:T(8,128)S(1)}, f32[32,128]{1,0:T(8,128)S(1)}, u32[]{:S(2)}, u32[]{:S(2)}) collective-permute-start(f32[32,128]{1,0:T(8,128)S(1)} %get-tuple-element.39.refs_0_), channel_id=1, source_target_pairs={{0,16},{8,24},{16,0},{24,8},{1,17},{9,25},{17,1},{25,9},{2,18},{10... | collective-permute-start | bytes 49160 | tf_op jit(solution)/shard_map/ppermute | solution.py:255
  48.9 5.0 %collective-permute-start.17 = (f32[32,128]{1,0:T(8,128)S(1)}, f32[32,128]{1,0:T(8,128)S(1)}, u32[]{:S(2)}, u32[]{:S(2)}) collective-permute-start(f32[32,128]{1,0:T(8,128)S(1)} %get-tuple-element.39.refs_0_), channel_id=1, source_target_pairs={{0,8},{8,0},{16,24},{24,16},{1,9},{9,1},{17,25},{25,17},{2,10},{10... | collective-permute-start | bytes 49160 | tf_op jit(solution)/shard_map/ppermute | solution.py:255
  57.7 4.5 %collective-permute-start.26 = (f32[16,128]{1,0:T(8,128)S(1)}, f32[16,128]{1,0:T(8,128)S(1)}, u32[]{:S(2)}, u32[]{:S(2)}) collective-permute-start(f32[16,128]{1,0:T(8,128)S(1)} %get-tuple-element.42.refs_0_), channel_id=1, source_target_pairs={{0,7},{1,6},{2,5},{3,4},{4,3},{5,2},{6,1},{7,0},{8,15},{9,14},{10,... | collective-permute-start | bytes 24584 | tf_op jit(solution)/shard_map/ppermute | solution.py:255
  57.9 5.2 %collective-permute-start.25 = (f32[16,128]{1,0:T(8,128)S(1)}, f32[16,128]{1,0:T(8,128)S(1)}, u32[]{:S(2)}, u32[]{:S(2)}) collective-permute-start(f32[16,128]{1,0:T(8,128)S(1)} %get-tuple-element.42.refs_0_), channel_id=1, source_target_pairs={{0,6},{1,7},{2,4},{3,5},{4,2},{5,3},{6,0},{7,1},{8,14},{9,15},{10,... | collective-permute-start | bytes 24584 | tf_op jit(solution)/shard_map/ppermute | solution.py:255
  59.5 4.5 %collective-permute-start.24 = (f32[16,128]{1,0:T(8,128)S(1)}, f32[16,128]{1,0:T(8,128)S(1)}, u32[]{:S(2)}, u32[]{:S(2)}) collective-permute-start(f32[16,128]{1,0:T(8,128)S(1)} %get-tuple-element.42.refs_0_), channel_id=1, source_target_pairs={{0,5},{1,4},{2,7},{3,6},{4,1},{5,0},{6,3},{7,2},{8,13},{9,12},{10,... | collective-permute-start | bytes 24584 | tf_op jit(solution)/shard_map/ppermute | solution.py:255
  61.2 3.7 %collective-permute-start.23 = (f32[16,128]{1,0:T(8,128)S(1)}, f32[16,128]{1,0:T(8,128)S(1)}, u32[]{:S(2)}, u32[]{:S(2)}) collective-permute-start(f32[16,128]{1,0:T(8,128)S(1)} %get-tuple-element.42.refs_0_), channel_id=1, source_target_pairs={{0,4},{1,5},{2,6},{3,7},{4,0},{5,1},{6,2},{7,3},{8,12},{9,13},{10,... | collective-permute-start | bytes 24584 | tf_op jit(solution)/shard_map/ppermute | solution.py:255
  62.2 3.1 %collective-permute-start.22 = (f32[16,128]{1,0:T(8,128)S(1)}, f32[16,128]{1,0:T(8,128)S(1)}, u32[]{:S(2)}, u32[]{:S(2)}) collective-permute-start(f32[16,128]{1,0:T(8,128)S(1)} %get-tuple-element.42.refs_0_), channel_id=1, source_target_pairs={{0,3},{1,2},{2,1},{3,0},{4,7},{5,6},{6,5},{7,4},{8,11},{9,10},{10,... | collective-permute-start | bytes 24584 | tf_op jit(solution)/shard_map/ppermute | solution.py:255
  62.2 3.7 %collective-permute-start.21 = (f32[16,128]{1,0:T(8,128)S(1)}, f32[16,128]{1,0:T(8,128)S(1)}, u32[]{:S(2)}, u32[]{:S(2)}) collective-permute-start(f32[16,128]{1,0:T(8,128)S(1)} %get-tuple-element.42.refs_0_), channel_id=1, source_target_pairs={{0,2},{1,3},{2,0},{3,1},{4,6},{5,7},{6,4},{7,5},{8,10},{9,11},{10,... | collective-permute-start | bytes 24584 | tf_op jit(solution)/shard_map/ppermute | solution.py:255
  63.1 2.8 %collective-permute-start.20 = (f32[16,128]{1,0:T(8,128)S(1)}, f32[16,128]{1,0:T(8,128)S(1)}, u32[]{:S(2)}, u32[]{:S(2)}) collective-permute-start(f32[16,128]{1,0:T(8,128)S(1)} %get-tuple-element.42.refs_0_), channel_id=1, source_target_pairs={{0,1},{1,0},{2,3},{3,2},{4,5},{5,4},{6,7},{7,6},{8,9},{9,8},{10,11... | collective-permute-start | bytes 24584 | tf_op jit(solution)/shard_map/ppermute | solution.py:255
  67.0 5.6 %collective-permute-start.29 = (f32[24,128]{1,0:T(8,128)S(1)}, f32[24,128]{1,0:T(8,128)S(1)}, u32[]{:S(2)}, u32[]{:S(2)}) collective-permute-start(f32[24,128]{1,0:T(8,128)S(1)} %get-tuple-element.46.refs_1_), channel_id=1, source_target_pairs={{0,24},{8,16},{16,8},{24,0},{1,25},{9,17},{17,9},{25,1},{2,26},{10... | collective-permute-start | bytes 36872 | tf_op jit(solution)/shard_map/ppermute | solution.py:255
  69.3 4.6 %collective-permute-start.28 = (f32[24,128]{1,0:T(8,128)S(1)}, f32[24,128]{1,0:T(8,128)S(1)}, u32[]{:S(2)}, u32[]{:S(2)}) collective-permute-start(f32[24,128]{1,0:T(8,128)S(1)} %get-tuple-element.46.refs_1_), channel_id=1, source_target_pairs={{0,16},{8,24},{16,0},{24,8},{1,17},{9,25},{17,1},{25,9},{2,18},{10... | collective-permute-start | bytes 36872 | tf_op jit(solution)/shard_map/ppermute | solution.py:255
  70.5 3.7 %collective-permute-start.27 = (f32[24,128]{1,0:T(8,128)S(1)}, f32[24,128]{1,0:T(8,128)S(1)}, u32[]{:S(2)}, u32[]{:S(2)}) collective-permute-start(f32[24,128]{1,0:T(8,128)S(1)} %get-tuple-element.46.refs_1_), channel_id=1, source_target_pairs={{0,8},{8,0},{16,24},{24,16},{1,9},{9,1},{17,25},{25,17},{2,10},{10... | collective-permute-start | bytes 36872 | tf_op jit(solution)/shard_map/ppermute | solution.py:255
  76.3 4.5 %collective-permute-start.36 = (f32[16,128]{1,0:T(8,128)S(1)}, f32[16,128]{1,0:T(8,128)S(1)}, u32[]{:S(2)}, u32[]{:S(2)}) collective-permute-start(f32[16,128]{1,0:T(8,128)S(1)} %get-tuple-element.47.refs_0_), channel_id=1, source_target_pairs={{0,7},{1,6},{2,5},{3,4},{4,3},{5,2},{6,1},{7,0},{8,15},{9,14},{10,... | collective-permute-start | bytes 24584 | tf_op jit(solution)/shard_map/ppermute | solution.py:255
  76.3 5.2 %collective-permute-start.35 = (f32[16,128]{1,0:T(8,128)S(1)}, f32[16,128]{1,0:T(8,128)S(1)}, u32[]{:S(2)}, u32[]{:S(2)}) collective-permute-start(f32[16,128]{1,0:T(8,128)S(1)} %get-tuple-element.47.refs_0_), channel_id=1, source_target_pairs={{0,6},{1,7},{2,4},{3,5},{4,2},{5,3},{6,0},{7,1},{8,14},{9,15},{10,... | collective-permute-start | bytes 24584 | tf_op jit(solution)/shard_map/ppermute | solution.py:255
  78.1 4.5 %collective-permute-start.34 = (f32[16,128]{1,0:T(8,128)S(1)}, f32[16,128]{1,0:T(8,128)S(1)}, u32[]{:S(2)}, u32[]{:S(2)}) collective-permute-start(f32[16,128]{1,0:T(8,128)S(1)} %get-tuple-element.47.refs_0_), channel_id=1, source_target_pairs={{0,5},{1,4},{2,7},{3,6},{4,1},{5,0},{6,3},{7,2},{8,13},{9,12},{10,... | collective-permute-start | bytes 24584 | tf_op jit(solution)/shard_map/ppermute | solution.py:255
  79.4 3.7 %collective-permute-start.33 = (f32[16,128]{1,0:T(8,128)S(1)}, f32[16,128]{1,0:T(8,128)S(1)}, u32[]{:S(2)}, u32[]{:S(2)}) collective-permute-start(f32[16,128]{1,0:T(8,128)S(1)} %get-tuple-element.47.refs_0_), channel_id=1, source_target_pairs={{0,4},{1,5},{2,6},{3,7},{4,0},{5,1},{6,2},{7,3},{8,12},{9,13},{10,... | collective-permute-start | bytes 24584 | tf_op jit(solution)/shard_map/ppermute | solution.py:255
  80.7 3.1 %collective-permute-start.32 = (f32[16,128]{1,0:T(8,128)S(1)}, f32[16,128]{1,0:T(8,128)S(1)}, u32[]{:S(2)}, u32[]{:S(2)}) collective-permute-start(f32[16,128]{1,0:T(8,128)S(1)} %get-tuple-element.47.refs_0_), channel_id=1, source_target_pairs={{0,3},{1,2},{2,1},{3,0},{4,7},{5,6},{6,5},{7,4},{8,11},{9,10},{10,... | collective-permute-start | bytes 24584 | tf_op jit(solution)/shard_map/ppermute | solution.py:255
  80.7 3.7 %collective-permute-start.31 = (f32[16,128]{1,0:T(8,128)S(1)}, f32[16,128]{1,0:T(8,128)S(1)}, u32[]{:S(2)}, u32[]{:S(2)}) collective-permute-start(f32[16,128]{1,0:T(8,128)S(1)} %get-tuple-element.47.refs_0_), channel_id=1, source_target_pairs={{0,2},{1,3},{2,0},{3,1},{4,6},{5,7},{6,4},{7,5},{8,10},{9,11},{10,... | collective-permute-start | bytes 24584 | tf_op jit(solution)/shard_map/ppermute | solution.py:255
  81.6 2.8 %collective-permute-start.30 = (f32[16,128]{1,0:T(8,128)S(1)}, f32[16,128]{1,0:T(8,128)S(1)}, u32[]{:S(2)}, u32[]{:S(2)}) collective-permute-start(f32[16,128]{1,0:T(8,128)S(1)} %get-tuple-element.47.refs_0_), channel_id=1, source_target_pairs={{0,1},{1,0},{2,3},{3,2},{4,5},{5,4},{6,7},{7,6},{8,9},{9,8},{10,11... | collective-permute-start | bytes 24584 | tf_op jit(solution)/shard_map/ppermute | solution.py:255
  85.5 5.5 %collective-permute-start.39 = (f32[24,128]{1,0:T(8,128)S(1)}, f32[24,128]{1,0:T(8,128)S(1)}, u32[]{:S(2)}, u32[]{:S(2)}) collective-permute-start(f32[24,128]{1,0:T(8,128)S(1)} %get-tuple-element.51.refs_1_), channel_id=1, source_target_pairs={{0,24},{8,16},{16,8},{24,0},{1,25},{9,17},{17,9},{25,1},{2,26},{10... | collective-permute-start | bytes 36872 | tf_op jit(solution)/shard_map/ppermute | solution.py:255
  86.9 4.6 %collective-permute-start.38 = (f32[24,128]{1,0:T(8,128)S(1)}, f32[24,128]{1,0:T(8,128)S(1)}, u32[]{:S(2)}, u32[]{:S(2)}) collective-permute-start(f32[24,128]{1,0:T(8,128)S(1)} %get-tuple-element.51.refs_1_), channel_id=1, source_target_pairs={{0,16},{8,24},{16,0},{24,8},{1,17},{9,25},{17,1},{25,9},{2,18},{10... | collective-permute-start | bytes 36872 | tf_op jit(solution)/shard_map/ppermute | solution.py:255
  88.0 3.7 %collective-permute-start.37 = (f32[24,128]{1,0:T(8,128)S(1)}, f32[24,128]{1,0:T(8,128)S(1)}, u32[]{:S(2)}, u32[]{:S(2)}) collective-permute-start(f32[24,128]{1,0:T(8,128)S(1)} %get-tuple-element.51.refs_1_), channel_id=1, source_target_pairs={{0,8},{8,0},{16,24},{24,16},{1,9},{9,1},{17,25},{25,17},{2,10},{10... | collective-permute-start | bytes 36872 | tf_op jit(solution)/shard_map/ppermute | solution.py:255
  93.4 4.5 %collective-permute-start.46 = (f32[8,128]{1,0:T(8,128)S(1)}, f32[8,128]{1,0:T(8,128)S(1)}, u32[]{:S(2)}, u32[]{:S(2)}) collective-permute-start(f32[8,128]{1,0:T(8,128)S(1)} %get-tuple-element.52.refs_0_), channel_id=1, source_target_pairs={{0,7},{1,6},{2,5},{3,4},{4,3},{5,2},{6,1},{7,0},{8,15},{9,14},{10,... | collective-permute-start | bytes 12296 | tf_op jit(solution)/shard_map/ppermute | solution.py:255
  93.5 5.3 %collective-permute-start.45 = (f32[8,128]{1,0:T(8,128)S(1)}, f32[8,128]{1,0:T(8,128)S(1)}, u32[]{:S(2)}, u32[]{:S(2)}) collective-permute-start(f32[8,128]{1,0:T(8,128)S(1)} %get-tuple-element.52.refs_0_), channel_id=1, source_target_pairs={{0,6},{1,7},{2,4},{3,5},{4,2},{5,3},{6,0},{7,1},{8,14},{9,15},{10,... | collective-permute-start | bytes 12296 | tf_op jit(solution)/shard_map/ppermute | solution.py:255
  95.2 4.6 %collective-permute-start.44 = (f32[8,128]{1,0:T(8,128)S(1)}, f32[8,128]{1,0:T(8,128)S(1)}, u32[]{:S(2)}, u32[]{:S(2)}) collective-permute-start(f32[8,128]{1,0:T(8,128)S(1)} %get-tuple-element.52.refs_0_), channel_id=1, source_target_pairs={{0,5},{1,4},{2,7},{3,6},{4,1},{5,0},{6,3},{7,2},{8,13},{9,12},{10,... | collective-permute-start | bytes 12296 | tf_op jit(solution)/shard_map/ppermute | solution.py:255
  96.9 3.6 %collective-permute-start.43 = (f32[8,128]{1,0:T(8,128)S(1)}, f32[8,128]{1,0:T(8,128)S(1)}, u32[]{:S(2)}, u32[]{:S(2)}) collective-permute-start(f32[8,128]{1,0:T(8,128)S(1)} %get-tuple-element.52.refs_0_), channel_id=1, source_target_pairs={{0,4},{1,5},{2,6},{3,7},{4,0},{5,1},{6,2},{7,3},{8,12},{9,13},{10,... | collective-permute-start | bytes 12296 | tf_op jit(solution)/shard_map/ppermute | solution.py:255
  97.9 3.0 %collective-permute-start.42 = (f32[8,128]{1,0:T(8,128)S(1)}, f32[8,128]{1,0:T(8,128)S(1)}, u32[]{:S(2)}, u32[]{:S(2)}) collective-permute-start(f32[8,128]{1,0:T(8,128)S(1)} %get-tuple-element.52.refs_0_), channel_id=1, source_target_pairs={{0,3},{1,2},{2,1},{3,0},{4,7},{5,6},{6,5},{7,4},{8,11},{9,10},{10,... | collective-permute-start | bytes 12296 | tf_op jit(solution)/shard_map/ppermute | solution.py:255
  97.9 3.6 %collective-permute-start.41 = (f32[8,128]{1,0:T(8,128)S(1)}, f32[8,128]{1,0:T(8,128)S(1)}, u32[]{:S(2)}, u32[]{:S(2)}) collective-permute-start(f32[8,128]{1,0:T(8,128)S(1)} %get-tuple-element.52.refs_0_), channel_id=1, source_target_pairs={{0,2},{1,3},{2,0},{3,1},{4,6},{5,7},{6,4},{7,5},{8,10},{9,11},{10,... | collective-permute-start | bytes 12296 | tf_op jit(solution)/shard_map/ppermute | solution.py:255
  98.8 2.8 %collective-permute-start.40 = (f32[8,128]{1,0:T(8,128)S(1)}, f32[8,128]{1,0:T(8,128)S(1)}, u32[]{:S(2)}, u32[]{:S(2)}) collective-permute-start(f32[8,128]{1,0:T(8,128)S(1)} %get-tuple-element.52.refs_0_), channel_id=1, source_target_pairs={{0,1},{1,0},{2,3},{3,2},{4,5},{5,4},{6,7},{7,6},{8,9},{9,8},{10,11... | collective-permute-start | bytes 12296 | tf_op jit(solution)/shard_map/ppermute | solution.py:255
  (16 other events, 16.1 us)

commit v3 on v1

--- a/solution.py
+++ b/solution.py
@@ -14,6 +14,7 @@
 STEPS = 3
 ROWS = 8
 VMEM = pl.BlockSpec(memory_space=pltpu.VMEM)
+HBM = pl.BlockSpec(memory_space=pltpu.HBM)
 SMEM = pl.BlockSpec(memory_space=pltpu.SMEM)
 F32 = jnp.float32
 BF16 = jnp.bfloat16
@@ -40,12 +41,38 @@
         in_specs=specs,
         out_specs=jax.tree.map(lambda _: VMEM, outs),
         scratch_shapes=scratch,
-        compiler_params=pltpu.CompilerParams(vmem_limit_bytes=16 * 1024 * 1024),
+        compiler_params=pltpu.CompilerParams(vmem_limit_bytes=8 * 1024 * 1024),
     )(*args)
 
 
-def transform_kernel(dims, high_ref, low_ref, foot_ref, off_ref, sub_ref, out_ref):
+def tree_sum(parts):
+    parts = list(parts)
+    while len(parts) > 1:
+        parts = [sum(parts[at:at + 2][1:], parts[at]) for at in range(0, len(parts), 2)]
+    return parts[0]
+
+
+def transform_kernel(dims, high_any, low_any, foot_any, off_any, sub_any, count_any, rinv_any, *refs):
     nc, nb, modes, groups, band = dims
+    out_ref, weight_ref, high_ref, low_ref, foot_ref, off_ref, sub_ref, count_ref, rinv_ref, sems = refs
+    copies = [
+        pltpu.make_async_copy(source, target, sems.at[at])
+        for at, (source, target) in enumerate(
+            [
+                (foot_any, foot_ref),
+                (high_any, high_ref),
+                (low_any, low_ref),
+                (off_any, off_ref),
+                (sub_any, sub_ref),
+                (count_any, count_ref),
+                (rinv_any, rinv_ref),
+            ]
+        )
+    ]
+    for copy in copies:
+        copy.start()
+    for copy in copies:
+        copy.wait()
     ob = foot_ref.shape[1]
     lon = high_ref.shape[1]
     contract = (((1,), (1,)), ((), ()))
@@ -66,6 +93,12 @@
     ids = ids.astype(BF16)
     for c in range(nc):
         out_ref[c, nb * CR * modes:, :] = ids
+    row = lax.broadcasted_iota(jnp.int32, weight_ref.shape, 0)
+    limit = jnp.zeros(weight_ref.shape, jnp.int32)
+    for s in range(weight_ref.shape[0]):
+        limit = jnp.where(row == s, count_ref[s], limit)
+    lane = lax.broadcasted_iota(jnp.int32, weight_ref.shape, 1)
+    weight_ref[...] = jnp.where(lane < limit, rinv_ref[...], 0.0)
 
 
 def fold(ref):
@@ -100,22 +133,30 @@
         out_ref[c] = sim_ref[...]
 
 
-def first_kernel(dims, near_ref, lat_ref, foot_ref, ids_ref, out_ref, field_ref, sim_ref):
+def pieces(refs, size, rows):
+    found = []
+    for ref in refs:
+        found += [ref.at[at:at + rows] for at in range(0, ref.shape[0], rows)]
+    assert len(found) == size
+    return found
+
+
+def first_kernel(dims, no, own_ref, ids_ref, lat_ref, foot_ref, *refs):
     modes = dims[2]
-    per_dev = field_ref.shape[0] // near_ref.shape[0]
-    for i in range(near_ref.shape[0]):
+    near_refs, refs = refs[:-3], refs[-3:]
+    out_ref, field_ref, sim_ref = refs
+    per_dev = field_ref.shape[0] // no
+    for s, near_ref in enumerate(pieces(near_refs, no, per_dev * modes)):
         for l in range(per_dev):
-            field_ref[i * per_dev + l] = near_ref[i, l * modes:(l + 1) * modes, :]
+            field_ref[(own_ref[0] ^ s) * per_dev + l] = near_ref[l * modes:(l + 1) * modes, :]
     forward(dims, field_ref, lat_ref, foot_ref, ids_ref, sim_ref, out_ref)
 
 
-def adjoint_kernel(dims, sim_ref, weight_ref, foot_ref, ids_ref, out_ref, norm_ref, weighted_ref):
+def adjoint_kernel(dims, first, ids_ref, sim_ref, weight_ref, foot_ref, out_ref, norm_ref, weighted_ref):
     nc, nb, modes, groups, band = dims
     subs = weight_ref.shape[0]
     mine = nc * nb
-    total = sim_ref[0]
-    for c in range(1, nc):
-        total += sim_ref[c]
+    total = tree_sum(sim_ref[c] for c in range(nc))
     norm = jnp.sqrt(jnp.sum(total[subs:], keepdims=True))
     norm_ref[...] = jnp.broadcast_to(norm, norm_ref.shape)
     sim = total[:subs] / norm
@@ -134,27 +175,38 @@
     if rest:
         parts.append(jnp.zeros((rest, 128), F32))
     rows = jnp.concatenate(parts, axis=0).T
-    power = sim * weighted
-    for i in range(out_ref.shape[0]):
-        out_ref[i, :mine, :] = rows[:mine]
-        out_ref[i, mine:, :] = power
-
-
-def image_kernel(dims, first, last, *refs):
+    out_ref[:mine, :] = rows[:mine]
+    out_ref[mine:mine + subs, :] = sim * weighted
     if first:
-        coef_ref, norm_ref, field_ref, lat_ref, foot_ref, ids_ref, all_ref, *refs = refs
-        prior_ref = None
-    else:
-        coef_ref, norm_ref, field_ref, prior_ref, lat_ref, foot_ref, ids_ref, all_ref, *refs = refs
-    out_ref, vector_ref, next_ref, alpha_ref, sim_ref = refs
+        lane = lax.broadcasted_iota(jnp.int32, (ROWS, 128), 1)
+        tail = jnp.zeros((ROWS, 128), F32)
+        for j in range(nc):
+            for q in range(2 * nb):
+                tail = jnp.where(lane == j * 2 * nb + q, ids_ref[j, q].astype(F32), tail)
+        out_ref[mine + subs:, :] = tail
+
+
+def every_kernel(dims, no, at, *refs):
+    refs, out_ref = refs[:-1], refs[-1]
+    rows = sum(ref.shape[0] for ref in refs) // no
+    for s, ref in enumerate(pieces(refs, no, rows)):
+        out_ref[s:s + 1, :] = ref[at:at + ROWS, :][0:1].astype(jnp.int32)
+
+
+def image_kernel(dims, no, first, last, own_ref, ids_ref, all_ref, lat_ref, foot_ref, norm_ref, field_ref, *refs):
     nc, nb, modes, groups, band = dims
+    if not first:
+        prior_ref, refs = refs[0], refs[1:]
+    coef_refs, refs = refs[:-6], refs[-6:]
+    out_ref, vector_ref, next_ref, alpha_ref, held_ref, sim_ref = refs
     mine = nc * nb
-    no = coef_ref.shape[0]
     periods = field_ref.shape[0]
-    power = coef_ref[0, mine:, :]
-    for i in range(1, no):
-        power += coef_ref[i, mine:, :]
-    gain = jnp.sum(power, keepdims=True)
+    subs = sim_ref.shape[0] - ROWS
+    rows = sum(ref.shape[0] for ref in coef_refs) // no
+    coef_refs = pieces(coef_refs, no, rows)
+    for s in range(no):
+        held_ref[s] = coef_refs[s][:mine, :]
+    gain = jnp.sum(tree_sum(ref[mine:mine + subs, :] for ref in coef_refs), keepdims=True)
     alpha_ref[...] = jnp.broadcast_to(1.0 + gain, alpha_ref.shape)
     norm = norm_ref[0:1, :]
     for p in range(periods):
@@ -166,13 +218,14 @@
         next_ref[p] = rest
 
     def group(i, carry):
-        coef = coef_ref[i, :mine, :].T
+        at_i = own_ref[0] ^ i
+        coef = held_ref[at_i].T
         for j in range(nc):
             for b in range(nb):
-                off = all_ref[i, j * 2 * nb + b]
+                at = j * nb + b
+                off = all_ref[at_i, j * 2 * nb + b]
                 period = off // groups
                 row = j * band + off % groups * CR
-                at = j * nb + b
                 total = next_ref[period]
                 for r in range(CR):
                     total += coef[r * modes:(r + 1) * modes, at:at + 1] * lat_ref[row + r]
@@ -199,12 +252,10 @@
     norms, refs = refs[:STEPS - 1], refs[STEPS - 1:]
     out_ref, coef_ref = refs
     per_dev = out_ref.shape[1]
-    total = sum_ref[0]
-    for c in range(1, sum_ref.shape[0]):
-        total += sum_ref[c]
+    total = tree_sum(sum_ref[c] for c in range(sum_ref.shape[0]))
     norm = jnp.sqrt(jnp.sum(total, keepdims=True))
     for l in range(per_dev):
-        at = own_ref[0] * per_dev + l
+        at = own_ref[1] * per_dev + l
         for k in range(STEPS):
             out_ref[k, l] = vectors[k][at] * factor
         out_ref[STEPS, l] = field_ref[at] / norm * factor
@@ -216,6 +267,31 @@
         coefs = jnp.where((row == 0) & (col == k), alphas[k][0:1, 0:1], coefs)
         coefs = jnp.where((row == 1) & (col == k), beta, coefs)
     coef_ref[...] = coefs
+
+
+def join_kernel(*refs):
+    refs, out_ref = refs[:-1], refs[-1]
+    rows = refs[0].shape[0]
+    for at, ref in enumerate(refs):
+        out_ref[at * rows:(at + 1) * rows, :] = ref[...]
+
+
+def doubled(size):
+    return size <= 4 and size & (size - 1) == 0
+
+
+def share(array, axis):
+    size = lax.axis_size(axis)
+    if not doubled(size):
+        return [swap(jnp.broadcast_to(array[None], (size,) + array.shape), axis).reshape(-1, array.shape[1])]
+    found, step = array, 1
+    while True:
+        came = lax.ppermute(found, axis, [(d, d ^ step) for d in range(size)])
+        step *= 2
+        if step == size:
+            return [found, came]
+        rows, lanes = found.shape
+        found = call(join_kernel, jax.ShapeDtypeStruct((2 * rows, lanes), F32), [VMEM] * 2, found, came)
 
 
 def swap(array, axis):
@@ -237,75 +313,85 @@
     dims = (nc, nb, modes, groups, band)
     shape = functools.partial(jax.ShapeDtypeStruct, dtype=F32)
 
-    valid = (jnp.arange(ob, dtype=jnp.int32)[None, :] < counts[:, None]).astype(F32)
-    weights = rinv.reshape(subs, ob) * valid
     high, low = lon_table(lon_cols, nc, modes)
     if modes != held:
         start = jnp.pad(start, ((0, 0), (0, modes - held), (0, 0)))
         lat_mats = jnp.pad(lat_mats, ((0, modes - held), (0, 0), (0, 0)))
     lat = lat_mats.transpose(1, 0, 2)
-
+    at_obs = lax.axis_index("obs").astype(jnp.int32)
+    own = jnp.stack([at_obs if doubled(no) else 0 * at_obs, at_obs])
+
+    near = share(start.reshape(per_dev * modes, lat_rows), "obs")
     foot_rows = nb * CR * modes
-    hats = call(
+    hats, weights = call(
         functools.partial(transform_kernel, dims),
-        jax.ShapeDtypeStruct((nc, foot_rows + 16, ob), BF16),
-        [VMEM, VMEM, VMEM, SMEM, SMEM],
-        jnp.asarray(high), jnp.asarray(low), footprints, blk_off, blk_sub,
+        (jax.ShapeDtypeStruct((nc, foot_rows + 16, ob), BF16), shape((subs, ob))),
+        [HBM] * 7,
+        jnp.asarray(high), jnp.asarray(low), footprints, blk_off, blk_sub, counts, rinv.reshape(subs, ob),
+        scratch=[
+            pltpu.VMEM(high.shape, BF16),
+            pltpu.VMEM(low.shape, BF16),
+            pltpu.VMEM(footprints.shape, BF16),
+            pltpu.SMEM((nb,), jnp.int32),
+            pltpu.SMEM((nb,), jnp.int32),
+            pltpu.SMEM((subs,), jnp.int32),
+            pltpu.VMEM((subs, ob), F32),
+            pltpu.SemaphoreType.DMA((7,)),
+        ],
     )
     foot = swap(hats, "cell")
-    ids = foot[:, foot_rows, :2 * nb].astype(F32)
-    tail = jnp.pad(ids.reshape(1, -1), ((0, ROWS - 1), (0, lat_rows - 2 * mine)))
-    ids = ids.astype(jnp.int32)
-    near = jnp.concatenate([start.reshape(per_dev * modes, lat_rows), tail], axis=0)
-    near = swap(jnp.broadcast_to(near[None], (no,) + near.shape), "obs")
-    every = near[:, per_dev * modes, :2 * mine].astype(jnp.int32)
+    ids = foot[:, foot_rows, :2 * nb].astype(jnp.int32)
 
     field_shape = shape((periods, modes, lat_rows))
     small = shape((ROWS, 128))
     sim_scratch = pltpu.VMEM((subs + ROWS, ob), F32)
     sims, field = call(
-        functools.partial(first_kernel, dims),
+        functools.partial(first_kernel, dims, no),
         (shape((nc, subs + ROWS, ob)), field_shape),
-        [VMEM, VMEM, VMEM, SMEM],
-        near, lat, foot, ids,
+        [SMEM, SMEM] + [VMEM] * (2 + len(near)),
+        own, ids, lat, foot, *near,
         scratch=[sim_scratch],
     )
     vectors, alphas, norms = [], [], []
     for step in range(STEPS):
-        last = step == STEPS - 1
-        sims = swap(sims, "cell")
+        first, last = step == 0, step == STEPS - 1
         coefs, norm = call(
-            functools.partial(adjoint_kernel, dims),
-            (shape((no, mine + subs, 128)), small),
-            [VMEM, VMEM, VMEM, SMEM],
-            sims, weights, foot, ids,
+            functools.partial(adjoint_kernel, dims, first),
+            (shape((mine + subs + (ROWS if first else 0), 128)), small),
+            [SMEM] + [VMEM] * 3,
+            ids, swap(sims, "cell"), weights, foot,
             scratch=[pltpu.VMEM((subs, ob), F32)],
         )
-        coefs = swap(coefs, "obs")
-        before = [vectors[-1]] if step else []
+        coefs = share(coefs, "obs")
+        if first:
+            every = call(
+                functools.partial(every_kernel, dims, no, mine + subs),
+                jax.ShapeDtypeStruct((no, 128), jnp.int32),
+                [VMEM] * len(coefs),
+                *coefs,
+            )
+        before = [] if first else [vectors[-1]]
         sims, vector, field, alpha = call(
-            functools.partial(image_kernel, dims, step == 0, last),
+            functools.partial(image_kernel, dims, no, first, last),
             (
                 shape((nc, ROWS if last else subs + ROWS, 128)),
                 field_shape,
                 field_shape,
                 small,
             ),
-            [VMEM] * (5 + len(before)) + [SMEM, SMEM],
-            coefs, norm, field, *before, lat, foot, ids, every,
-            scratch=[sim_scratch],
+            [SMEM] * 3 + [VMEM] * (4 + len(before) + len(coefs)),
+            own, ids, every, lat, foot, norm, field, *before, *coefs,
+            scratch=[pltpu.VMEM((no, mine, 128), F32), sim_scratch],
         )
         vectors.append(vector)
         alphas.append(alpha)
         norms.append(norm)
-    sums = swap(sims, "cell")
     factor = math.sqrt(periods * lon_cols * lat_rows)
-    own = lax.axis_index("obs").astype(jnp.int32).reshape(1)
     krylov, coeffs = call(
         functools.partial(finish_kernel, factor),
         (shape((STEPS + 1, per_dev, modes, lat_rows)), shape((2, STEPS))),
         [SMEM] + [VMEM] * (1 + STEPS + 1 + STEPS + STEPS - 1),
-        own, sums, *vectors, field, *alphas, *norms[1:],
+        own, swap(sims, "cell"), *vectors, field, *alphas, *norms[1:],
     )
     return krylov[:, :, :held], coeffs
 

time: 109 us -> 96.7 us (0.89)
  blocking collectives: 44.6 us -> 30.7 us
  local copies, waits for them, and re-layouts: 16.4 us -> 9.29 us
  Pallas kernels: 13.5 us -> 16.8 us
  waiting for transfers between devices: 17.4 us -> 20.4 us
  starting transfers between devices: 14.8 us -> 17.2 us
    ppermute x0 -> x8, waiting for transfers between devices: none -> 20.1 us  [share(): came = lax.ppermute(found, axis, [(d, d ^ step) for d in range(size)])]
    all_to_all x4 -> x1, waiting for transfers between devices: 17.4 us -> 0.28 us  [swap(): return lax.all_to_all(array, axis, split_axis=0, concat_axis=0, tiled=True)]
    all_to_all x5 -> x4, blocking collectives: 44.6 us -> 30.7 us  [swap(): return lax.all_to_all(array, axis, split_axis=0, concat_axis=0, tiled=True)]
    ppermute x0 -> x8, starting transfers between devices: none -> 12 us  [share(): came = lax.ppermute(found, axis, [(d, d ^ step) for d in range(size)])]
    all_to_all x4 -> x1, starting transfers between devices: 14.8 us -> 5.19 us  [swap(): return lax.all_to_all(array, axis, split_axis=0, concat_axis=0, tiled=True)]
    unnamed x41 -> x17, local copies, waits for them, and re-layouts: 15.6 us -> 9.29 us
    pallas_call x9 -> x14, Pallas kernels: 13.5 us -> 16.8 us  [call(): pl.pallas_call(kernel, out_shape=outs, in_specs=specs, out_specs=jax.tree...]
  transfers between devices with their start and end apart: 4 -> 9, of which waited for: 4 -> 8; matrix products, arithmetic and copies ran while one was open for 3% -> 5% of each run, Pallas kernels for 0% -> 0%
where the time goes in v3:
time: 96.7 us; the launch traced here: 95.8 us
  blocking collectives  30.7 us (32%)
  waiting for transfers between devices  20.4 us (21%)
  starting transfers between devices  17.2 us (18%)
  Pallas kernels  16.8 us (17%)
  local copies, waits for them, and re-layouts  9.29 us (10%)
    all_to_all x4, blocking collectives, swap(): return lax.all_to_all(array, axis, split_axis=0, concat_axis=0, tiled=True)  30.7 us
    ppermute x8, waiting for transfers between devices, share(): came = lax.ppermute(found, axis, [(d, d ^ step) for d in range(size)])  20.1 us
    pallas_call x14, Pallas kernels, call(): pl.pallas_call(kernel, out_shape=outs, in_specs=specs, out_specs=jax.tree...  16.8 us
    ppermute x8, starting transfers between devices, share(): came = lax.ppermute(found, axis, [(d, d ^ step) for d in range(size)])  12 us
    unnamed x17, local copies, waits for them, and re-layouts  9.29 us
    all_to_all x1, starting transfers between devices, swap(): return lax.all_to_all(array, axis, split_axis=0, concat_axis=0, tiled=True)  5.19 us
  transfers between devices with their start and end apart: 9, of which 8 were waited for; matrix products, arithmetic and copies ran while one was open for 5% of the time, Pallas kernels for 0%

profile of v3, /device:TPU:0, one launch (start us, length us, event | category | flops | bytes accessed | tf_op | source)
XLA Modules:
  0.0 95.8 jit_solution(10985110836127424895)
XLA Ops:
  0.6 0.0 copy-start
  0.6 1.0 %copy-done = bf16[2,128,768]{2,1,0:T(8,128)(2,1)S(1)} copy-done((bf16[2,128,768]{2,1,0:T(8,128)(2,1)S(1)}, bf16[2,128,768]{2,1,0:T(8,128)(2,1)}, u32[]{:S(2)}) %copy-start) | copy-done | bytes 393240
  1.6 0.0 copy-start.1
  1.6 1.0 %copy-done.1 = bf16[384,384]{1,0:T(8,128)(2,1)S(1)} copy-done((bf16[384,384]{1,0:T(8,128)(2,1)S(1)}, bf16[384,384]{1,0:T(8,128)(2,1)}, u32[]{:S(2)}) %copy-start.1) | copy-done | bytes 294936
  2.6 0.0 copy-start.2
  2.6 1.0 %copy-done.2 = bf16[384,384]{1,0:T(8,128)(2,1)S(1)} copy-done((bf16[384,384]{1,0:T(8,128)(2,1)S(1)}, bf16[384,384]{1,0:T(8,128)(2,1)}, u32[]{:S(2)}) %copy-start.2) | copy-done | bytes 294936
  3.6 0.0 copy-start.4
  3.6 0.7 copy-done.4
  4.2 0.0 copy-start.5
  4.2 0.7 copy-done.5
  4.9 0.0 copy-start.6
  4.9 0.7 copy-done.6
  5.6 0.7 copy-done.7
  6.2 2.5 %shard_map.104 = (bf16[8,208,128]{2,1,0:T(8,128)(2,1)}, f32[8,128]{1,0:T(8,128)S(1)}) custom-call(bf16[384,384]{1,0:T(8,128)(2,1)S(1)} %copy-done.2, bf16[384,384]{1,0:T(8,128)(2,1)S(1)} %copy-done.1, bf16[2,128,768]{2,1,0:T(8,128)(2,1)S(1)} %copy-done, s32[2]{0:T(128)S(1)} %copy-done.5, s32[2]{0:T(128)S(1)} %copy-done.6, s32[8]{0:T(128)S(1)} %copy-done.7, ...), custom_call_target="tpu_custom_call" | custom-call | tf_op jit(solution)/shard_map/pallas_call | solution.py:38
  8.7 5.2 %all-to-all-start = ((bf16[8,208,128]{2,1,0:T(8,128)(2,1)}), bf16[8,208,128]{2,1,0:T(8,128)(2,1)}, u32[]{:S(2)}, u32[]{:S(2)}) async-start(bf16[8,208,128]{2,1,0:T(8,128)(2,1)} %get-tuple-element.24), calls=%async_computation | async-start | bytes 851968 | tf_op jit(solution)/shard_map/all_to_all | solution.py:298
  13.9 2.0 %collective-permute-start = (f32[48,128]{1,0:T(8,128)}, f32[48,128]{1,0:T(8,128)S(1)}, u32[]{:S(2)}, u32[]{:S(2)}) collective-permute-start(f32[48,128]{1,0:T(8,128)} %bitcast.18), channel_id=1, source_target_pairs={{0,8},{8,0},{16,24},{24,16},{1,9},{9,1},{17,25},{25,17},{2,10},{10... | collective-permute-start | bytes 73736 | tf_op jit(solution)/shard_map/ppermute | solution.py:289
  15.9 0.1 pad_add_fusion.own_ref
  16.0 3.7 %copy.31 = f32[48,128,128]{2,0,1:T(8,128)S(1)} copy(f32[48,128,128]{2,1,0:T(8,128)} %param.10) | data formatting | bytes 6291456 | tf_op args[1]
  19.7 0.0 collective-permute-done.refs_1_
  19.7 0.0 copy-done.3
  19.7 2.7 %collective-permute-start.1 = (f32[96,128]{1,0:T(8,128)S(1)}, f32[96,128]{1,0:T(8,128)S(1)}, u32[]{:S(2)}, u32[]{:S(2)}) collective-permute-start(f32[96,128]{1,0:T(8,128)S(1)} %shard_map.105.refs_0_), channel_id=1, source_target_pairs={{0,16},{8,24},{16,0},{24,8},{1,17},{9,25},{17,1},{25,9},{2,18},{10... | collective-permute-start | bytes 147464 | tf_op jit(solution)/shard_map/ppermute | solution.py:289
  22.4 0.3 all-to-all-done.foot_ref
  22.7 0.7 slice_convert_fusion
  23.4 1.9 %collective-permute-done.1.refs_1_ = f32[96,128]{1,0:T(8,128)S(1)} collective-permute-done((f32[96,128]{1,0:T(8,128)S(1)}, f32[96,128]{1,0:T(8,128)S(1)}, u32[]{:S(2)}, u32[]{:S(2)}) %collective-permute-start.1) | collective-permute-done | bytes 49184 | tf_op jit(solution)/shard_map/ppermute | solution.py:289
  25.3 1.3 %shard_map.106 = (f32[8,16,128]{2,1,0:T(8,128)S(1)}, f32[4,48,128]{2,1,0:T(8,128)S(1)}) custom-call(s32[2]{0:T(128)S(1)} %pad_add_fusion.own_ref, s32[8,4]{1,0:T(8,128)S(1)} %bitcast.11, f32[128,48,128]{2,1,0:T(8,128)S(1)} %bitcast.7, bf16[8,208,128]{2,1,0:T(8,128)(2,1)} %all-to-all-done.foot_ref, f32[96,128]{1,0:T(8,128)S(1)} %shard_map.105.refs_0_, ...), custom_call_target="tpu_custom_call" | custom-call | tf_op jit(solution)/shard_map/pallas_call | solution.py:38
  26.6 8.7 %all_to_all.25.sim_ref = f32[8,16,128]{2,1,0:T(8,128)S(1)} all-to-all(f32[8,16,128]{2,1,0:T(8,128)S(1)} %get-tuple-element.25), channel_id=1, replica_groups=mesh['obs'=4,'cell'=8] {'cell'}, dimensions={0} | all-to-all | bytes 131072 | tf_op jit(solution)/shard_map/all_to_all | solution.py:298
  35.3 1.5 %shard_map.107 = (f32[32,128]{1,0:T(8,128)S(1)}, f32[8,128]{1,0:T(8,128)S(1)}) custom-call(s32[8,4]{1,0:T(8,128)S(1)} %bitcast.12, f32[8,16,128]{2,1,0:T(8,128)S(1)} %all_to_all.25.sim_ref, f32[8,128]{1,0:T(8,128)S(1)} %get-tuple-element.26.weight_ref, bf16[8,208,128]{2,1,0:T(8,128)(2,1)} %all-to-all-done.foot_ref), custom_call_target="tpu_custom_call" | custom-call | tf_op jit(solution)/shard_map/pallas_call | solution.py:38
  36.8 0.0 collective-permute-start.2
  36.8 3.7 %collective-permute-done.2.refs_1_ = f32[32,128]{1,0:T(8,128)S(1)} collective-permute-done((f32[32,128]{1,0:T(8,128)S(1)}, f32[32,128]{1,0:T(8,128)S(1)}, u32[]{:S(2)}, u32[]{:S(2)}) %collective-permute-start.2) | collective-permute-done | bytes 16416 | tf_op jit(solution)/shard_map/ppermute | solution.py:289
  40.5 2.3 %collective-permute-start.3 = (f32[64,128]{1,0:T(8,128)S(1)}, f32[64,128]{1,0:T(8,128)S(1)}, u32[]{:S(2)}, u32[]{:S(2)}) collective-permute-start(f32[64,128]{1,0:T(8,128)S(1)} %shard_map.108.refs_0_), channel_id=1, source_target_pairs={{0,16},{8,24},{16,0},{24,8},{1,17},{9,25},{17,1},{25,9},{2,18},{10... | collective-permute-start | bytes 98312 | tf_op jit(solution)/shard_map/ppermute | solution.py:289
  42.8 2.6 %collective-permute-done.3.refs_1_ = f32[64,128]{1,0:T(8,128)S(1)} collective-permute-done((f32[64,128]{1,0:T(8,128)S(1)}, f32[64,128]{1,0:T(8,128)S(1)}, u32[]{:S(2)}, u32[]{:S(2)}) %collective-permute-start.3) | collective-permute-done | bytes 32800 | tf_op jit(solution)/shard_map/ppermute | solution.py:289
  45.4 2.5 %shard_map.110 = (f32[8,16,128]{2,1,0:T(8,128)S(1)}, f32[4,48,128]{2,1,0:T(8,128)S(1)}, f32[4,48,128]{2,1,0:T(8,128)S(1)}, f32[8,128]{1,0:T(8,128)S(1)}) custom-call(s32[2]{0:T(128)S(1)} %pad_add_fusion.own_ref, s32[8,4]{1,0:T(8,128)S(1)} %bitcast.13, s32[4,128]{1,0:T(4,128)S(1)} %shard_map.109.all_ref, f32[128,48,128]{2,1,0:T(8,128)S(1)} %bitcast.8, ...), custom_call_target="tpu_custom_call" | custom-call | tf_op jit(solution)/shard_map/pallas_call | solution.py:38
  47.9 7.4 %all_to_all.26.sim_ref = f32[8,16,128]{2,1,0:T(8,128)S(1)} all-to-all(f32[8,16,128]{2,1,0:T(8,128)S(1)} %get-tuple-element.30), channel_id=1, replica_groups=mesh['obs'=4,'cell'=8] {'cell'}, dimensions={0} | all-to-all | bytes 131072 | tf_op jit(solution)/shard_map/all_to_all | solution.py:298
  55.3 1.5 %shard_map.111 = (f32[24,128]{1,0:T(8,128)S(1)}, f32[8,128]{1,0:T(8,128)S(1)}) custom-call(s32[8,4]{1,0:T(8,128)S(1)} %bitcast.14, f32[8,16,128]{2,1,0:T(8,128)S(1)} %all_to_all.26.sim_ref, f32[8,128]{1,0:T(8,128)S(1)} %get-tuple-element.26.weight_ref, bf16[8,208,128]{2,1,0:T(8,128)(2,1)} %all-to-all-done.foot_ref), custom_call_target="tpu_custom_call" | custom-call | tf_op jit(solution)/shard_map/pallas_call | solution.py:38
  56.8 0.2 collective-permute-start.4
  57.0 3.5 %collective-permute-done.4.refs_1_ = f32[24,128]{1,0:T(8,128)S(1)} collective-permute-done((f32[24,128]{1,0:T(8,128)S(1)}, f32[24,128]{1,0:T(8,128)S(1)}, u32[]{:S(2)}, u32[]{:S(2)}) %collective-permute-start.4) | collective-permute-done | bytes 12320 | tf_op jit(solution)/shard_map/ppermute | solution.py:289
  60.5 2.2 %collective-permute-start.5 = (f32[48,128]{1,0:T(8,128)S(1)}, f32[48,128]{1,0:T(8,128)S(1)}, u32[]{:S(2)}, u32[]{:S(2)}) collective-permute-start(f32[48,128]{1,0:T(8,128)S(1)} %shard_map.112.refs_1_), channel_id=1, source_target_pairs={{0,16},{8,24},{16,0},{24,8},{1,17},{9,25},{17,1},{25,9},{2,18},{10... | collective-permute-start | bytes 73736 | tf_op jit(solution)/shard_map/ppermute | solution.py:289
  62.8 2.5 %collective-permute-done.5.refs_2_ = f32[48,128]{1,0:T(8,128)S(1)} collective-permute-done((f32[48,128]{1,0:T(8,128)S(1)}, f32[48,128]{1,0:T(8,128)S(1)}, u32[]{:S(2)}, u32[]{:S(2)}) %collective-permute-start.5) | collective-permute-done | bytes 24608 | tf_op jit(solution)/shard_map/ppermute | solution.py:289
  65.2 2.5 %shard_map.113 = (f32[8,16,128]{2,1,0:T(8,128)S(1)}, f32[4,48,128]{2,1,0:T(8,128)S(1)}, f32[4,48,128]{2,1,0:T(8,128)S(1)}, f32[8,128]{1,0:T(8,128)S(1)}) custom-call(s32[2]{0:T(128)S(1)} %pad_add_fusion.own_ref, s32[8,4]{1,0:T(8,128)S(1)} %bitcast.15, s32[4,128]{1,0:T(4,128)S(1)} %shard_map.109.all_ref, f32[128,48,128]{2,1,0:T(8,128)S(1)} %bitcast.9, ...), custom_call_target="tpu_custom_call" | custom-call | tf_op jit(solution)/shard_map/pallas_call | solution.py:38
  67.8 7.4 %all_to_all.27.sim_ref = f32[8,16,128]{2,1,0:T(8,128)S(1)} all-to-all(f32[8,16,128]{2,1,0:T(8,128)S(1)} %get-tuple-element.35), channel_id=1, replica_groups=mesh['obs'=4,'cell'=8] {'cell'}, dimensions={0} | all-to-all | bytes 131072 | tf_op jit(solution)/shard_map/all_to_all | solution.py:298
  75.2 1.5 %shard_map.114 = (f32[24,128]{1,0:T(8,128)S(1)}, f32[8,128]{1,0:T(8,128)S(1)}) custom-call(s32[8,4]{1,0:T(8,128)S(1)} %bitcast.16, f32[8,16,128]{2,1,0:T(8,128)S(1)} %all_to_all.27.sim_ref, f32[8,128]{1,0:T(8,128)S(1)} %get-tuple-element.26.weight_ref, bf16[8,208,128]{2,1,0:T(8,128)(2,1)} %all-to-all-done.foot_ref), custom_call_target="tpu_custom_call" | custom-call | tf_op jit(solution)/shard_map/pallas_call | solution.py:38
  76.7 0.3 collective-permute-start.6
  76.9 3.5 %collective-permute-done.6.refs_1_ = f32[24,128]{1,0:T(8,128)S(1)} collective-permute-done((f32[24,128]{1,0:T(8,128)S(1)}, f32[24,128]{1,0:T(8,128)S(1)}, u32[]{:S(2)}, u32[]{:S(2)}) %collective-permute-start.6) | collective-permute-done | bytes 12320 | tf_op jit(solution)/shard_map/ppermute | solution.py:289
  80.4 2.2 %collective-permute-start.7 = (f32[48,128]{1,0:T(8,128)S(1)}, f32[48,128]{1,0:T(8,128)S(1)}, u32[]{:S(2)}, u32[]{:S(2)}) collective-permute-start(f32[48,128]{1,0:T(8,128)S(1)} %shard_map.115.refs_1_), channel_id=1, source_target_pairs={{0,16},{8,24},{16,0},{24,8},{1,17},{9,25},{17,1},{25,9},{2,18},{10... | collective-permute-start | bytes 73736 | tf_op jit(solution)/shard_map/ppermute | solution.py:289
  82.6 2.5 %collective-permute-done.7.refs_2_ = f32[48,128]{1,0:T(8,128)S(1)} collective-permute-done((f32[48,128]{1,0:T(8,128)S(1)}, f32[48,128]{1,0:T(8,128)S(1)}, u32[]{:S(2)}, u32[]{:S(2)}) %collective-permute-start.7) | collective-permute-done | bytes 24608 | tf_op jit(solution)/shard_map/ppermute | solution.py:289
  85.1 2.2 %shard_map.116 = (f32[8,8,128]{2,1,0:T(8,128)S(1)}, f32[4,48,128]{2,1,0:T(8,128)S(1)}, f32[4,48,128]{2,1,0:T(8,128)S(1)}, f32[8,128]{1,0:T(8,128)S(1)}) custom-call(s32[2]{0:T(128)S(1)} %pad_add_fusion.own_ref, s32[8,4]{1,0:T(8,128)S(1)} %bitcast.17, s32[4,128]{1,0:T(4,128)S(1)} %shard_map.109.all_ref, f32[128,48,128]{2,1,0:T(8,128)S(1)} %bitcast.10, ...), custom_call_target="tpu_custom_call" | custom-call | tf_op jit(solution)/shard_map/pallas_call | solution.py:38
  87.3 7.2 %all_to_all.28.sum_ref = f32[8,8,128]{2,1,0:T(8,128)S(1)} all-to-all(f32[8,8,128]{2,1,0:T(8,128)S(1)} %get-tuple-element.40), channel_id=1, replica_groups=mesh['obs'=4,'cell'=8] {'cell'}, dimensions={0} | all-to-all | bytes 65536 | tf_op jit(solution)/shard_map/all_to_all | solution.py:298
  94.5 1.3 %shard_map.117 = (f32[4,1,48,128]{3,2,1,0:T(8,128)}, f32[2,3]{1,0:T(2,128)}) custom-call(s32[2]{0:T(128)S(1)} %pad_add_fusion.own_ref, f32[8,8,128]{2,1,0:T(8,128)S(1)} %all_to_all.28.sum_ref, f32[4,48,128]{2,1,0:T(8,128)S(1)} %get-tuple-element.33.refs_0_, f32[4,48,128]{2,1,0:T(8,128)S(1)} %get-tuple-element.38.refs_0_.refs_1_, ...), custom_call_target="tpu_custom_call" | custom-call | tf_op jit(solution)/shard_map/pallas_call | solution.py:38
  (7 shorter events, 0.0 us)
Async XLA Ops:
  0.6 1.0 %copy-start = (bf16[2,128,768]{2,1,0:T(8,128)(2,1)S(1)}, bf16[2,128,768]{2,1,0:T(8,128)(2,1)}, u32[]{:S(2)}) copy-start(bf16[2,128,768]{2,1,0:T(8,128)(2,1)} %foot_any.1) | copy-start | bytes 1179652
  1.6 1.0 %copy-start.1 = (bf16[384,384]{1,0:T(8,128)(2,1)S(1)}, bf16[384,384]{1,0:T(8,128)(2,1)}, u32[]{:S(2)}) copy-start(bf16[384,384]{1,0:T(8,128)(2,1)} %constant.10.clone.low_any) | copy-start | bytes 884740
  2.6 1.0 %copy-start.2 = (bf16[384,384]{1,0:T(8,128)(2,1)S(1)}, bf16[384,384]{1,0:T(8,128)(2,1)}, u32[]{:S(2)}) copy-start(bf16[384,384]{1,0:T(8,128)(2,1)} %constant.9.clone.high_any) | copy-start | bytes 884740
  3.6 0.7 copy-start.4
  4.2 0.7 copy-start.5
  4.9 0.7 copy-start.6
  5.6 0.7 copy-start.7
  8.7 14.0 %all-to-all-start = ((bf16[8,208,128]{2,1,0:T(8,128)(2,1)}), bf16[8,208,128]{2,1,0:T(8,128)(2,1)}, u32[]{:S(2)}, u32[]{:S(2)}) async-start(bf16[8,208,128]{2,1,0:T(8,128)(2,1)} %get-tuple-element.24), calls=%async_computation | async-start | bytes 851968 | tf_op jit(solution)/shard_map/all_to_all | solution.py:298
  13.9 5.8 %collective-permute-start = (f32[48,128]{1,0:T(8,128)}, f32[48,128]{1,0:T(8,128)S(1)}, u32[]{:S(2)}, u32[]{:S(2)}) collective-permute-start(f32[48,128]{1,0:T(8,128)} %bitcast.18), channel_id=1, source_target_pairs={{0,8},{8,0},{16,24},{24,16},{1,9},{9,1},{17,25},{25,17},{2,10},{10... | collective-permute-start | bytes 73736 | tf_op jit(solution)/shard_map/ppermute | solution.py:289
  16.0 3.7 %copy-start.3 = (f32[1,48,128]{2,1,0:T(8,128)S(1)}, f32[1,48,128]{2,1,0:T(8,128)}, u32[]{:S(2)}) copy-start(f32[1,48,128]{2,1,0:T(8,128)} %param.9) | copy-start | bytes 73732
  19.7 5.5 %collective-permute-start.1 = (f32[96,128]{1,0:T(8,128)S(1)}, f32[96,128]{1,0:T(8,128)S(1)}, u32[]{:S(2)}, u32[]{:S(2)}) collective-permute-start(f32[96,128]{1,0:T(8,128)S(1)} %shard_map.105.refs_0_), channel_id=1, source_target_pairs={{0,16},{8,24},{16,0},{24,8},{1,17},{9,25},{17,1},{25,9},{2,18},{10... | collective-permute-start | bytes 147464 | tf_op jit(solution)/shard_map/ppermute | solution.py:289
  36.8 3.8 %collective-permute-start.2 = (f32[32,128]{1,0:T(8,128)S(1)}, f32[32,128]{1,0:T(8,128)S(1)}, u32[]{:S(2)}, u32[]{:S(2)}) collective-permute-start(f32[32,128]{1,0:T(8,128)S(1)} %get-tuple-element.27.refs_0_), channel_id=1, source_target_pairs={{0,8},{8,0},{16,24},{24,16},{1,9},{9,1},{17,25},{25,17},{2,10},{10... | collective-permute-start | bytes 49160 | tf_op jit(solution)/shard_map/ppermute | solution.py:289
  40.5 4.8 %collective-permute-start.3 = (f32[64,128]{1,0:T(8,128)S(1)}, f32[64,128]{1,0:T(8,128)S(1)}, u32[]{:S(2)}, u32[]{:S(2)}) collective-permute-start(f32[64,128]{1,0:T(8,128)S(1)} %shard_map.108.refs_0_), channel_id=1, source_target_pairs={{0,16},{8,24},{16,0},{24,8},{1,17},{9,25},{17,1},{25,9},{2,18},{10... | collective-permute-start | bytes 98312 | tf_op jit(solution)/shard_map/ppermute | solution.py:289
  56.8 3.7 %collective-permute-start.4 = (f32[24,128]{1,0:T(8,128)S(1)}, f32[24,128]{1,0:T(8,128)S(1)}, u32[]{:S(2)}, u32[]{:S(2)}) collective-permute-start(f32[24,128]{1,0:T(8,128)S(1)} %get-tuple-element.34.refs_0_), channel_id=1, source_target_pairs={{0,8},{8,0},{16,24},{24,16},{1,9},{9,1},{17,25},{25,17},{2,10},{10... | collective-permute-start | bytes 36872 | tf_op jit(solution)/shard_map/ppermute | solution.py:289
  60.5 4.7 %collective-permute-start.5 = (f32[48,128]{1,0:T(8,128)S(1)}, f32[48,128]{1,0:T(8,128)S(1)}, u32[]{:S(2)}, u32[]{:S(2)}) collective-permute-start(f32[48,128]{1,0:T(8,128)S(1)} %shard_map.112.refs_1_), channel_id=1, source_target_pairs={{0,16},{8,24},{16,0},{24,8},{1,17},{9,25},{17,1},{25,9},{2,18},{10... | collective-permute-start | bytes 73736 | tf_op jit(solution)/shard_map/ppermute | solution.py:289
  76.7 3.7 %collective-permute-start.6 = (f32[24,128]{1,0:T(8,128)S(1)}, f32[24,128]{1,0:T(8,128)S(1)}, u32[]{:S(2)}, u32[]{:S(2)}) collective-permute-start(f32[24,128]{1,0:T(8,128)S(1)} %get-tuple-element.39.refs_0_), channel_id=1, source_target_pairs={{0,8},{8,0},{16,24},{24,16},{1,9},{9,1},{17,25},{25,17},{2,10},{10... | collective-permute-start | bytes 36872 | tf_op jit(solution)/shard_map/ppermute | solution.py:289
  80.4 4.7 %collective-permute-start.7 = (f32[48,128]{1,0:T(8,128)S(1)}, f32[48,128]{1,0:T(8,128)S(1)}, u32[]{:S(2)}, u32[]{:S(2)}) collective-permute-start(f32[48,128]{1,0:T(8,128)S(1)} %shard_map.115.refs_1_), channel_id=1, source_target_pairs={{0,16},{8,24},{16,0},{24,8},{1,17},{9,25},{17,1},{25,9},{2,18},{10... | collective-permute-start | bytes 73736 | tf_op jit(solution)/shard_map/ppermute | solution.py:289

commit v4 on v3

--- a/solution.py
+++ b/solution.py
@@ -14,7 +14,7 @@
 STEPS = 3
 ROWS = 8
 VMEM = pl.BlockSpec(memory_space=pltpu.VMEM)
-HBM = pl.BlockSpec(memory_space=pltpu.HBM)
+ANY = pl.BlockSpec(memory_space=pl.ANY)
 SMEM = pl.BlockSpec(memory_space=pltpu.SMEM)
 F32 = jnp.float32
 BF16 = jnp.bfloat16
@@ -34,14 +34,14 @@
     return high, low
 
 
-def call(kernel, outs, specs, *args, scratch=()):
+def call(kernel, outs, specs, *args, scratch=(), limit=8):
     return pl.pallas_call(
         kernel,
         out_shape=outs,
         in_specs=specs,
         out_specs=jax.tree.map(lambda _: VMEM, outs),
         scratch_shapes=scratch,
-        compiler_params=pltpu.CompilerParams(vmem_limit_bytes=8 * 1024 * 1024),
+        compiler_params=pltpu.CompilerParams(vmem_limit_bytes=limit * 1024 * 1024),
     )(*args)
 
 
@@ -141,14 +141,22 @@
     return found
 
 
-def first_kernel(dims, no, own_ref, ids_ref, lat_ref, foot_ref, *refs):
-    modes = dims[2]
-    near_refs, refs = refs[:-3], refs[-3:]
-    out_ref, field_ref, sim_ref = refs
+def first_kernel(dims, no, own_ref, lat_ref, came_ref, *refs):
+    nc, nb, modes, _, _ = dims
+    near_refs, refs = refs[:-7], refs[-7:]
+    out_ref, field_ref, foot_ref, all_ref, sim_ref, ids_ref, sem = refs
+    rows = nb * CR * modes
+    for j in range(nc):
+        all_ref[j:j + 1, :] = came_ref[j, rows:rows + 16, :].astype(F32)[0:1].astype(jnp.int32)
+    copy = pltpu.make_async_copy(all_ref, ids_ref, sem)
+    copy.start()
+    for j in range(nc):
+        foot_ref[j] = came_ref[j, :rows, :]
     per_dev = field_ref.shape[0] // no
     for s, near_ref in enumerate(pieces(near_refs, no, per_dev * modes)):
         for l in range(per_dev):
             field_ref[(own_ref[0] ^ s) * per_dev + l] = near_ref[l * modes:(l + 1) * modes, :]
+    copy.wait()
     forward(dims, field_ref, lat_ref, foot_ref, ids_ref, sim_ref, out_ref)
 
 
@@ -197,10 +205,14 @@
     nc, nb, modes, groups, band = dims
     if not first:
         prior_ref, refs = refs[0], refs[1:]
-    coef_refs, refs = refs[:-6], refs[-6:]
-    out_ref, vector_ref, next_ref, alpha_ref, held_ref, sim_ref = refs
+    coef_refs, refs = refs[:-7], refs[-7:]
+    if last:
+        out_ref, row_ref, mine_ref, alpha_ref, next_ref, held_ref, sim_ref = refs
+    else:
+        out_ref, row_ref, next_ref, vector_ref, alpha_ref, held_ref, sim_ref = refs
     mine = nc * nb
     periods = field_ref.shape[0]
+    per_dev = row_ref.shape[0]
     subs = sim_ref.shape[0] - ROWS
     rows = sum(ref.shape[0] for ref in coef_refs) // no
     coef_refs = pieces(coef_refs, no, rows)
@@ -209,13 +221,17 @@
     gain = jnp.sum(tree_sum(ref[mine:mine + subs, :] for ref in coef_refs), keepdims=True)
     alpha_ref[...] = jnp.broadcast_to(1.0 + gain, alpha_ref.shape)
     norm = norm_ref[0:1, :]
+    scale = 1.0 / norm
     for p in range(periods):
-        vector = field_ref[p] / norm
-        vector_ref[p] = vector
+        vector = field_ref[p] * scale
+        if not last:
+            vector_ref[p] = vector
         rest = vector * -gain
         if not first:
             rest -= prior_ref[p] * norm
         next_ref[p] = rest
+    for l in range(per_dev):
+        row_ref[l] = field_ref[own_ref[1] * per_dev + l] * scale
 
     def group(i, carry):
         at_i = own_ref[0] ^ i
@@ -241,24 +257,23 @@
         total = fold(next_ref)
         for c in range(nc):
             out_ref[c] = total
+        for l in range(per_dev):
+            mine_ref[l] = next_ref[own_ref[1] * per_dev + l]
     else:
         forward(dims, next_ref, lat_ref, foot_ref, ids_ref, sim_ref, out_ref)
 
 
-def finish_kernel(factor, own_ref, sum_ref, *refs):
-    vectors, refs = refs[:STEPS], refs[STEPS:]
-    field_ref, refs = refs[0], refs[1:]
+def finish_kernel(factor, sum_ref, *refs):
+    row_refs, refs = refs[:STEPS], refs[STEPS:]
+    mine_ref, refs = refs[0], refs[1:]
     alphas, refs = refs[:STEPS], refs[STEPS:]
     norms, refs = refs[:STEPS - 1], refs[STEPS - 1:]
     out_ref, coef_ref = refs
-    per_dev = out_ref.shape[1]
     total = tree_sum(sum_ref[c] for c in range(sum_ref.shape[0]))
     norm = jnp.sqrt(jnp.sum(total, keepdims=True))
-    for l in range(per_dev):
-        at = own_ref[1] * per_dev + l
-        for k in range(STEPS):
-            out_ref[k, l] = vectors[k][at] * factor
-        out_ref[STEPS, l] = field_ref[at] / norm * factor
+    for k in range(STEPS):
+        out_ref[k] = row_refs[k][...] * factor
+    out_ref[STEPS] = mine_ref[...] * (factor / norm)
     row = lax.broadcasted_iota(jnp.int32, coef_ref.shape, 0)
     col = lax.broadcasted_iota(jnp.int32, coef_ref.shape, 1)
     coefs = jnp.zeros(coef_ref.shape, F32)
@@ -269,29 +284,15 @@
     coef_ref[...] = coefs
 
 
-def join_kernel(*refs):
-    refs, out_ref = refs[:-1], refs[-1]
-    rows = refs[0].shape[0]
-    for at, ref in enumerate(refs):
-        out_ref[at * rows:(at + 1) * rows, :] = ref[...]
-
-
-def doubled(size):
+def permuted(size):
     return size <= 4 and size & (size - 1) == 0
 
 
 def share(array, axis):
     size = lax.axis_size(axis)
-    if not doubled(size):
+    if not permuted(size):
         return [swap(jnp.broadcast_to(array[None], (size,) + array.shape), axis).reshape(-1, array.shape[1])]
-    found, step = array, 1
-    while True:
-        came = lax.ppermute(found, axis, [(d, d ^ step) for d in range(size)])
-        step *= 2
-        if step == size:
-            return [found, came]
-        rows, lanes = found.shape
-        found = call(join_kernel, jax.ShapeDtypeStruct((2 * rows, lanes), F32), [VMEM] * 2, found, came)
+    return [array] + [lax.ppermute(array, axis, [(d, d ^ s) for d in range(size)]) for s in range(1, size)]
 
 
 def swap(array, axis):
@@ -319,14 +320,14 @@
         lat_mats = jnp.pad(lat_mats, ((0, modes - held), (0, 0), (0, 0)))
     lat = lat_mats.transpose(1, 0, 2)
     at_obs = lax.axis_index("obs").astype(jnp.int32)
-    own = jnp.stack([at_obs if doubled(no) else 0 * at_obs, at_obs])
+    own = jnp.stack([at_obs if permuted(no) else 0 * at_obs, at_obs])
 
     near = share(start.reshape(per_dev * modes, lat_rows), "obs")
     foot_rows = nb * CR * modes
     hats, weights = call(
         functools.partial(transform_kernel, dims),
         (jax.ShapeDtypeStruct((nc, foot_rows + 16, ob), BF16), shape((subs, ob))),
-        [HBM] * 7,
+        [ANY] * 7,
         jnp.asarray(high), jnp.asarray(low), footprints, blk_off, blk_sub, counts, rinv.reshape(subs, ob),
         scratch=[
             pltpu.VMEM(high.shape, BF16),
@@ -338,21 +339,28 @@
             pltpu.VMEM((subs, ob), F32),
             pltpu.SemaphoreType.DMA((7,)),
         ],
+        limit=48,
     )
-    foot = swap(hats, "cell")
-    ids = foot[:, foot_rows, :2 * nb].astype(jnp.int32)
+    came = swap(hats, "cell")
 
     field_shape = shape((periods, modes, lat_rows))
     small = shape((ROWS, 128))
     sim_scratch = pltpu.VMEM((subs + ROWS, ob), F32)
-    sims, field = call(
+    own_shape = shape((per_dev, modes, lat_rows))
+    sims, field, foot, ids = call(
         functools.partial(first_kernel, dims, no),
-        (shape((nc, subs + ROWS, ob)), field_shape),
-        [SMEM, SMEM] + [VMEM] * (2 + len(near)),
-        own, ids, lat, foot, *near,
-        scratch=[sim_scratch],
+        (
+            shape((nc, subs + ROWS, ob)),
+            field_shape,
+            jax.ShapeDtypeStruct((nc, foot_rows, ob), BF16),
+            jax.ShapeDtypeStruct((nc, 128), jnp.int32),
+        ),
+        [SMEM] + [VMEM] * (2 + len(near)),
+        own, lat, came, *near,
+        scratch=[sim_scratch, pltpu.SMEM((nc, 128), jnp.int32), pltpu.SemaphoreType.DMA],
     )
-    vectors, alphas, norms = [], [], []
+    rows, alphas, norms = [], [], []
+    vector = None
     for step in range(STEPS):
         first, last = step == 0, step == STEPS - 1
         coefs, norm = call(
@@ -370,28 +378,30 @@
                 [VMEM] * len(coefs),
                 *coefs,
             )
-        before = [] if first else [vectors[-1]]
-        sims, vector, field, alpha = call(
+        before = [] if first else [vector]
+        sims, row, field, *vector, alpha = call(
             functools.partial(image_kernel, dims, no, first, last),
             (
                 shape((nc, ROWS if last else subs + ROWS, 128)),
-                field_shape,
-                field_shape,
+                own_shape,
+                own_shape if last else field_shape,
+                *([] if last else [field_shape]),
                 small,
             ),
             [SMEM] * 3 + [VMEM] * (4 + len(before) + len(coefs)),
             own, ids, every, lat, foot, norm, field, *before, *coefs,
-            scratch=[pltpu.VMEM((no, mine, 128), F32), sim_scratch],
+            scratch=[pltpu.VMEM(field_shape.shape, F32)] * last + [pltpu.VMEM((no, mine, 128), F32), sim_scratch],
         )
-        vectors.append(vector)
+        vector = None if last else vector[0]
+        rows.append(row)
         alphas.append(alpha)
         norms.append(norm)
     factor = math.sqrt(periods * lon_cols * lat_rows)
     krylov, coeffs = call(
         functools.partial(finish_kernel, factor),
         (shape((STEPS + 1, per_dev, modes, lat_rows)), shape((2, STEPS))),
-        [SMEM] + [VMEM] * (1 + STEPS + 1 + STEPS + STEPS - 1),
-        own, swap(sims, "cell"), *vectors, field, *alphas, *norms[1:],
+        [VMEM] * (1 + STEPS + 1 + STEPS + STEPS - 1),
+        swap(sims, "cell"), *rows, field, *alphas, *norms[1:],
     )
     return krylov[:, :, :held], coeffs
 

time: 96.7 us -> 87.6 us (0.906)
  waiting for transfers between devices: 20.4 us -> 8.62 us
  starting transfers between devices: 17.2 us -> 23.1 us
  Pallas kernels: 16.8 us -> 14.4 us
    ppermute x8 -> x12, waiting for transfers between devices: 20.1 us -> 8.62 us  [share(): lax.ppermute(array, axis, [(d, d ^ s) for d in range(size)])]
    ppermute x8 -> x12, starting transfers between devices: 12 us -> 17.9 us  [share(): lax.ppermute(array, axis, [(d, d ^ s) for d in range(size)])]
    pallas_call x14 -> x10, Pallas kernels: 16.8 us -> 14.4 us  [call(): pl.pallas_call(kernel, out_shape=outs, in_specs=specs, out_specs=jax.tree...]
  transfers between devices with their start and end apart: 9 -> 13, of which waited for: 8 -> 9; matrix products, arithmetic and copies ran while one was open for 5% -> 4% of each run, Pallas kernels for 0% -> 0%
where the time goes in v4:
time: 87.6 us; the launch traced here: 87.1 us
  blocking collectives  30.9 us (35%)
  starting transfers between devices  23.1 us (26%)
  Pallas kernels  14.4 us (16%)
  local copies, waits for them, and re-layouts  9.29 us (11%)
  waiting for transfers between devices  8.62 us (10%)
    all_to_all x4, blocking collectives, swap(): return lax.all_to_all(array, axis, split_axis=0, concat_axis=0, tiled=True)  30.9 us
    ppermute x12, starting transfers between devices, share(): lax.ppermute(array, axis, [(d, d ^ s) for d in range(size)])  17.9 us
    pallas_call x10, Pallas kernels, call(): pl.pallas_call(kernel, out_shape=outs, in_specs=specs, out_specs=jax.tree...  14.4 us
    unnamed x17, local copies, waits for them, and re-layouts  9.29 us
    ppermute x12, waiting for transfers between devices, share(): lax.ppermute(array, axis, [(d, d ^ s) for d in range(size)])  8.62 us
    all_to_all x1, starting transfers between devices, swap(): return lax.all_to_all(array, axis, split_axis=0, concat_axis=0, tiled=True)  5.19 us
  transfers between devices with their start and end apart: 13, of which 9 were waited for; matrix products, arithmetic and copies ran while one was open for 4% of the time, Pallas kernels for 0%

profile of v4, /device:TPU:0, one launch (start us, length us, event | category | flops | bytes accessed | tf_op | source)
XLA Modules:
  0.0 87.1 jit_solution(7387297844062031199)
XLA Ops:
  0.6 1.0 %copy-done = bf16[2,128,768]{2,1,0:T(8,128)(2,1)S(1)} copy-done((bf16[2,128,768]{2,1,0:T(8,128)(2,1)S(1)}, bf16[2,128,768]{2,1,0:T(8,128)(2,1)}, u32[]{:S(2)}) %copy-start) | copy-done | bytes 393240
  1.6 1.0 %copy-done.1 = bf16[384,384]{1,0:T(8,128)(2,1)S(1)} copy-done((bf16[384,384]{1,0:T(8,128)(2,1)S(1)}, bf16[384,384]{1,0:T(8,128)(2,1)}, u32[]{:S(2)}) %copy-start.1) | copy-done | bytes 294936
  2.6 1.0 %copy-done.2 = bf16[384,384]{1,0:T(8,128)(2,1)S(1)} copy-done((bf16[384,384]{1,0:T(8,128)(2,1)S(1)}, bf16[384,384]{1,0:T(8,128)(2,1)}, u32[]{:S(2)}) %copy-start.2) | copy-done | bytes 294936
  3.6 0.7 copy-done.4
  4.2 0.7 copy-done.5
  4.9 0.7 copy-done.6
  5.6 0.7 copy-done.7
  6.2 2.5 %shard_map.104 = (bf16[8,208,128]{2,1,0:T(8,128)(2,1)}, f32[8,128]{1,0:T(8,128)S(1)}) custom-call(bf16[384,384]{1,0:T(8,128)(2,1)S(1)} %copy-done.2, bf16[384,384]{1,0:T(8,128)(2,1)S(1)} %copy-done.1, bf16[2,128,768]{2,1,0:T(8,128)(2,1)S(1)} %copy-done, s32[2]{0:T(128)S(1)} %copy-done.5, s32[2]{0:T(128)S(1)} %copy-done.6, s32[8]{0:T(128)S(1)} %copy-done.7, ...), custom_call_target="tpu_custom_call" | custom-call | tf_op jit(solution)/shard_map/pallas_call | solution.py:38
  8.7 5.2 %all-to-all-start = ((bf16[8,208,128]{2,1,0:T(8,128)(2,1)}), bf16[8,208,128]{2,1,0:T(8,128)(2,1)}, u32[]{:S(2)}, u32[]{:S(2)}) async-start(bf16[8,208,128]{2,1,0:T(8,128)(2,1)} %get-tuple-element.28), calls=%async_computation | async-start | bytes 851968 | tf_op jit(solution)/shard_map/all_to_all | solution.py:299
  13.9 4.0 %collective-permute-start.2 = (f32[48,128]{1,0:T(8,128)}, f32[48,128]{1,0:T(8,128)S(1)}, u32[]{:S(2)}, u32[]{:S(2)}) collective-permute-start(f32[48,128]{1,0:T(8,128)} %bitcast.10), channel_id=1, source_target_pairs={{0,24},{8,16},{16,8},{24,0},{1,25},{9,17},{17,9},{25,1},{2,26},{10... | collective-permute-start | bytes 73736 | tf_op jit(solution)/shard_map/ppermute | solution.py:295
  17.9 0.0 collective-permute-start.1
  17.9 0.6 collective-permute-start
  18.6 0.1 pad_add_fusion.own_ref
  18.7 3.7 %copy.13 = f32[48,128,128]{2,0,1:T(8,128)S(1)} copy(f32[48,128,128]{2,1,0:T(8,128)} %param.10) | data formatting | bytes 6291456 | tf_op args[1]
  22.4 0.0 collective-permute-done.2.refs_3_
  22.4 0.5 collective-permute-done.1.refs_2_
  22.9 0.0 collective-permute-done.refs_1_
  22.9 0.0 all-to-all-done.came_ref
  22.9 2.0 %shard_map.105 = (f32[8,16,128]{2,1,0:T(8,128)S(1)}, f32[4,48,128]{2,1,0:T(8,128)S(1)}, bf16[8,192,128]{2,1,0:T(8,128)(2,1)S(1)}, s32[8,128]{1,0:T(8,128)S(1)}) custom-call(s32[2]{0:T(128)S(1)} %pad_add_fusion.own_ref, f32[128,48,128]{2,1,0:T(8,128)S(1)} %bitcast.6, bf16[8,208,128]{2,1,0:T(8,128)(2,1)} %all-to-all-done.came_ref, f32[48,128]{1,0:T(8,128)S(1)} %bitcast.13, ...), custom_call_target="tpu_custom_call" | custom-call | tf_op jit(solution)/shard_map/pallas_call | solution.py:38
  24.8 8.9 %all_to_all.25.sim_ref = f32[8,16,128]{2,1,0:T(8,128)S(1)} all-to-all(f32[8,16,128]{2,1,0:T(8,128)S(1)} %get-tuple-element.30), channel_id=1, replica_groups=mesh['obs'=4,'cell'=8] {'cell'}, dimensions={0} | all-to-all | bytes 131072 | tf_op jit(solution)/shard_map/all_to_all | solution.py:299
  33.7 1.1 %shard_map.106 = (f32[32,128]{1,0:T(8,128)S(1)}, f32[8,128]{1,0:T(8,128)S(1)}) custom-call(s32[8,128]{1,0:T(8,128)S(1)} %get-tuple-element.29.ids_ref, f32[8,16,128]{2,1,0:T(8,128)S(1)} %all_to_all.25.sim_ref, f32[8,128]{1,0:T(8,128)S(1)} %get-tuple-element.31.weight_ref, bf16[8,192,128]{2,1,0:T(8,128)(2,1)S(1)} %get-tuple-element.32.foot_ref), custom_call_target="tpu_custom_call" | custom-call | tf_op jit(solution)/shard_map/pallas_call | solution.py:38
  34.8 3.3 %collective-permute-start.5 = (f32[32,128]{1,0:T(8,128)S(1)}, f32[32,128]{1,0:T(8,128)S(1)}, u32[]{:S(2)}, u32[]{:S(2)}) collective-permute-start(f32[32,128]{1,0:T(8,128)S(1)} %get-tuple-element.33.refs_0_), channel_id=1, source_target_pairs={{0,24},{8,16},{16,8},{24,0},{1,25},{9,17},{17,9},{25,1},{2,26},{10... | collective-permute-start | bytes 49160 | tf_op jit(solution)/shard_map/ppermute | solution.py:295
  38.1 0.0 collective-permute-start.4
  38.1 1.1 %collective-permute-start.3 = (f32[32,128]{1,0:T(8,128)S(1)}, f32[32,128]{1,0:T(8,128)S(1)}, u32[]{:S(2)}, u32[]{:S(2)}) collective-permute-start(f32[32,128]{1,0:T(8,128)S(1)} %get-tuple-element.33.refs_0_), channel_id=1, source_target_pairs={{0,8},{8,0},{16,24},{24,16},{1,9},{9,1},{17,25},{25,17},{2,10},{10... | collective-permute-start | bytes 49160 | tf_op jit(solution)/shard_map/ppermute | solution.py:295
  39.2 1.2 %collective-permute-done.5.refs_3_ = f32[32,128]{1,0:T(8,128)S(1)} collective-permute-done((f32[32,128]{1,0:T(8,128)S(1)}, f32[32,128]{1,0:T(8,128)S(1)}, u32[]{:S(2)}, u32[]{:S(2)}) %collective-permute-start.5) | collective-permute-done | bytes 16416 | tf_op jit(solution)/shard_map/ppermute | solution.py:295
  40.4 2.3 %collective-permute-done.4.refs_2_ = f32[32,128]{1,0:T(8,128)S(1)} collective-permute-done((f32[32,128]{1,0:T(8,128)S(1)}, f32[32,128]{1,0:T(8,128)S(1)}, u32[]{:S(2)}, u32[]{:S(2)}) %collective-permute-start.4) | collective-permute-done | bytes 16416 | tf_op jit(solution)/shard_map/ppermute | solution.py:295
  42.7 0.0 collective-permute-done.3.refs_1_
  42.7 2.1 %shard_map.108 = (f32[8,16,128]{2,1,0:T(8,128)S(1)}, f32[1,48,128]{2,1,0:T(8,128)S(1)}, f32[4,48,128]{2,1,0:T(8,128)S(1)}, f32[4,48,128]{2,1,0:T(8,128)S(1)}, f32[8,128]{1,0:T(8,128)S(1)}) custom-call(s32[2]{0:T(128)S(1)} %pad_add_fusion.own_ref, s32[8,128]{1,0:T(8,128)S(1)} %get-tuple-element.29.ids_ref, s32[4,128]{1,0:T(4,128)S(1)} %shard_map.107.all_ref, ...), custom_call_target="tpu_custom_call" | custom-call | tf_op jit(solution)/shard_map/pallas_call | solution.py:38
  44.9 7.4 %all_to_all.26.sim_ref = f32[8,16,128]{2,1,0:T(8,128)S(1)} all-to-all(f32[8,16,128]{2,1,0:T(8,128)S(1)} %get-tuple-element.36), channel_id=1, replica_groups=mesh['obs'=4,'cell'=8] {'cell'}, dimensions={0} | all-to-all | bytes 131072 | tf_op jit(solution)/shard_map/all_to_all | solution.py:299
  52.3 1.1 %shard_map.109 = (f32[24,128]{1,0:T(8,128)S(1)}, f32[8,128]{1,0:T(8,128)S(1)}) custom-call(s32[8,128]{1,0:T(8,128)S(1)} %get-tuple-element.29.ids_ref, f32[8,16,128]{2,1,0:T(8,128)S(1)} %all_to_all.26.sim_ref, f32[8,128]{1,0:T(8,128)S(1)} %get-tuple-element.31.weight_ref, bf16[8,192,128]{2,1,0:T(8,128)(2,1)S(1)} %get-tuple-element.32.foot_ref), custom_call_target="tpu_custom_call" | custom-call | tf_op jit(solution)/shard_map/pallas_call | solution.py:38
  53.3 1.5 %collective-permute-start.8 = (f32[24,128]{1,0:T(8,128)S(1)}, f32[24,128]{1,0:T(8,128)S(1)}, u32[]{:S(2)}, u32[]{:S(2)}) collective-permute-start(f32[24,128]{1,0:T(8,128)S(1)} %get-tuple-element.40.refs_1_), channel_id=1, source_target_pairs={{0,24},{8,16},{16,8},{24,0},{1,25},{9,17},{17,9},{25,1},{2,26},{10... | collective-permute-start | bytes 36872 | tf_op jit(solution)/shard_map/ppermute | solution.py:295
  54.8 0.6 collective-permute-start.7
  55.4 2.3 %collective-permute-start.6 = (f32[24,128]{1,0:T(8,128)S(1)}, f32[24,128]{1,0:T(8,128)S(1)}, u32[]{:S(2)}, u32[]{:S(2)}) collective-permute-start(f32[24,128]{1,0:T(8,128)S(1)} %get-tuple-element.40.refs_1_), channel_id=1, source_target_pairs={{0,8},{8,0},{16,24},{24,16},{1,9},{9,1},{17,25},{25,17},{2,10},{10... | collective-permute-start | bytes 36872 | tf_op jit(solution)/shard_map/ppermute | solution.py:295
  57.7 1.1 %collective-permute-done.8.refs_4_ = f32[24,128]{1,0:T(8,128)S(1)} collective-permute-done((f32[24,128]{1,0:T(8,128)S(1)}, f32[24,128]{1,0:T(8,128)S(1)}, u32[]{:S(2)}, u32[]{:S(2)}) %collective-permute-start.8) | collective-permute-done | bytes 12320 | tf_op jit(solution)/shard_map/ppermute | solution.py:295
  58.8 0.6 collective-permute-done.7.refs_3_
  59.4 0.1 collective-permute-done.6.refs_2_
  59.5 2.1 %shard_map.110 = (f32[8,16,128]{2,1,0:T(8,128)S(1)}, f32[1,48,128]{2,1,0:T(8,128)S(1)}, f32[4,48,128]{2,1,0:T(8,128)S(1)}, f32[4,48,128]{2,1,0:T(8,128)S(1)}, f32[8,128]{1,0:T(8,128)S(1)}) custom-call(s32[2]{0:T(128)S(1)} %pad_add_fusion.own_ref, s32[8,128]{1,0:T(8,128)S(1)} %get-tuple-element.29.ids_ref, s32[4,128]{1,0:T(4,128)S(1)} %shard_map.107.all_ref, ...), custom_call_target="tpu_custom_call" | custom-call | tf_op jit(solution)/shard_map/pallas_call | solution.py:38
  61.6 7.4 %all_to_all.27.sim_ref = f32[8,16,128]{2,1,0:T(8,128)S(1)} all-to-all(f32[8,16,128]{2,1,0:T(8,128)S(1)} %get-tuple-element.41), channel_id=1, replica_groups=mesh['obs'=4,'cell'=8] {'cell'}, dimensions={0} | all-to-all | bytes 131072 | tf_op jit(solution)/shard_map/all_to_all | solution.py:299
  69.0 1.1 %shard_map.111 = (f32[24,128]{1,0:T(8,128)S(1)}, f32[8,128]{1,0:T(8,128)S(1)}) custom-call(s32[8,128]{1,0:T(8,128)S(1)} %get-tuple-element.29.ids_ref, f32[8,16,128]{2,1,0:T(8,128)S(1)} %all_to_all.27.sim_ref, f32[8,128]{1,0:T(8,128)S(1)} %get-tuple-element.31.weight_ref, bf16[8,192,128]{2,1,0:T(8,128)(2,1)S(1)} %get-tuple-element.32.foot_ref), custom_call_target="tpu_custom_call" | custom-call | tf_op jit(solution)/shard_map/pallas_call | solution.py:38
  70.1 2.5 %collective-permute-start.11 = (f32[24,128]{1,0:T(8,128)S(1)}, f32[24,128]{1,0:T(8,128)S(1)}, u32[]{:S(2)}, u32[]{:S(2)}) collective-permute-start(f32[24,128]{1,0:T(8,128)S(1)} %get-tuple-element.45.refs_1_), channel_id=1, source_target_pairs={{0,24},{8,16},{16,8},{24,0},{1,25},{9,17},{17,9},{25,1},{2,26},{10... | collective-permute-start | bytes 36872 | tf_op jit(solution)/shard_map/ppermute | solution.py:295
  72.6 0.9 %collective-permute-start.10 = (f32[24,128]{1,0:T(8,128)S(1)}, f32[24,128]{1,0:T(8,128)S(1)}, u32[]{:S(2)}, u32[]{:S(2)}) collective-permute-start(f32[24,128]{1,0:T(8,128)S(1)} %get-tuple-element.45.refs_1_), channel_id=1, source_target_pairs={{0,16},{8,24},{16,0},{24,8},{1,17},{9,25},{17,1},{25,9},{2,18},{10... | collective-permute-start | bytes 36872 | tf_op jit(solution)/shard_map/ppermute | solution.py:295
  73.5 1.0 %collective-permute-start.9 = (f32[24,128]{1,0:T(8,128)S(1)}, f32[24,128]{1,0:T(8,128)S(1)}, u32[]{:S(2)}, u32[]{:S(2)}) collective-permute-start(f32[24,128]{1,0:T(8,128)S(1)} %get-tuple-element.45.refs_1_), channel_id=1, source_target_pairs={{0,8},{8,0},{16,24},{24,16},{1,9},{9,1},{17,25},{25,17},{2,10},{10... | collective-permute-start | bytes 36872 | tf_op jit(solution)/shard_map/ppermute | solution.py:295
  74.5 1.2 %collective-permute-done.11.refs_4_ = f32[24,128]{1,0:T(8,128)S(1)} collective-permute-done((f32[24,128]{1,0:T(8,128)S(1)}, f32[24,128]{1,0:T(8,128)S(1)}, u32[]{:S(2)}, u32[]{:S(2)}) %collective-permute-start.11) | collective-permute-done | bytes 12320 | tf_op jit(solution)/shard_map/ppermute | solution.py:295
  75.7 1.5 %collective-permute-done.10.refs_3_ = f32[24,128]{1,0:T(8,128)S(1)} collective-permute-done((f32[24,128]{1,0:T(8,128)S(1)}, f32[24,128]{1,0:T(8,128)S(1)}, u32[]{:S(2)}, u32[]{:S(2)}) %collective-permute-start.10) | collective-permute-done | bytes 12320 | tf_op jit(solution)/shard_map/ppermute | solution.py:295
  77.2 0.1 collective-permute-done.9.refs_2_
  77.3 1.8 %shard_map.112 = (f32[8,8,128]{2,1,0:T(8,128)S(1)}, f32[1,48,128]{2,1,0:T(8,128)S(1)}, f32[1,48,128]{2,1,0:T(8,128)S(1)}, f32[8,128]{1,0:T(8,128)S(1)}) custom-call(s32[2]{0:T(128)S(1)} %pad_add_fusion.own_ref, s32[8,128]{1,0:T(8,128)S(1)} %get-tuple-element.29.ids_ref, s32[4,128]{1,0:T(4,128)S(1)} %shard_map.107.all_ref, f32[128,48,128]{2,1,0:T(8,128)S(1)} %bitcast.9, ...), custom_call_target="tpu_custom_call" | custom-call | tf_op jit(solution)/shard_map/pallas_call | solution.py:38
  79.1 7.2 %all_to_all.28.sum_ref = f32[8,8,128]{2,1,0:T(8,128)S(1)} all-to-all(f32[8,8,128]{2,1,0:T(8,128)S(1)} %get-tuple-element.46), channel_id=1, replica_groups=mesh['obs'=4,'cell'=8] {'cell'}, dimensions={0} | all-to-all | bytes 65536 | tf_op jit(solution)/shard_map/all_to_all | solution.py:299
  86.3 0.8 shard_map.113
  (10 shorter events, 0.0 us)
Async XLA Ops:
  0.6 1.0 %copy-start = (bf16[2,128,768]{2,1,0:T(8,128)(2,1)S(1)}, bf16[2,128,768]{2,1,0:T(8,128)(2,1)}, u32[]{:S(2)}) copy-start(bf16[2,128,768]{2,1,0:T(8,128)(2,1)} %foot_any.1) | copy-start | bytes 1179652
  1.6 1.0 %copy-start.1 = (bf16[384,384]{1,0:T(8,128)(2,1)S(1)}, bf16[384,384]{1,0:T(8,128)(2,1)}, u32[]{:S(2)}) copy-start(bf16[384,384]{1,0:T(8,128)(2,1)} %constant.10.clone.low_any) | copy-start | bytes 884740
  2.6 1.0 %copy-start.2 = (bf16[384,384]{1,0:T(8,128)(2,1)S(1)}, bf16[384,384]{1,0:T(8,128)(2,1)}, u32[]{:S(2)}) copy-start(bf16[384,384]{1,0:T(8,128)(2,1)} %constant.9.clone.high_any) | copy-start | bytes 884740
  3.6 0.7 copy-start.4
  4.2 0.7 copy-start.5
  4.9 0.7 copy-start.6
  5.6 0.7 copy-start.7
  8.7 14.2 %all-to-all-start = ((bf16[8,208,128]{2,1,0:T(8,128)(2,1)}), bf16[8,208,128]{2,1,0:T(8,128)(2,1)}, u32[]{:S(2)}, u32[]{:S(2)}) async-start(bf16[8,208,128]{2,1,0:T(8,128)(2,1)} %get-tuple-element.28), calls=%async_computation | async-start | bytes 851968 | tf_op jit(solution)/shard_map/all_to_all | solution.py:299
  13.9 8.5 %collective-permute-start.2 = (f32[48,128]{1,0:T(8,128)}, f32[48,128]{1,0:T(8,128)S(1)}, u32[]{:S(2)}, u32[]{:S(2)}) collective-permute-start(f32[48,128]{1,0:T(8,128)} %bitcast.10), channel_id=1, source_target_pairs={{0,24},{8,16},{16,8},{24,0},{1,25},{9,17},{17,9},{25,1},{2,26},{10... | collective-permute-start | bytes 73736 | tf_op jit(solution)/shard_map/ppermute | solution.py:295
  17.9 4.9 %collective-permute-start.1 = (f32[48,128]{1,0:T(8,128)}, f32[48,128]{1,0:T(8,128)S(1)}, u32[]{:S(2)}, u32[]{:S(2)}) collective-permute-start(f32[48,128]{1,0:T(8,128)} %bitcast.11), channel_id=1, source_target_pairs={{0,16},{8,24},{16,0},{24,8},{1,17},{9,25},{17,1},{25,9},{2,18},{10... | collective-permute-start | bytes 73736 | tf_op jit(solution)/shard_map/ppermute | solution.py:295
  17.9 4.9 %collective-permute-start = (f32[48,128]{1,0:T(8,128)}, f32[48,128]{1,0:T(8,128)S(1)}, u32[]{:S(2)}, u32[]{:S(2)}) collective-permute-start(f32[48,128]{1,0:T(8,128)} %bitcast.12), channel_id=1, source_target_pairs={{0,8},{8,0},{16,24},{24,16},{1,9},{9,1},{17,25},{25,17},{2,10},{10... | collective-permute-start | bytes 73736 | tf_op jit(solution)/shard_map/ppermute | solution.py:295
  18.6 4.2 %copy-start.3 = (f32[1,48,128]{2,1,0:T(8,128)S(1)}, f32[1,48,128]{2,1,0:T(8,128)}, u32[]{:S(2)}) copy-start(f32[1,48,128]{2,1,0:T(8,128)} %param.9) | copy-start | bytes 73732
  34.8 5.6 %collective-permute-start.5 = (f32[32,128]{1,0:T(8,128)S(1)}, f32[32,128]{1,0:T(8,128)S(1)}, u32[]{:S(2)}, u32[]{:S(2)}) collective-permute-start(f32[32,128]{1,0:T(8,128)S(1)} %get-tuple-element.33.refs_0_), channel_id=1, source_target_pairs={{0,24},{8,16},{16,8},{24,0},{1,25},{9,17},{17,9},{25,1},{2,26},{10... | collective-permute-start | bytes 49160 | tf_op jit(solution)/shard_map/ppermute | solution.py:295
  38.1 4.6 %collective-permute-start.4 = (f32[32,128]{1,0:T(8,128)S(1)}, f32[32,128]{1,0:T(8,128)S(1)}, u32[]{:S(2)}, u32[]{:S(2)}) collective-permute-start(f32[32,128]{1,0:T(8,128)S(1)} %get-tuple-element.33.refs_0_), channel_id=1, source_target_pairs={{0,16},{8,24},{16,0},{24,8},{1,17},{9,25},{17,1},{25,9},{2,18},{10... | collective-permute-start | bytes 49160 | tf_op jit(solution)/shard_map/ppermute | solution.py:295
  38.1 4.6 %collective-permute-start.3 = (f32[32,128]{1,0:T(8,128)S(1)}, f32[32,128]{1,0:T(8,128)S(1)}, u32[]{:S(2)}, u32[]{:S(2)}) collective-permute-start(f32[32,128]{1,0:T(8,128)S(1)} %get-tuple-element.33.refs_0_), channel_id=1, source_target_pairs={{0,8},{8,0},{16,24},{24,16},{1,9},{9,1},{17,25},{25,17},{2,10},{10... | collective-permute-start | bytes 49160 | tf_op jit(solution)/shard_map/ppermute | solution.py:295
  53.3 5.5 %collective-permute-start.8 = (f32[24,128]{1,0:T(8,128)S(1)}, f32[24,128]{1,0:T(8,128)S(1)}, u32[]{:S(2)}, u32[]{:S(2)}) collective-permute-start(f32[24,128]{1,0:T(8,128)S(1)} %get-tuple-element.40.refs_1_), channel_id=1, source_target_pairs={{0,24},{8,16},{16,8},{24,0},{1,25},{9,17},{17,9},{25,1},{2,26},{10... | collective-permute-start | bytes 36872 | tf_op jit(solution)/shard_map/ppermute | solution.py:295
  54.8 4.6 %collective-permute-start.7 = (f32[24,128]{1,0:T(8,128)S(1)}, f32[24,128]{1,0:T(8,128)S(1)}, u32[]{:S(2)}, u32[]{:S(2)}) collective-permute-start(f32[24,128]{1,0:T(8,128)S(1)} %get-tuple-element.40.refs_1_), channel_id=1, source_target_pairs={{0,16},{8,24},{16,0},{24,8},{1,17},{9,25},{17,1},{25,9},{2,18},{10... | collective-permute-start | bytes 36872 | tf_op jit(solution)/shard_map/ppermute | solution.py:295
  55.4 4.1 %collective-permute-start.6 = (f32[24,128]{1,0:T(8,128)S(1)}, f32[24,128]{1,0:T(8,128)S(1)}, u32[]{:S(2)}, u32[]{:S(2)}) collective-permute-start(f32[24,128]{1,0:T(8,128)S(1)} %get-tuple-element.40.refs_1_), channel_id=1, source_target_pairs={{0,8},{8,0},{16,24},{24,16},{1,9},{9,1},{17,25},{25,17},{2,10},{10... | collective-permute-start | bytes 36872 | tf_op jit(solution)/shard_map/ppermute | solution.py:295
  70.1 5.6 %collective-permute-start.11 = (f32[24,128]{1,0:T(8,128)S(1)}, f32[24,128]{1,0:T(8,128)S(1)}, u32[]{:S(2)}, u32[]{:S(2)}) collective-permute-start(f32[24,128]{1,0:T(8,128)S(1)} %get-tuple-element.45.refs_1_), channel_id=1, source_target_pairs={{0,24},{8,16},{16,8},{24,0},{1,25},{9,17},{17,9},{25,1},{2,26},{10... | collective-permute-start | bytes 36872 | tf_op jit(solution)/shard_map/ppermute | solution.py:295
  72.6 4.6 %collective-permute-start.10 = (f32[24,128]{1,0:T(8,128)S(1)}, f32[24,128]{1,0:T(8,128)S(1)}, u32[]{:S(2)}, u32[]{:S(2)}) collective-permute-start(f32[24,128]{1,0:T(8,128)S(1)} %get-tuple-element.45.refs_1_), channel_id=1, source_target_pairs={{0,16},{8,24},{16,0},{24,8},{1,17},{9,25},{17,1},{25,9},{2,18},{10... | collective-permute-start | bytes 36872 | tf_op jit(solution)/shard_map/ppermute | solution.py:295
  73.5 3.8 %collective-permute-start.9 = (f32[24,128]{1,0:T(8,128)S(1)}, f32[24,128]{1,0:T(8,128)S(1)}, u32[]{:S(2)}, u32[]{:S(2)}) collective-permute-start(f32[24,128]{1,0:T(8,128)S(1)} %get-tuple-element.45.refs_1_), channel_id=1, source_target_pairs={{0,8},{8,0},{16,24},{24,16},{1,9},{9,1},{17,25},{25,17},{2,10},{10... | collective-permute-start | bytes 36872 | tf_op jit(solution)/shard_map/ppermute | solution.py:295

commit v5 on v4

--- a/solution.py
+++ b/solution.py
@@ -11,6 +11,7 @@
 from jax.sharding import PartitionSpec as P
 
 CR = 2
+WAYS = 4
 STEPS = 3
 ROWS = 8
 VMEM = pl.BlockSpec(memory_space=pltpu.VMEM)
@@ -111,7 +112,7 @@
     return total
 
 
-def forward(dims, field_ref, lat_ref, foot_ref, ids_ref, sim_ref, out_ref):
+def forward(dims, field_ref, lat_row, foot_ref, ids_ref, sim_ref, out_ref):
     nc, nb, modes, groups, band = dims
     subs = sim_ref.shape[0] - ROWS
     sim_ref[...] = jnp.zeros_like(sim_ref)
@@ -123,7 +124,7 @@
             row = j * band + off % groups * CR
             total = None
             for r in range(CR):
-                column = jnp.sum(lat_ref[row + r] * field_ref[period], axis=1, keepdims=True)
+                column = jnp.sum(lat_row(row + r) * field_ref[period], axis=1, keepdims=True)
                 at = (b * CR + r) * modes
                 term = foot_ref[j, at:at + modes, :].astype(F32) * column
                 total = term if total is None else total + term
@@ -157,7 +158,10 @@
         for l in range(per_dev):
             field_ref[(own_ref[0] ^ s) * per_dev + l] = near_ref[l * modes:(l + 1) * modes, :]
     copy.wait()
-    forward(dims, field_ref, lat_ref, foot_ref, ids_ref, sim_ref, out_ref)
+    lat_rows = lat_ref.shape[0] // modes
+    forward(
+        dims, field_ref, lambda row: lat_ref[pl.ds(row, modes, stride=lat_rows), :], foot_ref, ids_ref, sim_ref, out_ref
+    )
 
 
 def adjoint_kernel(dims, first, ids_ref, sim_ref, weight_ref, foot_ref, out_ref, norm_ref, weighted_ref):
@@ -167,7 +171,8 @@
     total = tree_sum(sim_ref[c] for c in range(nc))
     norm = jnp.sqrt(jnp.sum(total[subs:], keepdims=True))
     norm_ref[...] = jnp.broadcast_to(norm, norm_ref.shape)
-    sim = total[:subs] / norm
+    scale = 1.0 / norm
+    sim = total[:subs]
     weighted = sim * weight_ref[...]
     weighted_ref[...] = weighted
     lane = lax.broadcasted_iota(jnp.int32, (modes, 128), 1)
@@ -183,8 +188,8 @@
     if rest:
         parts.append(jnp.zeros((rest, 128), F32))
     rows = jnp.concatenate(parts, axis=0).T
-    out_ref[:mine, :] = rows[:mine]
-    out_ref[mine:mine + subs, :] = sim * weighted
+    out_ref[:mine, :] = rows[:mine] * scale
+    out_ref[mine:mine + subs, :] = (sim * scale) * (weighted * scale)
     if first:
         lane = lax.broadcasted_iota(jnp.int32, (ROWS, 128), 1)
         tail = jnp.zeros((ROWS, 128), F32)
@@ -205,19 +210,45 @@
     nc, nb, modes, groups, band = dims
     if not first:
         prior_ref, refs = refs[0], refs[1:]
-    coef_refs, refs = refs[:-7], refs[-7:]
+    ways = min(no, WAYS)
+    kept = (6 if last else 7) + ways
+    coef_refs, refs = refs[:-kept], refs[-kept:]
+    sum_refs, refs = refs[-ways:], refs[:-ways]
     if last:
-        out_ref, row_ref, mine_ref, alpha_ref, next_ref, held_ref, sim_ref = refs
+        out_ref, row_ref, mine_ref, alpha_ref, next_ref, held_ref = refs
     else:
-        out_ref, row_ref, next_ref, vector_ref, alpha_ref, held_ref, sim_ref = refs
+        out_ref, row_ref, next_ref, vector_ref, alpha_ref, sim_ref, held_ref = refs
     mine = nc * nb
     periods = field_ref.shape[0]
     per_dev = row_ref.shape[0]
-    subs = sim_ref.shape[0] - ROWS
+    subs = ROWS
     rows = sum(ref.shape[0] for ref in coef_refs) // no
     coef_refs = pieces(coef_refs, no, rows)
     for s in range(no):
         held_ref[s] = coef_refs[s][:mine, :]
+    for sum_ref in sum_refs:
+        sum_ref[...] = jnp.zeros_like(sum_ref)
+
+    def group(at, carry):
+        found = [own_ref[0] ^ (at * ways + i) for i in range(ways)]
+        coefs = [held_ref[at_i].T for at_i in found]
+        for j in range(nc):
+            for b in range(nb):
+                at_t = j * nb + b
+                for at_i, coef, sum_ref in zip(found, coefs, sum_refs):
+                    off = all_ref[at_i, j * 2 * nb + b]
+                    period = off // groups
+                    row = j * band + off % groups * CR
+                    total = sum_ref[period]
+                    for r in range(CR):
+                        total += coef[r * modes:(r + 1) * modes, at_t:at_t + 1] * lat_ref[row + r]
+                    sum_ref[period] = total
+        return carry
+
+    if no == ways:
+        group(0, 0)
+    else:
+        lax.fori_loop(0, no // ways, group, 0)
     gain = jnp.sum(tree_sum(ref[mine:mine + subs, :] for ref in coef_refs), keepdims=True)
     alpha_ref[...] = jnp.broadcast_to(1.0 + gain, alpha_ref.shape)
     norm = norm_ref[0:1, :]
@@ -226,33 +257,12 @@
         vector = field_ref[p] * scale
         if not last:
             vector_ref[p] = vector
-        rest = vector * -gain
+        rest = tree_sum(sum_ref[p] for sum_ref in sum_refs) - vector * gain
         if not first:
             rest -= prior_ref[p] * norm
         next_ref[p] = rest
     for l in range(per_dev):
         row_ref[l] = field_ref[own_ref[1] * per_dev + l] * scale
-
-    def group(i, carry):
-        at_i = own_ref[0] ^ i
-        coef = held_ref[at_i].T
-        for j in range(nc):
-            for b in range(nb):
-                at = j * nb + b
-                off = all_ref[at_i, j * 2 * nb + b]
-                period = off // groups
-                row = j * band + off % groups * CR
-                total = next_ref[period]
-                for r in range(CR):
-                    total += coef[r * modes:(r + 1) * modes, at:at + 1] * lat_ref[row + r]
-                next_ref[period] = total
-        return carry
-
-    if no <= 4:
-        for i in range(no):
-            group(i, 0)
-    else:
-        lax.fori_loop(0, no, group, 0)
     if last:
         total = fold(next_ref)
         for c in range(nc):
@@ -260,7 +270,7 @@
         for l in range(per_dev):
             mine_ref[l] = next_ref[own_ref[1] * per_dev + l]
     else:
-        forward(dims, next_ref, lat_ref, foot_ref, ids_ref, sim_ref, out_ref)
+        forward(dims, next_ref, lambda row: lat_ref[row], foot_ref, ids_ref, sim_ref, out_ref)
 
 
 def finish_kernel(factor, sum_ref, *refs):
@@ -318,7 +328,6 @@
     if modes != held:
         start = jnp.pad(start, ((0, 0), (0, modes - held), (0, 0)))
         lat_mats = jnp.pad(lat_mats, ((0, modes - held), (0, 0), (0, 0)))
-    lat = lat_mats.transpose(1, 0, 2)
     at_obs = lax.axis_index("obs").astype(jnp.int32)
     own = jnp.stack([at_obs if permuted(no) else 0 * at_obs, at_obs])
 
@@ -339,7 +348,7 @@
             pltpu.VMEM((subs, ob), F32),
             pltpu.SemaphoreType.DMA((7,)),
         ],
-        limit=48,
+        limit=60,
     )
     came = swap(hats, "cell")
 
@@ -356,9 +365,12 @@
             jax.ShapeDtypeStruct((nc, 128), jnp.int32),
         ),
         [SMEM] + [VMEM] * (2 + len(near)),
-        own, lat, came, *near,
+        own, lat_mats.reshape(modes * lat_rows, lat_rows), came, *near,
         scratch=[sim_scratch, pltpu.SMEM((nc, 128), jnp.int32), pltpu.SemaphoreType.DMA],
     )
+    lat_mats, sims = lax.optimization_barrier((lat_mats, sims))
+    lat = lat_mats.transpose(1, 0, 2)
+    ways = min(no, WAYS)
     rows, alphas, norms = [], [], []
     vector = None
     for step in range(STEPS):
@@ -390,7 +402,9 @@
             ),
             [SMEM] * 3 + [VMEM] * (4 + len(before) + len(coefs)),
             own, ids, every, lat, foot, norm, field, *before, *coefs,
-            scratch=[pltpu.VMEM(field_shape.shape, F32)] * last + [pltpu.VMEM((no, mine, 128), F32), sim_scratch],
+            scratch=[pltpu.VMEM(field_shape.shape, F32) if last else sim_scratch]
+            + [pltpu.VMEM((no, mine, 128), F32)]
+            + [pltpu.VMEM(field_shape.shape, F32)] * ways,
         )
         vector = None if last else vector[0]
         rows.append(row)

time: 87.6 us -> 82.7 us (0.944)
  local copies, waits for them, and re-layouts: 9.29 us -> 4.46 us
    unnamed x17 -> x8, local copies, waits for them, and re-layouts: 9.29 us -> 2.64 us
    optimization_barrier x0 -> x1, local copies, waits for them, and re-layouts: none -> 1.82 us  [body(): lat_mats, sims = lax.optimization_barrier((lat_mats, sims))]
  transfers between devices with their start and end apart: 13 -> 13, of which waited for: 9 -> 9; matrix products, arithmetic and copies ran while one was open for 4% -> 2% of each run, Pallas kernels for 0% -> 0%
where the time goes in v5:
time: 82.7 us; the launch traced here: 82.2 us
  blocking collectives  30.9 us (37%)
  starting transfers between devices  22.8 us (28%)
  Pallas kernels  14 us (17%)
  waiting for transfers between devices  9.38 us (11%)
  local copies, waits for them, and re-layouts  4.46 us (5%)
    all_to_all x4, blocking collectives, swap(): return lax.all_to_all(array, axis, split_axis=0, concat_axis=0, tiled=True)  30.9 us
    ppermute x12, starting transfers between devices, share(): lax.ppermute(array, axis, [(d, d ^ s) for d in range(size)])  17.6 us
    pallas_call x10, Pallas kernels, call(): pl.pallas_call(kernel, out_shape=outs, in_specs=specs, out_specs=jax.tree...  14 us
    ppermute x12, waiting for transfers between devices, share(): lax.ppermute(array, axis, [(d, d ^ s) for d in range(size)])  9.22 us
    all_to_all x1, starting transfers between devices, swap(): return lax.all_to_all(array, axis, split_axis=0, concat_axis=0, tiled=True)  5.18 us
    unnamed x8, local copies, waits for them, and re-layouts  2.64 us
    optimization_barrier x1, local copies, waits for them, and re-layouts, body(): lat_mats, sims = lax.optimization_barrier((lat_mats, sims))  1.82 us
  transfers between devices with their start and end apart: 13, of which 9 were waited for; matrix products, arithmetic and copies ran while one was open for 2% of the time, Pallas kernels for 0%

profile of v5, /device:TPU:0, one launch (start us, length us, event | category | flops | bytes accessed | tf_op | source)
XLA Modules:
  0.0 82.2 jit_solution(4678934567915781108)
XLA Ops:
  0.6 2.8 %shard_map.104 = (bf16[8,208,128]{2,1,0:T(8,128)(2,1)}, f32[8,128]{1,0:T(8,128)}) custom-call(bf16[384,384]{1,0:T(8,128)(2,1)} %constant.9.clone.high_any, bf16[384,384]{1,0:T(8,128)(2,1)} %constant.10.clone.low_any, bf16[2,128,768]{2,1,0:T(8,128)(2,1)} %foot_any.1, s32[2]{0:T(128)} %off_any.1, s32[2]{0:T(128)} %sub_any.1, s32[8]{0:T(128)} %count_any.1, ...), custom_call_target="tpu_custom_call" | custom-call | tf_op jit(solution)/shard_map/pallas_call | solution.py:39
  3.4 0.0 copy-start.2
  3.5 5.2 %all-to-all-start = ((bf16[8,208,128]{2,1,0:T(8,128)(2,1)}), bf16[8,208,128]{2,1,0:T(8,128)(2,1)S(1)}, u32[]{:S(2)}, u32[]{:S(2)}) async-start(bf16[8,208,128]{2,1,0:T(8,128)(2,1)} %get-tuple-element.30), calls=%async_computation | async-start | bytes 851968 | tf_op jit(solution)/shard_map/all_to_all | solution.py:309
  8.6 3.6 %collective-permute-start.2 = (f32[48,128]{1,0:T(8,128)}, f32[48,128]{1,0:T(8,128)S(1)}, u32[]{:S(2)}, u32[]{:S(2)}) collective-permute-start(f32[48,128]{1,0:T(8,128)} %bitcast.11), channel_id=1, source_target_pairs={{0,24},{8,16},{16,8},{24,0},{1,25},{9,17},{17,9},{25,1},{2,26},{10... | collective-permute-start | bytes 73736 | tf_op jit(solution)/shard_map/ppermute | solution.py:305
  12.2 0.0 collective-permute-start.1
  12.2 0.8 collective-permute-start
  13.0 0.1 pad_add_fusion.own_ref
  13.1 1.4 %collective-permute-done.2.refs_3_ = f32[48,128]{1,0:T(8,128)S(1)} collective-permute-done((f32[48,128]{1,0:T(8,128)}, f32[48,128]{1,0:T(8,128)S(1)}, u32[]{:S(2)}, u32[]{:S(2)}) %collective-permute-start.2) | collective-permute-done | bytes 24608 | tf_op jit(solution)/shard_map/ppermute | solution.py:305
  14.5 2.7 %collective-permute-done.1.refs_2_ = f32[48,128]{1,0:T(8,128)S(1)} collective-permute-done((f32[48,128]{1,0:T(8,128)}, f32[48,128]{1,0:T(8,128)S(1)}, u32[]{:S(2)}, u32[]{:S(2)}) %collective-permute-start.1) | collective-permute-done | bytes 24608 | tf_op jit(solution)/shard_map/ppermute | solution.py:305
  17.2 0.0 collective-permute-done.refs_1_
  17.2 0.2 all-to-all-done.came_ref
  17.3 0.0 copy-start
  17.3 1.9 %copy-done = f32[48,128,128]{2,1,0:T(8,128)S(1)} copy-done((f32[48,128,128]{2,1,0:T(8,128)S(1)}, f32[48,128,128]{2,1,0:T(8,128)}, u32[]{:S(2)}) %copy-start) | copy-done | bytes 3145752
  19.2 0.0 copy-start.3
  19.2 0.7 copy-done.3
  20.0 1.8 %shard_map.105 = (f32[8,16,128]{2,1,0:T(8,128)S(1)}, f32[4,48,128]{2,1,0:T(8,128)S(1)}, bf16[8,192,128]{2,1,0:T(8,128)(2,1)S(1)}, s32[8,128]{1,0:T(8,128)S(1)}) custom-call(s32[2]{0:T(128)S(1)} %pad_add_fusion.own_ref, f32[6144,128]{1,0:T(8,128)S(1)} %bitcast.10, bf16[8,208,128]{2,1,0:T(8,128)(2,1)S(1)} %all-to-all-done.came_ref, f32[48,128]{1,0:T(8,128)S(1)} %bitcast.14, ...), custom_call_target="tpu_custom_call" | custom-call | tf_op jit(solution)/shard_map/pallas_call | solution.py:39
  21.7 8.9 %all_to_all.25.sim_ref = f32[8,16,128]{2,1,0:T(8,128)S(1)} all-to-all(f32[8,16,128]{2,1,0:T(8,128)S(1)} %get-tuple-element.33), channel_id=1, replica_groups=mesh['obs'=4,'cell'=8] {'cell'}, dimensions={0} | all-to-all | bytes 131072 | tf_op jit(solution)/shard_map/all_to_all | solution.py:309
  30.6 0.0 copy-done.2
  30.6 0.9 %shard_map.106 = (f32[32,128]{1,0:T(8,128)S(1)}, f32[8,128]{1,0:T(8,128)S(1)}) custom-call(s32[8,128]{1,0:T(8,128)S(1)} %get-tuple-element.31.ids_ref, f32[8,16,128]{2,1,0:T(8,128)S(1)} %all_to_all.25.sim_ref, f32[8,128]{1,0:T(8,128)S(1)} %copy-done.2, bf16[8,192,128]{2,1,0:T(8,128)(2,1)S(1)} %get-tuple-element.35.foot_ref), custom_call_target="tpu_custom_call" | custom-call | tf_op jit(solution)/shard_map/pallas_call | solution.py:39
  31.6 2.1 %collective-permute-start.5 = (f32[32,128]{1,0:T(8,128)S(1)}, f32[32,128]{1,0:T(8,128)S(1)}, u32[]{:S(2)}, u32[]{:S(2)}) collective-permute-start(f32[32,128]{1,0:T(8,128)S(1)} %get-tuple-element.36.refs_0_), channel_id=1, source_target_pairs={{0,24},{8,16},{16,8},{24,0},{1,25},{9,17},{17,9},{25,1},{2,26},{10... | collective-permute-start | bytes 49160 | tf_op jit(solution)/shard_map/ppermute | solution.py:305
  33.7 0.0 collective-permute-start.4
  33.7 2.3 %collective-permute-start.3 = (f32[32,128]{1,0:T(8,128)S(1)}, f32[32,128]{1,0:T(8,128)S(1)}, u32[]{:S(2)}, u32[]{:S(2)}) collective-permute-start(f32[32,128]{1,0:T(8,128)S(1)} %get-tuple-element.36.refs_0_), channel_id=1, source_target_pairs={{0,8},{8,0},{16,24},{24,16},{1,9},{9,1},{17,25},{25,17},{2,10},{10... | collective-permute-start | bytes 49160 | tf_op jit(solution)/shard_map/ppermute | solution.py:305
  36.0 0.0 copy-done.1
  36.0 1.8 %copy.13 = f32[48,128,128]{2,0,1:T(8,128)S(1)} copy(f32[48,128,128]{2,1,0:T(8,128)S(1)} %copy-done.1) | data formatting | bytes 6291456 | tf_op jit(solution)/shard_map/optimization_barrier | solution.py:371
  37.8 0.0 collective-permute-done.5.refs_3_
  37.8 0.6 collective-permute-done.4.refs_2_
  38.4 0.0 collective-permute-done.3.refs_1_
  38.4 2.0 %shard_map.108 = (f32[8,16,128]{2,1,0:T(8,128)S(1)}, f32[1,48,128]{2,1,0:T(8,128)S(1)}, f32[4,48,128]{2,1,0:T(8,128)S(1)}, f32[4,48,128]{2,1,0:T(8,128)S(1)}, f32[8,128]{1,0:T(8,128)S(1)}) custom-call(s32[2]{0:T(128)S(1)} %pad_add_fusion.own_ref, s32[8,128]{1,0:T(8,128)S(1)} %get-tuple-element.31.ids_ref, s32[4,128]{1,0:T(4,128)S(1)} %shard_map.107.all_ref, ...), custom_call_target="tpu_custom_call" | custom-call | tf_op jit(solution)/shard_map/pallas_call | solution.py:39
  40.4 7.4 %all_to_all.26.sim_ref = f32[8,16,128]{2,1,0:T(8,128)S(1)} all-to-all(f32[8,16,128]{2,1,0:T(8,128)S(1)} %get-tuple-element.40), channel_id=1, replica_groups=mesh['obs'=4,'cell'=8] {'cell'}, dimensions={0} | all-to-all | bytes 131072 | tf_op jit(solution)/shard_map/all_to_all | solution.py:309
  47.8 0.9 %shard_map.109 = (f32[24,128]{1,0:T(8,128)S(1)}, f32[8,128]{1,0:T(8,128)S(1)}) custom-call(s32[8,128]{1,0:T(8,128)S(1)} %get-tuple-element.31.ids_ref, f32[8,16,128]{2,1,0:T(8,128)S(1)} %all_to_all.26.sim_ref, f32[8,128]{1,0:T(8,128)S(1)} %copy-done.2, bf16[8,192,128]{2,1,0:T(8,128)(2,1)S(1)} %get-tuple-element.35.foot_ref), custom_call_target="tpu_custom_call" | custom-call | tf_op jit(solution)/shard_map/pallas_call | solution.py:39
  48.8 1.9 %collective-permute-start.8 = (f32[24,128]{1,0:T(8,128)S(1)}, f32[24,128]{1,0:T(8,128)S(1)}, u32[]{:S(2)}, u32[]{:S(2)}) collective-permute-start(f32[24,128]{1,0:T(8,128)S(1)} %get-tuple-element.44.refs_1_), channel_id=1, source_target_pairs={{0,24},{8,16},{16,8},{24,0},{1,25},{9,17},{17,9},{25,1},{2,26},{10... | collective-permute-start | bytes 36872 | tf_op jit(solution)/shard_map/ppermute | solution.py:305
  50.7 0.9 %collective-permute-start.7 = (f32[24,128]{1,0:T(8,128)S(1)}, f32[24,128]{1,0:T(8,128)S(1)}, u32[]{:S(2)}, u32[]{:S(2)}) collective-permute-start(f32[24,128]{1,0:T(8,128)S(1)} %get-tuple-element.44.refs_1_), channel_id=1, source_target_pairs={{0,16},{8,24},{16,0},{24,8},{1,17},{9,25},{17,1},{25,9},{2,18},{10... | collective-permute-start | bytes 36872 | tf_op jit(solution)/shard_map/ppermute | solution.py:305
  51.5 1.7 %collective-permute-start.6 = (f32[24,128]{1,0:T(8,128)S(1)}, f32[24,128]{1,0:T(8,128)S(1)}, u32[]{:S(2)}, u32[]{:S(2)}) collective-permute-start(f32[24,128]{1,0:T(8,128)S(1)} %get-tuple-element.44.refs_1_), channel_id=1, source_target_pairs={{0,8},{8,0},{16,24},{24,16},{1,9},{9,1},{17,25},{25,17},{2,10},{10... | collective-permute-start | bytes 36872 | tf_op jit(solution)/shard_map/ppermute | solution.py:305
  53.2 1.1 %collective-permute-done.8.refs_4_ = f32[24,128]{1,0:T(8,128)S(1)} collective-permute-done((f32[24,128]{1,0:T(8,128)S(1)}, f32[24,128]{1,0:T(8,128)S(1)}, u32[]{:S(2)}, u32[]{:S(2)}) %collective-permute-start.8) | collective-permute-done | bytes 12320 | tf_op jit(solution)/shard_map/ppermute | solution.py:305
  54.3 1.0 %collective-permute-done.7.refs_3_ = f32[24,128]{1,0:T(8,128)S(1)} collective-permute-done((f32[24,128]{1,0:T(8,128)S(1)}, f32[24,128]{1,0:T(8,128)S(1)}, u32[]{:S(2)}, u32[]{:S(2)}) %collective-permute-start.7) | collective-permute-done | bytes 12320 | tf_op jit(solution)/shard_map/ppermute | solution.py:305
  55.4 0.0 collective-permute-done.6.refs_2_
  55.4 2.0 %shard_map.110 = (f32[8,16,128]{2,1,0:T(8,128)S(1)}, f32[1,48,128]{2,1,0:T(8,128)S(1)}, f32[4,48,128]{2,1,0:T(8,128)S(1)}, f32[4,48,128]{2,1,0:T(8,128)S(1)}, f32[8,128]{1,0:T(8,128)S(1)}) custom-call(s32[2]{0:T(128)S(1)} %pad_add_fusion.own_ref, s32[8,128]{1,0:T(8,128)S(1)} %get-tuple-element.31.ids_ref, s32[4,128]{1,0:T(4,128)S(1)} %shard_map.107.all_ref, ...), custom_call_target="tpu_custom_call" | custom-call | tf_op jit(solution)/shard_map/pallas_call | solution.py:39
  57.4 7.4 %all_to_all.27.sim_ref = f32[8,16,128]{2,1,0:T(8,128)S(1)} all-to-all(f32[8,16,128]{2,1,0:T(8,128)S(1)} %get-tuple-element.45), channel_id=1, replica_groups=mesh['obs'=4,'cell'=8] {'cell'}, dimensions={0} | all-to-all | bytes 131072 | tf_op jit(solution)/shard_map/all_to_all | solution.py:309
  64.8 0.9 %shard_map.111 = (f32[24,128]{1,0:T(8,128)S(1)}, f32[8,128]{1,0:T(8,128)S(1)}) custom-call(s32[8,128]{1,0:T(8,128)S(1)} %get-tuple-element.31.ids_ref, f32[8,16,128]{2,1,0:T(8,128)S(1)} %all_to_all.27.sim_ref, f32[8,128]{1,0:T(8,128)S(1)} %copy-done.2, bf16[8,192,128]{2,1,0:T(8,128)(2,1)S(1)} %get-tuple-element.35.foot_ref), custom_call_target="tpu_custom_call" | custom-call | tf_op jit(solution)/shard_map/pallas_call | solution.py:39
  65.7 2.0 %collective-permute-start.11 = (f32[24,128]{1,0:T(8,128)S(1)}, f32[24,128]{1,0:T(8,128)S(1)}, u32[]{:S(2)}, u32[]{:S(2)}) collective-permute-start(f32[24,128]{1,0:T(8,128)S(1)} %get-tuple-element.49.refs_1_), channel_id=1, source_target_pairs={{0,24},{8,16},{16,8},{24,0},{1,25},{9,17},{17,9},{25,1},{2,26},{10... | collective-permute-start | bytes 36872 | tf_op jit(solution)/shard_map/ppermute | solution.py:305
  67.8 1.0 %collective-permute-start.10 = (f32[24,128]{1,0:T(8,128)S(1)}, f32[24,128]{1,0:T(8,128)S(1)}, u32[]{:S(2)}, u32[]{:S(2)}) collective-permute-start(f32[24,128]{1,0:T(8,128)S(1)} %get-tuple-element.49.refs_1_), channel_id=1, source_target_pairs={{0,16},{8,24},{16,0},{24,8},{1,17},{9,25},{17,1},{25,9},{2,18},{10... | collective-permute-start | bytes 36872 | tf_op jit(solution)/shard_map/ppermute | solution.py:305
  68.7 1.4 %collective-permute-start.9 = (f32[24,128]{1,0:T(8,128)S(1)}, f32[24,128]{1,0:T(8,128)S(1)}, u32[]{:S(2)}, u32[]{:S(2)}) collective-permute-start(f32[24,128]{1,0:T(8,128)S(1)} %get-tuple-element.49.refs_1_), channel_id=1, source_target_pairs={{0,8},{8,0},{16,24},{24,16},{1,9},{9,1},{17,25},{25,17},{2,10},{10... | collective-permute-start | bytes 36872 | tf_op jit(solution)/shard_map/ppermute | solution.py:305
  70.1 1.1 %collective-permute-done.11.refs_4_ = f32[24,128]{1,0:T(8,128)S(1)} collective-permute-done((f32[24,128]{1,0:T(8,128)S(1)}, f32[24,128]{1,0:T(8,128)S(1)}, u32[]{:S(2)}, u32[]{:S(2)}) %collective-permute-start.11) | collective-permute-done | bytes 12320 | tf_op jit(solution)/shard_map/ppermute | solution.py:305
  71.3 1.1 %collective-permute-done.10.refs_3_ = f32[24,128]{1,0:T(8,128)S(1)} collective-permute-done((f32[24,128]{1,0:T(8,128)S(1)}, f32[24,128]{1,0:T(8,128)S(1)}, u32[]{:S(2)}, u32[]{:S(2)}) %collective-permute-start.10) | collective-permute-done | bytes 12320 | tf_op jit(solution)/shard_map/ppermute | solution.py:305
  72.4 0.1 collective-permute-done.9.refs_2_
  72.5 1.7 %shard_map.112 = (f32[8,8,128]{2,1,0:T(8,128)S(1)}, f32[1,48,128]{2,1,0:T(8,128)S(1)}, f32[1,48,128]{2,1,0:T(8,128)S(1)}, f32[8,128]{1,0:T(8,128)S(1)}) custom-call(s32[2]{0:T(128)S(1)} %pad_add_fusion.own_ref, s32[8,128]{1,0:T(8,128)S(1)} %get-tuple-element.31.ids_ref, s32[4,128]{1,0:T(4,128)S(1)} %shard_map.107.all_ref, f32[128,48,128]{2,1,0:T(8,128)S(1)} %bitcast.9, ...), custom_call_target="tpu_custom_call" | custom-call | tf_op jit(solution)/shard_map/pallas_call | solution.py:39
  74.2 7.2 %all_to_all.28.sum_ref = f32[8,8,128]{2,1,0:T(8,128)S(1)} all-to-all(f32[8,8,128]{2,1,0:T(8,128)S(1)} %get-tuple-element.50), channel_id=1, replica_groups=mesh['obs'=4,'cell'=8] {'cell'}, dimensions={0} | all-to-all | bytes 65536 | tf_op jit(solution)/shard_map/all_to_all | solution.py:309
  81.4 0.8 shard_map.113
  (2 shorter events, 0.0 us)
Async XLA Ops:
  3.4 27.2 %copy-start.2 = (f32[8,128]{1,0:T(8,128)S(1)}, f32[8,128]{1,0:T(8,128)}, u32[]{:S(2)}) copy-start(f32[8,128]{1,0:T(8,128)} %get-tuple-element.34.weight_ref) | copy-start | bytes 12292
  3.5 13.9 %all-to-all-start = ((bf16[8,208,128]{2,1,0:T(8,128)(2,1)}), bf16[8,208,128]{2,1,0:T(8,128)(2,1)S(1)}, u32[]{:S(2)}, u32[]{:S(2)}) async-start(bf16[8,208,128]{2,1,0:T(8,128)(2,1)} %get-tuple-element.30), calls=%async_computation | async-start | bytes 851968 | tf_op jit(solution)/shard_map/all_to_all | solution.py:309
  8.6 5.8 %collective-permute-start.2 = (f32[48,128]{1,0:T(8,128)}, f32[48,128]{1,0:T(8,128)S(1)}, u32[]{:S(2)}, u32[]{:S(2)}) collective-permute-start(f32[48,128]{1,0:T(8,128)} %bitcast.11), channel_id=1, source_target_pairs={{0,24},{8,16},{16,8},{24,0},{1,25},{9,17},{17,9},{25,1},{2,26},{10... | collective-permute-start | bytes 73736 | tf_op jit(solution)/shard_map/ppermute | solution.py:305
  12.2 4.9 %collective-permute-start.1 = (f32[48,128]{1,0:T(8,128)}, f32[48,128]{1,0:T(8,128)S(1)}, u32[]{:S(2)}, u32[]{:S(2)}) collective-permute-start(f32[48,128]{1,0:T(8,128)} %bitcast.12), channel_id=1, source_target_pairs={{0,16},{8,24},{16,0},{24,8},{1,17},{9,25},{17,1},{25,9},{2,18},{10... | collective-permute-start | bytes 73736 | tf_op jit(solution)/shard_map/ppermute | solution.py:305
  12.2 4.9 %collective-permute-start = (f32[48,128]{1,0:T(8,128)}, f32[48,128]{1,0:T(8,128)S(1)}, u32[]{:S(2)}, u32[]{:S(2)}) collective-permute-start(f32[48,128]{1,0:T(8,128)} %bitcast.13), channel_id=1, source_target_pairs={{0,8},{8,0},{16,24},{24,16},{1,9},{9,1},{17,25},{25,17},{2,10},{10... | collective-permute-start | bytes 73736 | tf_op jit(solution)/shard_map/ppermute | solution.py:305
  17.3 1.9 %copy-start = (f32[48,128,128]{2,1,0:T(8,128)S(1)}, f32[48,128,128]{2,1,0:T(8,128)}, u32[]{:S(2)}) copy-start(f32[48,128,128]{2,1,0:T(8,128)} %param.10) | copy-start | bytes 9437188
  19.2 0.7 copy-start.3
  20.0 16.0 %copy-start.1 = (f32[48,128,128]{2,1,0:T(8,128)S(1)}, f32[48,128,128]{2,1,0:T(8,128)}, u32[]{:S(2)}) copy-start(f32[48,128,128]{2,1,0:T(8,128)} %param.10) | copy-start | bytes 9437188
  31.6 6.2 %collective-permute-start.5 = (f32[32,128]{1,0:T(8,128)S(1)}, f32[32,128]{1,0:T(8,128)S(1)}, u32[]{:S(2)}, u32[]{:S(2)}) collective-permute-start(f32[32,128]{1,0:T(8,128)S(1)} %get-tuple-element.36.refs_0_), channel_id=1, source_target_pairs={{0,24},{8,16},{16,8},{24,0},{1,25},{9,17},{17,9},{25,1},{2,26},{10... | collective-permute-start | bytes 49160 | tf_op jit(solution)/shard_map/ppermute | solution.py:305
  33.7 4.7 %collective-permute-start.4 = (f32[32,128]{1,0:T(8,128)S(1)}, f32[32,128]{1,0:T(8,128)S(1)}, u32[]{:S(2)}, u32[]{:S(2)}) collective-permute-start(f32[32,128]{1,0:T(8,128)S(1)} %get-tuple-element.36.refs_0_), channel_id=1, source_target_pairs={{0,16},{8,24},{16,0},{24,8},{1,17},{9,25},{17,1},{25,9},{2,18},{10... | collective-permute-start | bytes 49160 | tf_op jit(solution)/shard_map/ppermute | solution.py:305
  33.7 4.7 %collective-permute-start.3 = (f32[32,128]{1,0:T(8,128)S(1)}, f32[32,128]{1,0:T(8,128)S(1)}, u32[]{:S(2)}, u32[]{:S(2)}) collective-permute-start(f32[32,128]{1,0:T(8,128)S(1)} %get-tuple-element.36.refs_0_), channel_id=1, source_target_pairs={{0,8},{8,0},{16,24},{24,16},{1,9},{9,1},{17,25},{25,17},{2,10},{10... | collective-permute-start | bytes 49160 | tf_op jit(solution)/shard_map/ppermute | solution.py:305
  48.8 5.5 %collective-permute-start.8 = (f32[24,128]{1,0:T(8,128)S(1)}, f32[24,128]{1,0:T(8,128)S(1)}, u32[]{:S(2)}, u32[]{:S(2)}) collective-permute-start(f32[24,128]{1,0:T(8,128)S(1)} %get-tuple-element.44.refs_1_), channel_id=1, source_target_pairs={{0,24},{8,16},{16,8},{24,0},{1,25},{9,17},{17,9},{25,1},{2,26},{10... | collective-permute-start | bytes 36872 | tf_op jit(solution)/shard_map/ppermute | solution.py:305
  50.7 4.7 %collective-permute-start.7 = (f32[24,128]{1,0:T(8,128)S(1)}, f32[24,128]{1,0:T(8,128)S(1)}, u32[]{:S(2)}, u32[]{:S(2)}) collective-permute-start(f32[24,128]{1,0:T(8,128)S(1)} %get-tuple-element.44.refs_1_), channel_id=1, source_target_pairs={{0,16},{8,24},{16,0},{24,8},{1,17},{9,25},{17,1},{25,9},{2,18},{10... | collective-permute-start | bytes 36872 | tf_op jit(solution)/shard_map/ppermute | solution.py:305
  51.5 3.8 %collective-permute-start.6 = (f32[24,128]{1,0:T(8,128)S(1)}, f32[24,128]{1,0:T(8,128)S(1)}, u32[]{:S(2)}, u32[]{:S(2)}) collective-permute-start(f32[24,128]{1,0:T(8,128)S(1)} %get-tuple-element.44.refs_1_), channel_id=1, source_target_pairs={{0,8},{8,0},{16,24},{24,16},{1,9},{9,1},{17,25},{25,17},{2,10},{10... | collective-permute-start | bytes 36872 | tf_op jit(solution)/shard_map/ppermute | solution.py:305
  65.7 5.5 %collective-permute-start.11 = (f32[24,128]{1,0:T(8,128)S(1)}, f32[24,128]{1,0:T(8,128)S(1)}, u32[]{:S(2)}, u32[]{:S(2)}) collective-permute-start(f32[24,128]{1,0:T(8,128)S(1)} %get-tuple-element.49.refs_1_), channel_id=1, source_target_pairs={{0,24},{8,16},{16,8},{24,0},{1,25},{9,17},{17,9},{25,1},{2,26},{10... | collective-permute-start | bytes 36872 | tf_op jit(solution)/shard_map/ppermute | solution.py:305
  67.8 4.6 %collective-permute-start.10 = (f32[24,128]{1,0:T(8,128)S(1)}, f32[24,128]{1,0:T(8,128)S(1)}, u32[]{:S(2)}, u32[]{:S(2)}) collective-permute-start(f32[24,128]{1,0:T(8,128)S(1)} %get-tuple-element.49.refs_1_), channel_id=1, source_target_pairs={{0,16},{8,24},{16,0},{24,8},{1,17},{9,25},{17,1},{25,9},{2,18},{10... | collective-permute-start | bytes 36872 | tf_op jit(solution)/shard_map/ppermute | solution.py:305
  68.7 3.8 %collective-permute-start.9 = (f32[24,128]{1,0:T(8,128)S(1)}, f32[24,128]{1,0:T(8,128)S(1)}, u32[]{:S(2)}, u32[]{:S(2)}) collective-permute-start(f32[24,128]{1,0:T(8,128)S(1)} %get-tuple-element.49.refs_1_), channel_id=1, source_target_pairs={{0,8},{8,0},{16,24},{24,16},{1,9},{9,1},{17,25},{25,17},{2,10},{10... | collective-permute-start | bytes 36872 | tf_op jit(solution)/shard_map/ppermute | solution.py:305

commit v6 on v5

--- a/solution.py
+++ b/solution.py
@@ -35,13 +35,14 @@
     return high, low
 
 
-def call(kernel, outs, specs, *args, scratch=(), limit=8):
+def call(kernel, outs, specs, *args, scratch=(), limit=8, cost=None):
     return pl.pallas_call(
         kernel,
         out_shape=outs,
         in_specs=specs,
         out_specs=jax.tree.map(lambda _: VMEM, outs),
         scratch_shapes=scratch,
+        cost_estimate=cost,
         compiler_params=pltpu.CompilerParams(vmem_limit_bytes=limit * 1024 * 1024),
     )(*args)
 
@@ -53,7 +54,7 @@
     return parts[0]
 
 
-def transform_kernel(dims, high_any, low_any, foot_any, off_any, sub_any, count_any, rinv_any, *refs):
+def transform_kernel(dims, cell_ref, high_any, low_any, foot_any, off_any, sub_any, count_any, rinv_any, *refs):
     nc, nb, modes, groups, band = dims
     out_ref, weight_ref, high_ref, low_ref, foot_ref, off_ref, sub_ref, count_ref, rinv_ref, sems = refs
     copies = [
@@ -89,8 +90,10 @@
     lane = lax.broadcasted_iota(jnp.int32, (16, ob), 1)
     ids = jnp.zeros((16, ob), F32)
     for b in range(nb):
-        ids = jnp.where(lane == b, off_ref[b].astype(F32), ids)
-        ids = jnp.where(lane == nb + b, sub_ref[b].astype(F32), ids)
+        off = off_ref[b]
+        values = (off // groups, cell_ref[0] * (band // CR) + off % groups, sub_ref[b])
+        for at, value in enumerate(values):
+            ids = jnp.where(lane == at * nb + b, value.astype(F32), ids)
     ids = ids.astype(BF16)
     for c in range(nc):
         out_ref[c, nb * CR * modes:, :] = ids
@@ -102,6 +105,16 @@
     weight_ref[...] = jnp.where(lane < limit, rinv_ref[...], 0.0)
 
 
+def fetch_kernel(*refs):
+    refs, sems = refs[:-1], refs[-1]
+    half = len(refs) // 2
+    copies = [pltpu.make_async_copy(refs[at], refs[half + at], sems.at[at]) for at in range(half)]
+    for copy in copies:
+        copy.start()
+    for copy in copies:
+        copy.wait()
+
+
 def fold(ref):
     periods, modes, _ = ref.shape
     total = jnp.zeros((ROWS, ref.shape[2]), F32)
@@ -112,19 +125,22 @@
     return total
 
 
-def forward(dims, field_ref, lat_row, foot_ref, ids_ref, sim_ref, out_ref):
+def lat_row(lat_ref, modes, row):
+    return lat_ref[pl.ds(row, modes, stride=lat_ref.shape[0] // modes), :]
+
+
+def forward(dims, field_ref, lat_ref, foot_ref, ids_ref, sim_ref, out_ref):
     nc, nb, modes, groups, band = dims
     subs = sim_ref.shape[0] - ROWS
     sim_ref[...] = jnp.zeros_like(sim_ref)
     for j in range(nc):
         for b in range(nb):
-            off = ids_ref[j, b]
-            sub = ids_ref[j, nb + b]
-            period = off // groups
-            row = j * band + off % groups * CR
+            period = ids_ref[j, b]
+            row = ids_ref[j, nb + b] * CR
+            sub = ids_ref[j, 2 * nb + b]
             total = None
             for r in range(CR):
-                column = jnp.sum(lat_row(row + r) * field_ref[period], axis=1, keepdims=True)
+                column = jnp.sum(lat_row(lat_ref, modes, row + r) * field_ref[period], axis=1, keepdims=True)
                 at = (b * CR + r) * modes
                 term = foot_ref[j, at:at + modes, :].astype(F32) * column
                 total = term if total is None else total + term
@@ -156,12 +172,9 @@
     per_dev = field_ref.shape[0] // no
     for s, near_ref in enumerate(pieces(near_refs, no, per_dev * modes)):
         for l in range(per_dev):
-            field_ref[(own_ref[0] ^ s) * per_dev + l] = near_ref[l * modes:(l + 1) * modes, :]
+            field_ref[((own_ref[0] ^ s) if permuted(no) else s) * per_dev + l] = near_ref[l * modes:(l + 1) * modes, :]
     copy.wait()
-    lat_rows = lat_ref.shape[0] // modes
-    forward(
-        dims, field_ref, lambda row: lat_ref[pl.ds(row, modes, stride=lat_rows), :], foot_ref, ids_ref, sim_ref, out_ref
-    )
+    forward(dims, field_ref, lat_ref, foot_ref, ids_ref, sim_ref, out_ref)
 
 
 def adjoint_kernel(dims, first, ids_ref, sim_ref, weight_ref, foot_ref, out_ref, norm_ref, weighted_ref):
@@ -179,7 +192,7 @@
     parts = [jnp.zeros((modes, 128), F32) for _ in range(CR)]
     for j in range(nc):
         for b in range(nb):
-            chosen = weighted_ref[pl.ds(ids_ref[j, nb + b], 1), :]
+            chosen = weighted_ref[pl.ds(ids_ref[j, 2 * nb + b], 1), :]
             for r in range(CR):
                 at = (b * CR + r) * modes
                 column = jnp.sum(foot_ref[j, at:at + modes, :].astype(F32) * chosen, axis=1, keepdims=True)
@@ -192,18 +205,20 @@
     out_ref[mine:mine + subs, :] = (sim * scale) * (weighted * scale)
     if first:
         lane = lax.broadcasted_iota(jnp.int32, (ROWS, 128), 1)
-        tail = jnp.zeros((ROWS, 128), F32)
+        line = lax.broadcasted_iota(jnp.int32, (ROWS, 128), 0)
+        tail = jnp.zeros((ROWS, 128), jnp.int32)
         for j in range(nc):
-            for q in range(2 * nb):
-                tail = jnp.where(lane == j * 2 * nb + q, ids_ref[j, q].astype(F32), tail)
-        out_ref[mine + subs:, :] = tail
+            for b in range(nb):
+                value = jnp.where(line == 0, ids_ref[j, b], ids_ref[j, nb + b])
+                tail = jnp.where(lane == j * nb + b, value, tail)
+        out_ref[mine + subs:, :] = tail.astype(F32)
 
 
 def every_kernel(dims, no, at, *refs):
     refs, out_ref = refs[:-1], refs[-1]
     rows = sum(ref.shape[0] for ref in refs) // no
     for s, ref in enumerate(pieces(refs, no, rows)):
-        out_ref[s:s + 1, :] = ref[at:at + ROWS, :][0:1].astype(jnp.int32)
+        out_ref[2 * s:2 * s + 2, :] = ref[at:at + ROWS, :][0:2].astype(jnp.int32)
 
 
 def image_kernel(dims, no, first, last, own_ref, ids_ref, all_ref, lat_ref, foot_ref, norm_ref, field_ref, *refs):
@@ -230,18 +245,19 @@
         sum_ref[...] = jnp.zeros_like(sum_ref)
 
     def group(at, carry):
-        found = [own_ref[0] ^ (at * ways + i) for i in range(ways)]
+        found = [at * ways + i for i in range(ways)]
+        if permuted(no):
+            found = [own_ref[0] ^ at_i for at_i in found]
         coefs = [held_ref[at_i].T for at_i in found]
         for j in range(nc):
             for b in range(nb):
                 at_t = j * nb + b
                 for at_i, coef, sum_ref in zip(found, coefs, sum_refs):
-                    off = all_ref[at_i, j * 2 * nb + b]
-                    period = off // groups
-                    row = j * band + off % groups * CR
+                    period = all_ref[2 * at_i, at_t]
+                    row = all_ref[2 * at_i + 1, at_t] * CR
                     total = sum_ref[period]
                     for r in range(CR):
-                        total += coef[r * modes:(r + 1) * modes, at_t:at_t + 1] * lat_ref[row + r]
+                        total += coef[r * modes:(r + 1) * modes, at_t:at_t + 1] * lat_row(lat_ref, modes, row + r)
                     sum_ref[period] = total
         return carry
 
@@ -262,15 +278,15 @@
             rest -= prior_ref[p] * norm
         next_ref[p] = rest
     for l in range(per_dev):
-        row_ref[l] = field_ref[own_ref[1] * per_dev + l] * scale
+        row_ref[l] = field_ref[own_ref[0] * per_dev + l] * scale
     if last:
         total = fold(next_ref)
         for c in range(nc):
             out_ref[c] = total
         for l in range(per_dev):
-            mine_ref[l] = next_ref[own_ref[1] * per_dev + l]
+            mine_ref[l] = next_ref[own_ref[0] * per_dev + l]
     else:
-        forward(dims, next_ref, lambda row: lat_ref[row], foot_ref, ids_ref, sim_ref, out_ref)
+        forward(dims, next_ref, lat_ref, foot_ref, ids_ref, sim_ref, out_ref)
 
 
 def finish_kernel(factor, sum_ref, *refs):
@@ -328,16 +344,17 @@
     if modes != held:
         start = jnp.pad(start, ((0, 0), (0, modes - held), (0, 0)))
         lat_mats = jnp.pad(lat_mats, ((0, modes - held), (0, 0), (0, 0)))
-    at_obs = lax.axis_index("obs").astype(jnp.int32)
-    own = jnp.stack([at_obs if permuted(no) else 0 * at_obs, at_obs])
-
-    near = share(start.reshape(per_dev * modes, lat_rows), "obs")
+    own = lax.axis_index("obs").astype(jnp.int32).reshape(1)
+    cell = lax.axis_index("cell").astype(jnp.int32).reshape(1)
+
+    start = start.reshape(per_dev * modes, lat_rows)
+    near = share(start, "obs")
     foot_rows = nb * CR * modes
     hats, weights = call(
         functools.partial(transform_kernel, dims),
         (jax.ShapeDtypeStruct((nc, foot_rows + 16, ob), BF16), shape((subs, ob))),
-        [ANY] * 7,
-        jnp.asarray(high), jnp.asarray(low), footprints, blk_off, blk_sub, counts, rinv.reshape(subs, ob),
+        [SMEM] + [ANY] * 7,
+        cell, jnp.asarray(high), jnp.asarray(low), footprints, blk_off, blk_sub, counts, rinv.reshape(subs, ob),
         scratch=[
             pltpu.VMEM(high.shape, BF16),
             pltpu.VMEM(low.shape, BF16),
@@ -351,6 +368,18 @@
         limit=60,
     )
     came = swap(hats, "cell")
+    lat, start, _ = lax.optimization_barrier((lat_mats.reshape(modes * lat_rows, lat_rows), start, weights))
+    lat, start = call(
+        fetch_kernel,
+        (shape(lat.shape), shape(start.shape)),
+        [ANY] * 2,
+        lat, start,
+        scratch=[pltpu.SemaphoreType.DMA((2,))],
+        limit=50,
+        cost=pl.CostEstimate(flops=0, transcendentals=0, bytes_accessed=8 * (lat.size + start.size)),
+    )
+    if permuted(no):
+        near[0] = start
 
     field_shape = shape((periods, modes, lat_rows))
     small = shape((ROWS, 128))
@@ -365,11 +394,9 @@
             jax.ShapeDtypeStruct((nc, 128), jnp.int32),
         ),
         [SMEM] + [VMEM] * (2 + len(near)),
-        own, lat_mats.reshape(modes * lat_rows, lat_rows), came, *near,
+        own, lat, came, *near,
         scratch=[sim_scratch, pltpu.SMEM((nc, 128), jnp.int32), pltpu.SemaphoreType.DMA],
     )
-    lat_mats, sims = lax.optimization_barrier((lat_mats, sims))
-    lat = lat_mats.transpose(1, 0, 2)
     ways = min(no, WAYS)
     rows, alphas, norms = [], [], []
     vector = None
@@ -386,7 +413,7 @@
         if first:
             every = call(
                 functools.partial(every_kernel, dims, no, mine + subs),
-                jax.ShapeDtypeStruct((no, 128), jnp.int32),
+                jax.ShapeDtypeStruct((2 * no, 128), jnp.int32),
                 [VMEM] * len(coefs),
                 *coefs,
             )

time: 82.7 us -> 84.8 us (1.025)
  Pallas kernels: 14 us -> 20.2 us
  local copies, waits for them, and re-layouts: 4.46 us -> 0.77 us
    pallas_call x10 -> x11, Pallas kernels: 14 us -> 20.2 us  [call(): pl.pallas_call(kernel, out_shape=outs, in_specs=specs, out_specs=jax.tree...]
    unnamed x8 -> x4, local copies, waits for them, and re-layouts: 2.64 us -> 0.77 us
    optimization_barrier x1 -> x0, local copies, waits for them, and re-layouts: 1.82 us -> none  [body(): lat_mats, sims = lax.optimization_barrier((lat_mats, sims))]
  transfers between devices with their start and end apart: 13 -> 13, of which waited for: 9 -> 7; matrix products, arithmetic and copies ran while one was open for 2% -> 0% of each run, Pallas kernels for 0% -> 2%
where the time goes in v6:
time: 84.8 us; the launch traced here: 84.3 us
  blocking collectives  30.9 us (36%)
  starting transfers between devices  23.1 us (27%)
  Pallas kernels  20.2 us (24%)
  waiting for transfers between devices  8.67 us (10%)
    all_to_all x4, blocking collectives, swap(): return lax.all_to_all(array, axis, split_axis=0, concat_axis=0, tiled=True)  30.9 us
    pallas_call x11, Pallas kernels, call(): pl.pallas_call(kernel, out_shape=outs, in_specs=specs, out_specs=jax.tree...  20.2 us
    ppermute x12, starting transfers between devices, share(): lax.ppermute(array, axis, [(d, d ^ s) for d in range(size)])  18 us
    ppermute x12, waiting for transfers between devices, share(): lax.ppermute(array, axis, [(d, d ^ s) for d in range(size)])  8.67 us
    all_to_all x1, starting transfers between devices, swap(): return lax.all_to_all(array, axis, split_axis=0, concat_axis=0, tiled=True)  5.18 us
  transfers between devices with their start and end apart: 13, of which 7 were waited for; matrix products, arithmetic and copies ran while one was open for 0% of the time, Pallas kernels for 2%

profile of v6, /device:TPU:0, one launch (start us, length us, event | category | flops | bytes accessed | tf_op | source)
XLA Modules:
  0.0 84.3 jit_solution(4850036091301731060)
XLA Ops:
  0.6 2.8 %shard_map.104 = (bf16[8,208,128]{2,1,0:T(8,128)(2,1)}, f32[8,128]{1,0:T(8,128)}) custom-call(s32[1]{0:T(128)} %bitcast.3.cell_ref, bf16[384,384]{1,0:T(8,128)(2,1)} %constant.12.clone.high_any, bf16[384,384]{1,0:T(8,128)(2,1)} %constant.13.clone.low_any, bf16[2,128,768]{2,1,0:T(8,128)(2,1)} %foot_any.1, s32[2]{0:T(128)} %off_any.1, s32[2]{0:T(128)} %sub_any.1, ...), custom_call_target="tpu_custom_call" | custom-call | tf_op jit(solution)/shard_map/pallas_call | solution.py:39
  3.4 5.2 %all-to-all-start = ((bf16[8,208,128]{2,1,0:T(8,128)(2,1)}), bf16[8,208,128]{2,1,0:T(8,128)(2,1)}, u32[]{:S(2)}, u32[]{:S(2)}) async-start(bf16[8,208,128]{2,1,0:T(8,128)(2,1)} %get-tuple-element.36), calls=%async_computation | async-start | bytes 851968 | tf_op jit(solution)/shard_map/all_to_all | solution.py:325
  8.6 4.1 %collective-permute-start.2 = (f32[48,128]{1,0:T(8,128)}, f32[48,128]{1,0:T(8,128)S(1)}, u32[]{:S(2)}, u32[]{:S(2)}) collective-permute-start(f32[48,128]{1,0:T(8,128)} %bitcast.5), channel_id=1, source_target_pairs={{0,24},{8,16},{16,8},{24,0},{1,25},{9,17},{17,9},{25,1},{2,26},{10... | collective-permute-start | bytes 73736 | tf_op jit(solution)/shard_map/ppermute | solution.py:321
  12.7 0.0 collective-permute-start.1
  12.7 0.6 collective-permute-start
  13.3 0.0 copy-start.1
  13.3 0.8 copy-done.1
  14.1 0.0 copy-start
  14.1 1.9 %shard_map.105 = (f32[6144,128]{1,0:T(8,128)S(1)}, f32[48,128]{1,0:T(8,128)S(1)}) custom-call(f32[6144,128]{1,0:T(8,128)} %bitcast.9, f32[48,128]{1,0:T(8,128)S(1)} %bitcast.8), custom_call_target="tpu_custom_call" | custom-call | bytes 6340608 | tf_op jit(solution)/shard_map/pallas_call | solution.py:39
  16.0 0.0 collective-permute-done.2.refs_3_
  16.1 1.6 %collective-permute-done.1.refs_2_ = f32[48,128]{1,0:T(8,128)S(1)} collective-permute-done((f32[48,128]{1,0:T(8,128)}, f32[48,128]{1,0:T(8,128)S(1)}, u32[]{:S(2)}, u32[]{:S(2)}) %collective-permute-start.1) | collective-permute-done | bytes 24608 | tf_op jit(solution)/shard_map/ppermute | solution.py:321
  17.6 0.0 collective-permute-done.refs_1_
  17.6 0.0 all-to-all-done.came_ref
  17.6 2.2 %shard_map.106 = (f32[8,16,128]{2,1,0:T(8,128)S(1)}, f32[4,48,128]{2,1,0:T(8,128)S(1)}, bf16[8,192,128]{2,1,0:T(8,128)(2,1)S(1)}, s32[8,128]{1,0:T(8,128)S(1)}) custom-call(s32[1]{0:T(128)} %bitcast.own_ref, f32[6144,128]{1,0:T(8,128)S(1)} %get-tuple-element.35.lat_ref, bf16[8,208,128]{2,1,0:T(8,128)(2,1)} %all-to-all-done.came_ref, ...), custom_call_target="tpu_custom_call" | custom-call | tf_op jit(solution)/shard_map/pallas_call | solution.py:39
  19.9 8.9 %all_to_all.25.sim_ref = f32[8,16,128]{2,1,0:T(8,128)S(1)} all-to-all(f32[8,16,128]{2,1,0:T(8,128)S(1)} %get-tuple-element.39), channel_id=1, replica_groups=mesh['obs'=4,'cell'=8] {'cell'}, dimensions={0} | all-to-all | bytes 131072 | tf_op jit(solution)/shard_map/all_to_all | solution.py:325
  28.7 0.0 copy-done
  28.7 0.9 %shard_map.107 = (f32[32,128]{1,0:T(8,128)S(1)}, f32[8,128]{1,0:T(8,128)S(1)}) custom-call(s32[8,128]{1,0:T(8,128)S(1)} %get-tuple-element.38.ids_ref, f32[8,16,128]{2,1,0:T(8,128)S(1)} %all_to_all.25.sim_ref, f32[8,128]{1,0:T(8,128)S(1)} %copy-done, bf16[8,192,128]{2,1,0:T(8,128)(2,1)S(1)} %get-tuple-element.40.foot_ref), custom_call_target="tpu_custom_call" | custom-call | tf_op jit(solution)/shard_map/pallas_call | solution.py:39
  29.7 2.3 %collective-permute-start.5 = (f32[32,128]{1,0:T(8,128)S(1)}, f32[32,128]{1,0:T(8,128)S(1)}, u32[]{:S(2)}, u32[]{:S(2)}) collective-permute-start(f32[32,128]{1,0:T(8,128)S(1)} %get-tuple-element.41.refs_0_), channel_id=1, source_target_pairs={{0,24},{8,16},{16,8},{24,0},{1,25},{9,17},{17,9},{25,1},{2,26},{10... | collective-permute-start | bytes 49160 | tf_op jit(solution)/shard_map/ppermute | solution.py:321
  31.9 0.0 collective-permute-start.4
  31.9 2.1 %collective-permute-start.3 = (f32[32,128]{1,0:T(8,128)S(1)}, f32[32,128]{1,0:T(8,128)S(1)}, u32[]{:S(2)}, u32[]{:S(2)}) collective-permute-start(f32[32,128]{1,0:T(8,128)S(1)} %get-tuple-element.41.refs_0_), channel_id=1, source_target_pairs={{0,8},{8,0},{16,24},{24,16},{1,9},{9,1},{17,25},{25,17},{2,10},{10... | collective-permute-start | bytes 49160 | tf_op jit(solution)/shard_map/ppermute | solution.py:321
  34.1 1.1 %collective-permute-done.5.refs_3_ = f32[32,128]{1,0:T(8,128)S(1)} collective-permute-done((f32[32,128]{1,0:T(8,128)S(1)}, f32[32,128]{1,0:T(8,128)S(1)}, u32[]{:S(2)}, u32[]{:S(2)}) %collective-permute-start.5) | collective-permute-done | bytes 16416 | tf_op jit(solution)/shard_map/ppermute | solution.py:321
  35.2 1.3 %collective-permute-done.4.refs_2_ = f32[32,128]{1,0:T(8,128)S(1)} collective-permute-done((f32[32,128]{1,0:T(8,128)S(1)}, f32[32,128]{1,0:T(8,128)S(1)}, u32[]{:S(2)}, u32[]{:S(2)}) %collective-permute-start.4) | collective-permute-done | bytes 16416 | tf_op jit(solution)/shard_map/ppermute | solution.py:321
  36.6 0.0 collective-permute-done.3.refs_1_
  36.6 3.4 %shard_map.109 = (f32[8,16,128]{2,1,0:T(8,128)S(1)}, f32[1,48,128]{2,1,0:T(8,128)S(1)}, f32[4,48,128]{2,1,0:T(8,128)S(1)}, f32[4,48,128]{2,1,0:T(8,128)S(1)}, f32[8,128]{1,0:T(8,128)S(1)}) custom-call(s32[1]{0:T(128)} %bitcast.own_ref, s32[8,128]{1,0:T(8,128)S(1)} %get-tuple-element.38.ids_ref, s32[8,128]{1,0:T(8,128)S(1)} %shard_map.108.all_ref, ...), custom_call_target="tpu_custom_call" | custom-call | tf_op jit(solution)/shard_map/pallas_call | solution.py:39
  40.0 7.4 %all_to_all.26.sim_ref = f32[8,16,128]{2,1,0:T(8,128)S(1)} all-to-all(f32[8,16,128]{2,1,0:T(8,128)S(1)} %get-tuple-element.44), channel_id=1, replica_groups=mesh['obs'=4,'cell'=8] {'cell'}, dimensions={0} | all-to-all | bytes 131072 | tf_op jit(solution)/shard_map/all_to_all | solution.py:325
  47.4 0.9 %shard_map.110 = (f32[24,128]{1,0:T(8,128)S(1)}, f32[8,128]{1,0:T(8,128)S(1)}) custom-call(s32[8,128]{1,0:T(8,128)S(1)} %get-tuple-element.38.ids_ref, f32[8,16,128]{2,1,0:T(8,128)S(1)} %all_to_all.26.sim_ref, f32[8,128]{1,0:T(8,128)S(1)} %copy-done, bf16[8,192,128]{2,1,0:T(8,128)(2,1)S(1)} %get-tuple-element.40.foot_ref), custom_call_target="tpu_custom_call" | custom-call | tf_op jit(solution)/shard_map/pallas_call | solution.py:39
  48.3 1.8 %collective-permute-start.8 = (f32[24,128]{1,0:T(8,128)S(1)}, f32[24,128]{1,0:T(8,128)S(1)}, u32[]{:S(2)}, u32[]{:S(2)}) collective-permute-start(f32[24,128]{1,0:T(8,128)S(1)} %get-tuple-element.48.refs_1_), channel_id=1, source_target_pairs={{0,24},{8,16},{16,8},{24,0},{1,25},{9,17},{17,9},{25,1},{2,26},{10... | collective-permute-start | bytes 36872 | tf_op jit(solution)/shard_map/ppermute | solution.py:321
  50.1 0.9 %collective-permute-start.7 = (f32[24,128]{1,0:T(8,128)S(1)}, f32[24,128]{1,0:T(8,128)S(1)}, u32[]{:S(2)}, u32[]{:S(2)}) collective-permute-start(f32[24,128]{1,0:T(8,128)S(1)} %get-tuple-element.48.refs_1_), channel_id=1, source_target_pairs={{0,16},{8,24},{16,0},{24,8},{1,17},{9,25},{17,1},{25,9},{2,18},{10... | collective-permute-start | bytes 36872 | tf_op jit(solution)/shard_map/ppermute | solution.py:321
  51.0 1.7 %collective-permute-start.6 = (f32[24,128]{1,0:T(8,128)S(1)}, f32[24,128]{1,0:T(8,128)S(1)}, u32[]{:S(2)}, u32[]{:S(2)}) collective-permute-start(f32[24,128]{1,0:T(8,128)S(1)} %get-tuple-element.48.refs_1_), channel_id=1, source_target_pairs={{0,8},{8,0},{16,24},{24,16},{1,9},{9,1},{17,25},{25,17},{2,10},{10... | collective-permute-start | bytes 36872 | tf_op jit(solution)/shard_map/ppermute | solution.py:321
  52.7 1.1 %collective-permute-done.8.refs_4_ = f32[24,128]{1,0:T(8,128)S(1)} collective-permute-done((f32[24,128]{1,0:T(8,128)S(1)}, f32[24,128]{1,0:T(8,128)S(1)}, u32[]{:S(2)}, u32[]{:S(2)}) %collective-permute-start.8) | collective-permute-done | bytes 12320 | tf_op jit(solution)/shard_map/ppermute | solution.py:321
  53.8 1.0 %collective-permute-done.7.refs_3_ = f32[24,128]{1,0:T(8,128)S(1)} collective-permute-done((f32[24,128]{1,0:T(8,128)S(1)}, f32[24,128]{1,0:T(8,128)S(1)}, u32[]{:S(2)}, u32[]{:S(2)}) %collective-permute-start.7) | collective-permute-done | bytes 12320 | tf_op jit(solution)/shard_map/ppermute | solution.py:321
  54.8 0.0 collective-permute-done.6.refs_2_
  54.9 3.4 %shard_map.111 = (f32[8,16,128]{2,1,0:T(8,128)S(1)}, f32[1,48,128]{2,1,0:T(8,128)S(1)}, f32[4,48,128]{2,1,0:T(8,128)S(1)}, f32[4,48,128]{2,1,0:T(8,128)S(1)}, f32[8,128]{1,0:T(8,128)S(1)}) custom-call(s32[1]{0:T(128)} %bitcast.own_ref, s32[8,128]{1,0:T(8,128)S(1)} %get-tuple-element.38.ids_ref, s32[8,128]{1,0:T(8,128)S(1)} %shard_map.108.all_ref, ...), custom_call_target="tpu_custom_call" | custom-call | tf_op jit(solution)/shard_map/pallas_call | solution.py:39
  58.2 7.4 %all_to_all.27.sim_ref = f32[8,16,128]{2,1,0:T(8,128)S(1)} all-to-all(f32[8,16,128]{2,1,0:T(8,128)S(1)} %get-tuple-element.49), channel_id=1, replica_groups=mesh['obs'=4,'cell'=8] {'cell'}, dimensions={0} | all-to-all | bytes 131072 | tf_op jit(solution)/shard_map/all_to_all | solution.py:325
  65.6 0.9 %shard_map.112 = (f32[24,128]{1,0:T(8,128)S(1)}, f32[8,128]{1,0:T(8,128)S(1)}) custom-call(s32[8,128]{1,0:T(8,128)S(1)} %get-tuple-element.38.ids_ref, f32[8,16,128]{2,1,0:T(8,128)S(1)} %all_to_all.27.sim_ref, f32[8,128]{1,0:T(8,128)S(1)} %copy-done, bf16[8,192,128]{2,1,0:T(8,128)(2,1)S(1)} %get-tuple-element.40.foot_ref), custom_call_target="tpu_custom_call" | custom-call | tf_op jit(solution)/shard_map/pallas_call | solution.py:39
  66.6 2.1 %collective-permute-start.11 = (f32[24,128]{1,0:T(8,128)S(1)}, f32[24,128]{1,0:T(8,128)S(1)}, u32[]{:S(2)}, u32[]{:S(2)}) collective-permute-start(f32[24,128]{1,0:T(8,128)S(1)} %get-tuple-element.53.refs_1_), channel_id=1, source_target_pairs={{0,24},{8,16},{16,8},{24,0},{1,25},{9,17},{17,9},{25,1},{2,26},{10... | collective-permute-start | bytes 36872 | tf_op jit(solution)/shard_map/ppermute | solution.py:321
  68.7 0.9 %collective-permute-start.10 = (f32[24,128]{1,0:T(8,128)S(1)}, f32[24,128]{1,0:T(8,128)S(1)}, u32[]{:S(2)}, u32[]{:S(2)}) collective-permute-start(f32[24,128]{1,0:T(8,128)S(1)} %get-tuple-element.53.refs_1_), channel_id=1, source_target_pairs={{0,16},{8,24},{16,0},{24,8},{1,17},{9,25},{17,1},{25,9},{2,18},{10... | collective-permute-start | bytes 36872 | tf_op jit(solution)/shard_map/ppermute | solution.py:321
  69.6 1.4 %collective-permute-start.9 = (f32[24,128]{1,0:T(8,128)S(1)}, f32[24,128]{1,0:T(8,128)S(1)}, u32[]{:S(2)}, u32[]{:S(2)}) collective-permute-start(f32[24,128]{1,0:T(8,128)S(1)} %get-tuple-element.53.refs_1_), channel_id=1, source_target_pairs={{0,8},{8,0},{16,24},{24,16},{1,9},{9,1},{17,25},{25,17},{2,10},{10... | collective-permute-start | bytes 36872 | tf_op jit(solution)/shard_map/ppermute | solution.py:321
  71.0 1.1 %collective-permute-done.11.refs_4_ = f32[24,128]{1,0:T(8,128)S(1)} collective-permute-done((f32[24,128]{1,0:T(8,128)S(1)}, f32[24,128]{1,0:T(8,128)S(1)}, u32[]{:S(2)}, u32[]{:S(2)}) %collective-permute-start.11) | collective-permute-done | bytes 12320 | tf_op jit(solution)/shard_map/ppermute | solution.py:321
  72.1 1.3 %collective-permute-done.10.refs_3_ = f32[24,128]{1,0:T(8,128)S(1)} collective-permute-done((f32[24,128]{1,0:T(8,128)S(1)}, f32[24,128]{1,0:T(8,128)S(1)}, u32[]{:S(2)}, u32[]{:S(2)}) %collective-permute-start.10) | collective-permute-done | bytes 12320 | tf_op jit(solution)/shard_map/ppermute | solution.py:321
  73.4 0.0 collective-permute-done.9.refs_2_
  73.4 2.8 %shard_map.113 = (f32[8,8,128]{2,1,0:T(8,128)S(1)}, f32[1,48,128]{2,1,0:T(8,128)S(1)}, f32[1,48,128]{2,1,0:T(8,128)S(1)}, f32[8,128]{1,0:T(8,128)S(1)}) custom-call(s32[1]{0:T(128)} %bitcast.own_ref, s32[8,128]{1,0:T(8,128)S(1)} %get-tuple-element.38.ids_ref, s32[8,128]{1,0:T(8,128)S(1)} %shard_map.108.all_ref, f32[6144,128]{1,0:T(8,128)S(1)} %get-tuple-element.35.lat_ref, ...), custom_call_target="tpu_custom_call" | custom-call | tf_op jit(solution)/shard_map/pallas_call | solution.py:39
  76.3 7.2 %all_to_all.28.sum_ref = f32[8,8,128]{2,1,0:T(8,128)S(1)} all-to-all(f32[8,8,128]{2,1,0:T(8,128)S(1)} %get-tuple-element.54), channel_id=1, replica_groups=mesh['obs'=4,'cell'=8] {'cell'}, dimensions={0} | all-to-all | bytes 65536 | tf_op jit(solution)/shard_map/all_to_all | solution.py:325
  83.5 0.8 shard_map.114
  (1 shorter events, 0.0 us)
Async XLA Ops:
  3.4 14.2 %all-to-all-start = ((bf16[8,208,128]{2,1,0:T(8,128)(2,1)}), bf16[8,208,128]{2,1,0:T(8,128)(2,1)}, u32[]{:S(2)}, u32[]{:S(2)}) async-start(bf16[8,208,128]{2,1,0:T(8,128)(2,1)} %get-tuple-element.36), calls=%async_computation | async-start | bytes 851968 | tf_op jit(solution)/shard_map/all_to_all | solution.py:325
  8.6 7.4 %collective-permute-start.2 = (f32[48,128]{1,0:T(8,128)}, f32[48,128]{1,0:T(8,128)S(1)}, u32[]{:S(2)}, u32[]{:S(2)}) collective-permute-start(f32[48,128]{1,0:T(8,128)} %bitcast.5), channel_id=1, source_target_pairs={{0,24},{8,16},{16,8},{24,0},{1,25},{9,17},{17,9},{25,1},{2,26},{10... | collective-permute-start | bytes 73736 | tf_op jit(solution)/shard_map/ppermute | solution.py:321
  12.7 4.9 %collective-permute-start.1 = (f32[48,128]{1,0:T(8,128)}, f32[48,128]{1,0:T(8,128)S(1)}, u32[]{:S(2)}, u32[]{:S(2)}) collective-permute-start(f32[48,128]{1,0:T(8,128)} %bitcast.6), channel_id=1, source_target_pairs={{0,16},{8,24},{16,0},{24,8},{1,17},{9,25},{17,1},{25,9},{2,18},{10... | collective-permute-start | bytes 73736 | tf_op jit(solution)/shard_map/ppermute | solution.py:321
  12.7 4.9 %collective-permute-start = (f32[48,128]{1,0:T(8,128)}, f32[48,128]{1,0:T(8,128)S(1)}, u32[]{:S(2)}, u32[]{:S(2)}) collective-permute-start(f32[48,128]{1,0:T(8,128)} %bitcast.7), channel_id=1, source_target_pairs={{0,8},{8,0},{16,24},{24,16},{1,9},{9,1},{17,25},{25,17},{2,10},{10... | collective-permute-start | bytes 73736 | tf_op jit(solution)/shard_map/ppermute | solution.py:321
  13.3 0.8 copy-start.1
  14.1 14.6 %copy-start = (f32[8,128]{1,0:T(8,128)S(1)}, f32[8,128]{1,0:T(8,128)}, u32[]{:S(2)}) copy-start(f32[8,128]{1,0:T(8,128)} %get-tuple-element.32.weight_ref) | copy-start | bytes 12292
  29.7 5.6 %collective-permute-start.5 = (f32[32,128]{1,0:T(8,128)S(1)}, f32[32,128]{1,0:T(8,128)S(1)}, u32[]{:S(2)}, u32[]{:S(2)}) collective-permute-start(f32[32,128]{1,0:T(8,128)S(1)} %get-tuple-element.41.refs_0_), channel_id=1, source_target_pairs={{0,24},{8,16},{16,8},{24,0},{1,25},{9,17},{17,9},{25,1},{2,26},{10... | collective-permute-start | bytes 49160 | tf_op jit(solution)/shard_map/ppermute | solution.py:321
  31.9 4.6 %collective-permute-start.4 = (f32[32,128]{1,0:T(8,128)S(1)}, f32[32,128]{1,0:T(8,128)S(1)}, u32[]{:S(2)}, u32[]{:S(2)}) collective-permute-start(f32[32,128]{1,0:T(8,128)S(1)} %get-tuple-element.41.refs_0_), channel_id=1, source_target_pairs={{0,16},{8,24},{16,0},{24,8},{1,17},{9,25},{17,1},{25,9},{2,18},{10... | collective-permute-start | bytes 49160 | tf_op jit(solution)/shard_map/ppermute | solution.py:321
  31.9 4.6 %collective-permute-start.3 = (f32[32,128]{1,0:T(8,128)S(1)}, f32[32,128]{1,0:T(8,128)S(1)}, u32[]{:S(2)}, u32[]{:S(2)}) collective-permute-start(f32[32,128]{1,0:T(8,128)S(1)} %get-tuple-element.41.refs_0_), channel_id=1, source_target_pairs={{0,8},{8,0},{16,24},{24,16},{1,9},{9,1},{17,25},{25,17},{2,10},{10... | collective-permute-start | bytes 49160 | tf_op jit(solution)/shard_map/ppermute | solution.py:321
  48.3 5.5 %collective-permute-start.8 = (f32[24,128]{1,0:T(8,128)S(1)}, f32[24,128]{1,0:T(8,128)S(1)}, u32[]{:S(2)}, u32[]{:S(2)}) collective-permute-start(f32[24,128]{1,0:T(8,128)S(1)} %get-tuple-element.48.refs_1_), channel_id=1, source_target_pairs={{0,24},{8,16},{16,8},{24,0},{1,25},{9,17},{17,9},{25,1},{2,26},{10... | collective-permute-start | bytes 36872 | tf_op jit(solution)/shard_map/ppermute | solution.py:321
  50.1 4.7 %collective-permute-start.7 = (f32[24,128]{1,0:T(8,128)S(1)}, f32[24,128]{1,0:T(8,128)S(1)}, u32[]{:S(2)}, u32[]{:S(2)}) collective-permute-start(f32[24,128]{1,0:T(8,128)S(1)} %get-tuple-element.48.refs_1_), channel_id=1, source_target_pairs={{0,16},{8,24},{16,0},{24,8},{1,17},{9,25},{17,1},{25,9},{2,18},{10... | collective-permute-start | bytes 36872 | tf_op jit(solution)/shard_map/ppermute | solution.py:321
  51.0 3.8 %collective-permute-start.6 = (f32[24,128]{1,0:T(8,128)S(1)}, f32[24,128]{1,0:T(8,128)S(1)}, u32[]{:S(2)}, u32[]{:S(2)}) collective-permute-start(f32[24,128]{1,0:T(8,128)S(1)} %get-tuple-element.48.refs_1_), channel_id=1, source_target_pairs={{0,8},{8,0},{16,24},{24,16},{1,9},{9,1},{17,25},{25,17},{2,10},{10... | collective-permute-start | bytes 36872 | tf_op jit(solution)/shard_map/ppermute | solution.py:321
  66.6 5.5 %collective-permute-start.11 = (f32[24,128]{1,0:T(8,128)S(1)}, f32[24,128]{1,0:T(8,128)S(1)}, u32[]{:S(2)}, u32[]{:S(2)}) collective-permute-start(f32[24,128]{1,0:T(8,128)S(1)} %get-tuple-element.53.refs_1_), channel_id=1, source_target_pairs={{0,24},{8,16},{16,8},{24,0},{1,25},{9,17},{17,9},{25,1},{2,26},{10... | collective-permute-start | bytes 36872 | tf_op jit(solution)/shard_map/ppermute | solution.py:321
  68.7 4.7 %collective-permute-start.10 = (f32[24,128]{1,0:T(8,128)S(1)}, f32[24,128]{1,0:T(8,128)S(1)}, u32[]{:S(2)}, u32[]{:S(2)}) collective-permute-start(f32[24,128]{1,0:T(8,128)S(1)} %get-tuple-element.53.refs_1_), channel_id=1, source_target_pairs={{0,16},{8,24},{16,0},{24,8},{1,17},{9,25},{17,1},{25,9},{2,18},{10... | collective-permute-start | bytes 36872 | tf_op jit(solution)/shard_map/ppermute | solution.py:321
  69.6 3.8 %collective-permute-start.9 = (f32[24,128]{1,0:T(8,128)S(1)}, f32[24,128]{1,0:T(8,128)S(1)}, u32[]{:S(2)}, u32[]{:S(2)}) collective-permute-start(f32[24,128]{1,0:T(8,128)S(1)} %get-tuple-element.53.refs_1_), channel_id=1, source_target_pairs={{0,8},{8,0},{16,24},{24,16},{1,9},{9,1},{17,25},{25,17},{2,10},{10... | collective-permute-start | bytes 36872 | tf_op jit(solution)/shard_map/ppermute | solution.py:321

commit v7 on v6

--- a/solution.py
+++ b/solution.py
@@ -105,10 +105,10 @@
     weight_ref[...] = jnp.where(lane < limit, rinv_ref[...], 0.0)
 
 
-def fetch_kernel(*refs):
-    refs, sems = refs[:-1], refs[-1]
-    half = len(refs) // 2
-    copies = [pltpu.make_async_copy(refs[at], refs[half + at], sems.at[at]) for at in range(half)]
+def fetch_kernel(lat_any, start_any, lat_ref, start_ref, sems):
+    modes = lat_any.shape[0]
+    copies = [pltpu.make_async_copy(lat_any.at[m], lat_ref.at[:, m, :], sems.at[m]) for m in range(modes)]
+    copies.append(pltpu.make_async_copy(start_any, start_ref, sems.at[modes]))
     for copy in copies:
         copy.start()
     for copy in copies:
@@ -123,10 +123,6 @@
             part = ref[p, at:at + ROWS, :]
             total += part * part
     return total
-
-
-def lat_row(lat_ref, modes, row):
-    return lat_ref[pl.ds(row, modes, stride=lat_ref.shape[0] // modes), :]
 
 
 def forward(dims, field_ref, lat_ref, foot_ref, ids_ref, sim_ref, out_ref):
@@ -140,7 +136,7 @@
             sub = ids_ref[j, 2 * nb + b]
             total = None
             for r in range(CR):
-                column = jnp.sum(lat_row(lat_ref, modes, row + r) * field_ref[period], axis=1, keepdims=True)
+                column = jnp.sum(lat_ref[row + r] * field_ref[period], axis=1, keepdims=True)
                 at = (b * CR + r) * modes
                 term = foot_ref[j, at:at + modes, :].astype(F32) * column
                 total = term if total is None else total + term
@@ -257,7 +253,7 @@
                     row = all_ref[2 * at_i + 1, at_t] * CR
                     total = sum_ref[period]
                     for r in range(CR):
-                        total += coef[r * modes:(r + 1) * modes, at_t:at_t + 1] * lat_row(lat_ref, modes, row + r)
+                        total += coef[r * modes:(r + 1) * modes, at_t:at_t + 1] * lat_ref[row + r]
                     sum_ref[period] = total
         return carry
 
@@ -368,13 +364,13 @@
         limit=60,
     )
     came = swap(hats, "cell")
-    lat, start, _ = lax.optimization_barrier((lat_mats.reshape(modes * lat_rows, lat_rows), start, weights))
+    lat, start, _ = lax.optimization_barrier((lat_mats, start, weights))
     lat, start = call(
         fetch_kernel,
-        (shape(lat.shape), shape(start.shape)),
+        (shape((lat_rows, modes, lat_rows)), shape(start.shape)),
         [ANY] * 2,
         lat, start,
-        scratch=[pltpu.SemaphoreType.DMA((2,))],
+        scratch=[pltpu.SemaphoreType.DMA((modes + 1,))],
         limit=50,
         cost=pl.CostEstimate(flops=0, transcendentals=0, bytes_accessed=8 * (lat.size + start.size)),
     )

time: 84.8 us -> 81.1 us (0.956)
  Pallas kernels: 20.2 us -> 16.5 us
    pallas_call x11, Pallas kernels: 20.2 us -> 16.5 us  [call(): pl.pallas_call(kernel, out_shape=outs, in_specs=specs, out_specs=jax.tree...]
  transfers between devices with their start and end apart: 13 -> 13, of which waited for: 7 -> 8; matrix products, arithmetic and copies ran while one was open for 0% -> 0% of each run, Pallas kernels for 2% -> 3%
where the time goes in v7:
time: 81.1 us; the launch traced here: 80.5 us
  blocking collectives  30.9 us (38%)
  starting transfers between devices  23.1 us (28%)
  Pallas kernels  16.5 us (20%)
  waiting for transfers between devices  8.61 us (11%)
    all_to_all x4, blocking collectives, swap(): return lax.all_to_all(array, axis, split_axis=0, concat_axis=0, tiled=True)  30.9 us
    ppermute x12, starting transfers between devices, share(): lax.ppermute(array, axis, [(d, d ^ s) for d in range(size)])  18 us
    pallas_call x11, Pallas kernels, call(): pl.pallas_call(kernel, out_shape=outs, in_specs=specs, out_specs=jax.tree...  16.5 us
    ppermute x12, waiting for transfers between devices, share(): lax.ppermute(array, axis, [(d, d ^ s) for d in range(size)])  8.61 us
    all_to_all x1, starting transfers between devices, swap(): return lax.all_to_all(array, axis, split_axis=0, concat_axis=0, tiled=True)  5.18 us
  transfers between devices with their start and end apart: 13, of which 8 were waited for; matrix products, arithmetic and copies ran while one was open for 0% of the time, Pallas kernels for 3%

profile of v7, /device:TPU:0, one launch (start us, length us, event | category | flops | bytes accessed | tf_op | source)
XLA Modules:
  0.0 80.5 jit_solution(10792429611303216889)
XLA Ops:
  0.6 2.8 %shard_map.104 = (bf16[8,208,128]{2,1,0:T(8,128)(2,1)}, f32[8,128]{1,0:T(8,128)}) custom-call(s32[1]{0:T(128)} %bitcast.2.cell_ref, bf16[384,384]{1,0:T(8,128)(2,1)} %constant.12.clone.high_any, bf16[384,384]{1,0:T(8,128)(2,1)} %constant.13.clone.low_any, bf16[2,128,768]{2,1,0:T(8,128)(2,1)} %foot_any.1, s32[2]{0:T(128)} %off_any.1, s32[2]{0:T(128)} %sub_any.1, ...), custom_call_target="tpu_custom_call" | custom-call | tf_op jit(solution)/shard_map/pallas_call | solution.py:39
  3.4 5.2 %all-to-all-start = ((bf16[8,208,128]{2,1,0:T(8,128)(2,1)}), bf16[8,208,128]{2,1,0:T(8,128)(2,1)}, u32[]{:S(2)}, u32[]{:S(2)}) async-start(bf16[8,208,128]{2,1,0:T(8,128)(2,1)} %get-tuple-element.36), calls=%async_computation | async-start | bytes 851968 | tf_op jit(solution)/shard_map/all_to_all | solution.py:321
  8.6 4.1 %collective-permute-start.2 = (f32[48,128]{1,0:T(8,128)}, f32[48,128]{1,0:T(8,128)S(1)}, u32[]{:S(2)}, u32[]{:S(2)}) collective-permute-start(f32[48,128]{1,0:T(8,128)} %bitcast.4), channel_id=1, source_target_pairs={{0,24},{8,16},{16,8},{24,0},{1,25},{9,17},{17,9},{25,1},{2,26},{10... | collective-permute-start | bytes 73736 | tf_op jit(solution)/shard_map/ppermute | solution.py:317
  12.7 0.0 collective-permute-start.1
  12.7 0.6 collective-permute-start
  13.3 0.0 copy-start.1
  13.3 0.8 copy-done.1
  14.1 0.0 copy-start
  14.1 2.3 %shard_map.105 = (f32[128,48,128]{2,1,0:T(8,128)S(1)}, f32[48,128]{1,0:T(8,128)S(1)}) custom-call(f32[48,128,128]{2,1,0:T(8,128)} %lat_any, f32[48,128]{1,0:T(8,128)S(1)} %bitcast.7), custom_call_target="tpu_custom_call" | custom-call | bytes 6340608 | tf_op jit(solution)/shard_map/pallas_call | solution.py:39
  16.4 0.0 collective-permute-done.2.refs_3_
  16.4 1.2 %collective-permute-done.1.refs_2_ = f32[48,128]{1,0:T(8,128)S(1)} collective-permute-done((f32[48,128]{1,0:T(8,128)}, f32[48,128]{1,0:T(8,128)S(1)}, u32[]{:S(2)}, u32[]{:S(2)}) %collective-permute-start.1) | collective-permute-done | bytes 24608 | tf_op jit(solution)/shard_map/ppermute | solution.py:317
  17.6 0.0 collective-permute-done.refs_1_
  17.6 0.0 all-to-all-done.came_ref
  17.6 1.9 %shard_map.106 = (f32[8,16,128]{2,1,0:T(8,128)S(1)}, f32[4,48,128]{2,1,0:T(8,128)S(1)}, bf16[8,192,128]{2,1,0:T(8,128)(2,1)S(1)}, s32[8,128]{1,0:T(8,128)S(1)}) custom-call(s32[1]{0:T(128)} %bitcast.own_ref, f32[128,48,128]{2,1,0:T(8,128)S(1)} %get-tuple-element.35.lat_ref, bf16[8,208,128]{2,1,0:T(8,128)(2,1)} %all-to-all-done.came_ref, ...), custom_call_target="tpu_custom_call" | custom-call | tf_op jit(solution)/shard_map/pallas_call | solution.py:39
  19.6 8.9 %all_to_all.25.sim_ref = f32[8,16,128]{2,1,0:T(8,128)S(1)} all-to-all(f32[8,16,128]{2,1,0:T(8,128)S(1)} %get-tuple-element.39), channel_id=1, replica_groups=mesh['obs'=4,'cell'=8] {'cell'}, dimensions={0} | all-to-all | bytes 131072 | tf_op jit(solution)/shard_map/all_to_all | solution.py:321
  28.4 0.0 copy-done
  28.4 0.9 %shard_map.107 = (f32[32,128]{1,0:T(8,128)S(1)}, f32[8,128]{1,0:T(8,128)S(1)}) custom-call(s32[8,128]{1,0:T(8,128)S(1)} %get-tuple-element.38.ids_ref, f32[8,16,128]{2,1,0:T(8,128)S(1)} %all_to_all.25.sim_ref, f32[8,128]{1,0:T(8,128)S(1)} %copy-done, bf16[8,192,128]{2,1,0:T(8,128)(2,1)S(1)} %get-tuple-element.40.foot_ref), custom_call_target="tpu_custom_call" | custom-call | tf_op jit(solution)/shard_map/pallas_call | solution.py:39
  29.4 2.6 %collective-permute-start.5 = (f32[32,128]{1,0:T(8,128)S(1)}, f32[32,128]{1,0:T(8,128)S(1)}, u32[]{:S(2)}, u32[]{:S(2)}) collective-permute-start(f32[32,128]{1,0:T(8,128)S(1)} %get-tuple-element.41.refs_0_), channel_id=1, source_target_pairs={{0,24},{8,16},{16,8},{24,0},{1,25},{9,17},{17,9},{25,1},{2,26},{10... | collective-permute-start | bytes 49160 | tf_op jit(solution)/shard_map/ppermute | solution.py:317
  32.0 0.0 collective-permute-start.4
  32.0 1.8 %collective-permute-start.3 = (f32[32,128]{1,0:T(8,128)S(1)}, f32[32,128]{1,0:T(8,128)S(1)}, u32[]{:S(2)}, u32[]{:S(2)}) collective-permute-start(f32[32,128]{1,0:T(8,128)S(1)} %get-tuple-element.41.refs_0_), channel_id=1, source_target_pairs={{0,8},{8,0},{16,24},{24,16},{1,9},{9,1},{17,25},{25,17},{2,10},{10... | collective-permute-start | bytes 49160 | tf_op jit(solution)/shard_map/ppermute | solution.py:317
  33.8 1.2 %collective-permute-done.5.refs_3_ = f32[32,128]{1,0:T(8,128)S(1)} collective-permute-done((f32[32,128]{1,0:T(8,128)S(1)}, f32[32,128]{1,0:T(8,128)S(1)}, u32[]{:S(2)}, u32[]{:S(2)}) %collective-permute-start.5) | collective-permute-done | bytes 16416 | tf_op jit(solution)/shard_map/ppermute | solution.py:317
  35.0 1.7 %collective-permute-done.4.refs_2_ = f32[32,128]{1,0:T(8,128)S(1)} collective-permute-done((f32[32,128]{1,0:T(8,128)S(1)}, f32[32,128]{1,0:T(8,128)S(1)}, u32[]{:S(2)}, u32[]{:S(2)}) %collective-permute-start.4) | collective-permute-done | bytes 16416 | tf_op jit(solution)/shard_map/ppermute | solution.py:317
  36.6 0.0 collective-permute-done.3.refs_1_
  36.6 2.0 %shard_map.109 = (f32[8,16,128]{2,1,0:T(8,128)S(1)}, f32[1,48,128]{2,1,0:T(8,128)S(1)}, f32[4,48,128]{2,1,0:T(8,128)S(1)}, f32[4,48,128]{2,1,0:T(8,128)S(1)}, f32[8,128]{1,0:T(8,128)S(1)}) custom-call(s32[1]{0:T(128)} %bitcast.own_ref, s32[8,128]{1,0:T(8,128)S(1)} %get-tuple-element.38.ids_ref, s32[8,128]{1,0:T(8,128)S(1)} %shard_map.108.all_ref, ...), custom_call_target="tpu_custom_call" | custom-call | tf_op jit(solution)/shard_map/pallas_call | solution.py:39
  38.7 7.4 %all_to_all.26.sim_ref = f32[8,16,128]{2,1,0:T(8,128)S(1)} all-to-all(f32[8,16,128]{2,1,0:T(8,128)S(1)} %get-tuple-element.44), channel_id=1, replica_groups=mesh['obs'=4,'cell'=8] {'cell'}, dimensions={0} | all-to-all | bytes 131072 | tf_op jit(solution)/shard_map/all_to_all | solution.py:321
  46.1 0.9 %shard_map.110 = (f32[24,128]{1,0:T(8,128)S(1)}, f32[8,128]{1,0:T(8,128)S(1)}) custom-call(s32[8,128]{1,0:T(8,128)S(1)} %get-tuple-element.38.ids_ref, f32[8,16,128]{2,1,0:T(8,128)S(1)} %all_to_all.26.sim_ref, f32[8,128]{1,0:T(8,128)S(1)} %copy-done, bf16[8,192,128]{2,1,0:T(8,128)(2,1)S(1)} %get-tuple-element.40.foot_ref), custom_call_target="tpu_custom_call" | custom-call | tf_op jit(solution)/shard_map/pallas_call | solution.py:39
  47.0 1.5 %collective-permute-start.8 = (f32[24,128]{1,0:T(8,128)S(1)}, f32[24,128]{1,0:T(8,128)S(1)}, u32[]{:S(2)}, u32[]{:S(2)}) collective-permute-start(f32[24,128]{1,0:T(8,128)S(1)} %get-tuple-element.48.refs_1_), channel_id=1, source_target_pairs={{0,24},{8,16},{16,8},{24,0},{1,25},{9,17},{17,9},{25,1},{2,26},{10... | collective-permute-start | bytes 36872 | tf_op jit(solution)/shard_map/ppermute | solution.py:317
  48.6 0.8 %collective-permute-start.7 = (f32[24,128]{1,0:T(8,128)S(1)}, f32[24,128]{1,0:T(8,128)S(1)}, u32[]{:S(2)}, u32[]{:S(2)}) collective-permute-start(f32[24,128]{1,0:T(8,128)S(1)} %get-tuple-element.48.refs_1_), channel_id=1, source_target_pairs={{0,16},{8,24},{16,0},{24,8},{1,17},{9,25},{17,1},{25,9},{2,18},{10... | collective-permute-start | bytes 36872 | tf_op jit(solution)/shard_map/ppermute | solution.py:317
  49.4 2.0 %collective-permute-start.6 = (f32[24,128]{1,0:T(8,128)S(1)}, f32[24,128]{1,0:T(8,128)S(1)}, u32[]{:S(2)}, u32[]{:S(2)}) collective-permute-start(f32[24,128]{1,0:T(8,128)S(1)} %get-tuple-element.48.refs_1_), channel_id=1, source_target_pairs={{0,8},{8,0},{16,24},{24,16},{1,9},{9,1},{17,25},{25,17},{2,10},{10... | collective-permute-start | bytes 36872 | tf_op jit(solution)/shard_map/ppermute | solution.py:317
  51.4 1.1 %collective-permute-done.8.refs_4_ = f32[24,128]{1,0:T(8,128)S(1)} collective-permute-done((f32[24,128]{1,0:T(8,128)S(1)}, f32[24,128]{1,0:T(8,128)S(1)}, u32[]{:S(2)}, u32[]{:S(2)}) %collective-permute-start.8) | collective-permute-done | bytes 12320 | tf_op jit(solution)/shard_map/ppermute | solution.py:317
  52.5 0.7 collective-permute-done.7.refs_3_
  53.2 0.0 collective-permute-done.6.refs_2_
  53.2 2.0 %shard_map.111 = (f32[8,16,128]{2,1,0:T(8,128)S(1)}, f32[1,48,128]{2,1,0:T(8,128)S(1)}, f32[4,48,128]{2,1,0:T(8,128)S(1)}, f32[4,48,128]{2,1,0:T(8,128)S(1)}, f32[8,128]{1,0:T(8,128)S(1)}) custom-call(s32[1]{0:T(128)} %bitcast.own_ref, s32[8,128]{1,0:T(8,128)S(1)} %get-tuple-element.38.ids_ref, s32[8,128]{1,0:T(8,128)S(1)} %shard_map.108.all_ref, ...), custom_call_target="tpu_custom_call" | custom-call | tf_op jit(solution)/shard_map/pallas_call | solution.py:39
  55.3 7.4 %all_to_all.27.sim_ref = f32[8,16,128]{2,1,0:T(8,128)S(1)} all-to-all(f32[8,16,128]{2,1,0:T(8,128)S(1)} %get-tuple-element.49), channel_id=1, replica_groups=mesh['obs'=4,'cell'=8] {'cell'}, dimensions={0} | all-to-all | bytes 131072 | tf_op jit(solution)/shard_map/all_to_all | solution.py:321
  62.7 0.9 %shard_map.112 = (f32[24,128]{1,0:T(8,128)S(1)}, f32[8,128]{1,0:T(8,128)S(1)}) custom-call(s32[8,128]{1,0:T(8,128)S(1)} %get-tuple-element.38.ids_ref, f32[8,16,128]{2,1,0:T(8,128)S(1)} %all_to_all.27.sim_ref, f32[8,128]{1,0:T(8,128)S(1)} %copy-done, bf16[8,192,128]{2,1,0:T(8,128)(2,1)S(1)} %get-tuple-element.40.foot_ref), custom_call_target="tpu_custom_call" | custom-call | tf_op jit(solution)/shard_map/pallas_call | solution.py:39
  63.6 2.5 %collective-permute-start.11 = (f32[24,128]{1,0:T(8,128)S(1)}, f32[24,128]{1,0:T(8,128)S(1)}, u32[]{:S(2)}, u32[]{:S(2)}) collective-permute-start(f32[24,128]{1,0:T(8,128)S(1)} %get-tuple-element.53.refs_1_), channel_id=1, source_target_pairs={{0,24},{8,16},{16,8},{24,0},{1,25},{9,17},{17,9},{25,1},{2,26},{10... | collective-permute-start | bytes 36872 | tf_op jit(solution)/shard_map/ppermute | solution.py:317
  66.1 0.9 %collective-permute-start.10 = (f32[24,128]{1,0:T(8,128)S(1)}, f32[24,128]{1,0:T(8,128)S(1)}, u32[]{:S(2)}, u32[]{:S(2)}) collective-permute-start(f32[24,128]{1,0:T(8,128)S(1)} %get-tuple-element.53.refs_1_), channel_id=1, source_target_pairs={{0,16},{8,24},{16,0},{24,8},{1,17},{9,25},{17,1},{25,9},{2,18},{10... | collective-permute-start | bytes 36872 | tf_op jit(solution)/shard_map/ppermute | solution.py:317
  67.0 1.0 %collective-permute-start.9 = (f32[24,128]{1,0:T(8,128)S(1)}, f32[24,128]{1,0:T(8,128)S(1)}, u32[]{:S(2)}, u32[]{:S(2)}) collective-permute-start(f32[24,128]{1,0:T(8,128)S(1)} %get-tuple-element.53.refs_1_), channel_id=1, source_target_pairs={{0,8},{8,0},{16,24},{24,16},{1,9},{9,1},{17,25},{25,17},{2,10},{10... | collective-permute-start | bytes 36872 | tf_op jit(solution)/shard_map/ppermute | solution.py:317
  68.0 1.1 %collective-permute-done.11.refs_4_ = f32[24,128]{1,0:T(8,128)S(1)} collective-permute-done((f32[24,128]{1,0:T(8,128)S(1)}, f32[24,128]{1,0:T(8,128)S(1)}, u32[]{:S(2)}, u32[]{:S(2)}) %collective-permute-start.11) | collective-permute-done | bytes 12320 | tf_op jit(solution)/shard_map/ppermute | solution.py:317
  69.1 1.5 %collective-permute-done.10.refs_3_ = f32[24,128]{1,0:T(8,128)S(1)} collective-permute-done((f32[24,128]{1,0:T(8,128)S(1)}, f32[24,128]{1,0:T(8,128)S(1)}, u32[]{:S(2)}, u32[]{:S(2)}) %collective-permute-start.10) | collective-permute-done | bytes 12320 | tf_op jit(solution)/shard_map/ppermute | solution.py:317
  70.7 0.1 collective-permute-done.9.refs_2_
  70.8 1.7 %shard_map.113 = (f32[8,8,128]{2,1,0:T(8,128)S(1)}, f32[1,48,128]{2,1,0:T(8,128)S(1)}, f32[1,48,128]{2,1,0:T(8,128)S(1)}, f32[8,128]{1,0:T(8,128)S(1)}) custom-call(s32[1]{0:T(128)} %bitcast.own_ref, s32[8,128]{1,0:T(8,128)S(1)} %get-tuple-element.38.ids_ref, s32[8,128]{1,0:T(8,128)S(1)} %shard_map.108.all_ref, ...), custom_call_target="tpu_custom_call" | custom-call | tf_op jit(solution)/shard_map/pallas_call | solution.py:39
  72.5 7.2 %all_to_all.28.sum_ref = f32[8,8,128]{2,1,0:T(8,128)S(1)} all-to-all(f32[8,8,128]{2,1,0:T(8,128)S(1)} %get-tuple-element.54), channel_id=1, replica_groups=mesh['obs'=4,'cell'=8] {'cell'}, dimensions={0} | all-to-all | bytes 65536 | tf_op jit(solution)/shard_map/all_to_all | solution.py:321
  79.7 0.8 shard_map.114
  (1 shorter events, 0.0 us)
Async XLA Ops:
  3.4 14.2 %all-to-all-start = ((bf16[8,208,128]{2,1,0:T(8,128)(2,1)}), bf16[8,208,128]{2,1,0:T(8,128)(2,1)}, u32[]{:S(2)}, u32[]{:S(2)}) async-start(bf16[8,208,128]{2,1,0:T(8,128)(2,1)} %get-tuple-element.36), calls=%async_computation | async-start | bytes 851968 | tf_op jit(solution)/shard_map/all_to_all | solution.py:321
  8.6 7.8 %collective-permute-start.2 = (f32[48,128]{1,0:T(8,128)}, f32[48,128]{1,0:T(8,128)S(1)}, u32[]{:S(2)}, u32[]{:S(2)}) collective-permute-start(f32[48,128]{1,0:T(8,128)} %bitcast.4), channel_id=1, source_target_pairs={{0,24},{8,16},{16,8},{24,0},{1,25},{9,17},{17,9},{25,1},{2,26},{10... | collective-permute-start | bytes 73736 | tf_op jit(solution)/shard_map/ppermute | solution.py:317
  12.7 4.9 %collective-permute-start.1 = (f32[48,128]{1,0:T(8,128)}, f32[48,128]{1,0:T(8,128)S(1)}, u32[]{:S(2)}, u32[]{:S(2)}) collective-permute-start(f32[48,128]{1,0:T(8,128)} %bitcast.5), channel_id=1, source_target_pairs={{0,16},{8,24},{16,0},{24,8},{1,17},{9,25},{17,1},{25,9},{2,18},{10... | collective-permute-start | bytes 73736 | tf_op jit(solution)/shard_map/ppermute | solution.py:317
  12.7 4.9 %collective-permute-start = (f32[48,128]{1,0:T(8,128)}, f32[48,128]{1,0:T(8,128)S(1)}, u32[]{:S(2)}, u32[]{:S(2)}) collective-permute-start(f32[48,128]{1,0:T(8,128)} %bitcast.6), channel_id=1, source_target_pairs={{0,8},{8,0},{16,24},{24,16},{1,9},{9,1},{17,25},{25,17},{2,10},{10... | collective-permute-start | bytes 73736 | tf_op jit(solution)/shard_map/ppermute | solution.py:317
  13.3 0.8 copy-start.1
  14.1 14.3 %copy-start = (f32[8,128]{1,0:T(8,128)S(1)}, f32[8,128]{1,0:T(8,128)}, u32[]{:S(2)}) copy-start(f32[8,128]{1,0:T(8,128)} %get-tuple-element.32.weight_ref) | copy-start | bytes 12292
  29.4 5.6 %collective-permute-start.5 = (f32[32,128]{1,0:T(8,128)S(1)}, f32[32,128]{1,0:T(8,128)S(1)}, u32[]{:S(2)}, u32[]{:S(2)}) collective-permute-start(f32[32,128]{1,0:T(8,128)S(1)} %get-tuple-element.41.refs_0_), channel_id=1, source_target_pairs={{0,24},{8,16},{16,8},{24,0},{1,25},{9,17},{17,9},{25,1},{2,26},{10... | collective-permute-start | bytes 49160 | tf_op jit(solution)/shard_map/ppermute | solution.py:317
  32.0 4.6 %collective-permute-start.4 = (f32[32,128]{1,0:T(8,128)S(1)}, f32[32,128]{1,0:T(8,128)S(1)}, u32[]{:S(2)}, u32[]{:S(2)}) collective-permute-start(f32[32,128]{1,0:T(8,128)S(1)} %get-tuple-element.41.refs_0_), channel_id=1, source_target_pairs={{0,16},{8,24},{16,0},{24,8},{1,17},{9,25},{17,1},{25,9},{2,18},{10... | collective-permute-start | bytes 49160 | tf_op jit(solution)/shard_map/ppermute | solution.py:317
  32.0 4.6 %collective-permute-start.3 = (f32[32,128]{1,0:T(8,128)S(1)}, f32[32,128]{1,0:T(8,128)S(1)}, u32[]{:S(2)}, u32[]{:S(2)}) collective-permute-start(f32[32,128]{1,0:T(8,128)S(1)} %get-tuple-element.41.refs_0_), channel_id=1, source_target_pairs={{0,8},{8,0},{16,24},{24,16},{1,9},{9,1},{17,25},{25,17},{2,10},{10... | collective-permute-start | bytes 49160 | tf_op jit(solution)/shard_map/ppermute | solution.py:317
  47.0 5.5 %collective-permute-start.8 = (f32[24,128]{1,0:T(8,128)S(1)}, f32[24,128]{1,0:T(8,128)S(1)}, u32[]{:S(2)}, u32[]{:S(2)}) collective-permute-start(f32[24,128]{1,0:T(8,128)S(1)} %get-tuple-element.48.refs_1_), channel_id=1, source_target_pairs={{0,24},{8,16},{16,8},{24,0},{1,25},{9,17},{17,9},{25,1},{2,26},{10... | collective-permute-start | bytes 36872 | tf_op jit(solution)/shard_map/ppermute | solution.py:317
  48.6 4.7 %collective-permute-start.7 = (f32[24,128]{1,0:T(8,128)S(1)}, f32[24,128]{1,0:T(8,128)S(1)}, u32[]{:S(2)}, u32[]{:S(2)}) collective-permute-start(f32[24,128]{1,0:T(8,128)S(1)} %get-tuple-element.48.refs_1_), channel_id=1, source_target_pairs={{0,16},{8,24},{16,0},{24,8},{1,17},{9,25},{17,1},{25,9},{2,18},{10... | collective-permute-start | bytes 36872 | tf_op jit(solution)/shard_map/ppermute | solution.py:317
  49.4 3.8 %collective-permute-start.6 = (f32[24,128]{1,0:T(8,128)S(1)}, f32[24,128]{1,0:T(8,128)S(1)}, u32[]{:S(2)}, u32[]{:S(2)}) collective-permute-start(f32[24,128]{1,0:T(8,128)S(1)} %get-tuple-element.48.refs_1_), channel_id=1, source_target_pairs={{0,8},{8,0},{16,24},{24,16},{1,9},{9,1},{17,25},{25,17},{2,10},{10... | collective-permute-start | bytes 36872 | tf_op jit(solution)/shard_map/ppermute | solution.py:317
  63.6 5.5 %collective-permute-start.11 = (f32[24,128]{1,0:T(8,128)S(1)}, f32[24,128]{1,0:T(8,128)S(1)}, u32[]{:S(2)}, u32[]{:S(2)}) collective-permute-start(f32[24,128]{1,0:T(8,128)S(1)} %get-tuple-element.53.refs_1_), channel_id=1, source_target_pairs={{0,24},{8,16},{16,8},{24,0},{1,25},{9,17},{17,9},{25,1},{2,26},{10... | collective-permute-start | bytes 36872 | tf_op jit(solution)/shard_map/ppermute | solution.py:317
  66.1 4.6 %collective-permute-start.10 = (f32[24,128]{1,0:T(8,128)S(1)}, f32[24,128]{1,0:T(8,128)S(1)}, u32[]{:S(2)}, u32[]{:S(2)}) collective-permute-start(f32[24,128]{1,0:T(8,128)S(1)} %get-tuple-element.53.refs_1_), channel_id=1, source_target_pairs={{0,16},{8,24},{16,0},{24,8},{1,17},{9,25},{17,1},{25,9},{2,18},{10... | collective-permute-start | bytes 36872 | tf_op jit(solution)/shard_map/ppermute | solution.py:317
  67.0 3.8 %collective-permute-start.9 = (f32[24,128]{1,0:T(8,128)S(1)}, f32[24,128]{1,0:T(8,128)S(1)}, u32[]{:S(2)}, u32[]{:S(2)}) collective-permute-start(f32[24,128]{1,0:T(8,128)S(1)} %get-tuple-element.53.refs_1_), channel_id=1, source_target_pairs={{0,8},{8,0},{16,24},{24,16},{1,9},{9,1},{17,25},{25,17},{2,10},{10... | collective-permute-start | bytes 36872 | tf_op jit(solution)/shard_map/ppermute | solution.py:317

commit v8 on v7

--- a/solution.py
+++ b/solution.py
@@ -12,6 +12,8 @@
 
 CR = 2
 WAYS = 4
+CHUNK = 16
+TERMS = 3
 STEPS = 3
 ROWS = 8
 VMEM = pl.BlockSpec(memory_space=pltpu.VMEM)
@@ -78,15 +80,15 @@
     ob = foot_ref.shape[1]
     lon = high_ref.shape[1]
     contract = (((1,), (1,)), ((), ()))
-    for b in range(nb):
-        for r in range(CR):
-            foot = foot_ref[b, :, r * lon:(r + 1) * lon]
-            hat = lax.dot_general(high_ref[...], foot, contract, preferred_element_type=F32)
-            hat += lax.dot_general(low_ref[...], foot, contract, preferred_element_type=F32)
-            hat = hat.astype(BF16)
+    for r in range(CR):
+        foot = foot_ref[:, :, r * lon:(r + 1) * lon].reshape(nb * ob, lon)
+        hat = lax.dot_general(high_ref[...], foot, contract, preferred_element_type=F32)
+        hat += lax.dot_general(low_ref[...], foot, contract, preferred_element_type=F32)
+        hat = hat.astype(BF16)
+        for b in range(nb):
             at = (b * CR + r) * modes
             for c in range(nc):
-                out_ref[c, at:at + modes, :] = hat[c * modes:(c + 1) * modes, :]
+                out_ref[c, at:at + modes, :] = hat[c * modes:(c + 1) * modes, b * ob:(b + 1) * ob]
     lane = lax.broadcasted_iota(jnp.int32, (16, ob), 1)
     ids = jnp.zeros((16, ob), F32)
     for b in range(nb):
@@ -217,13 +219,22 @@
         out_ref[2 * s:2 * s + 2, :] = ref[at:at + ROWS, :][0:2].astype(jnp.int32)
 
 
+def split(values):
+    terms = []
+    for _ in range(TERMS):
+        terms.append(values.astype(BF16))
+        values = values - terms[-1].astype(F32)
+    return jnp.concatenate(terms, axis=0)
+
+
 def image_kernel(dims, no, first, last, own_ref, ids_ref, all_ref, lat_ref, foot_ref, norm_ref, field_ref, *refs):
     nc, nb, modes, groups, band = dims
     if not first:
         prior_ref, refs = refs[0], refs[1:]
     ways = min(no, WAYS)
-    kept = (6 if last else 7) + ways
+    kept = (6 if last else 7) + 2 * ways
     coef_refs, refs = refs[:-kept], refs[-kept:]
+    wide_refs, refs = refs[-ways:], refs[:-ways]
     sum_refs, refs = refs[-ways:], refs[:-ways]
     if last:
         out_ref, row_ref, mine_ref, alpha_ref, next_ref, held_ref = refs
@@ -240,20 +251,27 @@
     for sum_ref in sum_refs:
         sum_ref[...] = jnp.zeros_like(sum_ref)
 
+    line = lax.broadcasted_iota(jnp.int32, (TERMS * CHUNK, CHUNK * 128), 0)
+    lane = lax.broadcasted_iota(jnp.int32, (TERMS * CHUNK, CHUNK * 128), 1)
+    pick = jnp.where(line % CHUNK == lane // 128, 1.0, 0.0).astype(BF16)
+
     def group(at, carry):
         found = [at * ways + i for i in range(ways)]
         if permuted(no):
             found = [own_ref[0] ^ at_i for at_i in found]
-        coefs = [held_ref[at_i].T for at_i in found]
-        for j in range(nc):
-            for b in range(nb):
-                at_t = j * nb + b
-                for at_i, coef, sum_ref in zip(found, coefs, sum_refs):
-                    period = all_ref[2 * at_i, at_t]
-                    row = all_ref[2 * at_i + 1, at_t] * CR
+        for chunk in range(0, mine, CHUNK):
+            for at_i, wide_ref in zip(found, wide_refs):
+                left = split(held_ref[at_i, chunk:chunk + CHUNK, :])
+                wide = lax.dot_general(left, pick, (((0,), (0,)), ((), ())), preferred_element_type=F32)
+                wide_ref[...] = wide[:CR * modes]
+            for at in range(CHUNK):
+                for at_i, wide_ref, sum_ref in zip(found, wide_refs, sum_refs):
+                    period = all_ref[2 * at_i, chunk + at]
+                    row = all_ref[2 * at_i + 1, chunk + at] * CR
                     total = sum_ref[period]
                     for r in range(CR):
-                        total += coef[r * modes:(r + 1) * modes, at_t:at_t + 1] * lat_ref[row + r]
+                        coef = wide_ref[r * modes:(r + 1) * modes, at * 128:(at + 1) * 128]
+                        total += coef * lat_ref[row + r]
                     sum_ref[period] = total
         return carry
 
@@ -427,7 +445,9 @@
             own, ids, every, lat, foot, norm, field, *before, *coefs,
             scratch=[pltpu.VMEM(field_shape.shape, F32) if last else sim_scratch]
             + [pltpu.VMEM((no, mine, 128), F32)]
-            + [pltpu.VMEM(field_shape.shape, F32)] * ways,
+            + [pltpu.VMEM(field_shape.shape, F32)] * ways
+            + [pltpu.VMEM((CR * modes, CHUNK * 128), F32)] * ways,
+            limit=16,
         )
         vector = None if last else vector[0]
         rows.append(row)

time: 81.1 us -> 80.2 us (0.989)
  Pallas kernels: 16.5 us -> 15.5 us
    pallas_call x11, Pallas kernels: 16.5 us -> 15.5 us  [call(): pl.pallas_call(kernel, out_shape=outs, in_specs=specs, out_specs=jax.tree...]
  transfers between devices with their start and end apart: 13 -> 13, of which waited for: 8 -> 7; matrix products, arithmetic and copies ran while one was open for 0% -> 0% of each run, Pallas kernels for 3% -> 3%
where the time goes in v8:
time: 80.2 us; the launch traced here: 79.6 us
  blocking collectives  30.9 us (39%)
  starting transfers between devices  23.1 us (29%)
  Pallas kernels  15.5 us (19%)
  waiting for transfers between devices  8.63 us (11%)
    all_to_all x4, blocking collectives, swap(): return lax.all_to_all(array, axis, split_axis=0, concat_axis=0, tiled=True)  30.9 us
    ppermute x12, starting transfers between devices, share(): lax.ppermute(array, axis, [(d, d ^ s) for d in range(size)])  18 us
    pallas_call x11, Pallas kernels, call(): pl.pallas_call(kernel, out_shape=outs, in_specs=specs, out_specs=jax.tree...  15.5 us
    ppermute x12, waiting for transfers between devices, share(): lax.ppermute(array, axis, [(d, d ^ s) for d in range(size)])  8.62 us
    all_to_all x1, starting transfers between devices, swap(): return lax.all_to_all(array, axis, split_axis=0, concat_axis=0, tiled=True)  5.18 us
  transfers between devices with their start and end apart: 13, of which 7 were waited for; matrix products, arithmetic and copies ran while one was open for 0% of the time, Pallas kernels for 3%

profile of v8, /device:TPU:0, one launch (start us, length us, event | category | flops | bytes accessed | tf_op | source)
XLA Modules:
  0.0 79.6 jit_solution(7184918691006919198)
XLA Ops:
  0.6 2.6 %shard_map.104 = (bf16[8,208,128]{2,1,0:T(8,128)(2,1)}, f32[8,128]{1,0:T(8,128)}) custom-call(s32[1]{0:T(128)} %bitcast.2.cell_ref, bf16[384,384]{1,0:T(8,128)(2,1)} %constant.12.clone.high_any, bf16[384,384]{1,0:T(8,128)(2,1)} %constant.13.clone.low_any, bf16[2,128,768]{2,1,0:T(8,128)(2,1)} %foot_any.1, s32[2]{0:T(128)} %off_any.1, s32[2]{0:T(128)} %sub_any.1, ...), custom_call_target="tpu_custom_call" | custom-call | tf_op jit(solution)/shard_map/pallas_call | solution.py:41
  3.3 5.2 %all-to-all-start = ((bf16[8,208,128]{2,1,0:T(8,128)(2,1)}), bf16[8,208,128]{2,1,0:T(8,128)(2,1)}, u32[]{:S(2)}, u32[]{:S(2)}) async-start(bf16[8,208,128]{2,1,0:T(8,128)(2,1)} %get-tuple-element.36), calls=%async_computation | async-start | bytes 851968 | tf_op jit(solution)/shard_map/all_to_all | solution.py:339
  8.5 4.1 %collective-permute-start.2 = (f32[48,128]{1,0:T(8,128)}, f32[48,128]{1,0:T(8,128)S(1)}, u32[]{:S(2)}, u32[]{:S(2)}) collective-permute-start(f32[48,128]{1,0:T(8,128)} %bitcast.4), channel_id=1, source_target_pairs={{0,24},{8,16},{16,8},{24,0},{1,25},{9,17},{17,9},{25,1},{2,26},{10... | collective-permute-start | bytes 73736 | tf_op jit(solution)/shard_map/ppermute | solution.py:335
  12.5 0.0 collective-permute-start.1
  12.5 0.6 collective-permute-start
  13.2 0.0 copy-start.1
  13.2 0.8 copy-done.1
  13.9 0.0 copy-start
  13.9 2.3 %shard_map.105 = (f32[128,48,128]{2,1,0:T(8,128)S(1)}, f32[48,128]{1,0:T(8,128)S(1)}) custom-call(f32[48,128,128]{2,1,0:T(8,128)} %lat_any, f32[48,128]{1,0:T(8,128)S(1)} %bitcast.7), custom_call_target="tpu_custom_call" | custom-call | bytes 6340608 | tf_op jit(solution)/shard_map/pallas_call | solution.py:41
  16.3 0.0 collective-permute-done.2.refs_3_
  16.3 1.2 %collective-permute-done.1.refs_2_ = f32[48,128]{1,0:T(8,128)S(1)} collective-permute-done((f32[48,128]{1,0:T(8,128)}, f32[48,128]{1,0:T(8,128)S(1)}, u32[]{:S(2)}, u32[]{:S(2)}) %collective-permute-start.1) | collective-permute-done | bytes 24608 | tf_op jit(solution)/shard_map/ppermute | solution.py:335
  17.5 0.0 collective-permute-done.refs_1_
  17.5 0.0 all-to-all-done.came_ref
  17.5 1.9 %shard_map.106 = (f32[8,16,128]{2,1,0:T(8,128)S(1)}, f32[4,48,128]{2,1,0:T(8,128)S(1)}, bf16[8,192,128]{2,1,0:T(8,128)(2,1)S(1)}, s32[8,128]{1,0:T(8,128)S(1)}) custom-call(s32[1]{0:T(128)} %bitcast.own_ref, f32[128,48,128]{2,1,0:T(8,128)S(1)} %get-tuple-element.35.lat_ref, bf16[8,208,128]{2,1,0:T(8,128)(2,1)} %all-to-all-done.came_ref, ...), custom_call_target="tpu_custom_call" | custom-call | tf_op jit(solution)/shard_map/pallas_call | solution.py:41
  19.4 8.9 %all_to_all.25.sim_ref = f32[8,16,128]{2,1,0:T(8,128)S(1)} all-to-all(f32[8,16,128]{2,1,0:T(8,128)S(1)} %get-tuple-element.39), channel_id=1, replica_groups=mesh['obs'=4,'cell'=8] {'cell'}, dimensions={0} | all-to-all | bytes 131072 | tf_op jit(solution)/shard_map/all_to_all | solution.py:339
  28.3 0.0 copy-done
  28.3 0.9 %shard_map.107 = (f32[32,128]{1,0:T(8,128)S(1)}, f32[8,128]{1,0:T(8,128)S(1)}) custom-call(s32[8,128]{1,0:T(8,128)S(1)} %get-tuple-element.38.ids_ref, f32[8,16,128]{2,1,0:T(8,128)S(1)} %all_to_all.25.sim_ref, f32[8,128]{1,0:T(8,128)S(1)} %copy-done, bf16[8,192,128]{2,1,0:T(8,128)(2,1)S(1)} %get-tuple-element.40.foot_ref), custom_call_target="tpu_custom_call" | custom-call | tf_op jit(solution)/shard_map/pallas_call | solution.py:41
  29.2 2.6 %collective-permute-start.5 = (f32[32,128]{1,0:T(8,128)S(1)}, f32[32,128]{1,0:T(8,128)S(1)}, u32[]{:S(2)}, u32[]{:S(2)}) collective-permute-start(f32[32,128]{1,0:T(8,128)S(1)} %get-tuple-element.41.refs_0_), channel_id=1, source_target_pairs={{0,24},{8,16},{16,8},{24,0},{1,25},{9,17},{17,9},{25,1},{2,26},{10... | collective-permute-start | bytes 49160 | tf_op jit(solution)/shard_map/ppermute | solution.py:335
  31.8 0.0 collective-permute-start.4
  31.8 1.8 %collective-permute-start.3 = (f32[32,128]{1,0:T(8,128)S(1)}, f32[32,128]{1,0:T(8,128)S(1)}, u32[]{:S(2)}, u32[]{:S(2)}) collective-permute-start(f32[32,128]{1,0:T(8,128)S(1)} %get-tuple-element.41.refs_0_), channel_id=1, source_target_pairs={{0,8},{8,0},{16,24},{24,16},{1,9},{9,1},{17,25},{25,17},{2,10},{10... | collective-permute-start | bytes 49160 | tf_op jit(solution)/shard_map/ppermute | solution.py:335
  33.6 1.2 %collective-permute-done.5.refs_3_ = f32[32,128]{1,0:T(8,128)S(1)} collective-permute-done((f32[32,128]{1,0:T(8,128)S(1)}, f32[32,128]{1,0:T(8,128)S(1)}, u32[]{:S(2)}, u32[]{:S(2)}) %collective-permute-start.5) | collective-permute-done | bytes 16416 | tf_op jit(solution)/shard_map/ppermute | solution.py:335
  34.8 1.7 %collective-permute-done.4.refs_2_ = f32[32,128]{1,0:T(8,128)S(1)} collective-permute-done((f32[32,128]{1,0:T(8,128)S(1)}, f32[32,128]{1,0:T(8,128)S(1)}, u32[]{:S(2)}, u32[]{:S(2)}) %collective-permute-start.4) | collective-permute-done | bytes 16416 | tf_op jit(solution)/shard_map/ppermute | solution.py:335
  36.5 0.0 collective-permute-done.3.refs_1_
  36.5 1.8 %shard_map.109 = (f32[8,16,128]{2,1,0:T(8,128)S(1)}, f32[1,48,128]{2,1,0:T(8,128)S(1)}, f32[4,48,128]{2,1,0:T(8,128)S(1)}, f32[4,48,128]{2,1,0:T(8,128)S(1)}, f32[8,128]{1,0:T(8,128)S(1)}) custom-call(s32[1]{0:T(128)} %bitcast.own_ref, s32[8,128]{1,0:T(8,128)S(1)} %get-tuple-element.38.ids_ref, s32[8,128]{1,0:T(8,128)S(1)} %shard_map.108.all_ref, ...), custom_call_target="tpu_custom_call" | custom-call | tf_op jit(solution)/shard_map/pallas_call | solution.py:41
  38.3 7.4 %all_to_all.26.sim_ref = f32[8,16,128]{2,1,0:T(8,128)S(1)} all-to-all(f32[8,16,128]{2,1,0:T(8,128)S(1)} %get-tuple-element.44), channel_id=1, replica_groups=mesh['obs'=4,'cell'=8] {'cell'}, dimensions={0} | all-to-all | bytes 131072 | tf_op jit(solution)/shard_map/all_to_all | solution.py:339
  45.7 0.9 %shard_map.110 = (f32[24,128]{1,0:T(8,128)S(1)}, f32[8,128]{1,0:T(8,128)S(1)}) custom-call(s32[8,128]{1,0:T(8,128)S(1)} %get-tuple-element.38.ids_ref, f32[8,16,128]{2,1,0:T(8,128)S(1)} %all_to_all.26.sim_ref, f32[8,128]{1,0:T(8,128)S(1)} %copy-done, bf16[8,192,128]{2,1,0:T(8,128)(2,1)S(1)} %get-tuple-element.40.foot_ref), custom_call_target="tpu_custom_call" | custom-call | tf_op jit(solution)/shard_map/pallas_call | solution.py:41
  46.6 1.5 %collective-permute-start.8 = (f32[24,128]{1,0:T(8,128)S(1)}, f32[24,128]{1,0:T(8,128)S(1)}, u32[]{:S(2)}, u32[]{:S(2)}) collective-permute-start(f32[24,128]{1,0:T(8,128)S(1)} %get-tuple-element.48.refs_1_), channel_id=1, source_target_pairs={{0,24},{8,16},{16,8},{24,0},{1,25},{9,17},{17,9},{25,1},{2,26},{10... | collective-permute-start | bytes 36872 | tf_op jit(solution)/shard_map/ppermute | solution.py:335
  48.1 0.8 %collective-permute-start.7 = (f32[24,128]{1,0:T(8,128)S(1)}, f32[24,128]{1,0:T(8,128)S(1)}, u32[]{:S(2)}, u32[]{:S(2)}) collective-permute-start(f32[24,128]{1,0:T(8,128)S(1)} %get-tuple-element.48.refs_1_), channel_id=1, source_target_pairs={{0,16},{8,24},{16,0},{24,8},{1,17},{9,25},{17,1},{25,9},{2,18},{10... | collective-permute-start | bytes 36872 | tf_op jit(solution)/shard_map/ppermute | solution.py:335
  49.0 2.0 %collective-permute-start.6 = (f32[24,128]{1,0:T(8,128)S(1)}, f32[24,128]{1,0:T(8,128)S(1)}, u32[]{:S(2)}, u32[]{:S(2)}) collective-permute-start(f32[24,128]{1,0:T(8,128)S(1)} %get-tuple-element.48.refs_1_), channel_id=1, source_target_pairs={{0,8},{8,0},{16,24},{24,16},{1,9},{9,1},{17,25},{25,17},{2,10},{10... | collective-permute-start | bytes 36872 | tf_op jit(solution)/shard_map/ppermute | solution.py:335
  51.0 1.1 %collective-permute-done.8.refs_4_ = f32[24,128]{1,0:T(8,128)S(1)} collective-permute-done((f32[24,128]{1,0:T(8,128)S(1)}, f32[24,128]{1,0:T(8,128)S(1)}, u32[]{:S(2)}, u32[]{:S(2)}) %collective-permute-start.8) | collective-permute-done | bytes 12320 | tf_op jit(solution)/shard_map/ppermute | solution.py:335
  52.1 0.7 collective-permute-done.7.refs_3_
  52.8 0.0 collective-permute-done.6.refs_2_
  52.8 1.8 %shard_map.111 = (f32[8,16,128]{2,1,0:T(8,128)S(1)}, f32[1,48,128]{2,1,0:T(8,128)S(1)}, f32[4,48,128]{2,1,0:T(8,128)S(1)}, f32[4,48,128]{2,1,0:T(8,128)S(1)}, f32[8,128]{1,0:T(8,128)S(1)}) custom-call(s32[1]{0:T(128)} %bitcast.own_ref, s32[8,128]{1,0:T(8,128)S(1)} %get-tuple-element.38.ids_ref, s32[8,128]{1,0:T(8,128)S(1)} %shard_map.108.all_ref, ...), custom_call_target="tpu_custom_call" | custom-call | tf_op jit(solution)/shard_map/pallas_call | solution.py:41
  54.6 7.4 %all_to_all.27.sim_ref = f32[8,16,128]{2,1,0:T(8,128)S(1)} all-to-all(f32[8,16,128]{2,1,0:T(8,128)S(1)} %get-tuple-element.49), channel_id=1, replica_groups=mesh['obs'=4,'cell'=8] {'cell'}, dimensions={0} | all-to-all | bytes 131072 | tf_op jit(solution)/shard_map/all_to_all | solution.py:339
  62.0 0.9 %shard_map.112 = (f32[24,128]{1,0:T(8,128)S(1)}, f32[8,128]{1,0:T(8,128)S(1)}) custom-call(s32[8,128]{1,0:T(8,128)S(1)} %get-tuple-element.38.ids_ref, f32[8,16,128]{2,1,0:T(8,128)S(1)} %all_to_all.27.sim_ref, f32[8,128]{1,0:T(8,128)S(1)} %copy-done, bf16[8,192,128]{2,1,0:T(8,128)(2,1)S(1)} %get-tuple-element.40.foot_ref), custom_call_target="tpu_custom_call" | custom-call | tf_op jit(solution)/shard_map/pallas_call | solution.py:41
  62.9 2.5 %collective-permute-start.11 = (f32[24,128]{1,0:T(8,128)S(1)}, f32[24,128]{1,0:T(8,128)S(1)}, u32[]{:S(2)}, u32[]{:S(2)}) collective-permute-start(f32[24,128]{1,0:T(8,128)S(1)} %get-tuple-element.53.refs_1_), channel_id=1, source_target_pairs={{0,24},{8,16},{16,8},{24,0},{1,25},{9,17},{17,9},{25,1},{2,26},{10... | collective-permute-start | bytes 36872 | tf_op jit(solution)/shard_map/ppermute | solution.py:335
  65.4 0.9 %collective-permute-start.10 = (f32[24,128]{1,0:T(8,128)S(1)}, f32[24,128]{1,0:T(8,128)S(1)}, u32[]{:S(2)}, u32[]{:S(2)}) collective-permute-start(f32[24,128]{1,0:T(8,128)S(1)} %get-tuple-element.53.refs_1_), channel_id=1, source_target_pairs={{0,16},{8,24},{16,0},{24,8},{1,17},{9,25},{17,1},{25,9},{2,18},{10... | collective-permute-start | bytes 36872 | tf_op jit(solution)/shard_map/ppermute | solution.py:335
  66.3 1.0 %collective-permute-start.9 = (f32[24,128]{1,0:T(8,128)S(1)}, f32[24,128]{1,0:T(8,128)S(1)}, u32[]{:S(2)}, u32[]{:S(2)}) collective-permute-start(f32[24,128]{1,0:T(8,128)S(1)} %get-tuple-element.53.refs_1_), channel_id=1, source_target_pairs={{0,8},{8,0},{16,24},{24,16},{1,9},{9,1},{17,25},{25,17},{2,10},{10... | collective-permute-start | bytes 36872 | tf_op jit(solution)/shard_map/ppermute | solution.py:335
  67.4 1.1 %collective-permute-done.11.refs_4_ = f32[24,128]{1,0:T(8,128)S(1)} collective-permute-done((f32[24,128]{1,0:T(8,128)S(1)}, f32[24,128]{1,0:T(8,128)S(1)}, u32[]{:S(2)}, u32[]{:S(2)}) %collective-permute-start.11) | collective-permute-done | bytes 12320 | tf_op jit(solution)/shard_map/ppermute | solution.py:335
  68.5 1.7 %collective-permute-done.10.refs_3_ = f32[24,128]{1,0:T(8,128)S(1)} collective-permute-done((f32[24,128]{1,0:T(8,128)S(1)}, f32[24,128]{1,0:T(8,128)S(1)}, u32[]{:S(2)}, u32[]{:S(2)}) %collective-permute-start.10) | collective-permute-done | bytes 12320 | tf_op jit(solution)/shard_map/ppermute | solution.py:335
  70.1 0.0 collective-permute-done.9.refs_2_
  70.1 1.5 %shard_map.113 = (f32[8,8,128]{2,1,0:T(8,128)S(1)}, f32[1,48,128]{2,1,0:T(8,128)S(1)}, f32[1,48,128]{2,1,0:T(8,128)S(1)}, f32[8,128]{1,0:T(8,128)S(1)}) custom-call(s32[1]{0:T(128)} %bitcast.own_ref, s32[8,128]{1,0:T(8,128)S(1)} %get-tuple-element.38.ids_ref, s32[8,128]{1,0:T(8,128)S(1)} %shard_map.108.all_ref, ...), custom_call_target="tpu_custom_call" | custom-call | tf_op jit(solution)/shard_map/pallas_call | solution.py:41
  71.6 7.2 %all_to_all.28.sum_ref = f32[8,8,128]{2,1,0:T(8,128)S(1)} all-to-all(f32[8,8,128]{2,1,0:T(8,128)S(1)} %get-tuple-element.54), channel_id=1, replica_groups=mesh['obs'=4,'cell'=8] {'cell'}, dimensions={0} | all-to-all | bytes 65536 | tf_op jit(solution)/shard_map/all_to_all | solution.py:339
  78.9 0.8 shard_map.114
  (1 shorter events, 0.0 us)
Async XLA Ops:
  3.3 14.2 %all-to-all-start = ((bf16[8,208,128]{2,1,0:T(8,128)(2,1)}), bf16[8,208,128]{2,1,0:T(8,128)(2,1)}, u32[]{:S(2)}, u32[]{:S(2)}) async-start(bf16[8,208,128]{2,1,0:T(8,128)(2,1)} %get-tuple-element.36), calls=%async_computation | async-start | bytes 851968 | tf_op jit(solution)/shard_map/all_to_all | solution.py:339
  8.5 7.8 %collective-permute-start.2 = (f32[48,128]{1,0:T(8,128)}, f32[48,128]{1,0:T(8,128)S(1)}, u32[]{:S(2)}, u32[]{:S(2)}) collective-permute-start(f32[48,128]{1,0:T(8,128)} %bitcast.4), channel_id=1, source_target_pairs={{0,24},{8,16},{16,8},{24,0},{1,25},{9,17},{17,9},{25,1},{2,26},{10... | collective-permute-start | bytes 73736 | tf_op jit(solution)/shard_map/ppermute | solution.py:335
  12.5 4.9 %collective-permute-start.1 = (f32[48,128]{1,0:T(8,128)}, f32[48,128]{1,0:T(8,128)S(1)}, u32[]{:S(2)}, u32[]{:S(2)}) collective-permute-start(f32[48,128]{1,0:T(8,128)} %bitcast.5), channel_id=1, source_target_pairs={{0,16},{8,24},{16,0},{24,8},{1,17},{9,25},{17,1},{25,9},{2,18},{10... | collective-permute-start | bytes 73736 | tf_op jit(solution)/shard_map/ppermute | solution.py:335
  12.5 4.9 %collective-permute-start = (f32[48,128]{1,0:T(8,128)}, f32[48,128]{1,0:T(8,128)S(1)}, u32[]{:S(2)}, u32[]{:S(2)}) collective-permute-start(f32[48,128]{1,0:T(8,128)} %bitcast.6), channel_id=1, source_target_pairs={{0,8},{8,0},{16,24},{24,16},{1,9},{9,1},{17,25},{25,17},{2,10},{10... | collective-permute-start | bytes 73736 | tf_op jit(solution)/shard_map/ppermute | solution.py:335
  13.2 0.8 copy-start.1
  13.9 14.3 %copy-start = (f32[8,128]{1,0:T(8,128)S(1)}, f32[8,128]{1,0:T(8,128)}, u32[]{:S(2)}) copy-start(f32[8,128]{1,0:T(8,128)} %get-tuple-element.32.weight_ref) | copy-start | bytes 12292
  29.2 5.6 %collective-permute-start.5 = (f32[32,128]{1,0:T(8,128)S(1)}, f32[32,128]{1,0:T(8,128)S(1)}, u32[]{:S(2)}, u32[]{:S(2)}) collective-permute-start(f32[32,128]{1,0:T(8,128)S(1)} %get-tuple-element.41.refs_0_), channel_id=1, source_target_pairs={{0,24},{8,16},{16,8},{24,0},{1,25},{9,17},{17,9},{25,1},{2,26},{10... | collective-permute-start | bytes 49160 | tf_op jit(solution)/shard_map/ppermute | solution.py:335
  31.8 4.6 %collective-permute-start.4 = (f32[32,128]{1,0:T(8,128)S(1)}, f32[32,128]{1,0:T(8,128)S(1)}, u32[]{:S(2)}, u32[]{:S(2)}) collective-permute-start(f32[32,128]{1,0:T(8,128)S(1)} %get-tuple-element.41.refs_0_), channel_id=1, source_target_pairs={{0,16},{8,24},{16,0},{24,8},{1,17},{9,25},{17,1},{25,9},{2,18},{10... | collective-permute-start | bytes 49160 | tf_op jit(solution)/shard_map/ppermute | solution.py:335
  31.8 4.6 %collective-permute-start.3 = (f32[32,128]{1,0:T(8,128)S(1)}, f32[32,128]{1,0:T(8,128)S(1)}, u32[]{:S(2)}, u32[]{:S(2)}) collective-permute-start(f32[32,128]{1,0:T(8,128)S(1)} %get-tuple-element.41.refs_0_), channel_id=1, source_target_pairs={{0,8},{8,0},{16,24},{24,16},{1,9},{9,1},{17,25},{25,17},{2,10},{10... | collective-permute-start | bytes 49160 | tf_op jit(solution)/shard_map/ppermute | solution.py:335
  46.6 5.5 %collective-permute-start.8 = (f32[24,128]{1,0:T(8,128)S(1)}, f32[24,128]{1,0:T(8,128)S(1)}, u32[]{:S(2)}, u32[]{:S(2)}) collective-permute-start(f32[24,128]{1,0:T(8,128)S(1)} %get-tuple-element.48.refs_1_), channel_id=1, source_target_pairs={{0,24},{8,16},{16,8},{24,0},{1,25},{9,17},{17,9},{25,1},{2,26},{10... | collective-permute-start | bytes 36872 | tf_op jit(solution)/shard_map/ppermute | solution.py:335
  48.1 4.7 %collective-permute-start.7 = (f32[24,128]{1,0:T(8,128)S(1)}, f32[24,128]{1,0:T(8,128)S(1)}, u32[]{:S(2)}, u32[]{:S(2)}) collective-permute-start(f32[24,128]{1,0:T(8,128)S(1)} %get-tuple-element.48.refs_1_), channel_id=1, source_target_pairs={{0,16},{8,24},{16,0},{24,8},{1,17},{9,25},{17,1},{25,9},{2,18},{10... | collective-permute-start | bytes 36872 | tf_op jit(solution)/shard_map/ppermute | solution.py:335
  49.0 3.8 %collective-permute-start.6 = (f32[24,128]{1,0:T(8,128)S(1)}, f32[24,128]{1,0:T(8,128)S(1)}, u32[]{:S(2)}, u32[]{:S(2)}) collective-permute-start(f32[24,128]{1,0:T(8,128)S(1)} %get-tuple-element.48.refs_1_), channel_id=1, source_target_pairs={{0,8},{8,0},{16,24},{24,16},{1,9},{9,1},{17,25},{25,17},{2,10},{10... | collective-permute-start | bytes 36872 | tf_op jit(solution)/shard_map/ppermute | solution.py:335
  62.9 5.5 %collective-permute-start.11 = (f32[24,128]{1,0:T(8,128)S(1)}, f32[24,128]{1,0:T(8,128)S(1)}, u32[]{:S(2)}, u32[]{:S(2)}) collective-permute-start(f32[24,128]{1,0:T(8,128)S(1)} %get-tuple-element.53.refs_1_), channel_id=1, source_target_pairs={{0,24},{8,16},{16,8},{24,0},{1,25},{9,17},{17,9},{25,1},{2,26},{10... | collective-permute-start | bytes 36872 | tf_op jit(solution)/shard_map/ppermute | solution.py:335
  65.4 4.7 %collective-permute-start.10 = (f32[24,128]{1,0:T(8,128)S(1)}, f32[24,128]{1,0:T(8,128)S(1)}, u32[]{:S(2)}, u32[]{:S(2)}) collective-permute-start(f32[24,128]{1,0:T(8,128)S(1)} %get-tuple-element.53.refs_1_), channel_id=1, source_target_pairs={{0,16},{8,24},{16,0},{24,8},{1,17},{9,25},{17,1},{25,9},{2,18},{10... | collective-permute-start | bytes 36872 | tf_op jit(solution)/shard_map/ppermute | solution.py:335
  66.3 3.8 %collective-permute-start.9 = (f32[24,128]{1,0:T(8,128)S(1)}, f32[24,128]{1,0:T(8,128)S(1)}, u32[]{:S(2)}, u32[]{:S(2)}) collective-permute-start(f32[24,128]{1,0:T(8,128)S(1)} %get-tuple-element.53.refs_1_), channel_id=1, source_target_pairs={{0,8},{8,0},{16,24},{24,16},{1,9},{9,1},{17,25},{25,17},{2,10},{10... | collective-permute-start | bytes 36872 | tf_op jit(solution)/shard_map/ppermute | solution.py:335

commit v9 on v8

--- a/solution.py
+++ b/solution.py
@@ -127,7 +127,7 @@
     return total
 
 
-def forward(dims, field_ref, lat_ref, foot_ref, ids_ref, sim_ref, out_ref):
+def forward(dims, field_ref, lat_ref, foot_ref, ids_ref, sim_ref):
     nc, nb, modes, groups, band = dims
     subs = sim_ref.shape[0] - ROWS
     sim_ref[...] = jnp.zeros_like(sim_ref)
@@ -144,8 +144,6 @@
                 total = term if total is None else total + term
             sim_ref[pl.ds(sub, 1), :] += jnp.sum(total, axis=0, keepdims=True)
     sim_ref[subs:, :] = fold(field_ref)
-    for c in range(nc):
-        out_ref[c] = sim_ref[...]
 
 
 def pieces(refs, size, rows):
@@ -156,10 +154,18 @@
     return found
 
 
+def added(refs, rows):
+    return tree_sum(ref[...] for ref in pieces(refs, sum(ref.shape[0] for ref in refs) // rows, rows))
+
+
+def add_kernel(one_ref, other_ref, out_ref):
+    out_ref[...] = one_ref[...] + other_ref[...]
+
+
 def first_kernel(dims, no, own_ref, lat_ref, came_ref, *refs):
     nc, nb, modes, _, _ = dims
-    near_refs, refs = refs[:-7], refs[-7:]
-    out_ref, field_ref, foot_ref, all_ref, sim_ref, ids_ref, sem = refs
+    near_refs, refs = refs[:-6], refs[-6:]
+    out_ref, field_ref, foot_ref, all_ref, ids_ref, sem = refs
     rows = nb * CR * modes
     for j in range(nc):
         all_ref[j:j + 1, :] = came_ref[j, rows:rows + 16, :].astype(F32)[0:1].astype(jnp.int32)
@@ -172,14 +178,16 @@
         for l in range(per_dev):
             field_ref[((own_ref[0] ^ s) if permuted(no) else s) * per_dev + l] = near_ref[l * modes:(l + 1) * modes, :]
     copy.wait()
-    forward(dims, field_ref, lat_ref, foot_ref, ids_ref, sim_ref, out_ref)
-
-
-def adjoint_kernel(dims, first, ids_ref, sim_ref, weight_ref, foot_ref, out_ref, norm_ref, weighted_ref):
+    forward(dims, field_ref, lat_ref, foot_ref, ids_ref, out_ref)
+
+
+def adjoint_kernel(dims, first, ids_ref, weight_ref, foot_ref, *refs):
     nc, nb, modes, groups, band = dims
+    sim_refs, refs = refs[:-3], refs[-3:]
+    out_ref, norm_ref, weighted_ref = refs
     subs = weight_ref.shape[0]
     mine = nc * nb
-    total = tree_sum(sim_ref[c] for c in range(nc))
+    total = added(sim_refs, subs + ROWS)
     norm = jnp.sqrt(jnp.sum(total[subs:], keepdims=True))
     norm_ref[...] = jnp.broadcast_to(norm, norm_ref.shape)
     scale = 1.0 / norm
@@ -232,14 +240,14 @@
     if not first:
         prior_ref, refs = refs[0], refs[1:]
     ways = min(no, WAYS)
-    kept = (6 if last else 7) + 2 * ways
+    kept = 6 + 2 * ways
     coef_refs, refs = refs[:-kept], refs[-kept:]
     wide_refs, refs = refs[-ways:], refs[:-ways]
     sum_refs, refs = refs[-ways:], refs[:-ways]
     if last:
         out_ref, row_ref, mine_ref, alpha_ref, next_ref, held_ref = refs
     else:
-        out_ref, row_ref, next_ref, vector_ref, alpha_ref, sim_ref, held_ref = refs
+        out_ref, row_ref, next_ref, vector_ref, alpha_ref, held_ref = refs
     mine = nc * nb
     periods = field_ref.shape[0]
     per_dev = row_ref.shape[0]
@@ -294,23 +302,21 @@
     for l in range(per_dev):
         row_ref[l] = field_ref[own_ref[0] * per_dev + l] * scale
     if last:
-        total = fold(next_ref)
-        for c in range(nc):
-            out_ref[c] = total
+        out_ref[...] = fold(next_ref)
         for l in range(per_dev):
             mine_ref[l] = next_ref[own_ref[0] * per_dev + l]
     else:
-        forward(dims, next_ref, lat_ref, foot_ref, ids_ref, sim_ref, out_ref)
-
-
-def finish_kernel(factor, sum_ref, *refs):
+        forward(dims, next_ref, lat_ref, foot_ref, ids_ref, out_ref)
+
+
+def finish_kernel(factor, sums, *refs):
+    sum_refs, refs = refs[:sums], refs[sums:]
     row_refs, refs = refs[:STEPS], refs[STEPS:]
     mine_ref, refs = refs[0], refs[1:]
     alphas, refs = refs[:STEPS], refs[STEPS:]
     norms, refs = refs[:STEPS - 1], refs[STEPS - 1:]
     out_ref, coef_ref = refs
-    total = tree_sum(sum_ref[c] for c in range(sum_ref.shape[0]))
-    norm = jnp.sqrt(jnp.sum(total, keepdims=True))
+    norm = jnp.sqrt(jnp.sum(added(sum_refs, ROWS), keepdims=True))
     for k in range(STEPS):
         out_ref[k] = row_refs[k][...] * factor
     out_ref[STEPS] = mine_ref[...] * (factor / norm)
@@ -333,6 +339,15 @@
     if not permuted(size):
         return [swap(jnp.broadcast_to(array[None], (size,) + array.shape), axis).reshape(-1, array.shape[1])]
     return [array] + [lax.ppermute(array, axis, [(d, d ^ s) for d in range(size)]) for s in range(1, size)]
+
+
+def addends(array, axis):
+    size = lax.axis_size(axis)
+    if size != 8:
+        return [swap(jnp.broadcast_to(array[None], (size,) + array.shape), axis).reshape(-1, array.shape[1])]
+    other = lax.ppermute(array, axis, [(d, d ^ 1) for d in range(size)])
+    both = call(add_kernel, jax.ShapeDtypeStruct(array.shape, F32), [VMEM] * 2, array, other)
+    return [both] + [lax.ppermute(both, axis, [(d, d ^ s) for d in range(size)]) for s in (2, 4, 6)]
 
 
 def swap(array, axis):
@@ -397,30 +412,30 @@
 
     field_shape = shape((periods, modes, lat_rows))
     small = shape((ROWS, 128))
-    sim_scratch = pltpu.VMEM((subs + ROWS, ob), F32)
     own_shape = shape((per_dev, modes, lat_rows))
     sims, field, foot, ids = call(
         functools.partial(first_kernel, dims, no),
         (
-            shape((nc, subs + ROWS, ob)),
+            shape((subs + ROWS, ob)),
             field_shape,
             jax.ShapeDtypeStruct((nc, foot_rows, ob), BF16),
             jax.ShapeDtypeStruct((nc, 128), jnp.int32),
         ),
         [SMEM] + [VMEM] * (2 + len(near)),
         own, lat, came, *near,
-        scratch=[sim_scratch, pltpu.SMEM((nc, 128), jnp.int32), pltpu.SemaphoreType.DMA],
+        scratch=[pltpu.SMEM((nc, 128), jnp.int32), pltpu.SemaphoreType.DMA],
     )
     ways = min(no, WAYS)
     rows, alphas, norms = [], [], []
     vector = None
     for step in range(STEPS):
         first, last = step == 0, step == STEPS - 1
+        parts = addends(sims, "cell")
         coefs, norm = call(
             functools.partial(adjoint_kernel, dims, first),
             (shape((mine + subs + (ROWS if first else 0), 128)), small),
-            [SMEM] + [VMEM] * 3,
-            ids, swap(sims, "cell"), weights, foot,
+            [SMEM] + [VMEM] * (2 + len(parts)),
+            ids, weights, foot, *parts,
             scratch=[pltpu.VMEM((subs, ob), F32)],
         )
         coefs = share(coefs, "obs")
@@ -435,7 +450,7 @@
         sims, row, field, *vector, alpha = call(
             functools.partial(image_kernel, dims, no, first, last),
             (
-                shape((nc, ROWS if last else subs + ROWS, 128)),
+                shape((ROWS if last else subs + ROWS, 128)),
                 own_shape,
                 own_shape if last else field_shape,
                 *([] if last else [field_shape]),
@@ -443,7 +458,7 @@
             ),
             [SMEM] * 3 + [VMEM] * (4 + len(before) + len(coefs)),
             own, ids, every, lat, foot, norm, field, *before, *coefs,
-            scratch=[pltpu.VMEM(field_shape.shape, F32) if last else sim_scratch]
+            scratch=[pltpu.VMEM(field_shape.shape, F32)] * last
             + [pltpu.VMEM((no, mine, 128), F32)]
             + [pltpu.VMEM(field_shape.shape, F32)] * ways
             + [pltpu.VMEM((CR * modes, CHUNK * 128), F32)] * ways,
@@ -454,11 +469,12 @@
         alphas.append(alpha)
         norms.append(norm)
     factor = math.sqrt(periods * lon_cols * lat_rows)
+    parts = addends(sims, "cell")
     krylov, coeffs = call(
-        functools.partial(finish_kernel, factor),
+        functools.partial(finish_kernel, factor, len(parts)),
         (shape((STEPS + 1, per_dev, modes, lat_rows)), shape((2, STEPS))),
-        [VMEM] * (1 + STEPS + 1 + STEPS + STEPS - 1),
-        swap(sims, "cell"), *rows, field, *alphas, *norms[1:],
+        [VMEM] * (len(parts) + STEPS + 1 + STEPS + STEPS - 1),
+        *parts, *rows, field, *alphas, *norms[1:],
     )
     return krylov[:, :, :held], coeffs
 

time: 80.2 us -> 79.7 us (level)
  blocking collectives: 30.9 us -> 0 us
  waiting for transfers between devices: 8.63 us -> 24.8 us
  starting transfers between devices: 23.1 us -> 37.4 us
    all_to_all x4 -> x0, blocking collectives: 30.9 us -> none  [swap(): return lax.all_to_all(array, axis, split_axis=0, concat_axis=0, tiled=True)]
    ppermute x0 -> x16, waiting for transfers between devices: none -> 16.2 us  [the longest x12 11.6 us: addends(): lax.ppermute(both, axis, [(d, d ^ s) for d in range(size)])]
    ppermute x0 -> x16, starting transfers between devices: none -> 14.2 us  [the longest x12 14 us: addends(): lax.ppermute(both, axis, [(d, d ^ s) for d in range(size)])]
    pallas_call x11 -> x15, Pallas kernels: 15.5 us -> 15.5 us  [call(): pl.pallas_call(kernel, out_shape=outs, in_specs=specs, out_specs=jax.tree...]
  transfers between devices with their start and end apart: 13 -> 29, of which waited for: 7 -> 25; matrix products, arithmetic and copies ran while one was open for 0% -> 0% of each run, Pallas kernels for 3% -> 3%
where the time goes in v9:
time: 79.7 us; the launch traced here: 79.3 us
  starting transfers between devices  37.4 us (47%)
  waiting for transfers between devices  24.8 us (31%)
  Pallas kernels  15.5 us (19%)
    ppermute x12, starting transfers between devices, share(): lax.ppermute(array, axis, [(d, d ^ s) for d in range(size)])  17.9 us
    pallas_call x15, Pallas kernels, call(): pl.pallas_call(kernel, out_shape=outs, in_specs=specs, out_specs=jax.tree...  15.5 us
    ppermute x12, starting transfers between devices, addends(): lax.ppermute(both, axis, [(d, d ^ s) for d in range(size)])  14 us
    ppermute x12, waiting for transfers between devices, addends(): lax.ppermute(both, axis, [(d, d ^ s) for d in range(size)])  11.6 us
    ppermute x12, waiting for transfers between devices, share(): lax.ppermute(array, axis, [(d, d ^ s) for d in range(size)])  8.6 us
    all_to_all x1, starting transfers between devices, swap(): return lax.all_to_all(array, axis, split_axis=0, concat_axis=0, tiled=True)  5.18 us
    ppermute x4, waiting for transfers between devices, addends(): other = lax.ppermute(array, axis, [(d, d ^ 1) for d in range(size)])  4.63 us
  transfers between devices with their start and end apart: 29, of which 25 were waited for; matrix products, arithmetic and copies ran while one was open for 0% of the time, Pallas kernels for 3%

profile of v9, /device:TPU:0, one launch (start us, length us, event | category | flops | bytes accessed | tf_op | source)
XLA Modules:
  0.0 79.3 jit_solution(16614740637720159105)
XLA Ops:
  0.6 2.6 %shard_map.104 = (bf16[8,208,128]{2,1,0:T(8,128)(2,1)}, f32[8,128]{1,0:T(8,128)}) custom-call(s32[1]{0:T(128)} %bitcast.2.cell_ref, bf16[384,384]{1,0:T(8,128)(2,1)} %constant.12.clone.high_any, bf16[384,384]{1,0:T(8,128)(2,1)} %constant.13.clone.low_any, bf16[2,128,768]{2,1,0:T(8,128)(2,1)} %foot_any.1, s32[2]{0:T(128)} %off_any.1, s32[2]{0:T(128)} %sub_any.1, ...), custom_call_target="tpu_custom_call" | custom-call | tf_op jit(solution)/shard_map/pallas_call | solution.py:41
  3.3 5.2 %all-to-all-start = ((bf16[8,208,128]{2,1,0:T(8,128)(2,1)}), bf16[8,208,128]{2,1,0:T(8,128)(2,1)}, u32[]{:S(2)}, u32[]{:S(2)}) async-start(bf16[8,208,128]{2,1,0:T(8,128)(2,1)} %get-tuple-element.36), calls=%async_computation | async-start | bytes 851968 | tf_op jit(solution)/shard_map/all_to_all | solution.py:354
  8.5 4.1 %collective-permute-start.2 = (f32[48,128]{1,0:T(8,128)}, f32[48,128]{1,0:T(8,128)S(1)}, u32[]{:S(2)}, u32[]{:S(2)}) collective-permute-start(f32[48,128]{1,0:T(8,128)} %bitcast.4), channel_id=1, source_target_pairs={{0,24},{8,16},{16,8},{24,0},{1,25},{9,17},{17,9},{25,1},{2,26},{10... | collective-permute-start | bytes 73736 | tf_op jit(solution)/shard_map/ppermute | solution.py:341
  13.2 0.8 copy-done.1
  13.9 2.3 %shard_map.105 = (f32[128,48,128]{2,1,0:T(8,128)S(1)}, f32[48,128]{1,0:T(8,128)S(1)}) custom-call(f32[48,128,128]{2,1,0:T(8,128)} %lat_any, f32[48,128]{1,0:T(8,128)S(1)} %bitcast.7), custom_call_target="tpu_custom_call" | custom-call | bytes 6340608 | tf_op jit(solution)/shard_map/pallas_call | solution.py:41
  16.3 1.2 %collective-permute-done.1.refs_2_ = f32[48,128]{1,0:T(8,128)S(1)} collective-permute-done((f32[48,128]{1,0:T(8,128)}, f32[48,128]{1,0:T(8,128)S(1)}, u32[]{:S(2)}, u32[]{:S(2)}) %collective-permute-start.1) | collective-permute-done | bytes 24608 | tf_op jit(solution)/shard_map/ppermute | solution.py:341
  17.5 1.9 %shard_map.106 = (f32[16,128]{1,0:T(8,128)S(1)}, f32[4,48,128]{2,1,0:T(8,128)S(1)}, bf16[8,192,128]{2,1,0:T(8,128)(2,1)S(1)}, s32[8,128]{1,0:T(8,128)S(1)}) custom-call(s32[1]{0:T(128)} %bitcast.own_ref, f32[128,48,128]{2,1,0:T(8,128)S(1)} %get-tuple-element.35.lat_ref, bf16[8,208,128]{2,1,0:T(8,128)(2,1)} %all-to-all-done.came_ref, ...), custom_call_target="tpu_custom_call" | custom-call | tf_op jit(solution)/shard_map/pallas_call | solution.py:41
  19.5 1.2 %collective-permute-done.3.other_ref = f32[16,128]{1,0:T(8,128)S(1)} collective-permute-done((f32[16,128]{1,0:T(8,128)S(1)}, f32[16,128]{1,0:T(8,128)S(1)}, u32[]{:S(2)}, u32[]{:S(2)}) %collective-permute-start.3) | collective-permute-done | bytes 8224 | tf_op jit(solution)/shard_map/ppermute | solution.py:348
  20.7 2.8 %collective-permute-start.6 = (f32[16,128]{1,0:T(8,128)S(1)}, f32[16,128]{1,0:T(8,128)S(1)}, u32[]{:S(2)}, u32[]{:S(2)}) collective-permute-start(f32[16,128]{1,0:T(8,128)S(1)} %shard_map.107.refs_0_), channel_id=1, source_target_pairs={{0,6},{1,7},{2,4},{3,5},{4,2},{5,3},{6,0},{7,1},{8,14},{9,15},{10,... | collective-permute-start | bytes 24584 | tf_op jit(solution)/shard_map/ppermute | solution.py:350
  24.1 1.1 %collective-permute-done.6.refs_3_ = f32[16,128]{1,0:T(8,128)S(1)} collective-permute-done((f32[16,128]{1,0:T(8,128)S(1)}, f32[16,128]{1,0:T(8,128)S(1)}, u32[]{:S(2)}, u32[]{:S(2)}) %collective-permute-start.6) | collective-permute-done | bytes 8224 | tf_op jit(solution)/shard_map/ppermute | solution.py:350
  25.2 1.9 %collective-permute-done.5.refs_2_ = f32[16,128]{1,0:T(8,128)S(1)} collective-permute-done((f32[16,128]{1,0:T(8,128)S(1)}, f32[16,128]{1,0:T(8,128)S(1)}, u32[]{:S(2)}, u32[]{:S(2)}) %collective-permute-start.5) | collective-permute-done | bytes 8224 | tf_op jit(solution)/shard_map/ppermute | solution.py:350
  27.6 0.9 %shard_map.108 = (f32[32,128]{1,0:T(8,128)S(1)}, f32[8,128]{1,0:T(8,128)S(1)}) custom-call(s32[8,128]{1,0:T(8,128)S(1)} %get-tuple-element.38.ids_ref, f32[8,128]{1,0:T(8,128)S(1)} %copy-done, bf16[8,192,128]{2,1,0:T(8,128)(2,1)S(1)} %get-tuple-element.39.foot_ref, f32[16,128]{1,0:T(8,128)S(1)} %shard_map.107.refs_0_, ...), custom_call_target="tpu_custom_call" | custom-call | tf_op jit(solution)/shard_map/pallas_call | solution.py:41
  28.5 2.6 %collective-permute-start.9 = (f32[32,128]{1,0:T(8,128)S(1)}, f32[32,128]{1,0:T(8,128)S(1)}, u32[]{:S(2)}, u32[]{:S(2)}) collective-permute-start(f32[32,128]{1,0:T(8,128)S(1)} %get-tuple-element.41.refs_0_), channel_id=1, source_target_pairs={{0,24},{8,16},{16,8},{24,0},{1,25},{9,17},{17,9},{25,1},{2,26},{10... | collective-permute-start | bytes 49160 | tf_op jit(solution)/shard_map/ppermute | solution.py:341
  31.2 1.8 %collective-permute-start.7 = (f32[32,128]{1,0:T(8,128)S(1)}, f32[32,128]{1,0:T(8,128)S(1)}, u32[]{:S(2)}, u32[]{:S(2)}) collective-permute-start(f32[32,128]{1,0:T(8,128)S(1)} %get-tuple-element.41.refs_0_), channel_id=1, source_target_pairs={{0,8},{8,0},{16,24},{24,16},{1,9},{9,1},{17,25},{25,17},{2,10},{10... | collective-permute-start | bytes 49160 | tf_op jit(solution)/shard_map/ppermute | solution.py:341
  33.0 1.1 %collective-permute-done.9.refs_3_ = f32[32,128]{1,0:T(8,128)S(1)} collective-permute-done((f32[32,128]{1,0:T(8,128)S(1)}, f32[32,128]{1,0:T(8,128)S(1)}, u32[]{:S(2)}, u32[]{:S(2)}) %collective-permute-start.9) | collective-permute-done | bytes 16416 | tf_op jit(solution)/shard_map/ppermute | solution.py:341
  34.1 1.7 %collective-permute-done.8.refs_2_ = f32[32,128]{1,0:T(8,128)S(1)} collective-permute-done((f32[32,128]{1,0:T(8,128)S(1)}, f32[32,128]{1,0:T(8,128)S(1)}, u32[]{:S(2)}, u32[]{:S(2)}) %collective-permute-start.8) | collective-permute-done | bytes 16416 | tf_op jit(solution)/shard_map/ppermute | solution.py:341
  35.8 1.8 %shard_map.110 = (f32[16,128]{1,0:T(8,128)S(1)}, f32[1,48,128]{2,1,0:T(8,128)S(1)}, f32[4,48,128]{2,1,0:T(8,128)S(1)}, f32[4,48,128]{2,1,0:T(8,128)S(1)}, f32[8,128]{1,0:T(8,128)S(1)}) custom-call(s32[1]{0:T(128)} %bitcast.own_ref, s32[8,128]{1,0:T(8,128)S(1)} %get-tuple-element.38.ids_ref, s32[8,128]{1,0:T(8,128)S(1)} %shard_map.109.all_ref, ...), custom_call_target="tpu_custom_call" | custom-call | tf_op jit(solution)/shard_map/pallas_call | solution.py:41
  37.7 1.2 %collective-permute-done.10.other_ref = f32[16,128]{1,0:T(8,128)S(1)} collective-permute-done((f32[16,128]{1,0:T(8,128)S(1)}, f32[16,128]{1,0:T(8,128)S(1)}, u32[]{:S(2)}, u32[]{:S(2)}) %collective-permute-start.10) | collective-permute-done | bytes 8224 | tf_op jit(solution)/shard_map/ppermute | solution.py:348
  38.8 1.5 %collective-permute-start.13 = (f32[16,128]{1,0:T(8,128)S(1)}, f32[16,128]{1,0:T(8,128)S(1)}, u32[]{:S(2)}, u32[]{:S(2)}) collective-permute-start(f32[16,128]{1,0:T(8,128)S(1)} %shard_map.111.refs_0_), channel_id=1, source_target_pairs={{0,6},{1,7},{2,4},{3,5},{4,2},{5,3},{6,0},{7,1},{8,14},{9,15},{10,... | collective-permute-start | bytes 24584 | tf_op jit(solution)/shard_map/ppermute | solution.py:350
  40.3 1.3 %collective-permute-start.12 = (f32[16,128]{1,0:T(8,128)S(1)}, f32[16,128]{1,0:T(8,128)S(1)}, u32[]{:S(2)}, u32[]{:S(2)}) collective-permute-start(f32[16,128]{1,0:T(8,128)S(1)} %shard_map.111.refs_0_), channel_id=1, source_target_pairs={{0,4},{1,5},{2,6},{3,7},{4,0},{5,1},{6,2},{7,3},{8,12},{9,13},{10,... | collective-permute-start | bytes 24584 | tf_op jit(solution)/shard_map/ppermute | solution.py:350
  41.6 0.7 collective-permute-start.11
  42.3 1.1 %collective-permute-done.13.refs_3_ = f32[16,128]{1,0:T(8,128)S(1)} collective-permute-done((f32[16,128]{1,0:T(8,128)S(1)}, f32[16,128]{1,0:T(8,128)S(1)}, u32[]{:S(2)}, u32[]{:S(2)}) %collective-permute-start.13) | collective-permute-done | bytes 8224 | tf_op jit(solution)/shard_map/ppermute | solution.py:350
  44.0 1.3 %collective-permute-done.11.refs_1_ = f32[16,128]{1,0:T(8,128)S(1)} collective-permute-done((f32[16,128]{1,0:T(8,128)S(1)}, f32[16,128]{1,0:T(8,128)S(1)}, u32[]{:S(2)}, u32[]{:S(2)}) %collective-permute-start.11) | collective-permute-done | bytes 8224 | tf_op jit(solution)/shard_map/ppermute | solution.py:350
  45.2 0.9 %shard_map.112 = (f32[24,128]{1,0:T(8,128)S(1)}, f32[8,128]{1,0:T(8,128)S(1)}) custom-call(s32[8,128]{1,0:T(8,128)S(1)} %get-tuple-element.38.ids_ref, f32[8,128]{1,0:T(8,128)S(1)} %copy-done, bf16[8,192,128]{2,1,0:T(8,128)(2,1)S(1)} %get-tuple-element.39.foot_ref, f32[16,128]{1,0:T(8,128)S(1)} %shard_map.111.refs_0_, ...), custom_call_target="tpu_custom_call" | custom-call | tf_op jit(solution)/shard_map/pallas_call | solution.py:41
  46.2 1.5 %collective-permute-start.16 = (f32[24,128]{1,0:T(8,128)S(1)}, f32[24,128]{1,0:T(8,128)S(1)}, u32[]{:S(2)}, u32[]{:S(2)}) collective-permute-start(f32[24,128]{1,0:T(8,128)S(1)} %get-tuple-element.48.refs_1_), channel_id=1, source_target_pairs={{0,24},{8,16},{16,8},{24,0},{1,25},{9,17},{17,9},{25,1},{2,26},{10... | collective-permute-start | bytes 36872 | tf_op jit(solution)/shard_map/ppermute | solution.py:341
  47.7 0.6 collective-permute-start.15
  48.3 2.3 %collective-permute-start.14 = (f32[24,128]{1,0:T(8,128)S(1)}, f32[24,128]{1,0:T(8,128)S(1)}, u32[]{:S(2)}, u32[]{:S(2)}) collective-permute-start(f32[24,128]{1,0:T(8,128)S(1)} %get-tuple-element.48.refs_1_), channel_id=1, source_target_pairs={{0,8},{8,0},{16,24},{24,16},{1,9},{9,1},{17,25},{25,17},{2,10},{10... | collective-permute-start | bytes 36872 | tf_op jit(solution)/shard_map/ppermute | solution.py:341
  50.6 1.1 %collective-permute-done.16.refs_4_ = f32[24,128]{1,0:T(8,128)S(1)} collective-permute-done((f32[24,128]{1,0:T(8,128)S(1)}, f32[24,128]{1,0:T(8,128)S(1)}, u32[]{:S(2)}, u32[]{:S(2)}) %collective-permute-start.16) | collective-permute-done | bytes 12320 | tf_op jit(solution)/shard_map/ppermute | solution.py:341
  52.4 1.8 %shard_map.113 = (f32[16,128]{1,0:T(8,128)S(1)}, f32[1,48,128]{2,1,0:T(8,128)S(1)}, f32[4,48,128]{2,1,0:T(8,128)S(1)}, f32[4,48,128]{2,1,0:T(8,128)S(1)}, f32[8,128]{1,0:T(8,128)S(1)}) custom-call(s32[1]{0:T(128)} %bitcast.own_ref, s32[8,128]{1,0:T(8,128)S(1)} %get-tuple-element.38.ids_ref, s32[8,128]{1,0:T(8,128)S(1)} %shard_map.109.all_ref, ...), custom_call_target="tpu_custom_call" | custom-call | tf_op jit(solution)/shard_map/pallas_call | solution.py:41
  54.2 1.2 %collective-permute-done.17.other_ref = f32[16,128]{1,0:T(8,128)S(1)} collective-permute-done((f32[16,128]{1,0:T(8,128)S(1)}, f32[16,128]{1,0:T(8,128)S(1)}, u32[]{:S(2)}, u32[]{:S(2)}) %collective-permute-start.17) | collective-permute-done | bytes 8224 | tf_op jit(solution)/shard_map/ppermute | solution.py:348
  55.4 1.7 %collective-permute-start.20 = (f32[16,128]{1,0:T(8,128)S(1)}, f32[16,128]{1,0:T(8,128)S(1)}, u32[]{:S(2)}, u32[]{:S(2)}) collective-permute-start(f32[16,128]{1,0:T(8,128)S(1)} %shard_map.114.refs_0_), channel_id=1, source_target_pairs={{0,6},{1,7},{2,4},{3,5},{4,2},{5,3},{6,0},{7,1},{8,14},{9,15},{10,... | collective-permute-start | bytes 24584 | tf_op jit(solution)/shard_map/ppermute | solution.py:350
  57.6 1.3 %collective-permute-start.18 = (f32[16,128]{1,0:T(8,128)S(1)}, f32[16,128]{1,0:T(8,128)S(1)}, u32[]{:S(2)}, u32[]{:S(2)}) collective-permute-start(f32[16,128]{1,0:T(8,128)S(1)} %shard_map.114.refs_0_), channel_id=1, source_target_pairs={{0,2},{1,3},{2,0},{3,1},{4,6},{5,7},{6,4},{7,5},{8,10},{9,11},{10,... | collective-permute-start | bytes 24584 | tf_op jit(solution)/shard_map/ppermute | solution.py:350
  58.9 1.1 %collective-permute-done.20.refs_3_ = f32[16,128]{1,0:T(8,128)S(1)} collective-permute-done((f32[16,128]{1,0:T(8,128)S(1)}, f32[16,128]{1,0:T(8,128)S(1)}, u32[]{:S(2)}, u32[]{:S(2)}) %collective-permute-start.20) | collective-permute-done | bytes 8224 | tf_op jit(solution)/shard_map/ppermute | solution.py:350
  60.0 0.8 collective-permute-done.19.refs_2_
  61.3 0.9 %shard_map.115 = (f32[24,128]{1,0:T(8,128)S(1)}, f32[8,128]{1,0:T(8,128)S(1)}) custom-call(s32[8,128]{1,0:T(8,128)S(1)} %get-tuple-element.38.ids_ref, f32[8,128]{1,0:T(8,128)S(1)} %copy-done, bf16[8,192,128]{2,1,0:T(8,128)(2,1)S(1)} %get-tuple-element.39.foot_ref, f32[16,128]{1,0:T(8,128)S(1)} %shard_map.114.refs_0_, ...), custom_call_target="tpu_custom_call" | custom-call | tf_op jit(solution)/shard_map/pallas_call | solution.py:41
  62.2 2.5 %collective-permute-start.23 = (f32[24,128]{1,0:T(8,128)S(1)}, f32[24,128]{1,0:T(8,128)S(1)}, u32[]{:S(2)}, u32[]{:S(2)}) collective-permute-start(f32[24,128]{1,0:T(8,128)S(1)} %get-tuple-element.53.refs_1_), channel_id=1, source_target_pairs={{0,24},{8,16},{16,8},{24,0},{1,25},{9,17},{17,9},{25,1},{2,26},{10... | collective-permute-start | bytes 36872 | tf_op jit(solution)/shard_map/ppermute | solution.py:341
  64.7 0.9 %collective-permute-start.22 = (f32[24,128]{1,0:T(8,128)S(1)}, f32[24,128]{1,0:T(8,128)S(1)}, u32[]{:S(2)}, u32[]{:S(2)}) collective-permute-start(f32[24,128]{1,0:T(8,128)S(1)} %get-tuple-element.53.refs_1_), channel_id=1, source_target_pairs={{0,16},{8,24},{16,0},{24,8},{1,17},{9,25},{17,1},{25,9},{2,18},{10... | collective-permute-start | bytes 36872 | tf_op jit(solution)/shard_map/ppermute | solution.py:341
  65.6 1.0 %collective-permute-start.21 = (f32[24,128]{1,0:T(8,128)S(1)}, f32[24,128]{1,0:T(8,128)S(1)}, u32[]{:S(2)}, u32[]{:S(2)}) collective-permute-start(f32[24,128]{1,0:T(8,128)S(1)} %get-tuple-element.53.refs_1_), channel_id=1, source_target_pairs={{0,8},{8,0},{16,24},{24,16},{1,9},{9,1},{17,25},{25,17},{2,10},{10... | collective-permute-start | bytes 36872 | tf_op jit(solution)/shard_map/ppermute | solution.py:341
  66.6 1.1 %collective-permute-done.23.refs_4_ = f32[24,128]{1,0:T(8,128)S(1)} collective-permute-done((f32[24,128]{1,0:T(8,128)S(1)}, f32[24,128]{1,0:T(8,128)S(1)}, u32[]{:S(2)}, u32[]{:S(2)}) %collective-permute-start.23) | collective-permute-done | bytes 12320 | tf_op jit(solution)/shard_map/ppermute | solution.py:341
  67.7 1.6 %collective-permute-done.22.refs_3_ = f32[24,128]{1,0:T(8,128)S(1)} collective-permute-done((f32[24,128]{1,0:T(8,128)S(1)}, f32[24,128]{1,0:T(8,128)S(1)}, u32[]{:S(2)}, u32[]{:S(2)}) %collective-permute-start.22) | collective-permute-done | bytes 12320 | tf_op jit(solution)/shard_map/ppermute | solution.py:341
  69.4 1.5 %shard_map.116 = (f32[8,128]{1,0:T(8,128)S(1)}, f32[1,48,128]{2,1,0:T(8,128)S(1)}, f32[1,48,128]{2,1,0:T(8,128)S(1)}, f32[8,128]{1,0:T(8,128)S(1)}) custom-call(s32[1]{0:T(128)} %bitcast.own_ref, s32[8,128]{1,0:T(8,128)S(1)} %get-tuple-element.38.ids_ref, s32[8,128]{1,0:T(8,128)S(1)} %shard_map.109.all_ref, f32[128,48,128]{2,1,0:T(8,128)S(1)} %get-tuple-element.35.lat_ref, ...), custom_call_target="tpu_custom_call" | custom-call | tf_op jit(solution)/shard_map/pallas_call | solution.py:41
  71.0 1.2 %collective-permute-done.24.other_ref = f32[8,128]{1,0:T(8,128)S(1)} collective-permute-done((f32[8,128]{1,0:T(8,128)S(1)}, f32[8,128]{1,0:T(8,128)S(1)}, u32[]{:S(2)}, u32[]{:S(2)}) %collective-permute-start.24) | collective-permute-done | bytes 4128 | tf_op jit(solution)/shard_map/ppermute | solution.py:348
  72.1 1.5 %collective-permute-start.27 = (f32[8,128]{1,0:T(8,128)S(1)}, f32[8,128]{1,0:T(8,128)S(1)}, u32[]{:S(2)}, u32[]{:S(2)}) collective-permute-start(f32[8,128]{1,0:T(8,128)S(1)} %shard_map.117.refs_0_), channel_id=1, source_target_pairs={{0,6},{1,7},{2,4},{3,5},{4,2},{5,3},{6,0},{7,1},{8,14},{9,15},{10,... | collective-permute-start | bytes 12296 | tf_op jit(solution)/shard_map/ppermute | solution.py:350
  73.6 1.3 %collective-permute-start.26 = (f32[8,128]{1,0:T(8,128)S(1)}, f32[8,128]{1,0:T(8,128)S(1)}, u32[]{:S(2)}, u32[]{:S(2)}) collective-permute-start(f32[8,128]{1,0:T(8,128)S(1)} %shard_map.117.refs_0_), channel_id=1, source_target_pairs={{0,4},{1,5},{2,6},{3,7},{4,0},{5,1},{6,2},{7,3},{8,12},{9,13},{10,... | collective-permute-start | bytes 12296 | tf_op jit(solution)/shard_map/ppermute | solution.py:350
  74.9 0.7 collective-permute-start.25
  75.6 1.0 %collective-permute-done.27.refs_3_ = f32[8,128]{1,0:T(8,128)S(1)} collective-permute-done((f32[8,128]{1,0:T(8,128)S(1)}, f32[8,128]{1,0:T(8,128)S(1)}, u32[]{:S(2)}, u32[]{:S(2)}) %collective-permute-start.27) | collective-permute-done | bytes 4128 | tf_op jit(solution)/shard_map/ppermute | solution.py:350
  77.2 1.3 %collective-permute-done.25.refs_1_ = f32[8,128]{1,0:T(8,128)S(1)} collective-permute-done((f32[8,128]{1,0:T(8,128)S(1)}, f32[8,128]{1,0:T(8,128)S(1)}, u32[]{:S(2)}, u32[]{:S(2)}) %collective-permute-start.25) | collective-permute-done | bytes 4128 | tf_op jit(solution)/shard_map/ppermute | solution.py:350
  78.5 0.8 shard_map.118
  (29 shorter events, 5.3 us)
Async XLA Ops:
  3.3 14.2 %all-to-all-start = ((bf16[8,208,128]{2,1,0:T(8,128)(2,1)}), bf16[8,208,128]{2,1,0:T(8,128)(2,1)}, u32[]{:S(2)}, u32[]{:S(2)}) async-start(bf16[8,208,128]{2,1,0:T(8,128)(2,1)} %get-tuple-element.36), calls=%async_computation | async-start | bytes 851968 | tf_op jit(solution)/shard_map/all_to_all | solution.py:354
  8.5 7.8 %collective-permute-start.2 = (f32[48,128]{1,0:T(8,128)}, f32[48,128]{1,0:T(8,128)S(1)}, u32[]{:S(2)}, u32[]{:S(2)}) collective-permute-start(f32[48,128]{1,0:T(8,128)} %bitcast.4), channel_id=1, source_target_pairs={{0,24},{8,16},{16,8},{24,0},{1,25},{9,17},{17,9},{25,1},{2,26},{10... | collective-permute-start | bytes 73736 | tf_op jit(solution)/shard_map/ppermute | solution.py:341
  12.5 4.9 %collective-permute-start.1 = (f32[48,128]{1,0:T(8,128)}, f32[48,128]{1,0:T(8,128)S(1)}, u32[]{:S(2)}, u32[]{:S(2)}) collective-permute-start(f32[48,128]{1,0:T(8,128)} %bitcast.5), channel_id=1, source_target_pairs={{0,16},{8,24},{16,0},{24,8},{1,17},{9,25},{17,1},{25,9},{2,18},{10... | collective-permute-start | bytes 73736 | tf_op jit(solution)/shard_map/ppermute | solution.py:341
  12.5 4.9 %collective-permute-start = (f32[48,128]{1,0:T(8,128)}, f32[48,128]{1,0:T(8,128)S(1)}, u32[]{:S(2)}, u32[]{:S(2)}) collective-permute-start(f32[48,128]{1,0:T(8,128)} %bitcast.6), channel_id=1, source_target_pairs={{0,8},{8,0},{16,24},{24,16},{1,9},{9,1},{17,25},{25,17},{2,10},{10... | collective-permute-start | bytes 73736 | tf_op jit(solution)/shard_map/ppermute | solution.py:341
  13.2 0.8 copy-start.1
  13.9 13.7 %copy-start = (f32[8,128]{1,0:T(8,128)S(1)}, f32[8,128]{1,0:T(8,128)}, u32[]{:S(2)}) copy-start(f32[8,128]{1,0:T(8,128)} %get-tuple-element.32.weight_ref) | copy-start | bytes 12292
  19.4 1.2 %collective-permute-start.3 = (f32[16,128]{1,0:T(8,128)S(1)}, f32[16,128]{1,0:T(8,128)S(1)}, u32[]{:S(2)}, u32[]{:S(2)}) collective-permute-start(f32[16,128]{1,0:T(8,128)S(1)} %get-tuple-element.40.one_ref), channel_id=1, source_target_pairs={{0,1},{1,0},{2,3},{3,2},{4,5},{5,4},{6,7},{7,6},{8,9},{9,8},{10,11... | collective-permute-start | bytes 24584 | tf_op jit(solution)/shard_map/ppermute | solution.py:348
  20.7 4.5 %collective-permute-start.6 = (f32[16,128]{1,0:T(8,128)S(1)}, f32[16,128]{1,0:T(8,128)S(1)}, u32[]{:S(2)}, u32[]{:S(2)}) collective-permute-start(f32[16,128]{1,0:T(8,128)S(1)} %shard_map.107.refs_0_), channel_id=1, source_target_pairs={{0,6},{1,7},{2,4},{3,5},{4,2},{5,3},{6,0},{7,1},{8,14},{9,15},{10,... | collective-permute-start | bytes 24584 | tf_op jit(solution)/shard_map/ppermute | solution.py:350
  23.4 3.7 %collective-permute-start.5 = (f32[16,128]{1,0:T(8,128)S(1)}, f32[16,128]{1,0:T(8,128)S(1)}, u32[]{:S(2)}, u32[]{:S(2)}) collective-permute-start(f32[16,128]{1,0:T(8,128)S(1)} %shard_map.107.refs_0_), channel_id=1, source_target_pairs={{0,4},{1,5},{2,6},{3,7},{4,0},{5,1},{6,2},{7,3},{8,12},{9,13},{10,... | collective-permute-start | bytes 24584 | tf_op jit(solution)/shard_map/ppermute | solution.py:350
  24.0 3.7 %collective-permute-start.4 = (f32[16,128]{1,0:T(8,128)S(1)}, f32[16,128]{1,0:T(8,128)S(1)}, u32[]{:S(2)}, u32[]{:S(2)}) collective-permute-start(f32[16,128]{1,0:T(8,128)S(1)} %shard_map.107.refs_0_), channel_id=1, source_target_pairs={{0,2},{1,3},{2,0},{3,1},{4,6},{5,7},{6,4},{7,5},{8,10},{9,11},{10,... | collective-permute-start | bytes 24584 | tf_op jit(solution)/shard_map/ppermute | solution.py:350
  28.5 5.6 %collective-permute-start.9 = (f32[32,128]{1,0:T(8,128)S(1)}, f32[32,128]{1,0:T(8,128)S(1)}, u32[]{:S(2)}, u32[]{:S(2)}) collective-permute-start(f32[32,128]{1,0:T(8,128)S(1)} %get-tuple-element.41.refs_0_), channel_id=1, source_target_pairs={{0,24},{8,16},{16,8},{24,0},{1,25},{9,17},{17,9},{25,1},{2,26},{10... | collective-permute-start | bytes 49160 | tf_op jit(solution)/shard_map/ppermute | solution.py:341
  31.2 4.6 %collective-permute-start.8 = (f32[32,128]{1,0:T(8,128)S(1)}, f32[32,128]{1,0:T(8,128)S(1)}, u32[]{:S(2)}, u32[]{:S(2)}) collective-permute-start(f32[32,128]{1,0:T(8,128)S(1)} %get-tuple-element.41.refs_0_), channel_id=1, source_target_pairs={{0,16},{8,24},{16,0},{24,8},{1,17},{9,25},{17,1},{25,9},{2,18},{10... | collective-permute-start | bytes 49160 | tf_op jit(solution)/shard_map/ppermute | solution.py:341
  31.2 4.6 %collective-permute-start.7 = (f32[32,128]{1,0:T(8,128)S(1)}, f32[32,128]{1,0:T(8,128)S(1)}, u32[]{:S(2)}, u32[]{:S(2)}) collective-permute-start(f32[32,128]{1,0:T(8,128)S(1)} %get-tuple-element.41.refs_0_), channel_id=1, source_target_pairs={{0,8},{8,0},{16,24},{24,16},{1,9},{9,1},{17,25},{25,17},{2,10},{10... | collective-permute-start | bytes 49160 | tf_op jit(solution)/shard_map/ppermute | solution.py:341
  37.6 1.2 %collective-permute-start.10 = (f32[16,128]{1,0:T(8,128)S(1)}, f32[16,128]{1,0:T(8,128)S(1)}, u32[]{:S(2)}, u32[]{:S(2)}) collective-permute-start(f32[16,128]{1,0:T(8,128)S(1)} %get-tuple-element.44.one_ref), channel_id=1, source_target_pairs={{0,1},{1,0},{2,3},{3,2},{4,5},{5,4},{6,7},{7,6},{8,9},{9,8},{10,11... | collective-permute-start | bytes 24584 | tf_op jit(solution)/shard_map/ppermute | solution.py:348
  38.8 4.5 %collective-permute-start.13 = (f32[16,128]{1,0:T(8,128)S(1)}, f32[16,128]{1,0:T(8,128)S(1)}, u32[]{:S(2)}, u32[]{:S(2)}) collective-permute-start(f32[16,128]{1,0:T(8,128)S(1)} %shard_map.111.refs_0_), channel_id=1, source_target_pairs={{0,6},{1,7},{2,4},{3,5},{4,2},{5,3},{6,0},{7,1},{8,14},{9,15},{10,... | collective-permute-start | bytes 24584 | tf_op jit(solution)/shard_map/ppermute | solution.py:350
  40.3 3.7 %collective-permute-start.12 = (f32[16,128]{1,0:T(8,128)S(1)}, f32[16,128]{1,0:T(8,128)S(1)}, u32[]{:S(2)}, u32[]{:S(2)}) collective-permute-start(f32[16,128]{1,0:T(8,128)S(1)} %shard_map.111.refs_0_), channel_id=1, source_target_pairs={{0,4},{1,5},{2,6},{3,7},{4,0},{5,1},{6,2},{7,3},{8,12},{9,13},{10,... | collective-permute-start | bytes 24584 | tf_op jit(solution)/shard_map/ppermute | solution.py:350
  41.6 3.7 %collective-permute-start.11 = (f32[16,128]{1,0:T(8,128)S(1)}, f32[16,128]{1,0:T(8,128)S(1)}, u32[]{:S(2)}, u32[]{:S(2)}) collective-permute-start(f32[16,128]{1,0:T(8,128)S(1)} %shard_map.111.refs_0_), channel_id=1, source_target_pairs={{0,2},{1,3},{2,0},{3,1},{4,6},{5,7},{6,4},{7,5},{8,10},{9,11},{10,... | collective-permute-start | bytes 24584 | tf_op jit(solution)/shard_map/ppermute | solution.py:350
  46.2 5.5 %collective-permute-start.16 = (f32[24,128]{1,0:T(8,128)S(1)}, f32[24,128]{1,0:T(8,128)S(1)}, u32[]{:S(2)}, u32[]{:S(2)}) collective-permute-start(f32[24,128]{1,0:T(8,128)S(1)} %get-tuple-element.48.refs_1_), channel_id=1, source_target_pairs={{0,24},{8,16},{16,8},{24,0},{1,25},{9,17},{17,9},{25,1},{2,26},{10... | collective-permute-start | bytes 36872 | tf_op jit(solution)/shard_map/ppermute | solution.py:341
  47.7 4.6 %collective-permute-start.15 = (f32[24,128]{1,0:T(8,128)S(1)}, f32[24,128]{1,0:T(8,128)S(1)}, u32[]{:S(2)}, u32[]{:S(2)}) collective-permute-start(f32[24,128]{1,0:T(8,128)S(1)} %get-tuple-element.48.refs_1_), channel_id=1, source_target_pairs={{0,16},{8,24},{16,0},{24,8},{1,17},{9,25},{17,1},{25,9},{2,18},{10... | collective-permute-start | bytes 36872 | tf_op jit(solution)/shard_map/ppermute | solution.py:341
  48.3 4.1 %collective-permute-start.14 = (f32[24,128]{1,0:T(8,128)S(1)}, f32[24,128]{1,0:T(8,128)S(1)}, u32[]{:S(2)}, u32[]{:S(2)}) collective-permute-start(f32[24,128]{1,0:T(8,128)S(1)} %get-tuple-element.48.refs_1_), channel_id=1, source_target_pairs={{0,8},{8,0},{16,24},{24,16},{1,9},{9,1},{17,25},{25,17},{2,10},{10... | collective-permute-start | bytes 36872 | tf_op jit(solution)/shard_map/ppermute | solution.py:341
  54.2 1.2 %collective-permute-start.17 = (f32[16,128]{1,0:T(8,128)S(1)}, f32[16,128]{1,0:T(8,128)S(1)}, u32[]{:S(2)}, u32[]{:S(2)}) collective-permute-start(f32[16,128]{1,0:T(8,128)S(1)} %get-tuple-element.49.one_ref), channel_id=1, source_target_pairs={{0,1},{1,0},{2,3},{3,2},{4,5},{5,4},{6,7},{7,6},{8,9},{9,8},{10,11... | collective-permute-start | bytes 24584 | tf_op jit(solution)/shard_map/ppermute | solution.py:348
  55.4 4.5 %collective-permute-start.20 = (f32[16,128]{1,0:T(8,128)S(1)}, f32[16,128]{1,0:T(8,128)S(1)}, u32[]{:S(2)}, u32[]{:S(2)}) collective-permute-start(f32[16,128]{1,0:T(8,128)S(1)} %shard_map.114.refs_0_), channel_id=1, source_target_pairs={{0,6},{1,7},{2,4},{3,5},{4,2},{5,3},{6,0},{7,1},{8,14},{9,15},{10,... | collective-permute-start | bytes 24584 | tf_op jit(solution)/shard_map/ppermute | solution.py:350
  57.1 3.7 %collective-permute-start.19 = (f32[16,128]{1,0:T(8,128)S(1)}, f32[16,128]{1,0:T(8,128)S(1)}, u32[]{:S(2)}, u32[]{:S(2)}) collective-permute-start(f32[16,128]{1,0:T(8,128)S(1)} %shard_map.114.refs_0_), channel_id=1, source_target_pairs={{0,4},{1,5},{2,6},{3,7},{4,0},{5,1},{6,2},{7,3},{8,12},{9,13},{10,... | collective-permute-start | bytes 24584 | tf_op jit(solution)/shard_map/ppermute | solution.py:350
  57.6 3.7 %collective-permute-start.18 = (f32[16,128]{1,0:T(8,128)S(1)}, f32[16,128]{1,0:T(8,128)S(1)}, u32[]{:S(2)}, u32[]{:S(2)}) collective-permute-start(f32[16,128]{1,0:T(8,128)S(1)} %shard_map.114.refs_0_), channel_id=1, source_target_pairs={{0,2},{1,3},{2,0},{3,1},{4,6},{5,7},{6,4},{7,5},{8,10},{9,11},{10,... | collective-permute-start | bytes 24584 | tf_op jit(solution)/shard_map/ppermute | solution.py:350
  62.2 5.5 %collective-permute-start.23 = (f32[24,128]{1,0:T(8,128)S(1)}, f32[24,128]{1,0:T(8,128)S(1)}, u32[]{:S(2)}, u32[]{:S(2)}) collective-permute-start(f32[24,128]{1,0:T(8,128)S(1)} %get-tuple-element.53.refs_1_), channel_id=1, source_target_pairs={{0,24},{8,16},{16,8},{24,0},{1,25},{9,17},{17,9},{25,1},{2,26},{10... | collective-permute-start | bytes 36872 | tf_op jit(solution)/shard_map/ppermute | solution.py:341
  64.7 4.6 %collective-permute-start.22 = (f32[24,128]{1,0:T(8,128)S(1)}, f32[24,128]{1,0:T(8,128)S(1)}, u32[]{:S(2)}, u32[]{:S(2)}) collective-permute-start(f32[24,128]{1,0:T(8,128)S(1)} %get-tuple-element.53.refs_1_), channel_id=1, source_target_pairs={{0,16},{8,24},{16,0},{24,8},{1,17},{9,25},{17,1},{25,9},{2,18},{10... | collective-permute-start | bytes 36872 | tf_op jit(solution)/shard_map/ppermute | solution.py:341
  65.6 3.8 %collective-permute-start.21 = (f32[24,128]{1,0:T(8,128)S(1)}, f32[24,128]{1,0:T(8,128)S(1)}, u32[]{:S(2)}, u32[]{:S(2)}) collective-permute-start(f32[24,128]{1,0:T(8,128)S(1)} %get-tuple-element.53.refs_1_), channel_id=1, source_target_pairs={{0,8},{8,0},{16,24},{24,16},{1,9},{9,1},{17,25},{25,17},{2,10},{10... | collective-permute-start | bytes 36872 | tf_op jit(solution)/shard_map/ppermute | solution.py:341
  70.9 1.2 %collective-permute-start.24 = (f32[8,128]{1,0:T(8,128)S(1)}, f32[8,128]{1,0:T(8,128)S(1)}, u32[]{:S(2)}, u32[]{:S(2)}) collective-permute-start(f32[8,128]{1,0:T(8,128)S(1)} %get-tuple-element.54.one_ref), channel_id=1, source_target_pairs={{0,1},{1,0},{2,3},{3,2},{4,5},{5,4},{6,7},{7,6},{8,9},{9,8},{10,11... | collective-permute-start | bytes 12296 | tf_op jit(solution)/shard_map/ppermute | solution.py:348
  72.1 4.5 %collective-permute-start.27 = (f32[8,128]{1,0:T(8,128)S(1)}, f32[8,128]{1,0:T(8,128)S(1)}, u32[]{:S(2)}, u32[]{:S(2)}) collective-permute-start(f32[8,128]{1,0:T(8,128)S(1)} %shard_map.117.refs_0_), channel_id=1, source_target_pairs={{0,6},{1,7},{2,4},{3,5},{4,2},{5,3},{6,0},{7,1},{8,14},{9,15},{10,... | collective-permute-start | bytes 12296 | tf_op jit(solution)/shard_map/ppermute | solution.py:350
  73.6 3.6 %collective-permute-start.26 = (f32[8,128]{1,0:T(8,128)S(1)}, f32[8,128]{1,0:T(8,128)S(1)}, u32[]{:S(2)}, u32[]{:S(2)}) collective-permute-start(f32[8,128]{1,0:T(8,128)S(1)} %shard_map.117.refs_0_), channel_id=1, source_target_pairs={{0,4},{1,5},{2,6},{3,7},{4,0},{5,1},{6,2},{7,3},{8,12},{9,13},{10,... | collective-permute-start | bytes 12296 | tf_op jit(solution)/shard_map/ppermute | solution.py:350
  74.9 3.6 %collective-permute-start.25 = (f32[8,128]{1,0:T(8,128)S(1)}, f32[8,128]{1,0:T(8,128)S(1)}, u32[]{:S(2)}, u32[]{:S(2)}) collective-permute-start(f32[8,128]{1,0:T(8,128)S(1)} %shard_map.117.refs_0_), channel_id=1, source_target_pairs={{0,2},{1,3},{2,0},{3,1},{4,6},{5,7},{6,4},{7,5},{8,10},{9,11},{10,... | collective-permute-start | bytes 12296 | tf_op jit(solution)/shard_map/ppermute | solution.py:350

commit v10 on v9

--- a/solution.py
+++ b/solution.py
@@ -11,7 +11,7 @@
 from jax.sharding import PartitionSpec as P
 
 CR = 2
-WAYS = 4
+WAYS = 2
 CHUNK = 16
 TERMS = 3
 STEPS = 3
@@ -107,12 +107,15 @@
     weight_ref[...] = jnp.where(lane < limit, rinv_ref[...], 0.0)
 
 
-def fetch_kernel(lat_any, start_any, lat_ref, start_ref, sems):
+def fetch_kernel(lat_any, start_any, lat_ref, start_ref, pick_ref, sems):
     modes = lat_any.shape[0]
     copies = [pltpu.make_async_copy(lat_any.at[m], lat_ref.at[:, m, :], sems.at[m]) for m in range(modes)]
     copies.append(pltpu.make_async_copy(start_any, start_ref, sems.at[modes]))
     for copy in copies:
         copy.start()
+    line = lax.broadcasted_iota(jnp.int32, pick_ref.shape, 0)
+    lane = lax.broadcasted_iota(jnp.int32, pick_ref.shape, 1)
+    pick_ref[...] = jnp.where(line % CHUNK == lane // 128, 1.0, 0.0).astype(BF16)
     for copy in copies:
         copy.wait()
 
@@ -164,8 +167,8 @@
 
 def first_kernel(dims, no, own_ref, lat_ref, came_ref, *refs):
     nc, nb, modes, _, _ = dims
-    near_refs, refs = refs[:-6], refs[-6:]
-    out_ref, field_ref, foot_ref, all_ref, ids_ref, sem = refs
+    near_refs, refs = refs[:-8], refs[-8:]
+    out_ref, field_ref, foot_ref, all_ref, choose_ref, tail_ref, ids_ref, sem = refs
     rows = nb * CR * modes
     for j in range(nc):
         all_ref[j:j + 1, :] = came_ref[j, rows:rows + 16, :].astype(F32)[0:1].astype(jnp.int32)
@@ -178,13 +181,35 @@
         for l in range(per_dev):
             field_ref[((own_ref[0] ^ s) if permuted(no) else s) * per_dev + l] = near_ref[l * modes:(l + 1) * modes, :]
     copy.wait()
+    line = lax.broadcasted_iota(jnp.int32, choose_ref.shape, 0)
+    lane = lax.broadcasted_iota(jnp.int32, choose_ref.shape, 1)
+    tail_line = lax.broadcasted_iota(jnp.int32, tail_ref.shape, 0)
+    tail_lane = lax.broadcasted_iota(jnp.int32, tail_ref.shape, 1)
+    subs = jnp.zeros(choose_ref.shape, jnp.int32)
+    tail = jnp.zeros(tail_ref.shape, jnp.int32)
+    for j in range(nc):
+        for b in range(nb):
+            subs = jnp.where(line == j * nb + b, ids_ref[j, 2 * nb + b], subs)
+            value = jnp.where(tail_line == 0, ids_ref[j, b], ids_ref[j, nb + b])
+            tail = jnp.where(tail_lane == j * nb + b, value, tail)
+    choose_ref[...] = jnp.where(lane % (choose_ref.shape[1] // TERMS) == subs, 1.0, 0.0).astype(BF16)
+    tail_ref[...] = tail.astype(F32)
     forward(dims, field_ref, lat_ref, foot_ref, ids_ref, out_ref)
 
 
-def adjoint_kernel(dims, first, ids_ref, weight_ref, foot_ref, *refs):
+def split(values):
+    terms = []
+    for _ in range(TERMS):
+        terms.append(values.astype(BF16).astype(F32))
+        values = values - terms[-1]
+    return jnp.concatenate(terms, axis=0).astype(BF16)
+
+
+def adjoint_kernel(dims, tails, choose_ref, weight_ref, foot_ref, *refs):
     nc, nb, modes, groups, band = dims
+    tail_refs, refs = refs[:tails], refs[tails:]
     sim_refs, refs = refs[:-3], refs[-3:]
-    out_ref, norm_ref, weighted_ref = refs
+    out_ref, norm_ref, chosen_ref = refs
     subs = weight_ref.shape[0]
     mine = nc * nb
     total = added(sim_refs, subs + ROWS)
@@ -193,31 +218,25 @@
     scale = 1.0 / norm
     sim = total[:subs]
     weighted = sim * weight_ref[...]
-    weighted_ref[...] = weighted
+    chosen_ref[...] = jnp.dot(choose_ref[...], split(weighted), preferred_element_type=F32)
     lane = lax.broadcasted_iota(jnp.int32, (modes, 128), 1)
     parts = [jnp.zeros((modes, 128), F32) for _ in range(CR)]
     for j in range(nc):
         for b in range(nb):
-            chosen = weighted_ref[pl.ds(ids_ref[j, 2 * nb + b], 1), :]
+            at_t = j * nb + b
+            chosen = chosen_ref[at_t:at_t + 1, :]
             for r in range(CR):
                 at = (b * CR + r) * modes
                 column = jnp.sum(foot_ref[j, at:at + modes, :].astype(F32) * chosen, axis=1, keepdims=True)
-                parts[r] = jnp.where(lane == j * nb + b, column, parts[r])
+                parts[r] = jnp.where(lane == at_t, column, parts[r])
     rest = 128 - CR * modes
     if rest:
         parts.append(jnp.zeros((rest, 128), F32))
     rows = jnp.concatenate(parts, axis=0).T
     out_ref[:mine, :] = rows[:mine] * scale
     out_ref[mine:mine + subs, :] = (sim * scale) * (weighted * scale)
-    if first:
-        lane = lax.broadcasted_iota(jnp.int32, (ROWS, 128), 1)
-        line = lax.broadcasted_iota(jnp.int32, (ROWS, 128), 0)
-        tail = jnp.zeros((ROWS, 128), jnp.int32)
-        for j in range(nc):
-            for b in range(nb):
-                value = jnp.where(line == 0, ids_ref[j, b], ids_ref[j, nb + b])
-                tail = jnp.where(lane == j * nb + b, value, tail)
-        out_ref[mine + subs:, :] = tail.astype(F32)
+    for tail_ref in tail_refs:
+        out_ref[mine + subs:, :] = tail_ref[...]
 
 
 def every_kernel(dims, no, at, *refs):
@@ -227,15 +246,7 @@
         out_ref[2 * s:2 * s + 2, :] = ref[at:at + ROWS, :][0:2].astype(jnp.int32)
 
 
-def split(values):
-    terms = []
-    for _ in range(TERMS):
-        terms.append(values.astype(BF16))
-        values = values - terms[-1].astype(F32)
-    return jnp.concatenate(terms, axis=0)
-
-
-def image_kernel(dims, no, first, last, own_ref, ids_ref, all_ref, lat_ref, foot_ref, norm_ref, field_ref, *refs):
+def image_kernel(dims, no, first, last, own_ref, ids_ref, all_ref, lat_ref, foot_ref, pick_ref, norm_ref, field_ref, *refs):
     nc, nb, modes, groups, band = dims
     if not first:
         prior_ref, refs = refs[0], refs[1:]
@@ -259,10 +270,6 @@
     for sum_ref in sum_refs:
         sum_ref[...] = jnp.zeros_like(sum_ref)
 
-    line = lax.broadcasted_iota(jnp.int32, (TERMS * CHUNK, CHUNK * 128), 0)
-    lane = lax.broadcasted_iota(jnp.int32, (TERMS * CHUNK, CHUNK * 128), 1)
-    pick = jnp.where(line % CHUNK == lane // 128, 1.0, 0.0).astype(BF16)
-
     def group(at, carry):
         found = [at * ways + i for i in range(ways)]
         if permuted(no):
@@ -270,7 +277,7 @@
         for chunk in range(0, mine, CHUNK):
             for at_i, wide_ref in zip(found, wide_refs):
                 left = split(held_ref[at_i, chunk:chunk + CHUNK, :])
-                wide = lax.dot_general(left, pick, (((0,), (0,)), ((), ())), preferred_element_type=F32)
+                wide = lax.dot_general(left, pick_ref[...], (((0,), (0,)), ((), ())), preferred_element_type=F32)
                 wide_ref[...] = wide[:CR * modes]
             for at in range(CHUNK):
                 for at_i, wide_ref, sum_ref in zip(found, wide_refs, sum_refs):
@@ -283,8 +290,9 @@
                     sum_ref[period] = total
         return carry
 
-    if no == ways:
-        group(0, 0)
+    if no <= 4:
+        for at in range(no // ways):
+            group(at, 0)
     else:
         lax.fori_loop(0, no // ways, group, 0)
     gain = jnp.sum(tree_sum(ref[mine:mine + subs, :] for ref in coef_refs), keepdims=True)
@@ -398,9 +406,13 @@
     )
     came = swap(hats, "cell")
     lat, start, _ = lax.optimization_barrier((lat_mats, start, weights))
-    lat, start = call(
+    lat, start, pick = call(
         fetch_kernel,
-        (shape((lat_rows, modes, lat_rows)), shape(start.shape)),
+        (
+            shape((lat_rows, modes, lat_rows)),
+            shape(start.shape),
+            jax.ShapeDtypeStruct((TERMS * CHUNK, CHUNK * 128), BF16),
+        ),
         [ANY] * 2,
         lat, start,
         scratch=[pltpu.SemaphoreType.DMA((modes + 1,))],
@@ -413,13 +425,15 @@
     field_shape = shape((periods, modes, lat_rows))
     small = shape((ROWS, 128))
     own_shape = shape((per_dev, modes, lat_rows))
-    sims, field, foot, ids = call(
+    sims, field, foot, ids, choose, tail = call(
         functools.partial(first_kernel, dims, no),
         (
             shape((subs + ROWS, ob)),
             field_shape,
             jax.ShapeDtypeStruct((nc, foot_rows, ob), BF16),
             jax.ShapeDtypeStruct((nc, 128), jnp.int32),
+            jax.ShapeDtypeStruct((mine, TERMS * subs), BF16),
+            shape((ROWS, 128)),
         ),
         [SMEM] + [VMEM] * (2 + len(near)),
         own, lat, came, *near,
@@ -431,12 +445,13 @@
     for step in range(STEPS):
         first, last = step == 0, step == STEPS - 1
         parts = addends(sims, "cell")
+        tails = [tail] if first else []
         coefs, norm = call(
-            functools.partial(adjoint_kernel, dims, first),
+            functools.partial(adjoint_kernel, dims, len(tails)),
             (shape((mine + subs + (ROWS if first else 0), 128)), small),
-            [SMEM] + [VMEM] * (2 + len(parts)),
-            ids, weights, foot, *parts,
-            scratch=[pltpu.VMEM((subs, ob), F32)],
+            [VMEM] * (3 + len(tails) + len(parts)),
+            choose, weights, foot, *tails, *parts,
+            scratch=[pltpu.VMEM((mine, ob), F32)],
         )
         coefs = share(coefs, "obs")
         if first:
@@ -456,8 +471,8 @@
                 *([] if last else [field_shape]),
                 small,
             ),
-            [SMEM] * 3 + [VMEM] * (4 + len(before) + len(coefs)),
-            own, ids, every, lat, foot, norm, field, *before, *coefs,
+            [SMEM] * 3 + [VMEM] * (5 + len(before) + len(coefs)),
+            own, ids, every, lat, foot, pick, norm, field, *before, *coefs,
             scratch=[pltpu.VMEM(field_shape.shape, F32)] * last
             + [pltpu.VMEM((no, mine, 128), F32)]
             + [pltpu.VMEM(field_shape.shape, F32)] * ways

time: 79.7 us -> 78.1 us (0.980)
  Pallas kernels: 15.5 us -> 14 us
    pallas_call x15, Pallas kernels: 15.5 us -> 14 us  [call(): pl.pallas_call(kernel, out_shape=outs, in_specs=specs, out_specs=jax.tree...]
where the time goes in v10:
time: 78.1 us; the launch traced here: 77.7 us
  starting transfers between devices  37.4 us (48%)
  waiting for transfers between devices  24.9 us (32%)
  Pallas kernels  14 us (18%)
    ppermute x12, starting transfers between devices, share(): lax.ppermute(array, axis, [(d, d ^ s) for d in range(size)])  18 us
    pallas_call x15, Pallas kernels, call(): pl.pallas_call(kernel, out_shape=outs, in_specs=specs, out_specs=jax.tree...  14 us
    ppermute x12, starting transfers between devices, addends(): lax.ppermute(both, axis, [(d, d ^ s) for d in range(size)])  14 us
    ppermute x12, waiting for transfers between devices, addends(): lax.ppermute(both, axis, [(d, d ^ s) for d in range(size)])  11.6 us
    ppermute x12, waiting for transfers between devices, share(): lax.ppermute(array, axis, [(d, d ^ s) for d in range(size)])  8.62 us
    all_to_all x1, starting transfers between devices, swap(): return lax.all_to_all(array, axis, split_axis=0, concat_axis=0, tiled=True)  5.18 us
    ppermute x4, waiting for transfers between devices, addends(): other = lax.ppermute(array, axis, [(d, d ^ 1) for d in range(size)])  4.63 us
  transfers between devices with their start and end apart: 29, of which 25 were waited for; matrix products, arithmetic and copies ran while one was open for 0% of the time, Pallas kernels for 3%

profile of v10, /device:TPU:0, one launch (start us, length us, event | category | flops | bytes accessed | tf_op | source)
XLA Modules:
  0.0 77.7 jit_solution(12375986043170021174)
XLA Ops:
  0.6 2.6 %shard_map.104 = (bf16[8,208,128]{2,1,0:T(8,128)(2,1)}, f32[8,128]{1,0:T(8,128)}) custom-call(s32[1]{0:T(128)} %bitcast.2.cell_ref, bf16[384,384]{1,0:T(8,128)(2,1)} %constant.12.clone.high_any, bf16[384,384]{1,0:T(8,128)(2,1)} %constant.13.clone.low_any, bf16[2,128,768]{2,1,0:T(8,128)(2,1)} %foot_any.1, s32[2]{0:T(128)} %off_any.1, s32[2]{0:T(128)} %sub_any.1, ...), custom_call_target="tpu_custom_call" | custom-call | tf_op jit(solution)/shard_map/pallas_call | solution.py:41
  3.3 5.2 %all-to-all-start = ((bf16[8,208,128]{2,1,0:T(8,128)(2,1)}), bf16[8,208,128]{2,1,0:T(8,128)(2,1)}, u32[]{:S(2)}, u32[]{:S(2)}) async-start(bf16[8,208,128]{2,1,0:T(8,128)(2,1)} %get-tuple-element.39), calls=%async_computation | async-start | bytes 851968 | tf_op jit(solution)/shard_map/all_to_all | solution.py:362
  8.5 4.1 %collective-permute-start.2 = (f32[48,128]{1,0:T(8,128)}, f32[48,128]{1,0:T(8,128)S(1)}, u32[]{:S(2)}, u32[]{:S(2)}) collective-permute-start(f32[48,128]{1,0:T(8,128)} %bitcast.4), channel_id=1, source_target_pairs={{0,24},{8,16},{16,8},{24,0},{1,25},{9,17},{17,9},{25,1},{2,26},{10... | collective-permute-start | bytes 73736 | tf_op jit(solution)/shard_map/ppermute | solution.py:349
  12.5 0.6 collective-permute-start
  13.2 0.8 copy-done.1
  13.9 2.3 %shard_map.105 = (f32[128,48,128]{2,1,0:T(8,128)S(1)}, f32[48,128]{1,0:T(8,128)S(1)}, bf16[48,2048]{1,0:T(8,128)(2,1)S(1)}) custom-call(f32[48,128,128]{2,1,0:T(8,128)} %lat_any, f32[48,128]{1,0:T(8,128)S(1)} %bitcast.7), custom_call_target="tpu_custom_call" | custom-call | bytes 6340608 | tf_op jit(solution)/shard_map/pallas_call | solution.py:41
  16.3 1.2 %collective-permute-done.1.refs_2_ = f32[48,128]{1,0:T(8,128)S(1)} collective-permute-done((f32[48,128]{1,0:T(8,128)}, f32[48,128]{1,0:T(8,128)S(1)}, u32[]{:S(2)}, u32[]{:S(2)}) %collective-permute-start.1) | collective-permute-done | bytes 24608 | tf_op jit(solution)/shard_map/ppermute | solution.py:349
  17.5 1.9 %shard_map.106 = (f32[16,128]{1,0:T(8,128)S(1)}, f32[4,48,128]{2,1,0:T(8,128)S(1)}, bf16[8,192,128]{2,1,0:T(8,128)(2,1)S(1)}, s32[8,128]{1,0:T(8,128)S(1)}, bf16...) custom-call(s32[1]{0:T(128)} %bitcast.own_ref, f32[128,48,128]{2,1,0:T(8,128)S(1)} %get-tuple-element.38.lat_ref, ...), custom_call_target="tpu_custom_call" | custom-call | tf_op jit(solution)/shard_map/pallas_call | solution.py:41
  19.5 1.2 %collective-permute-done.3.other_ref = f32[16,128]{1,0:T(8,128)S(1)} collective-permute-done((f32[16,128]{1,0:T(8,128)S(1)}, f32[16,128]{1,0:T(8,128)S(1)}, u32[]{:S(2)}, u32[]{:S(2)}) %collective-permute-start.3) | collective-permute-done | bytes 8224 | tf_op jit(solution)/shard_map/ppermute | solution.py:356
  20.7 2.8 %collective-permute-start.6 = (f32[16,128]{1,0:T(8,128)S(1)}, f32[16,128]{1,0:T(8,128)S(1)}, u32[]{:S(2)}, u32[]{:S(2)}) collective-permute-start(f32[16,128]{1,0:T(8,128)S(1)} %shard_map.107.refs_1_), channel_id=1, source_target_pairs={{0,6},{1,7},{2,4},{3,5},{4,2},{5,3},{6,0},{7,1},{8,14},{9,15},{10,... | collective-permute-start | bytes 24584 | tf_op jit(solution)/shard_map/ppermute | solution.py:358
  24.1 1.1 %collective-permute-done.6.refs_4_ = f32[16,128]{1,0:T(8,128)S(1)} collective-permute-done((f32[16,128]{1,0:T(8,128)S(1)}, f32[16,128]{1,0:T(8,128)S(1)}, u32[]{:S(2)}, u32[]{:S(2)}) %collective-permute-start.6) | collective-permute-done | bytes 8224 | tf_op jit(solution)/shard_map/ppermute | solution.py:358
  25.2 1.9 %collective-permute-done.5.refs_3_ = f32[16,128]{1,0:T(8,128)S(1)} collective-permute-done((f32[16,128]{1,0:T(8,128)S(1)}, f32[16,128]{1,0:T(8,128)S(1)}, u32[]{:S(2)}, u32[]{:S(2)}) %collective-permute-start.5) | collective-permute-done | bytes 8224 | tf_op jit(solution)/shard_map/ppermute | solution.py:358
  28.1 2.6 %collective-permute-start.9 = (f32[32,128]{1,0:T(8,128)S(1)}, f32[32,128]{1,0:T(8,128)S(1)}, u32[]{:S(2)}, u32[]{:S(2)}) collective-permute-start(f32[32,128]{1,0:T(8,128)S(1)} %get-tuple-element.46.refs_0_), channel_id=1, source_target_pairs={{0,24},{8,16},{16,8},{24,0},{1,25},{9,17},{17,9},{25,1},{2,26},{10... | collective-permute-start | bytes 49160 | tf_op jit(solution)/shard_map/ppermute | solution.py:349
  30.7 1.8 %collective-permute-start.7 = (f32[32,128]{1,0:T(8,128)S(1)}, f32[32,128]{1,0:T(8,128)S(1)}, u32[]{:S(2)}, u32[]{:S(2)}) collective-permute-start(f32[32,128]{1,0:T(8,128)S(1)} %get-tuple-element.46.refs_0_), channel_id=1, source_target_pairs={{0,8},{8,0},{16,24},{24,16},{1,9},{9,1},{17,25},{25,17},{2,10},{10... | collective-permute-start | bytes 49160 | tf_op jit(solution)/shard_map/ppermute | solution.py:349
  32.5 1.1 %collective-permute-done.9.refs_3_ = f32[32,128]{1,0:T(8,128)S(1)} collective-permute-done((f32[32,128]{1,0:T(8,128)S(1)}, f32[32,128]{1,0:T(8,128)S(1)}, u32[]{:S(2)}, u32[]{:S(2)}) %collective-permute-start.9) | collective-permute-done | bytes 16416 | tf_op jit(solution)/shard_map/ppermute | solution.py:349
  33.6 1.7 %collective-permute-done.8.refs_2_ = f32[32,128]{1,0:T(8,128)S(1)} collective-permute-done((f32[32,128]{1,0:T(8,128)S(1)}, f32[32,128]{1,0:T(8,128)S(1)}, u32[]{:S(2)}, u32[]{:S(2)}) %collective-permute-start.8) | collective-permute-done | bytes 16416 | tf_op jit(solution)/shard_map/ppermute | solution.py:349
  35.3 1.7 %shard_map.110 = (f32[16,128]{1,0:T(8,128)S(1)}, f32[1,48,128]{2,1,0:T(8,128)S(1)}, f32[4,48,128]{2,1,0:T(8,128)S(1)}, f32[4,48,128]{2,1,0:T(8,128)S(1)}, f32[8,128]{1,0:T(8,128)S(1)}) custom-call(s32[1]{0:T(128)} %bitcast.own_ref, s32[8,128]{1,0:T(8,128)S(1)} %get-tuple-element.41.ids_ref, s32[8,128]{1,0:T(8,128)S(1)} %shard_map.109.all_ref, ...), custom_call_target="tpu_custom_call" | custom-call | tf_op jit(solution)/shard_map/pallas_call | solution.py:41
  37.2 1.2 %collective-permute-done.10.other_ref = f32[16,128]{1,0:T(8,128)S(1)} collective-permute-done((f32[16,128]{1,0:T(8,128)S(1)}, f32[16,128]{1,0:T(8,128)S(1)}, u32[]{:S(2)}, u32[]{:S(2)}) %collective-permute-start.10) | collective-permute-done | bytes 8224 | tf_op jit(solution)/shard_map/ppermute | solution.py:356
  38.3 1.5 %collective-permute-start.13 = (f32[16,128]{1,0:T(8,128)S(1)}, f32[16,128]{1,0:T(8,128)S(1)}, u32[]{:S(2)}, u32[]{:S(2)}) collective-permute-start(f32[16,128]{1,0:T(8,128)S(1)} %shard_map.111.refs_0_), channel_id=1, source_target_pairs={{0,6},{1,7},{2,4},{3,5},{4,2},{5,3},{6,0},{7,1},{8,14},{9,15},{10,... | collective-permute-start | bytes 24584 | tf_op jit(solution)/shard_map/ppermute | solution.py:358
  39.8 1.3 %collective-permute-start.12 = (f32[16,128]{1,0:T(8,128)S(1)}, f32[16,128]{1,0:T(8,128)S(1)}, u32[]{:S(2)}, u32[]{:S(2)}) collective-permute-start(f32[16,128]{1,0:T(8,128)S(1)} %shard_map.111.refs_0_), channel_id=1, source_target_pairs={{0,4},{1,5},{2,6},{3,7},{4,0},{5,1},{6,2},{7,3},{8,12},{9,13},{10,... | collective-permute-start | bytes 24584 | tf_op jit(solution)/shard_map/ppermute | solution.py:358
  41.1 0.7 collective-permute-start.11
  41.8 1.1 %collective-permute-done.13.refs_3_ = f32[16,128]{1,0:T(8,128)S(1)} collective-permute-done((f32[16,128]{1,0:T(8,128)S(1)}, f32[16,128]{1,0:T(8,128)S(1)}, u32[]{:S(2)}, u32[]{:S(2)}) %collective-permute-start.13) | collective-permute-done | bytes 8224 | tf_op jit(solution)/shard_map/ppermute | solution.py:358
  42.9 0.6 collective-permute-done.12.refs_2_
  43.5 1.3 %collective-permute-done.11.refs_1_ = f32[16,128]{1,0:T(8,128)S(1)} collective-permute-done((f32[16,128]{1,0:T(8,128)S(1)}, f32[16,128]{1,0:T(8,128)S(1)}, u32[]{:S(2)}, u32[]{:S(2)}) %collective-permute-start.11) | collective-permute-done | bytes 8224 | tf_op jit(solution)/shard_map/ppermute | solution.py:358
  45.2 1.5 %collective-permute-start.16 = (f32[24,128]{1,0:T(8,128)S(1)}, f32[24,128]{1,0:T(8,128)S(1)}, u32[]{:S(2)}, u32[]{:S(2)}) collective-permute-start(f32[24,128]{1,0:T(8,128)S(1)} %get-tuple-element.54.refs_1_), channel_id=1, source_target_pairs={{0,24},{8,16},{16,8},{24,0},{1,25},{9,17},{17,9},{25,1},{2,26},{10... | collective-permute-start | bytes 36872 | tf_op jit(solution)/shard_map/ppermute | solution.py:349
  46.7 0.6 collective-permute-start.15
  47.3 2.3 %collective-permute-start.14 = (f32[24,128]{1,0:T(8,128)S(1)}, f32[24,128]{1,0:T(8,128)S(1)}, u32[]{:S(2)}, u32[]{:S(2)}) collective-permute-start(f32[24,128]{1,0:T(8,128)S(1)} %get-tuple-element.54.refs_1_), channel_id=1, source_target_pairs={{0,8},{8,0},{16,24},{24,16},{1,9},{9,1},{17,25},{25,17},{2,10},{10... | collective-permute-start | bytes 36872 | tf_op jit(solution)/shard_map/ppermute | solution.py:349
  49.6 1.1 %collective-permute-done.16.refs_4_ = f32[24,128]{1,0:T(8,128)S(1)} collective-permute-done((f32[24,128]{1,0:T(8,128)S(1)}, f32[24,128]{1,0:T(8,128)S(1)}, u32[]{:S(2)}, u32[]{:S(2)}) %collective-permute-start.16) | collective-permute-done | bytes 12320 | tf_op jit(solution)/shard_map/ppermute | solution.py:349
  51.4 1.7 %shard_map.113 = (f32[16,128]{1,0:T(8,128)S(1)}, f32[1,48,128]{2,1,0:T(8,128)S(1)}, f32[4,48,128]{2,1,0:T(8,128)S(1)}, f32[4,48,128]{2,1,0:T(8,128)S(1)}, f32[8,128]{1,0:T(8,128)S(1)}) custom-call(s32[1]{0:T(128)} %bitcast.own_ref, s32[8,128]{1,0:T(8,128)S(1)} %get-tuple-element.41.ids_ref, s32[8,128]{1,0:T(8,128)S(1)} %shard_map.109.all_ref, ...), custom_call_target="tpu_custom_call" | custom-call | tf_op jit(solution)/shard_map/pallas_call | solution.py:41
  53.2 1.2 %collective-permute-done.17.other_ref = f32[16,128]{1,0:T(8,128)S(1)} collective-permute-done((f32[16,128]{1,0:T(8,128)S(1)}, f32[16,128]{1,0:T(8,128)S(1)}, u32[]{:S(2)}, u32[]{:S(2)}) %collective-permute-start.17) | collective-permute-done | bytes 8224 | tf_op jit(solution)/shard_map/ppermute | solution.py:356
  54.4 1.7 %collective-permute-start.20 = (f32[16,128]{1,0:T(8,128)S(1)}, f32[16,128]{1,0:T(8,128)S(1)}, u32[]{:S(2)}, u32[]{:S(2)}) collective-permute-start(f32[16,128]{1,0:T(8,128)S(1)} %shard_map.114.refs_0_), channel_id=1, source_target_pairs={{0,6},{1,7},{2,4},{3,5},{4,2},{5,3},{6,0},{7,1},{8,14},{9,15},{10,... | collective-permute-start | bytes 24584 | tf_op jit(solution)/shard_map/ppermute | solution.py:358
  56.6 1.3 %collective-permute-start.18 = (f32[16,128]{1,0:T(8,128)S(1)}, f32[16,128]{1,0:T(8,128)S(1)}, u32[]{:S(2)}, u32[]{:S(2)}) collective-permute-start(f32[16,128]{1,0:T(8,128)S(1)} %shard_map.114.refs_0_), channel_id=1, source_target_pairs={{0,2},{1,3},{2,0},{3,1},{4,6},{5,7},{6,4},{7,5},{8,10},{9,11},{10,... | collective-permute-start | bytes 24584 | tf_op jit(solution)/shard_map/ppermute | solution.py:358
  57.9 1.1 %collective-permute-done.20.refs_3_ = f32[16,128]{1,0:T(8,128)S(1)} collective-permute-done((f32[16,128]{1,0:T(8,128)S(1)}, f32[16,128]{1,0:T(8,128)S(1)}, u32[]{:S(2)}, u32[]{:S(2)}) %collective-permute-start.20) | collective-permute-done | bytes 8224 | tf_op jit(solution)/shard_map/ppermute | solution.py:358
  58.9 0.8 collective-permute-done.19.refs_2_
  60.7 2.5 %collective-permute-start.23 = (f32[24,128]{1,0:T(8,128)S(1)}, f32[24,128]{1,0:T(8,128)S(1)}, u32[]{:S(2)}, u32[]{:S(2)}) collective-permute-start(f32[24,128]{1,0:T(8,128)S(1)} %get-tuple-element.59.refs_1_), channel_id=1, source_target_pairs={{0,24},{8,16},{16,8},{24,0},{1,25},{9,17},{17,9},{25,1},{2,26},{10... | collective-permute-start | bytes 36872 | tf_op jit(solution)/shard_map/ppermute | solution.py:349
  63.2 0.9 %collective-permute-start.22 = (f32[24,128]{1,0:T(8,128)S(1)}, f32[24,128]{1,0:T(8,128)S(1)}, u32[]{:S(2)}, u32[]{:S(2)}) collective-permute-start(f32[24,128]{1,0:T(8,128)S(1)} %get-tuple-element.59.refs_1_), channel_id=1, source_target_pairs={{0,16},{8,24},{16,0},{24,8},{1,17},{9,25},{17,1},{25,9},{2,18},{10... | collective-permute-start | bytes 36872 | tf_op jit(solution)/shard_map/ppermute | solution.py:349
  64.1 1.0 %collective-permute-start.21 = (f32[24,128]{1,0:T(8,128)S(1)}, f32[24,128]{1,0:T(8,128)S(1)}, u32[]{:S(2)}, u32[]{:S(2)}) collective-permute-start(f32[24,128]{1,0:T(8,128)S(1)} %get-tuple-element.59.refs_1_), channel_id=1, source_target_pairs={{0,8},{8,0},{16,24},{24,16},{1,9},{9,1},{17,25},{25,17},{2,10},{10... | collective-permute-start | bytes 36872 | tf_op jit(solution)/shard_map/ppermute | solution.py:349
  65.1 1.1 %collective-permute-done.23.refs_4_ = f32[24,128]{1,0:T(8,128)S(1)} collective-permute-done((f32[24,128]{1,0:T(8,128)S(1)}, f32[24,128]{1,0:T(8,128)S(1)}, u32[]{:S(2)}, u32[]{:S(2)}) %collective-permute-start.23) | collective-permute-done | bytes 12320 | tf_op jit(solution)/shard_map/ppermute | solution.py:349
  66.2 1.6 %collective-permute-done.22.refs_3_ = f32[24,128]{1,0:T(8,128)S(1)} collective-permute-done((f32[24,128]{1,0:T(8,128)S(1)}, f32[24,128]{1,0:T(8,128)S(1)}, u32[]{:S(2)}, u32[]{:S(2)}) %collective-permute-start.22) | collective-permute-done | bytes 12320 | tf_op jit(solution)/shard_map/ppermute | solution.py:349
  67.9 1.5 %shard_map.116 = (f32[8,128]{1,0:T(8,128)S(1)}, f32[1,48,128]{2,1,0:T(8,128)S(1)}, f32[1,48,128]{2,1,0:T(8,128)S(1)}, f32[8,128]{1,0:T(8,128)S(1)}) custom-call(s32[1]{0:T(128)} %bitcast.own_ref, s32[8,128]{1,0:T(8,128)S(1)} %get-tuple-element.41.ids_ref, s32[8,128]{1,0:T(8,128)S(1)} %shard_map.109.all_ref, f32[128,48,128]{2,1,0:T(8,128)S(1)} %get-tuple-element.38.lat_ref, ...), custom_call_target="tpu_custom_call" | custom-call | tf_op jit(solution)/shard_map/pallas_call | solution.py:41
  69.4 1.2 %collective-permute-done.24.other_ref = f32[8,128]{1,0:T(8,128)S(1)} collective-permute-done((f32[8,128]{1,0:T(8,128)S(1)}, f32[8,128]{1,0:T(8,128)S(1)}, u32[]{:S(2)}, u32[]{:S(2)}) %collective-permute-start.24) | collective-permute-done | bytes 4128 | tf_op jit(solution)/shard_map/ppermute | solution.py:356
  70.6 1.5 %collective-permute-start.27 = (f32[8,128]{1,0:T(8,128)S(1)}, f32[8,128]{1,0:T(8,128)S(1)}, u32[]{:S(2)}, u32[]{:S(2)}) collective-permute-start(f32[8,128]{1,0:T(8,128)S(1)} %shard_map.117.refs_0_), channel_id=1, source_target_pairs={{0,6},{1,7},{2,4},{3,5},{4,2},{5,3},{6,0},{7,1},{8,14},{9,15},{10,... | collective-permute-start | bytes 12296 | tf_op jit(solution)/shard_map/ppermute | solution.py:358
  72.1 1.3 %collective-permute-start.26 = (f32[8,128]{1,0:T(8,128)S(1)}, f32[8,128]{1,0:T(8,128)S(1)}, u32[]{:S(2)}, u32[]{:S(2)}) collective-permute-start(f32[8,128]{1,0:T(8,128)S(1)} %shard_map.117.refs_0_), channel_id=1, source_target_pairs={{0,4},{1,5},{2,6},{3,7},{4,0},{5,1},{6,2},{7,3},{8,12},{9,13},{10,... | collective-permute-start | bytes 12296 | tf_op jit(solution)/shard_map/ppermute | solution.py:358
  73.3 0.7 collective-permute-start.25
  74.1 1.0 %collective-permute-done.27.refs_3_ = f32[8,128]{1,0:T(8,128)S(1)} collective-permute-done((f32[8,128]{1,0:T(8,128)S(1)}, f32[8,128]{1,0:T(8,128)S(1)}, u32[]{:S(2)}, u32[]{:S(2)}) %collective-permute-start.27) | collective-permute-done | bytes 4128 | tf_op jit(solution)/shard_map/ppermute | solution.py:358
  75.1 0.6 collective-permute-done.26.refs_2_
  75.7 1.3 %collective-permute-done.25.refs_1_ = f32[8,128]{1,0:T(8,128)S(1)} collective-permute-done((f32[8,128]{1,0:T(8,128)S(1)}, f32[8,128]{1,0:T(8,128)S(1)}, u32[]{:S(2)}, u32[]{:S(2)}) %collective-permute-start.25) | collective-permute-done | bytes 4128 | tf_op jit(solution)/shard_map/ppermute | solution.py:358
  77.0 0.8 %shard_map.118 = (f32[4,1,48,128]{3,2,1,0:T(8,128)}, f32[2,3]{1,0:T(2,128)}) custom-call(f32[8,128]{1,0:T(8,128)S(1)} %shard_map.117.refs_0_, f32[8,128]{1,0:T(8,128)S(1)} %collective-permute-done.25.refs_1_, f32[8,128]{1,0:T(8,128)S(1)} %collective-permute-done.26.refs_2_, f32[8,128]{1,0:T(8,128)S(1)} %collective-permute-done.27.refs_3_, ...), custom_call_target="tpu_custom_call" | custom-call | tf_op jit(solution)/shard_map/pallas_call | solution.py:41
  (29 shorter events, 4.8 us)
Async XLA Ops:
  3.3 14.2 %all-to-all-start = ((bf16[8,208,128]{2,1,0:T(8,128)(2,1)}), bf16[8,208,128]{2,1,0:T(8,128)(2,1)}, u32[]{:S(2)}, u32[]{:S(2)}) async-start(bf16[8,208,128]{2,1,0:T(8,128)(2,1)} %get-tuple-element.39), calls=%async_computation | async-start | bytes 851968 | tf_op jit(solution)/shard_map/all_to_all | solution.py:362
  8.5 7.8 %collective-permute-start.2 = (f32[48,128]{1,0:T(8,128)}, f32[48,128]{1,0:T(8,128)S(1)}, u32[]{:S(2)}, u32[]{:S(2)}) collective-permute-start(f32[48,128]{1,0:T(8,128)} %bitcast.4), channel_id=1, source_target_pairs={{0,24},{8,16},{16,8},{24,0},{1,25},{9,17},{17,9},{25,1},{2,26},{10... | collective-permute-start | bytes 73736 | tf_op jit(solution)/shard_map/ppermute | solution.py:349
  12.5 4.9 %collective-permute-start.1 = (f32[48,128]{1,0:T(8,128)}, f32[48,128]{1,0:T(8,128)S(1)}, u32[]{:S(2)}, u32[]{:S(2)}) collective-permute-start(f32[48,128]{1,0:T(8,128)} %bitcast.5), channel_id=1, source_target_pairs={{0,16},{8,24},{16,0},{24,8},{1,17},{9,25},{17,1},{25,9},{2,18},{10... | collective-permute-start | bytes 73736 | tf_op jit(solution)/shard_map/ppermute | solution.py:349
  12.5 4.9 %collective-permute-start = (f32[48,128]{1,0:T(8,128)}, f32[48,128]{1,0:T(8,128)S(1)}, u32[]{:S(2)}, u32[]{:S(2)}) collective-permute-start(f32[48,128]{1,0:T(8,128)} %bitcast.6), channel_id=1, source_target_pairs={{0,8},{8,0},{16,24},{24,16},{1,9},{9,1},{17,25},{25,17},{2,10},{10... | collective-permute-start | bytes 73736 | tf_op jit(solution)/shard_map/ppermute | solution.py:349
  13.2 0.8 copy-start.1
  13.9 13.7 %copy-start = (f32[8,128]{1,0:T(8,128)S(1)}, f32[8,128]{1,0:T(8,128)}, u32[]{:S(2)}) copy-start(f32[8,128]{1,0:T(8,128)} %get-tuple-element.35.weight_ref) | copy-start | bytes 12292
  19.4 1.2 %collective-permute-start.3 = (f32[16,128]{1,0:T(8,128)S(1)}, f32[16,128]{1,0:T(8,128)S(1)}, u32[]{:S(2)}, u32[]{:S(2)}) collective-permute-start(f32[16,128]{1,0:T(8,128)S(1)} %get-tuple-element.45.one_ref), channel_id=1, source_target_pairs={{0,1},{1,0},{2,3},{3,2},{4,5},{5,4},{6,7},{7,6},{8,9},{9,8},{10,11... | collective-permute-start | bytes 24584 | tf_op jit(solution)/shard_map/ppermute | solution.py:356
  20.7 4.5 %collective-permute-start.6 = (f32[16,128]{1,0:T(8,128)S(1)}, f32[16,128]{1,0:T(8,128)S(1)}, u32[]{:S(2)}, u32[]{:S(2)}) collective-permute-start(f32[16,128]{1,0:T(8,128)S(1)} %shard_map.107.refs_1_), channel_id=1, source_target_pairs={{0,6},{1,7},{2,4},{3,5},{4,2},{5,3},{6,0},{7,1},{8,14},{9,15},{10,... | collective-permute-start | bytes 24584 | tf_op jit(solution)/shard_map/ppermute | solution.py:358
  23.4 3.7 %collective-permute-start.5 = (f32[16,128]{1,0:T(8,128)S(1)}, f32[16,128]{1,0:T(8,128)S(1)}, u32[]{:S(2)}, u32[]{:S(2)}) collective-permute-start(f32[16,128]{1,0:T(8,128)S(1)} %shard_map.107.refs_1_), channel_id=1, source_target_pairs={{0,4},{1,5},{2,6},{3,7},{4,0},{5,1},{6,2},{7,3},{8,12},{9,13},{10,... | collective-permute-start | bytes 24584 | tf_op jit(solution)/shard_map/ppermute | solution.py:358
  24.0 3.7 %collective-permute-start.4 = (f32[16,128]{1,0:T(8,128)S(1)}, f32[16,128]{1,0:T(8,128)S(1)}, u32[]{:S(2)}, u32[]{:S(2)}) collective-permute-start(f32[16,128]{1,0:T(8,128)S(1)} %shard_map.107.refs_1_), channel_id=1, source_target_pairs={{0,2},{1,3},{2,0},{3,1},{4,6},{5,7},{6,4},{7,5},{8,10},{9,11},{10,... | collective-permute-start | bytes 24584 | tf_op jit(solution)/shard_map/ppermute | solution.py:358
  28.1 5.6 %collective-permute-start.9 = (f32[32,128]{1,0:T(8,128)S(1)}, f32[32,128]{1,0:T(8,128)S(1)}, u32[]{:S(2)}, u32[]{:S(2)}) collective-permute-start(f32[32,128]{1,0:T(8,128)S(1)} %get-tuple-element.46.refs_0_), channel_id=1, source_target_pairs={{0,24},{8,16},{16,8},{24,0},{1,25},{9,17},{17,9},{25,1},{2,26},{10... | collective-permute-start | bytes 49160 | tf_op jit(solution)/shard_map/ppermute | solution.py:349
  30.7 4.6 %collective-permute-start.8 = (f32[32,128]{1,0:T(8,128)S(1)}, f32[32,128]{1,0:T(8,128)S(1)}, u32[]{:S(2)}, u32[]{:S(2)}) collective-permute-start(f32[32,128]{1,0:T(8,128)S(1)} %get-tuple-element.46.refs_0_), channel_id=1, source_target_pairs={{0,16},{8,24},{16,0},{24,8},{1,17},{9,25},{17,1},{25,9},{2,18},{10... | collective-permute-start | bytes 49160 | tf_op jit(solution)/shard_map/ppermute | solution.py:349
  30.7 4.6 %collective-permute-start.7 = (f32[32,128]{1,0:T(8,128)S(1)}, f32[32,128]{1,0:T(8,128)S(1)}, u32[]{:S(2)}, u32[]{:S(2)}) collective-permute-start(f32[32,128]{1,0:T(8,128)S(1)} %get-tuple-element.46.refs_0_), channel_id=1, source_target_pairs={{0,8},{8,0},{16,24},{24,16},{1,9},{9,1},{17,25},{25,17},{2,10},{10... | collective-permute-start | bytes 49160 | tf_op jit(solution)/shard_map/ppermute | solution.py:349
  37.1 1.2 %collective-permute-start.10 = (f32[16,128]{1,0:T(8,128)S(1)}, f32[16,128]{1,0:T(8,128)S(1)}, u32[]{:S(2)}, u32[]{:S(2)}) collective-permute-start(f32[16,128]{1,0:T(8,128)S(1)} %get-tuple-element.50.one_ref), channel_id=1, source_target_pairs={{0,1},{1,0},{2,3},{3,2},{4,5},{5,4},{6,7},{7,6},{8,9},{9,8},{10,11... | collective-permute-start | bytes 24584 | tf_op jit(solution)/shard_map/ppermute | solution.py:356
  38.3 4.5 %collective-permute-start.13 = (f32[16,128]{1,0:T(8,128)S(1)}, f32[16,128]{1,0:T(8,128)S(1)}, u32[]{:S(2)}, u32[]{:S(2)}) collective-permute-start(f32[16,128]{1,0:T(8,128)S(1)} %shard_map.111.refs_0_), channel_id=1, source_target_pairs={{0,6},{1,7},{2,4},{3,5},{4,2},{5,3},{6,0},{7,1},{8,14},{9,15},{10,... | collective-permute-start | bytes 24584 | tf_op jit(solution)/shard_map/ppermute | solution.py:358
  39.8 3.7 %collective-permute-start.12 = (f32[16,128]{1,0:T(8,128)S(1)}, f32[16,128]{1,0:T(8,128)S(1)}, u32[]{:S(2)}, u32[]{:S(2)}) collective-permute-start(f32[16,128]{1,0:T(8,128)S(1)} %shard_map.111.refs_0_), channel_id=1, source_target_pairs={{0,4},{1,5},{2,6},{3,7},{4,0},{5,1},{6,2},{7,3},{8,12},{9,13},{10,... | collective-permute-start | bytes 24584 | tf_op jit(solution)/shard_map/ppermute | solution.py:358
  41.1 3.7 %collective-permute-start.11 = (f32[16,128]{1,0:T(8,128)S(1)}, f32[16,128]{1,0:T(8,128)S(1)}, u32[]{:S(2)}, u32[]{:S(2)}) collective-permute-start(f32[16,128]{1,0:T(8,128)S(1)} %shard_map.111.refs_0_), channel_id=1, source_target_pairs={{0,2},{1,3},{2,0},{3,1},{4,6},{5,7},{6,4},{7,5},{8,10},{9,11},{10,... | collective-permute-start | bytes 24584 | tf_op jit(solution)/shard_map/ppermute | solution.py:358
  45.2 5.5 %collective-permute-start.16 = (f32[24,128]{1,0:T(8,128)S(1)}, f32[24,128]{1,0:T(8,128)S(1)}, u32[]{:S(2)}, u32[]{:S(2)}) collective-permute-start(f32[24,128]{1,0:T(8,128)S(1)} %get-tuple-element.54.refs_1_), channel_id=1, source_target_pairs={{0,24},{8,16},{16,8},{24,0},{1,25},{9,17},{17,9},{25,1},{2,26},{10... | collective-permute-start | bytes 36872 | tf_op jit(solution)/shard_map/ppermute | solution.py:349
  46.7 4.6 %collective-permute-start.15 = (f32[24,128]{1,0:T(8,128)S(1)}, f32[24,128]{1,0:T(8,128)S(1)}, u32[]{:S(2)}, u32[]{:S(2)}) collective-permute-start(f32[24,128]{1,0:T(8,128)S(1)} %get-tuple-element.54.refs_1_), channel_id=1, source_target_pairs={{0,16},{8,24},{16,0},{24,8},{1,17},{9,25},{17,1},{25,9},{2,18},{10... | collective-permute-start | bytes 36872 | tf_op jit(solution)/shard_map/ppermute | solution.py:349
  47.3 4.1 %collective-permute-start.14 = (f32[24,128]{1,0:T(8,128)S(1)}, f32[24,128]{1,0:T(8,128)S(1)}, u32[]{:S(2)}, u32[]{:S(2)}) collective-permute-start(f32[24,128]{1,0:T(8,128)S(1)} %get-tuple-element.54.refs_1_), channel_id=1, source_target_pairs={{0,8},{8,0},{16,24},{24,16},{1,9},{9,1},{17,25},{25,17},{2,10},{10... | collective-permute-start | bytes 36872 | tf_op jit(solution)/shard_map/ppermute | solution.py:349
  53.1 1.2 %collective-permute-start.17 = (f32[16,128]{1,0:T(8,128)S(1)}, f32[16,128]{1,0:T(8,128)S(1)}, u32[]{:S(2)}, u32[]{:S(2)}) collective-permute-start(f32[16,128]{1,0:T(8,128)S(1)} %get-tuple-element.55.one_ref), channel_id=1, source_target_pairs={{0,1},{1,0},{2,3},{3,2},{4,5},{5,4},{6,7},{7,6},{8,9},{9,8},{10,11... | collective-permute-start | bytes 24584 | tf_op jit(solution)/shard_map/ppermute | solution.py:356
  54.4 4.5 %collective-permute-start.20 = (f32[16,128]{1,0:T(8,128)S(1)}, f32[16,128]{1,0:T(8,128)S(1)}, u32[]{:S(2)}, u32[]{:S(2)}) collective-permute-start(f32[16,128]{1,0:T(8,128)S(1)} %shard_map.114.refs_0_), channel_id=1, source_target_pairs={{0,6},{1,7},{2,4},{3,5},{4,2},{5,3},{6,0},{7,1},{8,14},{9,15},{10,... | collective-permute-start | bytes 24584 | tf_op jit(solution)/shard_map/ppermute | solution.py:358
  56.0 3.7 %collective-permute-start.19 = (f32[16,128]{1,0:T(8,128)S(1)}, f32[16,128]{1,0:T(8,128)S(1)}, u32[]{:S(2)}, u32[]{:S(2)}) collective-permute-start(f32[16,128]{1,0:T(8,128)S(1)} %shard_map.114.refs_0_), channel_id=1, source_target_pairs={{0,4},{1,5},{2,6},{3,7},{4,0},{5,1},{6,2},{7,3},{8,12},{9,13},{10,... | collective-permute-start | bytes 24584 | tf_op jit(solution)/shard_map/ppermute | solution.py:358
  56.6 3.7 %collective-permute-start.18 = (f32[16,128]{1,0:T(8,128)S(1)}, f32[16,128]{1,0:T(8,128)S(1)}, u32[]{:S(2)}, u32[]{:S(2)}) collective-permute-start(f32[16,128]{1,0:T(8,128)S(1)} %shard_map.114.refs_0_), channel_id=1, source_target_pairs={{0,2},{1,3},{2,0},{3,1},{4,6},{5,7},{6,4},{7,5},{8,10},{9,11},{10,... | collective-permute-start | bytes 24584 | tf_op jit(solution)/shard_map/ppermute | solution.py:358
  60.7 5.5 %collective-permute-start.23 = (f32[24,128]{1,0:T(8,128)S(1)}, f32[24,128]{1,0:T(8,128)S(1)}, u32[]{:S(2)}, u32[]{:S(2)}) collective-permute-start(f32[24,128]{1,0:T(8,128)S(1)} %get-tuple-element.59.refs_1_), channel_id=1, source_target_pairs={{0,24},{8,16},{16,8},{24,0},{1,25},{9,17},{17,9},{25,1},{2,26},{10... | collective-permute-start | bytes 36872 | tf_op jit(solution)/shard_map/ppermute | solution.py:349
  63.2 4.6 %collective-permute-start.22 = (f32[24,128]{1,0:T(8,128)S(1)}, f32[24,128]{1,0:T(8,128)S(1)}, u32[]{:S(2)}, u32[]{:S(2)}) collective-permute-start(f32[24,128]{1,0:T(8,128)S(1)} %get-tuple-element.59.refs_1_), channel_id=1, source_target_pairs={{0,16},{8,24},{16,0},{24,8},{1,17},{9,25},{17,1},{25,9},{2,18},{10... | collective-permute-start | bytes 36872 | tf_op jit(solution)/shard_map/ppermute | solution.py:349
  64.1 3.8 %collective-permute-start.21 = (f32[24,128]{1,0:T(8,128)S(1)}, f32[24,128]{1,0:T(8,128)S(1)}, u32[]{:S(2)}, u32[]{:S(2)}) collective-permute-start(f32[24,128]{1,0:T(8,128)S(1)} %get-tuple-element.59.refs_1_), channel_id=1, source_target_pairs={{0,8},{8,0},{16,24},{24,16},{1,9},{9,1},{17,25},{25,17},{2,10},{10... | collective-permute-start | bytes 36872 | tf_op jit(solution)/shard_map/ppermute | solution.py:349
  69.3 1.2 %collective-permute-start.24 = (f32[8,128]{1,0:T(8,128)S(1)}, f32[8,128]{1,0:T(8,128)S(1)}, u32[]{:S(2)}, u32[]{:S(2)}) collective-permute-start(f32[8,128]{1,0:T(8,128)S(1)} %get-tuple-element.60.one_ref), channel_id=1, source_target_pairs={{0,1},{1,0},{2,3},{3,2},{4,5},{5,4},{6,7},{7,6},{8,9},{9,8},{10,11... | collective-permute-start | bytes 12296 | tf_op jit(solution)/shard_map/ppermute | solution.py:356
  70.6 4.5 %collective-permute-start.27 = (f32[8,128]{1,0:T(8,128)S(1)}, f32[8,128]{1,0:T(8,128)S(1)}, u32[]{:S(2)}, u32[]{:S(2)}) collective-permute-start(f32[8,128]{1,0:T(8,128)S(1)} %shard_map.117.refs_0_), channel_id=1, source_target_pairs={{0,6},{1,7},{2,4},{3,5},{4,2},{5,3},{6,0},{7,1},{8,14},{9,15},{10,... | collective-permute-start | bytes 12296 | tf_op jit(solution)/shard_map/ppermute | solution.py:358
  72.1 3.6 %collective-permute-start.26 = (f32[8,128]{1,0:T(8,128)S(1)}, f32[8,128]{1,0:T(8,128)S(1)}, u32[]{:S(2)}, u32[]{:S(2)}) collective-permute-start(f32[8,128]{1,0:T(8,128)S(1)} %shard_map.117.refs_0_), channel_id=1, source_target_pairs={{0,4},{1,5},{2,6},{3,7},{4,0},{5,1},{6,2},{7,3},{8,12},{9,13},{10,... | collective-permute-start | bytes 12296 | tf_op jit(solution)/shard_map/ppermute | solution.py:358
  73.3 3.6 %collective-permute-start.25 = (f32[8,128]{1,0:T(8,128)S(1)}, f32[8,128]{1,0:T(8,128)S(1)}, u32[]{:S(2)}, u32[]{:S(2)}) collective-permute-start(f32[8,128]{1,0:T(8,128)S(1)} %shard_map.117.refs_0_), channel_id=1, source_target_pairs={{0,2},{1,3},{2,0},{3,1},{4,6},{5,7},{6,4},{7,5},{8,10},{9,11},{10,... | collective-permute-start | bytes 12296 | tf_op jit(solution)/shard_map/ppermute | solution.py:358

commit v11 on v10

--- a/solution.py
+++ b/solution.py
@@ -18,7 +18,6 @@
 ROWS = 8
 VMEM = pl.BlockSpec(memory_space=pltpu.VMEM)
 ANY = pl.BlockSpec(memory_space=pl.ANY)
-SMEM = pl.BlockSpec(memory_space=pltpu.SMEM)
 F32 = jnp.float32
 BF16 = jnp.bfloat16
 
@@ -56,9 +55,9 @@
     return parts[0]
 
 
-def transform_kernel(dims, cell_ref, high_any, low_any, foot_any, off_any, sub_any, count_any, rinv_any, *refs):
+def transform_kernel(dims, place_any, high_any, low_any, foot_any, off_any, sub_any, count_any, rinv_any, *refs):
     nc, nb, modes, groups, band = dims
-    out_ref, weight_ref, high_ref, low_ref, foot_ref, off_ref, sub_ref, count_ref, rinv_ref, sems = refs
+    out_ref, weight_ref, high_ref, low_ref, foot_ref, off_ref, sub_ref, count_ref, rinv_ref, place_ref, sems = refs
     copies = [
         pltpu.make_async_copy(source, target, sems.at[at])
         for at, (source, target) in enumerate(
@@ -70,6 +69,7 @@
                 (sub_any, sub_ref),
                 (count_any, count_ref),
                 (rinv_any, rinv_ref),
+                (place_any, place_ref),
             ]
         )
     ]
@@ -77,6 +77,8 @@
         copy.start()
     for copy in copies:
         copy.wait()
+    cell = place_ref[0] % nc
+    obs = place_ref[0] // nc
     ob = foot_ref.shape[1]
     lon = high_ref.shape[1]
     contract = (((1,), (1,)), ((), ()))
@@ -93,10 +95,10 @@
     ids = jnp.zeros((16, ob), F32)
     for b in range(nb):
         off = off_ref[b]
-        values = (off // groups, cell_ref[0] * (band // CR) + off % groups, sub_ref[b])
+        values = (off // groups, cell * (band // CR) + off % groups, sub_ref[b])
         for at, value in enumerate(values):
             ids = jnp.where(lane == at * nb + b, value.astype(F32), ids)
-    ids = ids.astype(BF16)
+    ids = jnp.where(lane == 3 * nb, obs.astype(F32), ids).astype(BF16)
     for c in range(nc):
         out_ref[c, nb * CR * modes:, :] = ids
     row = lax.broadcasted_iota(jnp.int32, weight_ref.shape, 0)
@@ -165,7 +167,7 @@
     out_ref[...] = one_ref[...] + other_ref[...]
 
 
-def first_kernel(dims, no, own_ref, lat_ref, came_ref, *refs):
+def first_kernel(dims, no, lat_ref, came_ref, *refs):
     nc, nb, modes, _, _ = dims
     near_refs, refs = refs[:-8], refs[-8:]
     out_ref, field_ref, foot_ref, all_ref, choose_ref, tail_ref, ids_ref, sem = refs
@@ -177,10 +179,11 @@
     for j in range(nc):
         foot_ref[j] = came_ref[j, :rows, :]
     per_dev = field_ref.shape[0] // no
+    copy.wait()
+    own = ids_ref[0, 3 * nb]
     for s, near_ref in enumerate(pieces(near_refs, no, per_dev * modes)):
         for l in range(per_dev):
-            field_ref[((own_ref[0] ^ s) if permuted(no) else s) * per_dev + l] = near_ref[l * modes:(l + 1) * modes, :]
-    copy.wait()
+            field_ref[((own ^ s) if permuted(no) else s) * per_dev + l] = near_ref[l * modes:(l + 1) * modes, :]
     line = lax.broadcasted_iota(jnp.int32, choose_ref.shape, 0)
     lane = lax.broadcasted_iota(jnp.int32, choose_ref.shape, 1)
     tail_line = lax.broadcasted_iota(jnp.int32, tail_ref.shape, 0)
@@ -246,46 +249,71 @@
         out_ref[2 * s:2 * s + 2, :] = ref[at:at + ROWS, :][0:2].astype(jnp.int32)
 
 
-def image_kernel(dims, no, first, last, own_ref, ids_ref, all_ref, lat_ref, foot_ref, pick_ref, norm_ref, field_ref, *refs):
+def widen(rows, pick_ref):
+    return lax.dot_general(split(rows), pick_ref[...], (((0,), (0,)), ((), ())), preferred_element_type=F32)
+
+
+def image_kernel(dims, no, first, last, ids_in, all_in, lat_ref, foot_ref, pick_ref, norm_ref, field_ref, *refs):
     nc, nb, modes, groups, band = dims
     if not first:
         prior_ref, refs = refs[0], refs[1:]
     ways = min(no, WAYS)
-    kept = 6 + 2 * ways
+    ids_ref, all_ref, sems = refs[-3:]
+    refs = refs[:-3]
+    copies = [
+        pltpu.make_async_copy(ids_in, ids_ref, sems.at[0]),
+        pltpu.make_async_copy(all_in, all_ref, sems.at[1]),
+    ]
+    for copy in copies:
+        copy.start()
+    kept = 7 + ways
     coef_refs, refs = refs[:-kept], refs[-kept:]
-    wide_refs, refs = refs[-ways:], refs[:-ways]
+    wide_ref, refs = refs[-1], refs[:-1]
     sum_refs, refs = refs[-ways:], refs[:-ways]
     if last:
         out_ref, row_ref, mine_ref, alpha_ref, next_ref, held_ref = refs
     else:
         out_ref, row_ref, next_ref, vector_ref, alpha_ref, held_ref = refs
     mine = nc * nb
+    chunks = mine // CHUNK
     periods = field_ref.shape[0]
     per_dev = row_ref.shape[0]
     subs = ROWS
     rows = sum(ref.shape[0] for ref in coef_refs) // no
     coef_refs = pieces(coef_refs, no, rows)
+    ahead = no <= 4
     for s in range(no):
-        held_ref[s] = coef_refs[s][:mine, :]
+        if ahead:
+            for q in range(chunks):
+                wide_ref[s * chunks + q] = widen(coef_refs[s][q * CHUNK:(q + 1) * CHUNK, :], pick_ref)[:CR * modes]
+        else:
+            held_ref[s] = coef_refs[s][:mine, :]
     for sum_ref in sum_refs:
         sum_ref[...] = jnp.zeros_like(sum_ref)
+    gain = jnp.sum(tree_sum(ref[mine:mine + subs, :] for ref in coef_refs), keepdims=True)
+    alpha_ref[...] = jnp.broadcast_to(1.0 + gain, alpha_ref.shape)
+    norm = norm_ref[0:1, :]
+    scale = 1.0 / norm
+    for copy in copies:
+        copy.wait()
+    own = ids_ref[0, 3 * nb]
 
     def group(at, carry):
         found = [at * ways + i for i in range(ways)]
         if permuted(no):
-            found = [own_ref[0] ^ at_i for at_i in found]
-        for chunk in range(0, mine, CHUNK):
-            for at_i, wide_ref in zip(found, wide_refs):
-                left = split(held_ref[at_i, chunk:chunk + CHUNK, :])
-                wide = lax.dot_general(left, pick_ref[...], (((0,), (0,)), ((), ())), preferred_element_type=F32)
-                wide_ref[...] = wide[:CR * modes]
+            found = [own ^ at_i for at_i in found]
+        for q in range(chunks):
+            slots = [at_i * chunks + q for at_i in found] if ahead else range(ways)
+            if not ahead:
+                for at_i, slot in zip(found, slots):
+                    wide_ref[slot] = widen(held_ref[at_i, q * CHUNK:(q + 1) * CHUNK, :], pick_ref)[:CR * modes]
             for at in range(CHUNK):
-                for at_i, wide_ref, sum_ref in zip(found, wide_refs, sum_refs):
-                    period = all_ref[2 * at_i, chunk + at]
-                    row = all_ref[2 * at_i + 1, chunk + at] * CR
+                for at_i, slot, sum_ref in zip(found, slots, sum_refs):
+                    period = all_ref[2 * at_i, q * CHUNK + at]
+                    row = all_ref[2 * at_i + 1, q * CHUNK + at] * CR
                     total = sum_ref[period]
                     for r in range(CR):
-                        coef = wide_ref[r * modes:(r + 1) * modes, at * 128:(at + 1) * 128]
+                        coef = wide_ref[slot, r * modes:(r + 1) * modes, at * 128:(at + 1) * 128]
                         total += coef * lat_ref[row + r]
                     sum_ref[period] = total
         return carry
@@ -295,10 +323,6 @@
             group(at, 0)
     else:
         lax.fori_loop(0, no // ways, group, 0)
-    gain = jnp.sum(tree_sum(ref[mine:mine + subs, :] for ref in coef_refs), keepdims=True)
-    alpha_ref[...] = jnp.broadcast_to(1.0 + gain, alpha_ref.shape)
-    norm = norm_ref[0:1, :]
-    scale = 1.0 / norm
     for p in range(periods):
         vector = field_ref[p] * scale
         if not last:
@@ -308,11 +332,11 @@
             rest -= prior_ref[p] * norm
         next_ref[p] = rest
     for l in range(per_dev):
-        row_ref[l] = field_ref[own_ref[0] * per_dev + l] * scale
+        row_ref[l] = field_ref[own * per_dev + l] * scale
     if last:
         out_ref[...] = fold(next_ref)
         for l in range(per_dev):
-            mine_ref[l] = next_ref[own_ref[0] * per_dev + l]
+            mine_ref[l] = next_ref[own * per_dev + l]
     else:
         forward(dims, next_ref, lat_ref, foot_ref, ids_ref, out_ref)
 
@@ -381,8 +405,7 @@
     if modes != held:
         start = jnp.pad(start, ((0, 0), (0, modes - held), (0, 0)))
         lat_mats = jnp.pad(lat_mats, ((0, modes - held), (0, 0), (0, 0)))
-    own = lax.axis_index("obs").astype(jnp.int32).reshape(1)
-    cell = lax.axis_index("cell").astype(jnp.int32).reshape(1)
+    place = lax.axis_index(("obs", "cell")).astype(jnp.int32).reshape(1)
 
     start = start.reshape(per_dev * modes, lat_rows)
     near = share(start, "obs")
@@ -390,8 +413,8 @@
     hats, weights = call(
         functools.partial(transform_kernel, dims),
         (jax.ShapeDtypeStruct((nc, foot_rows + 16, ob), BF16), shape((subs, ob))),
-        [SMEM] + [ANY] * 7,
-        cell, jnp.asarray(high), jnp.asarray(low), footprints, blk_off, blk_sub, counts, rinv.reshape(subs, ob),
+        [ANY] * 8,
+        place, jnp.asarray(high), jnp.asarray(low), footprints, blk_off, blk_sub, counts, rinv.reshape(subs, ob),
         scratch=[
             pltpu.VMEM(high.shape, BF16),
             pltpu.VMEM(low.shape, BF16),
@@ -400,7 +423,8 @@
             pltpu.SMEM((nb,), jnp.int32),
             pltpu.SMEM((subs,), jnp.int32),
             pltpu.VMEM((subs, ob), F32),
-            pltpu.SemaphoreType.DMA((7,)),
+            pltpu.SMEM((1,), jnp.int32),
+            pltpu.SemaphoreType.DMA((8,)),
         ],
         limit=60,
     )
@@ -435,8 +459,8 @@
             jax.ShapeDtypeStruct((mine, TERMS * subs), BF16),
             shape((ROWS, 128)),
         ),
-        [SMEM] + [VMEM] * (2 + len(near)),
-        own, lat, came, *near,
+        [VMEM] * (2 + len(near)),
+        lat, came, *near,
         scratch=[pltpu.SMEM((nc, 128), jnp.int32), pltpu.SemaphoreType.DMA],
     )
     ways = min(no, WAYS)
@@ -471,12 +495,14 @@
                 *([] if last else [field_shape]),
                 small,
             ),
-            [SMEM] * 3 + [VMEM] * (5 + len(before) + len(coefs)),
-            own, ids, every, lat, foot, pick, norm, field, *before, *coefs,
+            [VMEM] * (7 + len(before) + len(coefs)),
+            ids, every, lat, foot, pick, norm, field, *before, *coefs,
             scratch=[pltpu.VMEM(field_shape.shape, F32)] * last
             + [pltpu.VMEM((no, mine, 128), F32)]
             + [pltpu.VMEM(field_shape.shape, F32)] * ways
-            + [pltpu.VMEM((CR * modes, CHUNK * 128), F32)] * ways,
+            + [pltpu.VMEM((no * mine // CHUNK if no <= 4 else ways, CR * modes, CHUNK * 128), F32)]
+            + [pltpu.SMEM((nc, 128), jnp.int32), pltpu.SMEM((2 * no, 128), jnp.int32)]
+            + [pltpu.SemaphoreType.DMA((2,))],
             limit=16,
         )
         vector = None if last else vector[0]

time: 78.1 us -> 78.8 us (level)
  no operation moved by 1% of the time
where the time goes in v11:
time: 78.8 us; the launch traced here: 78.4 us
  starting transfers between devices  37.4 us (47%)
  waiting for transfers between devices  24.9 us (32%)
  Pallas kernels  14.6 us (19%)
    ppermute x12, starting transfers between devices, share(): lax.ppermute(array, axis, [(d, d ^ s) for d in range(size)])  17.9 us
    pallas_call x15, Pallas kernels, call(): pl.pallas_call(kernel, out_shape=outs, in_specs=specs, out_specs=jax.tree...  14.6 us
    ppermute x12, starting transfers between devices, addends(): lax.ppermute(both, axis, [(d, d ^ s) for d in range(size)])  14 us
    ppermute x12, waiting for transfers between devices, addends(): lax.ppermute(both, axis, [(d, d ^ s) for d in range(size)])  11.6 us
    ppermute x12, waiting for transfers between devices, share(): lax.ppermute(array, axis, [(d, d ^ s) for d in range(size)])  8.62 us
    all_to_all x1, starting transfers between devices, swap(): return lax.all_to_all(array, axis, split_axis=0, concat_axis=0, tiled=True)  5.18 us
    ppermute x4, waiting for transfers between devices, addends(): other = lax.ppermute(array, axis, [(d, d ^ 1) for d in range(size)])  4.63 us
  transfers between devices with their start and end apart: 29, of which 25 were waited for; matrix products, arithmetic and copies ran while one was open for 0% of the time, Pallas kernels for 3%

profile of v11, /device:TPU:0, one launch (start us, length us, event | category | flops | bytes accessed | tf_op | source)
XLA Modules:
  0.0 78.4 jit_solution(1129811176311032379)
XLA Ops:
  0.6 2.7 %shard_map.104 = (bf16[8,208,128]{2,1,0:T(8,128)(2,1)}, f32[8,128]{1,0:T(8,128)}) custom-call(s32[1]{0:T(128)} %bitcast.1.place_any, bf16[384,384]{1,0:T(8,128)(2,1)} %constant.14.clone.high_any, bf16[384,384]{1,0:T(8,128)(2,1)} %constant.15.clone.low_any, bf16[2,128,768]{2,1,0:T(8,128)(2,1)} %foot_any.1, s32[2]{0:T(128)} %off_any.1, s32[2]{0:T(128)} %sub_any.1, ...), custom_call_target="tpu_custom_call" | custom-call | tf_op jit(solution)/shard_map/pallas_call | solution.py:40
  3.3 5.2 %all-to-all-start = ((bf16[8,208,128]{2,1,0:T(8,128)(2,1)}), bf16[8,208,128]{2,1,0:T(8,128)(2,1)}, u32[]{:S(2)}, u32[]{:S(2)}) async-start(bf16[8,208,128]{2,1,0:T(8,128)(2,1)} %get-tuple-element.39), calls=%async_computation | async-start | bytes 851968 | tf_op jit(solution)/shard_map/all_to_all | solution.py:386
  8.5 4.1 %collective-permute-start.2 = (f32[48,128]{1,0:T(8,128)}, f32[48,128]{1,0:T(8,128)S(1)}, u32[]{:S(2)}, u32[]{:S(2)}) collective-permute-start(f32[48,128]{1,0:T(8,128)} %bitcast.3), channel_id=1, source_target_pairs={{0,24},{8,16},{16,8},{24,0},{1,25},{9,17},{17,9},{25,1},{2,26},{10... | collective-permute-start | bytes 73736 | tf_op jit(solution)/shard_map/ppermute | solution.py:373
  12.6 0.6 collective-permute-start
  13.2 0.8 copy-done.1
  14.0 2.3 %shard_map.105 = (f32[128,48,128]{2,1,0:T(8,128)S(1)}, f32[48,128]{1,0:T(8,128)S(1)}, bf16[48,2048]{1,0:T(8,128)(2,1)S(1)}) custom-call(f32[48,128,128]{2,1,0:T(8,128)} %lat_any, f32[48,128]{1,0:T(8,128)S(1)} %bitcast.6), custom_call_target="tpu_custom_call" | custom-call | bytes 6340608 | tf_op jit(solution)/shard_map/pallas_call | solution.py:40
  16.3 1.2 %collective-permute-done.1.refs_2_ = f32[48,128]{1,0:T(8,128)S(1)} collective-permute-done((f32[48,128]{1,0:T(8,128)}, f32[48,128]{1,0:T(8,128)S(1)}, u32[]{:S(2)}, u32[]{:S(2)}) %collective-permute-start.1) | collective-permute-done | bytes 24608 | tf_op jit(solution)/shard_map/ppermute | solution.py:373
  17.5 1.9 %shard_map.106 = (f32[16,128]{1,0:T(8,128)S(1)}, f32[4,48,128]{2,1,0:T(8,128)S(1)}, bf16[8,192,128]{2,1,0:T(8,128)(2,1)S(1)}, s32[8,128]{1,0:T(8,128)S(1)}, bf16...) custom-call(f32[128,48,128]{2,1,0:T(8,128)S(1)} %get-tuple-element.38.lat_ref, bf16[8,208,128]{2,1,0:T(8,128)(2,1)} %all-to-all-done.came_ref, ...), custom_call_target="tpu_custom_call" | custom-call | tf_op jit(solution)/shard_map/pallas_call | solution.py:40
  19.5 1.2 %collective-permute-done.3.other_ref = f32[16,128]{1,0:T(8,128)S(1)} collective-permute-done((f32[16,128]{1,0:T(8,128)S(1)}, f32[16,128]{1,0:T(8,128)S(1)}, u32[]{:S(2)}, u32[]{:S(2)}) %collective-permute-start.3) | collective-permute-done | bytes 8224 | tf_op jit(solution)/shard_map/ppermute | solution.py:380
  20.7 2.8 %collective-permute-start.6 = (f32[16,128]{1,0:T(8,128)S(1)}, f32[16,128]{1,0:T(8,128)S(1)}, u32[]{:S(2)}, u32[]{:S(2)}) collective-permute-start(f32[16,128]{1,0:T(8,128)S(1)} %shard_map.107.refs_1_), channel_id=1, source_target_pairs={{0,6},{1,7},{2,4},{3,5},{4,2},{5,3},{6,0},{7,1},{8,14},{9,15},{10,... | collective-permute-start | bytes 24584 | tf_op jit(solution)/shard_map/ppermute | solution.py:382
  24.2 1.1 %collective-permute-done.6.refs_4_ = f32[16,128]{1,0:T(8,128)S(1)} collective-permute-done((f32[16,128]{1,0:T(8,128)S(1)}, f32[16,128]{1,0:T(8,128)S(1)}, u32[]{:S(2)}, u32[]{:S(2)}) %collective-permute-start.6) | collective-permute-done | bytes 8224 | tf_op jit(solution)/shard_map/ppermute | solution.py:382
  25.2 1.9 %collective-permute-done.5.refs_3_ = f32[16,128]{1,0:T(8,128)S(1)} collective-permute-done((f32[16,128]{1,0:T(8,128)S(1)}, f32[16,128]{1,0:T(8,128)S(1)}, u32[]{:S(2)}, u32[]{:S(2)}) %collective-permute-start.5) | collective-permute-done | bytes 8224 | tf_op jit(solution)/shard_map/ppermute | solution.py:382
  28.1 2.6 %collective-permute-start.9 = (f32[32,128]{1,0:T(8,128)S(1)}, f32[32,128]{1,0:T(8,128)S(1)}, u32[]{:S(2)}, u32[]{:S(2)}) collective-permute-start(f32[32,128]{1,0:T(8,128)S(1)} %get-tuple-element.46.refs_0_), channel_id=1, source_target_pairs={{0,24},{8,16},{16,8},{24,0},{1,25},{9,17},{17,9},{25,1},{2,26},{10... | collective-permute-start | bytes 49160 | tf_op jit(solution)/shard_map/ppermute | solution.py:373
  30.7 1.8 %collective-permute-start.7 = (f32[32,128]{1,0:T(8,128)S(1)}, f32[32,128]{1,0:T(8,128)S(1)}, u32[]{:S(2)}, u32[]{:S(2)}) collective-permute-start(f32[32,128]{1,0:T(8,128)S(1)} %get-tuple-element.46.refs_0_), channel_id=1, source_target_pairs={{0,8},{8,0},{16,24},{24,16},{1,9},{9,1},{17,25},{25,17},{2,10},{10... | collective-permute-start | bytes 49160 | tf_op jit(solution)/shard_map/ppermute | solution.py:373
  32.5 1.1 %collective-permute-done.9.refs_3_ = f32[32,128]{1,0:T(8,128)S(1)} collective-permute-done((f32[32,128]{1,0:T(8,128)S(1)}, f32[32,128]{1,0:T(8,128)S(1)}, u32[]{:S(2)}, u32[]{:S(2)}) %collective-permute-start.9) | collective-permute-done | bytes 16416 | tf_op jit(solution)/shard_map/ppermute | solution.py:373
  33.6 1.7 %collective-permute-done.8.refs_2_ = f32[32,128]{1,0:T(8,128)S(1)} collective-permute-done((f32[32,128]{1,0:T(8,128)S(1)}, f32[32,128]{1,0:T(8,128)S(1)}, u32[]{:S(2)}, u32[]{:S(2)}) %collective-permute-start.8) | collective-permute-done | bytes 16416 | tf_op jit(solution)/shard_map/ppermute | solution.py:373
  35.3 1.9 %shard_map.110 = (f32[16,128]{1,0:T(8,128)S(1)}, f32[1,48,128]{2,1,0:T(8,128)S(1)}, f32[4,48,128]{2,1,0:T(8,128)S(1)}, f32[4,48,128]{2,1,0:T(8,128)S(1)}, f32[8,128]{1,0:T(8,128)S(1)}) custom-call(s32[8,128]{1,0:T(8,128)S(1)} %get-tuple-element.41.ids_in, s32[8,128]{1,0:T(8,128)S(1)} %shard_map.109.all_in, f32[128,48,128]{2,1,0:T(8,128)S(1)} %get-tuple-element.38.lat_ref, ...), custom_call_target="tpu_custom_call" | custom-call | tf_op jit(solution)/shard_map/pallas_call | solution.py:40
  37.4 1.2 %collective-permute-done.10.other_ref = f32[16,128]{1,0:T(8,128)S(1)} collective-permute-done((f32[16,128]{1,0:T(8,128)S(1)}, f32[16,128]{1,0:T(8,128)S(1)}, u32[]{:S(2)}, u32[]{:S(2)}) %collective-permute-start.10) | collective-permute-done | bytes 8224 | tf_op jit(solution)/shard_map/ppermute | solution.py:380
  38.5 1.5 %collective-permute-start.13 = (f32[16,128]{1,0:T(8,128)S(1)}, f32[16,128]{1,0:T(8,128)S(1)}, u32[]{:S(2)}, u32[]{:S(2)}) collective-permute-start(f32[16,128]{1,0:T(8,128)S(1)} %shard_map.111.refs_0_), channel_id=1, source_target_pairs={{0,6},{1,7},{2,4},{3,5},{4,2},{5,3},{6,0},{7,1},{8,14},{9,15},{10,... | collective-permute-start | bytes 24584 | tf_op jit(solution)/shard_map/ppermute | solution.py:382
  40.0 1.3 %collective-permute-start.12 = (f32[16,128]{1,0:T(8,128)S(1)}, f32[16,128]{1,0:T(8,128)S(1)}, u32[]{:S(2)}, u32[]{:S(2)}) collective-permute-start(f32[16,128]{1,0:T(8,128)S(1)} %shard_map.111.refs_0_), channel_id=1, source_target_pairs={{0,4},{1,5},{2,6},{3,7},{4,0},{5,1},{6,2},{7,3},{8,12},{9,13},{10,... | collective-permute-start | bytes 24584 | tf_op jit(solution)/shard_map/ppermute | solution.py:382
  41.3 0.7 collective-permute-start.11
  42.0 1.1 %collective-permute-done.13.refs_3_ = f32[16,128]{1,0:T(8,128)S(1)} collective-permute-done((f32[16,128]{1,0:T(8,128)S(1)}, f32[16,128]{1,0:T(8,128)S(1)}, u32[]{:S(2)}, u32[]{:S(2)}) %collective-permute-start.13) | collective-permute-done | bytes 8224 | tf_op jit(solution)/shard_map/ppermute | solution.py:382
  43.1 0.6 collective-permute-done.12.refs_2_
  43.7 1.3 %collective-permute-done.11.refs_1_ = f32[16,128]{1,0:T(8,128)S(1)} collective-permute-done((f32[16,128]{1,0:T(8,128)S(1)}, f32[16,128]{1,0:T(8,128)S(1)}, u32[]{:S(2)}, u32[]{:S(2)}) %collective-permute-start.11) | collective-permute-done | bytes 8224 | tf_op jit(solution)/shard_map/ppermute | solution.py:382
  45.4 1.5 %collective-permute-start.16 = (f32[24,128]{1,0:T(8,128)S(1)}, f32[24,128]{1,0:T(8,128)S(1)}, u32[]{:S(2)}, u32[]{:S(2)}) collective-permute-start(f32[24,128]{1,0:T(8,128)S(1)} %get-tuple-element.54.refs_1_), channel_id=1, source_target_pairs={{0,24},{8,16},{16,8},{24,0},{1,25},{9,17},{17,9},{25,1},{2,26},{10... | collective-permute-start | bytes 36872 | tf_op jit(solution)/shard_map/ppermute | solution.py:373
  46.9 0.6 collective-permute-start.15
  47.5 2.3 %collective-permute-start.14 = (f32[24,128]{1,0:T(8,128)S(1)}, f32[24,128]{1,0:T(8,128)S(1)}, u32[]{:S(2)}, u32[]{:S(2)}) collective-permute-start(f32[24,128]{1,0:T(8,128)S(1)} %get-tuple-element.54.refs_1_), channel_id=1, source_target_pairs={{0,8},{8,0},{16,24},{24,16},{1,9},{9,1},{17,25},{25,17},{2,10},{10... | collective-permute-start | bytes 36872 | tf_op jit(solution)/shard_map/ppermute | solution.py:373
  49.8 1.1 %collective-permute-done.16.refs_4_ = f32[24,128]{1,0:T(8,128)S(1)} collective-permute-done((f32[24,128]{1,0:T(8,128)S(1)}, f32[24,128]{1,0:T(8,128)S(1)}, u32[]{:S(2)}, u32[]{:S(2)}) %collective-permute-start.16) | collective-permute-done | bytes 12320 | tf_op jit(solution)/shard_map/ppermute | solution.py:373
  51.6 1.9 %shard_map.113 = (f32[16,128]{1,0:T(8,128)S(1)}, f32[1,48,128]{2,1,0:T(8,128)S(1)}, f32[4,48,128]{2,1,0:T(8,128)S(1)}, f32[4,48,128]{2,1,0:T(8,128)S(1)}, f32[8,128]{1,0:T(8,128)S(1)}) custom-call(s32[8,128]{1,0:T(8,128)S(1)} %get-tuple-element.41.ids_in, s32[8,128]{1,0:T(8,128)S(1)} %shard_map.109.all_in, f32[128,48,128]{2,1,0:T(8,128)S(1)} %get-tuple-element.38.lat_ref, ...), custom_call_target="tpu_custom_call" | custom-call | tf_op jit(solution)/shard_map/pallas_call | solution.py:40
  53.6 1.2 %collective-permute-done.17.other_ref = f32[16,128]{1,0:T(8,128)S(1)} collective-permute-done((f32[16,128]{1,0:T(8,128)S(1)}, f32[16,128]{1,0:T(8,128)S(1)}, u32[]{:S(2)}, u32[]{:S(2)}) %collective-permute-start.17) | collective-permute-done | bytes 8224 | tf_op jit(solution)/shard_map/ppermute | solution.py:380
  54.8 1.7 %collective-permute-start.20 = (f32[16,128]{1,0:T(8,128)S(1)}, f32[16,128]{1,0:T(8,128)S(1)}, u32[]{:S(2)}, u32[]{:S(2)}) collective-permute-start(f32[16,128]{1,0:T(8,128)S(1)} %shard_map.114.refs_0_), channel_id=1, source_target_pairs={{0,6},{1,7},{2,4},{3,5},{4,2},{5,3},{6,0},{7,1},{8,14},{9,15},{10,... | collective-permute-start | bytes 24584 | tf_op jit(solution)/shard_map/ppermute | solution.py:382
  57.0 1.3 %collective-permute-start.18 = (f32[16,128]{1,0:T(8,128)S(1)}, f32[16,128]{1,0:T(8,128)S(1)}, u32[]{:S(2)}, u32[]{:S(2)}) collective-permute-start(f32[16,128]{1,0:T(8,128)S(1)} %shard_map.114.refs_0_), channel_id=1, source_target_pairs={{0,2},{1,3},{2,0},{3,1},{4,6},{5,7},{6,4},{7,5},{8,10},{9,11},{10,... | collective-permute-start | bytes 24584 | tf_op jit(solution)/shard_map/ppermute | solution.py:382
  58.3 1.1 %collective-permute-done.20.refs_3_ = f32[16,128]{1,0:T(8,128)S(1)} collective-permute-done((f32[16,128]{1,0:T(8,128)S(1)}, f32[16,128]{1,0:T(8,128)S(1)}, u32[]{:S(2)}, u32[]{:S(2)}) %collective-permute-start.20) | collective-permute-done | bytes 8224 | tf_op jit(solution)/shard_map/ppermute | solution.py:382
  59.3 0.8 collective-permute-done.19.refs_2_
  61.1 2.5 %collective-permute-start.23 = (f32[24,128]{1,0:T(8,128)S(1)}, f32[24,128]{1,0:T(8,128)S(1)}, u32[]{:S(2)}, u32[]{:S(2)}) collective-permute-start(f32[24,128]{1,0:T(8,128)S(1)} %get-tuple-element.59.refs_1_), channel_id=1, source_target_pairs={{0,24},{8,16},{16,8},{24,0},{1,25},{9,17},{17,9},{25,1},{2,26},{10... | collective-permute-start | bytes 36872 | tf_op jit(solution)/shard_map/ppermute | solution.py:373
  63.6 0.9 %collective-permute-start.22 = (f32[24,128]{1,0:T(8,128)S(1)}, f32[24,128]{1,0:T(8,128)S(1)}, u32[]{:S(2)}, u32[]{:S(2)}) collective-permute-start(f32[24,128]{1,0:T(8,128)S(1)} %get-tuple-element.59.refs_1_), channel_id=1, source_target_pairs={{0,16},{8,24},{16,0},{24,8},{1,17},{9,25},{17,1},{25,9},{2,18},{10... | collective-permute-start | bytes 36872 | tf_op jit(solution)/shard_map/ppermute | solution.py:373
  64.5 1.0 %collective-permute-start.21 = (f32[24,128]{1,0:T(8,128)S(1)}, f32[24,128]{1,0:T(8,128)S(1)}, u32[]{:S(2)}, u32[]{:S(2)}) collective-permute-start(f32[24,128]{1,0:T(8,128)S(1)} %get-tuple-element.59.refs_1_), channel_id=1, source_target_pairs={{0,8},{8,0},{16,24},{24,16},{1,9},{9,1},{17,25},{25,17},{2,10},{10... | collective-permute-start | bytes 36872 | tf_op jit(solution)/shard_map/ppermute | solution.py:373
  65.5 1.1 %collective-permute-done.23.refs_4_ = f32[24,128]{1,0:T(8,128)S(1)} collective-permute-done((f32[24,128]{1,0:T(8,128)S(1)}, f32[24,128]{1,0:T(8,128)S(1)}, u32[]{:S(2)}, u32[]{:S(2)}) %collective-permute-start.23) | collective-permute-done | bytes 12320 | tf_op jit(solution)/shard_map/ppermute | solution.py:373
  66.6 1.6 %collective-permute-done.22.refs_3_ = f32[24,128]{1,0:T(8,128)S(1)} collective-permute-done((f32[24,128]{1,0:T(8,128)S(1)}, f32[24,128]{1,0:T(8,128)S(1)}, u32[]{:S(2)}, u32[]{:S(2)}) %collective-permute-start.22) | collective-permute-done | bytes 12320 | tf_op jit(solution)/shard_map/ppermute | solution.py:373
  68.3 1.7 %shard_map.116 = (f32[8,128]{1,0:T(8,128)S(1)}, f32[1,48,128]{2,1,0:T(8,128)S(1)}, f32[1,48,128]{2,1,0:T(8,128)S(1)}, f32[8,128]{1,0:T(8,128)S(1)}) custom-call(s32[8,128]{1,0:T(8,128)S(1)} %get-tuple-element.41.ids_in, s32[8,128]{1,0:T(8,128)S(1)} %shard_map.109.all_in, f32[128,48,128]{2,1,0:T(8,128)S(1)} %get-tuple-element.38.lat_ref, ...), custom_call_target="tpu_custom_call" | custom-call | tf_op jit(solution)/shard_map/pallas_call | solution.py:40
  70.1 1.2 %collective-permute-done.24.other_ref = f32[8,128]{1,0:T(8,128)S(1)} collective-permute-done((f32[8,128]{1,0:T(8,128)S(1)}, f32[8,128]{1,0:T(8,128)S(1)}, u32[]{:S(2)}, u32[]{:S(2)}) %collective-permute-start.24) | collective-permute-done | bytes 4128 | tf_op jit(solution)/shard_map/ppermute | solution.py:380
  71.2 1.5 %collective-permute-start.27 = (f32[8,128]{1,0:T(8,128)S(1)}, f32[8,128]{1,0:T(8,128)S(1)}, u32[]{:S(2)}, u32[]{:S(2)}) collective-permute-start(f32[8,128]{1,0:T(8,128)S(1)} %shard_map.117.refs_0_), channel_id=1, source_target_pairs={{0,6},{1,7},{2,4},{3,5},{4,2},{5,3},{6,0},{7,1},{8,14},{9,15},{10,... | collective-permute-start | bytes 12296 | tf_op jit(solution)/shard_map/ppermute | solution.py:382
  72.7 1.3 %collective-permute-start.26 = (f32[8,128]{1,0:T(8,128)S(1)}, f32[8,128]{1,0:T(8,128)S(1)}, u32[]{:S(2)}, u32[]{:S(2)}) collective-permute-start(f32[8,128]{1,0:T(8,128)S(1)} %shard_map.117.refs_0_), channel_id=1, source_target_pairs={{0,4},{1,5},{2,6},{3,7},{4,0},{5,1},{6,2},{7,3},{8,12},{9,13},{10,... | collective-permute-start | bytes 12296 | tf_op jit(solution)/shard_map/ppermute | solution.py:382
  74.0 0.7 collective-permute-start.25
  74.7 1.0 %collective-permute-done.27.refs_3_ = f32[8,128]{1,0:T(8,128)S(1)} collective-permute-done((f32[8,128]{1,0:T(8,128)S(1)}, f32[8,128]{1,0:T(8,128)S(1)}, u32[]{:S(2)}, u32[]{:S(2)}) %collective-permute-start.27) | collective-permute-done | bytes 4128 | tf_op jit(solution)/shard_map/ppermute | solution.py:382
  75.7 0.6 collective-permute-done.26.refs_2_
  76.3 1.3 %collective-permute-done.25.refs_1_ = f32[8,128]{1,0:T(8,128)S(1)} collective-permute-done((f32[8,128]{1,0:T(8,128)S(1)}, f32[8,128]{1,0:T(8,128)S(1)}, u32[]{:S(2)}, u32[]{:S(2)}) %collective-permute-start.25) | collective-permute-done | bytes 4128 | tf_op jit(solution)/shard_map/ppermute | solution.py:382
  77.6 0.8 shard_map.118
  (29 shorter events, 4.8 us)
Async XLA Ops:
  3.3 14.2 %all-to-all-start = ((bf16[8,208,128]{2,1,0:T(8,128)(2,1)}), bf16[8,208,128]{2,1,0:T(8,128)(2,1)}, u32[]{:S(2)}, u32[]{:S(2)}) async-start(bf16[8,208,128]{2,1,0:T(8,128)(2,1)} %get-tuple-element.39), calls=%async_computation | async-start | bytes 851968 | tf_op jit(solution)/shard_map/all_to_all | solution.py:386
  8.5 7.8 %collective-permute-start.2 = (f32[48,128]{1,0:T(8,128)}, f32[48,128]{1,0:T(8,128)S(1)}, u32[]{:S(2)}, u32[]{:S(2)}) collective-permute-start(f32[48,128]{1,0:T(8,128)} %bitcast.3), channel_id=1, source_target_pairs={{0,24},{8,16},{16,8},{24,0},{1,25},{9,17},{17,9},{25,1},{2,26},{10... | collective-permute-start | bytes 73736 | tf_op jit(solution)/shard_map/ppermute | solution.py:373
  12.5 4.9 %collective-permute-start.1 = (f32[48,128]{1,0:T(8,128)}, f32[48,128]{1,0:T(8,128)S(1)}, u32[]{:S(2)}, u32[]{:S(2)}) collective-permute-start(f32[48,128]{1,0:T(8,128)} %bitcast.4), channel_id=1, source_target_pairs={{0,16},{8,24},{16,0},{24,8},{1,17},{9,25},{17,1},{25,9},{2,18},{10... | collective-permute-start | bytes 73736 | tf_op jit(solution)/shard_map/ppermute | solution.py:373
  12.6 4.9 %collective-permute-start = (f32[48,128]{1,0:T(8,128)}, f32[48,128]{1,0:T(8,128)S(1)}, u32[]{:S(2)}, u32[]{:S(2)}) collective-permute-start(f32[48,128]{1,0:T(8,128)} %bitcast.5), channel_id=1, source_target_pairs={{0,8},{8,0},{16,24},{24,16},{1,9},{9,1},{17,25},{25,17},{2,10},{10... | collective-permute-start | bytes 73736 | tf_op jit(solution)/shard_map/ppermute | solution.py:373
  13.2 0.8 copy-start.1
  14.0 13.7 %copy-start = (f32[8,128]{1,0:T(8,128)S(1)}, f32[8,128]{1,0:T(8,128)}, u32[]{:S(2)}) copy-start(f32[8,128]{1,0:T(8,128)} %get-tuple-element.35.weight_ref) | copy-start | bytes 12292
  19.4 1.2 %collective-permute-start.3 = (f32[16,128]{1,0:T(8,128)S(1)}, f32[16,128]{1,0:T(8,128)S(1)}, u32[]{:S(2)}, u32[]{:S(2)}) collective-permute-start(f32[16,128]{1,0:T(8,128)S(1)} %get-tuple-element.45.one_ref), channel_id=1, source_target_pairs={{0,1},{1,0},{2,3},{3,2},{4,5},{5,4},{6,7},{7,6},{8,9},{9,8},{10,11... | collective-permute-start | bytes 24584 | tf_op jit(solution)/shard_map/ppermute | solution.py:380
  20.7 4.5 %collective-permute-start.6 = (f32[16,128]{1,0:T(8,128)S(1)}, f32[16,128]{1,0:T(8,128)S(1)}, u32[]{:S(2)}, u32[]{:S(2)}) collective-permute-start(f32[16,128]{1,0:T(8,128)S(1)} %shard_map.107.refs_1_), channel_id=1, source_target_pairs={{0,6},{1,7},{2,4},{3,5},{4,2},{5,3},{6,0},{7,1},{8,14},{9,15},{10,... | collective-permute-start | bytes 24584 | tf_op jit(solution)/shard_map/ppermute | solution.py:382
  23.4 3.7 %collective-permute-start.5 = (f32[16,128]{1,0:T(8,128)S(1)}, f32[16,128]{1,0:T(8,128)S(1)}, u32[]{:S(2)}, u32[]{:S(2)}) collective-permute-start(f32[16,128]{1,0:T(8,128)S(1)} %shard_map.107.refs_1_), channel_id=1, source_target_pairs={{0,4},{1,5},{2,6},{3,7},{4,0},{5,1},{6,2},{7,3},{8,12},{9,13},{10,... | collective-permute-start | bytes 24584 | tf_op jit(solution)/shard_map/ppermute | solution.py:382
  24.0 3.7 %collective-permute-start.4 = (f32[16,128]{1,0:T(8,128)S(1)}, f32[16,128]{1,0:T(8,128)S(1)}, u32[]{:S(2)}, u32[]{:S(2)}) collective-permute-start(f32[16,128]{1,0:T(8,128)S(1)} %shard_map.107.refs_1_), channel_id=1, source_target_pairs={{0,2},{1,3},{2,0},{3,1},{4,6},{5,7},{6,4},{7,5},{8,10},{9,11},{10,... | collective-permute-start | bytes 24584 | tf_op jit(solution)/shard_map/ppermute | solution.py:382
  28.1 5.6 %collective-permute-start.9 = (f32[32,128]{1,0:T(8,128)S(1)}, f32[32,128]{1,0:T(8,128)S(1)}, u32[]{:S(2)}, u32[]{:S(2)}) collective-permute-start(f32[32,128]{1,0:T(8,128)S(1)} %get-tuple-element.46.refs_0_), channel_id=1, source_target_pairs={{0,24},{8,16},{16,8},{24,0},{1,25},{9,17},{17,9},{25,1},{2,26},{10... | collective-permute-start | bytes 49160 | tf_op jit(solution)/shard_map/ppermute | solution.py:373
  30.7 4.6 %collective-permute-start.8 = (f32[32,128]{1,0:T(8,128)S(1)}, f32[32,128]{1,0:T(8,128)S(1)}, u32[]{:S(2)}, u32[]{:S(2)}) collective-permute-start(f32[32,128]{1,0:T(8,128)S(1)} %get-tuple-element.46.refs_0_), channel_id=1, source_target_pairs={{0,16},{8,24},{16,0},{24,8},{1,17},{9,25},{17,1},{25,9},{2,18},{10... | collective-permute-start | bytes 49160 | tf_op jit(solution)/shard_map/ppermute | solution.py:373
  30.7 4.6 %collective-permute-start.7 = (f32[32,128]{1,0:T(8,128)S(1)}, f32[32,128]{1,0:T(8,128)S(1)}, u32[]{:S(2)}, u32[]{:S(2)}) collective-permute-start(f32[32,128]{1,0:T(8,128)S(1)} %get-tuple-element.46.refs_0_), channel_id=1, source_target_pairs={{0,8},{8,0},{16,24},{24,16},{1,9},{9,1},{17,25},{25,17},{2,10},{10... | collective-permute-start | bytes 49160 | tf_op jit(solution)/shard_map/ppermute | solution.py:373
  37.3 1.2 %collective-permute-start.10 = (f32[16,128]{1,0:T(8,128)S(1)}, f32[16,128]{1,0:T(8,128)S(1)}, u32[]{:S(2)}, u32[]{:S(2)}) collective-permute-start(f32[16,128]{1,0:T(8,128)S(1)} %get-tuple-element.50.one_ref), channel_id=1, source_target_pairs={{0,1},{1,0},{2,3},{3,2},{4,5},{5,4},{6,7},{7,6},{8,9},{9,8},{10,11... | collective-permute-start | bytes 24584 | tf_op jit(solution)/shard_map/ppermute | solution.py:380
  38.5 4.5 %collective-permute-start.13 = (f32[16,128]{1,0:T(8,128)S(1)}, f32[16,128]{1,0:T(8,128)S(1)}, u32[]{:S(2)}, u32[]{:S(2)}) collective-permute-start(f32[16,128]{1,0:T(8,128)S(1)} %shard_map.111.refs_0_), channel_id=1, source_target_pairs={{0,6},{1,7},{2,4},{3,5},{4,2},{5,3},{6,0},{7,1},{8,14},{9,15},{10,... | collective-permute-start | bytes 24584 | tf_op jit(solution)/shard_map/ppermute | solution.py:382
  40.0 3.7 %collective-permute-start.12 = (f32[16,128]{1,0:T(8,128)S(1)}, f32[16,128]{1,0:T(8,128)S(1)}, u32[]{:S(2)}, u32[]{:S(2)}) collective-permute-start(f32[16,128]{1,0:T(8,128)S(1)} %shard_map.111.refs_0_), channel_id=1, source_target_pairs={{0,4},{1,5},{2,6},{3,7},{4,0},{5,1},{6,2},{7,3},{8,12},{9,13},{10,... | collective-permute-start | bytes 24584 | tf_op jit(solution)/shard_map/ppermute | solution.py:382
  41.3 3.7 %collective-permute-start.11 = (f32[16,128]{1,0:T(8,128)S(1)}, f32[16,128]{1,0:T(8,128)S(1)}, u32[]{:S(2)}, u32[]{:S(2)}) collective-permute-start(f32[16,128]{1,0:T(8,128)S(1)} %shard_map.111.refs_0_), channel_id=1, source_target_pairs={{0,2},{1,3},{2,0},{3,1},{4,6},{5,7},{6,4},{7,5},{8,10},{9,11},{10,... | collective-permute-start | bytes 24584 | tf_op jit(solution)/shard_map/ppermute | solution.py:382
  45.4 5.5 %collective-permute-start.16 = (f32[24,128]{1,0:T(8,128)S(1)}, f32[24,128]{1,0:T(8,128)S(1)}, u32[]{:S(2)}, u32[]{:S(2)}) collective-permute-start(f32[24,128]{1,0:T(8,128)S(1)} %get-tuple-element.54.refs_1_), channel_id=1, source_target_pairs={{0,24},{8,16},{16,8},{24,0},{1,25},{9,17},{17,9},{25,1},{2,26},{10... | collective-permute-start | bytes 36872 | tf_op jit(solution)/shard_map/ppermute | solution.py:373
  46.9 4.6 %collective-permute-start.15 = (f32[24,128]{1,0:T(8,128)S(1)}, f32[24,128]{1,0:T(8,128)S(1)}, u32[]{:S(2)}, u32[]{:S(2)}) collective-permute-start(f32[24,128]{1,0:T(8,128)S(1)} %get-tuple-element.54.refs_1_), channel_id=1, source_target_pairs={{0,16},{8,24},{16,0},{24,8},{1,17},{9,25},{17,1},{25,9},{2,18},{10... | collective-permute-start | bytes 36872 | tf_op jit(solution)/shard_map/ppermute | solution.py:373
  47.5 4.1 %collective-permute-start.14 = (f32[24,128]{1,0:T(8,128)S(1)}, f32[24,128]{1,0:T(8,128)S(1)}, u32[]{:S(2)}, u32[]{:S(2)}) collective-permute-start(f32[24,128]{1,0:T(8,128)S(1)} %get-tuple-element.54.refs_1_), channel_id=1, source_target_pairs={{0,8},{8,0},{16,24},{24,16},{1,9},{9,1},{17,25},{25,17},{2,10},{10... | collective-permute-start | bytes 36872 | tf_op jit(solution)/shard_map/ppermute | solution.py:373
  53.6 1.2 %collective-permute-start.17 = (f32[16,128]{1,0:T(8,128)S(1)}, f32[16,128]{1,0:T(8,128)S(1)}, u32[]{:S(2)}, u32[]{:S(2)}) collective-permute-start(f32[16,128]{1,0:T(8,128)S(1)} %get-tuple-element.55.one_ref), channel_id=1, source_target_pairs={{0,1},{1,0},{2,3},{3,2},{4,5},{5,4},{6,7},{7,6},{8,9},{9,8},{10,11... | collective-permute-start | bytes 24584 | tf_op jit(solution)/shard_map/ppermute | solution.py:380
  54.8 4.5 %collective-permute-start.20 = (f32[16,128]{1,0:T(8,128)S(1)}, f32[16,128]{1,0:T(8,128)S(1)}, u32[]{:S(2)}, u32[]{:S(2)}) collective-permute-start(f32[16,128]{1,0:T(8,128)S(1)} %shard_map.114.refs_0_), channel_id=1, source_target_pairs={{0,6},{1,7},{2,4},{3,5},{4,2},{5,3},{6,0},{7,1},{8,14},{9,15},{10,... | collective-permute-start | bytes 24584 | tf_op jit(solution)/shard_map/ppermute | solution.py:382
  56.5 3.7 %collective-permute-start.19 = (f32[16,128]{1,0:T(8,128)S(1)}, f32[16,128]{1,0:T(8,128)S(1)}, u32[]{:S(2)}, u32[]{:S(2)}) collective-permute-start(f32[16,128]{1,0:T(8,128)S(1)} %shard_map.114.refs_0_), channel_id=1, source_target_pairs={{0,4},{1,5},{2,6},{3,7},{4,0},{5,1},{6,2},{7,3},{8,12},{9,13},{10,... | collective-permute-start | bytes 24584 | tf_op jit(solution)/shard_map/ppermute | solution.py:382
  57.0 3.7 %collective-permute-start.18 = (f32[16,128]{1,0:T(8,128)S(1)}, f32[16,128]{1,0:T(8,128)S(1)}, u32[]{:S(2)}, u32[]{:S(2)}) collective-permute-start(f32[16,128]{1,0:T(8,128)S(1)} %shard_map.114.refs_0_), channel_id=1, source_target_pairs={{0,2},{1,3},{2,0},{3,1},{4,6},{5,7},{6,4},{7,5},{8,10},{9,11},{10,... | collective-permute-start | bytes 24584 | tf_op jit(solution)/shard_map/ppermute | solution.py:382
  61.1 5.5 %collective-permute-start.23 = (f32[24,128]{1,0:T(8,128)S(1)}, f32[24,128]{1,0:T(8,128)S(1)}, u32[]{:S(2)}, u32[]{:S(2)}) collective-permute-start(f32[24,128]{1,0:T(8,128)S(1)} %get-tuple-element.59.refs_1_), channel_id=1, source_target_pairs={{0,24},{8,16},{16,8},{24,0},{1,25},{9,17},{17,9},{25,1},{2,26},{10... | collective-permute-start | bytes 36872 | tf_op jit(solution)/shard_map/ppermute | solution.py:373
  63.6 4.6 %collective-permute-start.22 = (f32[24,128]{1,0:T(8,128)S(1)}, f32[24,128]{1,0:T(8,128)S(1)}, u32[]{:S(2)}, u32[]{:S(2)}) collective-permute-start(f32[24,128]{1,0:T(8,128)S(1)} %get-tuple-element.59.refs_1_), channel_id=1, source_target_pairs={{0,16},{8,24},{16,0},{24,8},{1,17},{9,25},{17,1},{25,9},{2,18},{10... | collective-permute-start | bytes 36872 | tf_op jit(solution)/shard_map/ppermute | solution.py:373
  64.5 3.8 %collective-permute-start.21 = (f32[24,128]{1,0:T(8,128)S(1)}, f32[24,128]{1,0:T(8,128)S(1)}, u32[]{:S(2)}, u32[]{:S(2)}) collective-permute-start(f32[24,128]{1,0:T(8,128)S(1)} %get-tuple-element.59.refs_1_), channel_id=1, source_target_pairs={{0,8},{8,0},{16,24},{24,16},{1,9},{9,1},{17,25},{25,17},{2,10},{10... | collective-permute-start | bytes 36872 | tf_op jit(solution)/shard_map/ppermute | solution.py:373
  70.0 1.2 %collective-permute-start.24 = (f32[8,128]{1,0:T(8,128)S(1)}, f32[8,128]{1,0:T(8,128)S(1)}, u32[]{:S(2)}, u32[]{:S(2)}) collective-permute-start(f32[8,128]{1,0:T(8,128)S(1)} %get-tuple-element.60.one_ref), channel_id=1, source_target_pairs={{0,1},{1,0},{2,3},{3,2},{4,5},{5,4},{6,7},{7,6},{8,9},{9,8},{10,11... | collective-permute-start | bytes 12296 | tf_op jit(solution)/shard_map/ppermute | solution.py:380
  71.2 4.5 %collective-permute-start.27 = (f32[8,128]{1,0:T(8,128)S(1)}, f32[8,128]{1,0:T(8,128)S(1)}, u32[]{:S(2)}, u32[]{:S(2)}) collective-permute-start(f32[8,128]{1,0:T(8,128)S(1)} %shard_map.117.refs_0_), channel_id=1, source_target_pairs={{0,6},{1,7},{2,4},{3,5},{4,2},{5,3},{6,0},{7,1},{8,14},{9,15},{10,... | collective-permute-start | bytes 12296 | tf_op jit(solution)/shard_map/ppermute | solution.py:382
  72.7 3.6 %collective-permute-start.26 = (f32[8,128]{1,0:T(8,128)S(1)}, f32[8,128]{1,0:T(8,128)S(1)}, u32[]{:S(2)}, u32[]{:S(2)}) collective-permute-start(f32[8,128]{1,0:T(8,128)S(1)} %shard_map.117.refs_0_), channel_id=1, source_target_pairs={{0,4},{1,5},{2,6},{3,7},{4,0},{5,1},{6,2},{7,3},{8,12},{9,13},{10,... | collective-permute-start | bytes 12296 | tf_op jit(solution)/shard_map/ppermute | solution.py:382
  74.0 3.6 %collective-permute-start.25 = (f32[8,128]{1,0:T(8,128)S(1)}, f32[8,128]{1,0:T(8,128)S(1)}, u32[]{:S(2)}, u32[]{:S(2)}) collective-permute-start(f32[8,128]{1,0:T(8,128)S(1)} %shard_map.117.refs_0_), channel_id=1, source_target_pairs={{0,2},{1,3},{2,0},{3,1},{4,6},{5,7},{6,4},{7,5},{8,10},{9,11},{10,... | collective-permute-start | bytes 12296 | tf_op jit(solution)/shard_map/ppermute | solution.py:382

commit v12 on v11

--- a/solution.py
+++ b/solution.py
@@ -17,6 +17,7 @@
 STEPS = 3
 ROWS = 8
 VMEM = pl.BlockSpec(memory_space=pltpu.VMEM)
+SMEM = pl.BlockSpec(memory_space=pltpu.SMEM)
 ANY = pl.BlockSpec(memory_space=pl.ANY)
 F32 = jnp.float32
 BF16 = jnp.bfloat16
@@ -132,22 +133,29 @@
     return total
 
 
-def forward(dims, field_ref, lat_ref, foot_ref, ids_ref, sim_ref):
+def split(values):
+    terms = []
+    for _ in range(TERMS):
+        terms.append(values.astype(BF16).astype(F32))
+        values = values - terms[-1]
+    return jnp.concatenate(terms, axis=0).astype(BF16)
+
+
+def forward(dims, field_ref, lat_ref, foot_ref, ids_ref, place_ref, prod_ref, sim_ref):
     nc, nb, modes, groups, band = dims
     subs = sim_ref.shape[0] - ROWS
-    sim_ref[...] = jnp.zeros_like(sim_ref)
     for j in range(nc):
         for b in range(nb):
             period = ids_ref[j, b]
             row = ids_ref[j, nb + b] * CR
-            sub = ids_ref[j, 2 * nb + b]
             total = None
             for r in range(CR):
                 column = jnp.sum(lat_ref[row + r] * field_ref[period], axis=1, keepdims=True)
                 at = (b * CR + r) * modes
                 term = foot_ref[j, at:at + modes, :].astype(F32) * column
                 total = term if total is None else total + term
-            sim_ref[pl.ds(sub, 1), :] += jnp.sum(total, axis=0, keepdims=True)
+            prod_ref[j * nb + b:j * nb + b + 1, :] = jnp.sum(total, axis=0, keepdims=True)
+    sim_ref[:subs, :] = jnp.dot(place_ref[...], split(prod_ref[...]), preferred_element_type=F32)
     sim_ref[subs:, :] = fold(field_ref)
 
 
@@ -169,8 +177,8 @@
 
 def first_kernel(dims, no, lat_ref, came_ref, *refs):
     nc, nb, modes, _, _ = dims
-    near_refs, refs = refs[:-8], refs[-8:]
-    out_ref, field_ref, foot_ref, all_ref, choose_ref, tail_ref, ids_ref, sem = refs
+    near_refs, refs = refs[:-10], refs[-10:]
+    out_ref, field_ref, foot_ref, all_ref, choose_ref, place_ref, tail_ref, ids_ref, prod_ref, sem = refs
     rows = nb * CR * modes
     for j in range(nc):
         all_ref[j:j + 1, :] = came_ref[j, rows:rows + 16, :].astype(F32)[0:1].astype(jnp.int32)
@@ -188,24 +196,21 @@
     lane = lax.broadcasted_iota(jnp.int32, choose_ref.shape, 1)
     tail_line = lax.broadcasted_iota(jnp.int32, tail_ref.shape, 0)
     tail_lane = lax.broadcasted_iota(jnp.int32, tail_ref.shape, 1)
+    place_line = lax.broadcasted_iota(jnp.int32, place_ref.shape, 0)
+    place_lane = lax.broadcasted_iota(jnp.int32, place_ref.shape, 1) % (nc * nb)
     subs = jnp.zeros(choose_ref.shape, jnp.int32)
+    place = jnp.zeros(place_ref.shape, jnp.int32)
     tail = jnp.zeros(tail_ref.shape, jnp.int32)
     for j in range(nc):
         for b in range(nb):
             subs = jnp.where(line == j * nb + b, ids_ref[j, 2 * nb + b], subs)
+            place = jnp.where(place_lane == j * nb + b, ids_ref[j, 2 * nb + b], place)
             value = jnp.where(tail_line == 0, ids_ref[j, b], ids_ref[j, nb + b])
             tail = jnp.where(tail_lane == j * nb + b, value, tail)
     choose_ref[...] = jnp.where(lane % (choose_ref.shape[1] // TERMS) == subs, 1.0, 0.0).astype(BF16)
+    place_ref[...] = jnp.where(place_line == place, 1.0, 0.0).astype(BF16)
     tail_ref[...] = tail.astype(F32)
-    forward(dims, field_ref, lat_ref, foot_ref, ids_ref, out_ref)
-
-
-def split(values):
-    terms = []
-    for _ in range(TERMS):
-        terms.append(values.astype(BF16).astype(F32))
-        values = values - terms[-1]
-    return jnp.concatenate(terms, axis=0).astype(BF16)
+    forward(dims, field_ref, lat_ref, foot_ref, ids_ref, place_ref, prod_ref, out_ref)
 
 
 def adjoint_kernel(dims, tails, choose_ref, weight_ref, foot_ref, *refs):
@@ -253,68 +258,51 @@
     return lax.dot_general(split(rows), pick_ref[...], (((0,), (0,)), ((), ())), preferred_element_type=F32)
 
 
-def image_kernel(dims, no, first, last, ids_in, all_in, lat_ref, foot_ref, pick_ref, norm_ref, field_ref, *refs):
+def image_kernel(dims, no, first, last, ids_ref, all_ref, lat_ref, foot_ref, pick_ref, place_ref, norm_ref, field_ref, *refs):
     nc, nb, modes, groups, band = dims
     if not first:
         prior_ref, refs = refs[0], refs[1:]
     ways = min(no, WAYS)
-    ids_ref, all_ref, sems = refs[-3:]
-    refs = refs[:-3]
-    copies = [
-        pltpu.make_async_copy(ids_in, ids_ref, sems.at[0]),
-        pltpu.make_async_copy(all_in, all_ref, sems.at[1]),
-    ]
-    for copy in copies:
-        copy.start()
-    kept = 7 + ways
+    kept = 7 + 2 * ways
     coef_refs, refs = refs[:-kept], refs[-kept:]
-    wide_ref, refs = refs[-1], refs[:-1]
+    wide_refs, refs = refs[-ways:], refs[:-ways]
     sum_refs, refs = refs[-ways:], refs[:-ways]
     if last:
-        out_ref, row_ref, mine_ref, alpha_ref, next_ref, held_ref = refs
+        out_ref, row_ref, mine_ref, alpha_ref, next_ref, prod_ref, held_ref = refs
     else:
-        out_ref, row_ref, next_ref, vector_ref, alpha_ref, held_ref = refs
+        out_ref, row_ref, next_ref, vector_ref, alpha_ref, prod_ref, held_ref = refs
     mine = nc * nb
-    chunks = mine // CHUNK
     periods = field_ref.shape[0]
     per_dev = row_ref.shape[0]
     subs = ROWS
     rows = sum(ref.shape[0] for ref in coef_refs) // no
     coef_refs = pieces(coef_refs, no, rows)
-    ahead = no <= 4
     for s in range(no):
-        if ahead:
-            for q in range(chunks):
-                wide_ref[s * chunks + q] = widen(coef_refs[s][q * CHUNK:(q + 1) * CHUNK, :], pick_ref)[:CR * modes]
-        else:
-            held_ref[s] = coef_refs[s][:mine, :]
+        held_ref[s] = coef_refs[s][:mine, :]
     for sum_ref in sum_refs:
         sum_ref[...] = jnp.zeros_like(sum_ref)
     gain = jnp.sum(tree_sum(ref[mine:mine + subs, :] for ref in coef_refs), keepdims=True)
     alpha_ref[...] = jnp.broadcast_to(1.0 + gain, alpha_ref.shape)
     norm = norm_ref[0:1, :]
     scale = 1.0 / norm
-    for copy in copies:
-        copy.wait()
     own = ids_ref[0, 3 * nb]
 
     def group(at, carry):
         found = [at * ways + i for i in range(ways)]
         if permuted(no):
             found = [own ^ at_i for at_i in found]
-        for q in range(chunks):
-            slots = [at_i * chunks + q for at_i in found] if ahead else range(ways)
-            if not ahead:
-                for at_i, slot in zip(found, slots):
-                    wide_ref[slot] = widen(held_ref[at_i, q * CHUNK:(q + 1) * CHUNK, :], pick_ref)[:CR * modes]
-            for at in range(CHUNK):
-                for at_i, slot, sum_ref in zip(found, slots, sum_refs):
-                    period = all_ref[2 * at_i, q * CHUNK + at]
-                    row = all_ref[2 * at_i + 1, q * CHUNK + at] * CR
-                    total = sum_ref[period]
-                    for r in range(CR):
-                        coef = wide_ref[slot, r * modes:(r + 1) * modes, at * 128:(at + 1) * 128]
-                        total += coef * lat_ref[row + r]
+        for chunk in range(0, mine, CHUNK):
+            helds = [held_ref[at_i, chunk:chunk + CHUNK, :] for at_i in found]
+            for held, wide_ref in zip(helds, wide_refs):
+                wide_ref[...] = widen(held[:, :modes], pick_ref)
+            columns = [held.T for held in helds]
+            for at_t in range(CHUNK):
+                for at_i, wide_ref, column, sum_ref in zip(found, wide_refs, columns, sum_refs):
+                    period = all_ref[2 * at_i, chunk + at_t]
+                    row = all_ref[2 * at_i + 1, chunk + at_t] * CR
+                    total = sum_ref[period] + wide_ref[:, at_t * 128:(at_t + 1) * 128] * lat_ref[row]
+                    for r in range(1, CR):
+                        total += column[r * modes:(r + 1) * modes, at_t:at_t + 1] * lat_ref[row + r]
                     sum_ref[period] = total
         return carry
 
@@ -338,7 +326,7 @@
         for l in range(per_dev):
             mine_ref[l] = next_ref[own * per_dev + l]
     else:
-        forward(dims, next_ref, lat_ref, foot_ref, ids_ref, out_ref)
+        forward(dims, next_ref, lat_ref, foot_ref, ids_ref, place_ref, prod_ref, out_ref)
 
 
 def finish_kernel(factor, sums, *refs):
@@ -449,7 +437,7 @@
     field_shape = shape((periods, modes, lat_rows))
     small = shape((ROWS, 128))
     own_shape = shape((per_dev, modes, lat_rows))
-    sims, field, foot, ids, choose, tail = call(
+    sims, field, foot, ids, choose, spots, tail = call(
         functools.partial(first_kernel, dims, no),
         (
             shape((subs + ROWS, ob)),
@@ -457,11 +445,12 @@
             jax.ShapeDtypeStruct((nc, foot_rows, ob), BF16),
             jax.ShapeDtypeStruct((nc, 128), jnp.int32),
             jax.ShapeDtypeStruct((mine, TERMS * subs), BF16),
+            jax.ShapeDtypeStruct((subs, TERMS * mine), BF16),
             shape((ROWS, 128)),
         ),
         [VMEM] * (2 + len(near)),
         lat, came, *near,
-        scratch=[pltpu.SMEM((nc, 128), jnp.int32), pltpu.SemaphoreType.DMA],
+        scratch=[pltpu.SMEM((nc, 128), jnp.int32), pltpu.VMEM((mine, ob), F32), pltpu.SemaphoreType.DMA],
     )
     ways = min(no, WAYS)
     rows, alphas, norms = [], [], []
@@ -495,14 +484,13 @@
                 *([] if last else [field_shape]),
                 small,
             ),
-            [VMEM] * (7 + len(before) + len(coefs)),
-            ids, every, lat, foot, pick, norm, field, *before, *coefs,
+            [SMEM] * 2 + [VMEM] * (6 + len(before) + len(coefs)),
+            ids, every, lat, foot, pick, spots, norm, field, *before, *coefs,
             scratch=[pltpu.VMEM(field_shape.shape, F32)] * last
+            + [pltpu.VMEM((mine, ob), F32)]
             + [pltpu.VMEM((no, mine, 128), F32)]
             + [pltpu.VMEM(field_shape.shape, F32)] * ways
-            + [pltpu.VMEM((no * mine // CHUNK if no <= 4 else ways, CR * modes, CHUNK * 128), F32)]
-            + [pltpu.SMEM((nc, 128), jnp.int32), pltpu.SMEM((2 * no, 128), jnp.int32)]
-            + [pltpu.SemaphoreType.DMA((2,))],
+            + [pltpu.VMEM((modes, CHUNK * 128), F32)] * ways,
             limit=16,
         )
         vector = None if last else vector[0]

time: 78.8 us -> 78.8 us (level)
  no operation moved by 1% of the time
where the time goes in v12:
time: 78.8 us; the launch traced here: 78.4 us
  starting transfers between devices  37.2 us (47%)
  waiting for transfers between devices  24.9 us (32%)
  Pallas kernels  14.8 us (19%)
    ppermute x12, starting transfers between devices, share(): lax.ppermute(array, axis, [(d, d ^ s) for d in range(size)])  17.9 us
    pallas_call x15, Pallas kernels, call(): pl.pallas_call(kernel, out_shape=outs, in_specs=specs, out_specs=jax.tree...  14.8 us
    ppermute x12, starting transfers between devices, addends(): lax.ppermute(both, axis, [(d, d ^ s) for d in range(size)])  14 us
    ppermute x12, waiting for transfers between devices, addends(): lax.ppermute(both, axis, [(d, d ^ s) for d in range(size)])  11.6 us
    ppermute x12, waiting for transfers between devices, share(): lax.ppermute(array, axis, [(d, d ^ s) for d in range(size)])  8.59 us
    all_to_all x1, starting transfers between devices, swap(): return lax.all_to_all(array, axis, split_axis=0, concat_axis=0, tiled=True)  5.18 us
    ppermute x4, waiting for transfers between devices, addends(): other = lax.ppermute(array, axis, [(d, d ^ 1) for d in range(size)])  4.66 us
  transfers between devices with their start and end apart: 29, of which 25 were waited for; matrix products, arithmetic and copies ran while one was open for 0% of the time, Pallas kernels for 3%

profile of v12, /device:TPU:0, one launch (start us, length us, event | category | flops | bytes accessed | tf_op | source)
XLA Modules:
  0.0 78.4 jit_solution(1571237149602503974)
XLA Ops:
  0.6 2.7 %shard_map.104 = (bf16[8,208,128]{2,1,0:T(8,128)(2,1)}, f32[8,128]{1,0:T(8,128)}) custom-call(s32[1]{0:T(128)} %bitcast.1.place_any, bf16[384,384]{1,0:T(8,128)(2,1)} %constant.14.clone.high_any, bf16[384,384]{1,0:T(8,128)(2,1)} %constant.15.clone.low_any, bf16[2,128,768]{2,1,0:T(8,128)(2,1)} %foot_any.1, s32[2]{0:T(128)} %off_any.1, s32[2]{0:T(128)} %sub_any.1, ...), custom_call_target="tpu_custom_call" | custom-call | tf_op jit(solution)/shard_map/pallas_call | solution.py:41
  3.3 5.2 %all-to-all-start = ((bf16[8,208,128]{2,1,0:T(8,128)(2,1)}), bf16[8,208,128]{2,1,0:T(8,128)(2,1)}, u32[]{:S(2)}, u32[]{:S(2)}) async-start(bf16[8,208,128]{2,1,0:T(8,128)(2,1)} %get-tuple-element.40), calls=%async_computation | async-start | bytes 851968 | tf_op jit(solution)/shard_map/all_to_all | solution.py:374
  8.5 4.1 %collective-permute-start.2 = (f32[48,128]{1,0:T(8,128)}, f32[48,128]{1,0:T(8,128)S(1)}, u32[]{:S(2)}, u32[]{:S(2)}) collective-permute-start(f32[48,128]{1,0:T(8,128)} %bitcast.3), channel_id=1, source_target_pairs={{0,24},{8,16},{16,8},{24,0},{1,25},{9,17},{17,9},{25,1},{2,26},{10... | collective-permute-start | bytes 73736 | tf_op jit(solution)/shard_map/ppermute | solution.py:361
  12.6 0.6 collective-permute-start
  13.2 0.8 copy-done.1
  14.0 2.3 %shard_map.105 = (f32[128,48,128]{2,1,0:T(8,128)S(1)}, f32[48,128]{1,0:T(8,128)S(1)}, bf16[48,2048]{1,0:T(8,128)(2,1)S(1)}) custom-call(f32[48,128,128]{2,1,0:T(8,128)} %lat_any, f32[48,128]{1,0:T(8,128)S(1)} %bitcast.6), custom_call_target="tpu_custom_call" | custom-call | bytes 6340608 | tf_op jit(solution)/shard_map/pallas_call | solution.py:41
  16.3 1.2 %collective-permute-done.1.refs_2_ = f32[48,128]{1,0:T(8,128)S(1)} collective-permute-done((f32[48,128]{1,0:T(8,128)}, f32[48,128]{1,0:T(8,128)S(1)}, u32[]{:S(2)}, u32[]{:S(2)}) %collective-permute-start.1) | collective-permute-done | bytes 24608 | tf_op jit(solution)/shard_map/ppermute | solution.py:361
  17.5 2.1 %shard_map.106 = (f32[16,128]{1,0:T(8,128)S(1)}, f32[4,48,128]{2,1,0:T(8,128)S(1)}, bf16[8,192,128]{2,1,0:T(8,128)(2,1)S(1)}, s32[8,128]{1,0:T(8,128)S(1)}, bf16...) custom-call(f32[128,48,128]{2,1,0:T(8,128)S(1)} %get-tuple-element.39.lat_ref, ...), custom_call_target="tpu_custom_call" | custom-call | tf_op jit(solution)/shard_map/pallas_call | solution.py:41
  19.6 1.2 %collective-permute-done.3.other_ref = f32[16,128]{1,0:T(8,128)S(1)} collective-permute-done((f32[16,128]{1,0:T(8,128)S(1)}, f32[16,128]{1,0:T(8,128)S(1)}, u32[]{:S(2)}, u32[]{:S(2)}) %collective-permute-start.3) | collective-permute-done | bytes 8224 | tf_op jit(solution)/shard_map/ppermute | solution.py:368
  20.8 2.8 %collective-permute-start.6 = (f32[16,128]{1,0:T(8,128)S(1)}, f32[16,128]{1,0:T(8,128)S(1)}, u32[]{:S(2)}, u32[]{:S(2)}) collective-permute-start(f32[16,128]{1,0:T(8,128)S(1)} %shard_map.107.refs_1_), channel_id=1, source_target_pairs={{0,6},{1,7},{2,4},{3,5},{4,2},{5,3},{6,0},{7,1},{8,14},{9,15},{10,... | collective-permute-start | bytes 24584 | tf_op jit(solution)/shard_map/ppermute | solution.py:370
  24.3 1.1 %collective-permute-done.6.refs_4_ = f32[16,128]{1,0:T(8,128)S(1)} collective-permute-done((f32[16,128]{1,0:T(8,128)S(1)}, f32[16,128]{1,0:T(8,128)S(1)}, u32[]{:S(2)}, u32[]{:S(2)}) %collective-permute-start.6) | collective-permute-done | bytes 8224 | tf_op jit(solution)/shard_map/ppermute | solution.py:370
  25.4 1.9 %collective-permute-done.5.refs_3_ = f32[16,128]{1,0:T(8,128)S(1)} collective-permute-done((f32[16,128]{1,0:T(8,128)S(1)}, f32[16,128]{1,0:T(8,128)S(1)}, u32[]{:S(2)}, u32[]{:S(2)}) %collective-permute-start.5) | collective-permute-done | bytes 8224 | tf_op jit(solution)/shard_map/ppermute | solution.py:370
  28.2 2.6 %collective-permute-start.9 = (f32[32,128]{1,0:T(8,128)S(1)}, f32[32,128]{1,0:T(8,128)S(1)}, u32[]{:S(2)}, u32[]{:S(2)}) collective-permute-start(f32[32,128]{1,0:T(8,128)S(1)} %get-tuple-element.47.refs_0_), channel_id=1, source_target_pairs={{0,24},{8,16},{16,8},{24,0},{1,25},{9,17},{17,9},{25,1},{2,26},{10... | collective-permute-start | bytes 49160 | tf_op jit(solution)/shard_map/ppermute | solution.py:361
  30.8 1.8 %collective-permute-start.7 = (f32[32,128]{1,0:T(8,128)S(1)}, f32[32,128]{1,0:T(8,128)S(1)}, u32[]{:S(2)}, u32[]{:S(2)}) collective-permute-start(f32[32,128]{1,0:T(8,128)S(1)} %get-tuple-element.47.refs_0_), channel_id=1, source_target_pairs={{0,8},{8,0},{16,24},{24,16},{1,9},{9,1},{17,25},{25,17},{2,10},{10... | collective-permute-start | bytes 49160 | tf_op jit(solution)/shard_map/ppermute | solution.py:361
  32.6 1.1 %collective-permute-done.9.refs_3_ = f32[32,128]{1,0:T(8,128)S(1)} collective-permute-done((f32[32,128]{1,0:T(8,128)S(1)}, f32[32,128]{1,0:T(8,128)S(1)}, u32[]{:S(2)}, u32[]{:S(2)}) %collective-permute-start.9) | collective-permute-done | bytes 16416 | tf_op jit(solution)/shard_map/ppermute | solution.py:361
  33.8 1.7 %collective-permute-done.8.refs_2_ = f32[32,128]{1,0:T(8,128)S(1)} collective-permute-done((f32[32,128]{1,0:T(8,128)S(1)}, f32[32,128]{1,0:T(8,128)S(1)}, u32[]{:S(2)}, u32[]{:S(2)}) %collective-permute-start.8) | collective-permute-done | bytes 16416 | tf_op jit(solution)/shard_map/ppermute | solution.py:361
  35.5 2.0 %shard_map.110 = (f32[16,128]{1,0:T(8,128)S(1)}, f32[1,48,128]{2,1,0:T(8,128)S(1)}, f32[4,48,128]{2,1,0:T(8,128)S(1)}, f32[4,48,128]{2,1,0:T(8,128)S(1)}, f32[8,128]{1,0:T(8,128)S(1)}) custom-call(s32[8,128]{1,0:T(8,128)S(1)} %get-tuple-element.42.ids_ref, s32[8,128]{1,0:T(8,128)S(1)} %shard_map.109.all_ref, f32[128,48,128]{2,1,0:T(8,128)S(1)} %get-tuple-element.39.lat_ref, ...), custom_call_target="tpu_custom_call" | custom-call | tf_op jit(solution)/shard_map/pallas_call | solution.py:41
  37.5 1.2 %collective-permute-done.10.other_ref = f32[16,128]{1,0:T(8,128)S(1)} collective-permute-done((f32[16,128]{1,0:T(8,128)S(1)}, f32[16,128]{1,0:T(8,128)S(1)}, u32[]{:S(2)}, u32[]{:S(2)}) %collective-permute-start.10) | collective-permute-done | bytes 8224 | tf_op jit(solution)/shard_map/ppermute | solution.py:368
  38.7 1.5 %collective-permute-start.13 = (f32[16,128]{1,0:T(8,128)S(1)}, f32[16,128]{1,0:T(8,128)S(1)}, u32[]{:S(2)}, u32[]{:S(2)}) collective-permute-start(f32[16,128]{1,0:T(8,128)S(1)} %shard_map.111.refs_0_), channel_id=1, source_target_pairs={{0,6},{1,7},{2,4},{3,5},{4,2},{5,3},{6,0},{7,1},{8,14},{9,15},{10,... | collective-permute-start | bytes 24584 | tf_op jit(solution)/shard_map/ppermute | solution.py:370
  40.2 1.3 %collective-permute-start.12 = (f32[16,128]{1,0:T(8,128)S(1)}, f32[16,128]{1,0:T(8,128)S(1)}, u32[]{:S(2)}, u32[]{:S(2)}) collective-permute-start(f32[16,128]{1,0:T(8,128)S(1)} %shard_map.111.refs_0_), channel_id=1, source_target_pairs={{0,4},{1,5},{2,6},{3,7},{4,0},{5,1},{6,2},{7,3},{8,12},{9,13},{10,... | collective-permute-start | bytes 24584 | tf_op jit(solution)/shard_map/ppermute | solution.py:370
  41.4 0.7 collective-permute-start.11
  42.2 1.1 %collective-permute-done.13.refs_3_ = f32[16,128]{1,0:T(8,128)S(1)} collective-permute-done((f32[16,128]{1,0:T(8,128)S(1)}, f32[16,128]{1,0:T(8,128)S(1)}, u32[]{:S(2)}, u32[]{:S(2)}) %collective-permute-start.13) | collective-permute-done | bytes 8224 | tf_op jit(solution)/shard_map/ppermute | solution.py:370
  43.2 0.6 collective-permute-done.12.refs_2_
  43.8 1.3 %collective-permute-done.11.refs_1_ = f32[16,128]{1,0:T(8,128)S(1)} collective-permute-done((f32[16,128]{1,0:T(8,128)S(1)}, f32[16,128]{1,0:T(8,128)S(1)}, u32[]{:S(2)}, u32[]{:S(2)}) %collective-permute-start.11) | collective-permute-done | bytes 8224 | tf_op jit(solution)/shard_map/ppermute | solution.py:370
  45.5 1.5 %collective-permute-start.16 = (f32[24,128]{1,0:T(8,128)S(1)}, f32[24,128]{1,0:T(8,128)S(1)}, u32[]{:S(2)}, u32[]{:S(2)}) collective-permute-start(f32[24,128]{1,0:T(8,128)S(1)} %get-tuple-element.56.refs_1_), channel_id=1, source_target_pairs={{0,24},{8,16},{16,8},{24,0},{1,25},{9,17},{17,9},{25,1},{2,26},{10... | collective-permute-start | bytes 36872 | tf_op jit(solution)/shard_map/ppermute | solution.py:361
  47.0 0.6 collective-permute-start.15
  47.7 2.3 %collective-permute-start.14 = (f32[24,128]{1,0:T(8,128)S(1)}, f32[24,128]{1,0:T(8,128)S(1)}, u32[]{:S(2)}, u32[]{:S(2)}) collective-permute-start(f32[24,128]{1,0:T(8,128)S(1)} %get-tuple-element.56.refs_1_), channel_id=1, source_target_pairs={{0,8},{8,0},{16,24},{24,16},{1,9},{9,1},{17,25},{25,17},{2,10},{10... | collective-permute-start | bytes 36872 | tf_op jit(solution)/shard_map/ppermute | solution.py:361
  50.0 1.1 %collective-permute-done.16.refs_4_ = f32[24,128]{1,0:T(8,128)S(1)} collective-permute-done((f32[24,128]{1,0:T(8,128)S(1)}, f32[24,128]{1,0:T(8,128)S(1)}, u32[]{:S(2)}, u32[]{:S(2)}) %collective-permute-start.16) | collective-permute-done | bytes 12320 | tf_op jit(solution)/shard_map/ppermute | solution.py:361
  51.7 2.0 %shard_map.113 = (f32[16,128]{1,0:T(8,128)S(1)}, f32[1,48,128]{2,1,0:T(8,128)S(1)}, f32[4,48,128]{2,1,0:T(8,128)S(1)}, f32[4,48,128]{2,1,0:T(8,128)S(1)}, f32[8,128]{1,0:T(8,128)S(1)}) custom-call(s32[8,128]{1,0:T(8,128)S(1)} %get-tuple-element.42.ids_ref, s32[8,128]{1,0:T(8,128)S(1)} %shard_map.109.all_ref, f32[128,48,128]{2,1,0:T(8,128)S(1)} %get-tuple-element.39.lat_ref, ...), custom_call_target="tpu_custom_call" | custom-call | tf_op jit(solution)/shard_map/pallas_call | solution.py:41
  53.8 1.2 %collective-permute-done.17.other_ref = f32[16,128]{1,0:T(8,128)S(1)} collective-permute-done((f32[16,128]{1,0:T(8,128)S(1)}, f32[16,128]{1,0:T(8,128)S(1)}, u32[]{:S(2)}, u32[]{:S(2)}) %collective-permute-start.17) | collective-permute-done | bytes 8224 | tf_op jit(solution)/shard_map/ppermute | solution.py:368
  54.9 1.6 %collective-permute-start.20 = (f32[16,128]{1,0:T(8,128)S(1)}, f32[16,128]{1,0:T(8,128)S(1)}, u32[]{:S(2)}, u32[]{:S(2)}) collective-permute-start(f32[16,128]{1,0:T(8,128)S(1)} %shard_map.114.refs_0_), channel_id=1, source_target_pairs={{0,6},{1,7},{2,4},{3,5},{4,2},{5,3},{6,0},{7,1},{8,14},{9,15},{10,... | collective-permute-start | bytes 24584 | tf_op jit(solution)/shard_map/ppermute | solution.py:370
  57.1 1.3 %collective-permute-start.18 = (f32[16,128]{1,0:T(8,128)S(1)}, f32[16,128]{1,0:T(8,128)S(1)}, u32[]{:S(2)}, u32[]{:S(2)}) collective-permute-start(f32[16,128]{1,0:T(8,128)S(1)} %shard_map.114.refs_0_), channel_id=1, source_target_pairs={{0,2},{1,3},{2,0},{3,1},{4,6},{5,7},{6,4},{7,5},{8,10},{9,11},{10,... | collective-permute-start | bytes 24584 | tf_op jit(solution)/shard_map/ppermute | solution.py:370
  58.4 1.1 %collective-permute-done.20.refs_3_ = f32[16,128]{1,0:T(8,128)S(1)} collective-permute-done((f32[16,128]{1,0:T(8,128)S(1)}, f32[16,128]{1,0:T(8,128)S(1)}, u32[]{:S(2)}, u32[]{:S(2)}) %collective-permute-start.20) | collective-permute-done | bytes 8224 | tf_op jit(solution)/shard_map/ppermute | solution.py:370
  59.5 0.7 collective-permute-done.19.refs_2_
  61.2 2.5 %collective-permute-start.23 = (f32[24,128]{1,0:T(8,128)S(1)}, f32[24,128]{1,0:T(8,128)S(1)}, u32[]{:S(2)}, u32[]{:S(2)}) collective-permute-start(f32[24,128]{1,0:T(8,128)S(1)} %get-tuple-element.61.refs_1_), channel_id=1, source_target_pairs={{0,24},{8,16},{16,8},{24,0},{1,25},{9,17},{17,9},{25,1},{2,26},{10... | collective-permute-start | bytes 36872 | tf_op jit(solution)/shard_map/ppermute | solution.py:361
  63.7 0.9 %collective-permute-start.22 = (f32[24,128]{1,0:T(8,128)S(1)}, f32[24,128]{1,0:T(8,128)S(1)}, u32[]{:S(2)}, u32[]{:S(2)}) collective-permute-start(f32[24,128]{1,0:T(8,128)S(1)} %get-tuple-element.61.refs_1_), channel_id=1, source_target_pairs={{0,16},{8,24},{16,0},{24,8},{1,17},{9,25},{17,1},{25,9},{2,18},{10... | collective-permute-start | bytes 36872 | tf_op jit(solution)/shard_map/ppermute | solution.py:361
  64.6 1.0 %collective-permute-start.21 = (f32[24,128]{1,0:T(8,128)S(1)}, f32[24,128]{1,0:T(8,128)S(1)}, u32[]{:S(2)}, u32[]{:S(2)}) collective-permute-start(f32[24,128]{1,0:T(8,128)S(1)} %get-tuple-element.61.refs_1_), channel_id=1, source_target_pairs={{0,8},{8,0},{16,24},{24,16},{1,9},{9,1},{17,25},{25,17},{2,10},{10... | collective-permute-start | bytes 36872 | tf_op jit(solution)/shard_map/ppermute | solution.py:361
  65.7 1.1 %collective-permute-done.23.refs_4_ = f32[24,128]{1,0:T(8,128)S(1)} collective-permute-done((f32[24,128]{1,0:T(8,128)S(1)}, f32[24,128]{1,0:T(8,128)S(1)}, u32[]{:S(2)}, u32[]{:S(2)}) %collective-permute-start.23) | collective-permute-done | bytes 12320 | tf_op jit(solution)/shard_map/ppermute | solution.py:361
  66.8 1.6 %collective-permute-done.22.refs_3_ = f32[24,128]{1,0:T(8,128)S(1)} collective-permute-done((f32[24,128]{1,0:T(8,128)S(1)}, f32[24,128]{1,0:T(8,128)S(1)}, u32[]{:S(2)}, u32[]{:S(2)}) %collective-permute-start.22) | collective-permute-done | bytes 12320 | tf_op jit(solution)/shard_map/ppermute | solution.py:361
  68.4 1.5 %shard_map.116 = (f32[8,128]{1,0:T(8,128)S(1)}, f32[1,48,128]{2,1,0:T(8,128)S(1)}, f32[1,48,128]{2,1,0:T(8,128)S(1)}, f32[8,128]{1,0:T(8,128)S(1)}) custom-call(s32[8,128]{1,0:T(8,128)S(1)} %get-tuple-element.42.ids_ref, s32[8,128]{1,0:T(8,128)S(1)} %shard_map.109.all_ref, f32[128,48,128]{2,1,0:T(8,128)S(1)} %get-tuple-element.39.lat_ref, ...), custom_call_target="tpu_custom_call" | custom-call | tf_op jit(solution)/shard_map/pallas_call | solution.py:41
  70.1 1.2 %collective-permute-done.24.other_ref = f32[8,128]{1,0:T(8,128)S(1)} collective-permute-done((f32[8,128]{1,0:T(8,128)S(1)}, f32[8,128]{1,0:T(8,128)S(1)}, u32[]{:S(2)}, u32[]{:S(2)}) %collective-permute-start.24) | collective-permute-done | bytes 4128 | tf_op jit(solution)/shard_map/ppermute | solution.py:368
  71.2 1.5 %collective-permute-start.27 = (f32[8,128]{1,0:T(8,128)S(1)}, f32[8,128]{1,0:T(8,128)S(1)}, u32[]{:S(2)}, u32[]{:S(2)}) collective-permute-start(f32[8,128]{1,0:T(8,128)S(1)} %shard_map.117.refs_0_), channel_id=1, source_target_pairs={{0,6},{1,7},{2,4},{3,5},{4,2},{5,3},{6,0},{7,1},{8,14},{9,15},{10,... | collective-permute-start | bytes 12296 | tf_op jit(solution)/shard_map/ppermute | solution.py:370
  72.7 1.3 %collective-permute-start.26 = (f32[8,128]{1,0:T(8,128)S(1)}, f32[8,128]{1,0:T(8,128)S(1)}, u32[]{:S(2)}, u32[]{:S(2)}) collective-permute-start(f32[8,128]{1,0:T(8,128)S(1)} %shard_map.117.refs_0_), channel_id=1, source_target_pairs={{0,4},{1,5},{2,6},{3,7},{4,0},{5,1},{6,2},{7,3},{8,12},{9,13},{10,... | collective-permute-start | bytes 12296 | tf_op jit(solution)/shard_map/ppermute | solution.py:370
  74.0 0.7 collective-permute-start.25
  74.7 1.0 %collective-permute-done.27.refs_3_ = f32[8,128]{1,0:T(8,128)S(1)} collective-permute-done((f32[8,128]{1,0:T(8,128)S(1)}, f32[8,128]{1,0:T(8,128)S(1)}, u32[]{:S(2)}, u32[]{:S(2)}) %collective-permute-start.27) | collective-permute-done | bytes 4128 | tf_op jit(solution)/shard_map/ppermute | solution.py:370
  75.7 0.6 collective-permute-done.26.refs_2_
  76.3 1.3 %collective-permute-done.25.refs_1_ = f32[8,128]{1,0:T(8,128)S(1)} collective-permute-done((f32[8,128]{1,0:T(8,128)S(1)}, f32[8,128]{1,0:T(8,128)S(1)}, u32[]{:S(2)}, u32[]{:S(2)}) %collective-permute-start.25) | collective-permute-done | bytes 4128 | tf_op jit(solution)/shard_map/ppermute | solution.py:370
  77.6 0.8 shard_map.118
  (29 shorter events, 4.7 us)
Async XLA Ops:
  3.3 14.2 %all-to-all-start = ((bf16[8,208,128]{2,1,0:T(8,128)(2,1)}), bf16[8,208,128]{2,1,0:T(8,128)(2,1)}, u32[]{:S(2)}, u32[]{:S(2)}) async-start(bf16[8,208,128]{2,1,0:T(8,128)(2,1)} %get-tuple-element.40), calls=%async_computation | async-start | bytes 851968 | tf_op jit(solution)/shard_map/all_to_all | solution.py:374
  8.5 7.8 %collective-permute-start.2 = (f32[48,128]{1,0:T(8,128)}, f32[48,128]{1,0:T(8,128)S(1)}, u32[]{:S(2)}, u32[]{:S(2)}) collective-permute-start(f32[48,128]{1,0:T(8,128)} %bitcast.3), channel_id=1, source_target_pairs={{0,24},{8,16},{16,8},{24,0},{1,25},{9,17},{17,9},{25,1},{2,26},{10... | collective-permute-start | bytes 73736 | tf_op jit(solution)/shard_map/ppermute | solution.py:361
  12.5 4.9 %collective-permute-start.1 = (f32[48,128]{1,0:T(8,128)}, f32[48,128]{1,0:T(8,128)S(1)}, u32[]{:S(2)}, u32[]{:S(2)}) collective-permute-start(f32[48,128]{1,0:T(8,128)} %bitcast.4), channel_id=1, source_target_pairs={{0,16},{8,24},{16,0},{24,8},{1,17},{9,25},{17,1},{25,9},{2,18},{10... | collective-permute-start | bytes 73736 | tf_op jit(solution)/shard_map/ppermute | solution.py:361
  12.6 4.9 %collective-permute-start = (f32[48,128]{1,0:T(8,128)}, f32[48,128]{1,0:T(8,128)S(1)}, u32[]{:S(2)}, u32[]{:S(2)}) collective-permute-start(f32[48,128]{1,0:T(8,128)} %bitcast.5), channel_id=1, source_target_pairs={{0,8},{8,0},{16,24},{24,16},{1,9},{9,1},{17,25},{25,17},{2,10},{10... | collective-permute-start | bytes 73736 | tf_op jit(solution)/shard_map/ppermute | solution.py:361
  13.2 0.8 copy-start.1
  14.0 13.8 %copy-start = (f32[8,128]{1,0:T(8,128)S(1)}, f32[8,128]{1,0:T(8,128)}, u32[]{:S(2)}) copy-start(f32[8,128]{1,0:T(8,128)} %get-tuple-element.36.weight_ref) | copy-start | bytes 12292
  19.6 1.2 %collective-permute-start.3 = (f32[16,128]{1,0:T(8,128)S(1)}, f32[16,128]{1,0:T(8,128)S(1)}, u32[]{:S(2)}, u32[]{:S(2)}) collective-permute-start(f32[16,128]{1,0:T(8,128)S(1)} %get-tuple-element.46.one_ref), channel_id=1, source_target_pairs={{0,1},{1,0},{2,3},{3,2},{4,5},{5,4},{6,7},{7,6},{8,9},{9,8},{10,11... | collective-permute-start | bytes 24584 | tf_op jit(solution)/shard_map/ppermute | solution.py:368
  20.8 4.5 %collective-permute-start.6 = (f32[16,128]{1,0:T(8,128)S(1)}, f32[16,128]{1,0:T(8,128)S(1)}, u32[]{:S(2)}, u32[]{:S(2)}) collective-permute-start(f32[16,128]{1,0:T(8,128)S(1)} %shard_map.107.refs_1_), channel_id=1, source_target_pairs={{0,6},{1,7},{2,4},{3,5},{4,2},{5,3},{6,0},{7,1},{8,14},{9,15},{10,... | collective-permute-start | bytes 24584 | tf_op jit(solution)/shard_map/ppermute | solution.py:370
  23.6 3.7 %collective-permute-start.5 = (f32[16,128]{1,0:T(8,128)S(1)}, f32[16,128]{1,0:T(8,128)S(1)}, u32[]{:S(2)}, u32[]{:S(2)}) collective-permute-start(f32[16,128]{1,0:T(8,128)S(1)} %shard_map.107.refs_1_), channel_id=1, source_target_pairs={{0,4},{1,5},{2,6},{3,7},{4,0},{5,1},{6,2},{7,3},{8,12},{9,13},{10,... | collective-permute-start | bytes 24584 | tf_op jit(solution)/shard_map/ppermute | solution.py:370
  24.1 3.7 %collective-permute-start.4 = (f32[16,128]{1,0:T(8,128)S(1)}, f32[16,128]{1,0:T(8,128)S(1)}, u32[]{:S(2)}, u32[]{:S(2)}) collective-permute-start(f32[16,128]{1,0:T(8,128)S(1)} %shard_map.107.refs_1_), channel_id=1, source_target_pairs={{0,2},{1,3},{2,0},{3,1},{4,6},{5,7},{6,4},{7,5},{8,10},{9,11},{10,... | collective-permute-start | bytes 24584 | tf_op jit(solution)/shard_map/ppermute | solution.py:370
  28.2 5.6 %collective-permute-start.9 = (f32[32,128]{1,0:T(8,128)S(1)}, f32[32,128]{1,0:T(8,128)S(1)}, u32[]{:S(2)}, u32[]{:S(2)}) collective-permute-start(f32[32,128]{1,0:T(8,128)S(1)} %get-tuple-element.47.refs_0_), channel_id=1, source_target_pairs={{0,24},{8,16},{16,8},{24,0},{1,25},{9,17},{17,9},{25,1},{2,26},{10... | collective-permute-start | bytes 49160 | tf_op jit(solution)/shard_map/ppermute | solution.py:361
  30.8 4.6 %collective-permute-start.8 = (f32[32,128]{1,0:T(8,128)S(1)}, f32[32,128]{1,0:T(8,128)S(1)}, u32[]{:S(2)}, u32[]{:S(2)}) collective-permute-start(f32[32,128]{1,0:T(8,128)S(1)} %get-tuple-element.47.refs_0_), channel_id=1, source_target_pairs={{0,16},{8,24},{16,0},{24,8},{1,17},{9,25},{17,1},{25,9},{2,18},{10... | collective-permute-start | bytes 49160 | tf_op jit(solution)/shard_map/ppermute | solution.py:361
  30.8 4.6 %collective-permute-start.7 = (f32[32,128]{1,0:T(8,128)S(1)}, f32[32,128]{1,0:T(8,128)S(1)}, u32[]{:S(2)}, u32[]{:S(2)}) collective-permute-start(f32[32,128]{1,0:T(8,128)S(1)} %get-tuple-element.47.refs_0_), channel_id=1, source_target_pairs={{0,8},{8,0},{16,24},{24,16},{1,9},{9,1},{17,25},{25,17},{2,10},{10... | collective-permute-start | bytes 49160 | tf_op jit(solution)/shard_map/ppermute | solution.py:361
  37.5 1.2 %collective-permute-start.10 = (f32[16,128]{1,0:T(8,128)S(1)}, f32[16,128]{1,0:T(8,128)S(1)}, u32[]{:S(2)}, u32[]{:S(2)}) collective-permute-start(f32[16,128]{1,0:T(8,128)S(1)} %get-tuple-element.52.one_ref), channel_id=1, source_target_pairs={{0,1},{1,0},{2,3},{3,2},{4,5},{5,4},{6,7},{7,6},{8,9},{9,8},{10,11... | collective-permute-start | bytes 24584 | tf_op jit(solution)/shard_map/ppermute | solution.py:368
  38.7 4.5 %collective-permute-start.13 = (f32[16,128]{1,0:T(8,128)S(1)}, f32[16,128]{1,0:T(8,128)S(1)}, u32[]{:S(2)}, u32[]{:S(2)}) collective-permute-start(f32[16,128]{1,0:T(8,128)S(1)} %shard_map.111.refs_0_), channel_id=1, source_target_pairs={{0,6},{1,7},{2,4},{3,5},{4,2},{5,3},{6,0},{7,1},{8,14},{9,15},{10,... | collective-permute-start | bytes 24584 | tf_op jit(solution)/shard_map/ppermute | solution.py:370
  40.2 3.7 %collective-permute-start.12 = (f32[16,128]{1,0:T(8,128)S(1)}, f32[16,128]{1,0:T(8,128)S(1)}, u32[]{:S(2)}, u32[]{:S(2)}) collective-permute-start(f32[16,128]{1,0:T(8,128)S(1)} %shard_map.111.refs_0_), channel_id=1, source_target_pairs={{0,4},{1,5},{2,6},{3,7},{4,0},{5,1},{6,2},{7,3},{8,12},{9,13},{10,... | collective-permute-start | bytes 24584 | tf_op jit(solution)/shard_map/ppermute | solution.py:370
  41.4 3.7 %collective-permute-start.11 = (f32[16,128]{1,0:T(8,128)S(1)}, f32[16,128]{1,0:T(8,128)S(1)}, u32[]{:S(2)}, u32[]{:S(2)}) collective-permute-start(f32[16,128]{1,0:T(8,128)S(1)} %shard_map.111.refs_0_), channel_id=1, source_target_pairs={{0,2},{1,3},{2,0},{3,1},{4,6},{5,7},{6,4},{7,5},{8,10},{9,11},{10,... | collective-permute-start | bytes 24584 | tf_op jit(solution)/shard_map/ppermute | solution.py:370
  45.5 5.5 %collective-permute-start.16 = (f32[24,128]{1,0:T(8,128)S(1)}, f32[24,128]{1,0:T(8,128)S(1)}, u32[]{:S(2)}, u32[]{:S(2)}) collective-permute-start(f32[24,128]{1,0:T(8,128)S(1)} %get-tuple-element.56.refs_1_), channel_id=1, source_target_pairs={{0,24},{8,16},{16,8},{24,0},{1,25},{9,17},{17,9},{25,1},{2,26},{10... | collective-permute-start | bytes 36872 | tf_op jit(solution)/shard_map/ppermute | solution.py:361
  47.0 4.6 %collective-permute-start.15 = (f32[24,128]{1,0:T(8,128)S(1)}, f32[24,128]{1,0:T(8,128)S(1)}, u32[]{:S(2)}, u32[]{:S(2)}) collective-permute-start(f32[24,128]{1,0:T(8,128)S(1)} %get-tuple-element.56.refs_1_), channel_id=1, source_target_pairs={{0,16},{8,24},{16,0},{24,8},{1,17},{9,25},{17,1},{25,9},{2,18},{10... | collective-permute-start | bytes 36872 | tf_op jit(solution)/shard_map/ppermute | solution.py:361
  47.7 4.1 %collective-permute-start.14 = (f32[24,128]{1,0:T(8,128)S(1)}, f32[24,128]{1,0:T(8,128)S(1)}, u32[]{:S(2)}, u32[]{:S(2)}) collective-permute-start(f32[24,128]{1,0:T(8,128)S(1)} %get-tuple-element.56.refs_1_), channel_id=1, source_target_pairs={{0,8},{8,0},{16,24},{24,16},{1,9},{9,1},{17,25},{25,17},{2,10},{10... | collective-permute-start | bytes 36872 | tf_op jit(solution)/shard_map/ppermute | solution.py:361
  53.8 1.2 %collective-permute-start.17 = (f32[16,128]{1,0:T(8,128)S(1)}, f32[16,128]{1,0:T(8,128)S(1)}, u32[]{:S(2)}, u32[]{:S(2)}) collective-permute-start(f32[16,128]{1,0:T(8,128)S(1)} %get-tuple-element.57.one_ref), channel_id=1, source_target_pairs={{0,1},{1,0},{2,3},{3,2},{4,5},{5,4},{6,7},{7,6},{8,9},{9,8},{10,11... | collective-permute-start | bytes 24584 | tf_op jit(solution)/shard_map/ppermute | solution.py:368
  54.9 4.5 %collective-permute-start.20 = (f32[16,128]{1,0:T(8,128)S(1)}, f32[16,128]{1,0:T(8,128)S(1)}, u32[]{:S(2)}, u32[]{:S(2)}) collective-permute-start(f32[16,128]{1,0:T(8,128)S(1)} %shard_map.114.refs_0_), channel_id=1, source_target_pairs={{0,6},{1,7},{2,4},{3,5},{4,2},{5,3},{6,0},{7,1},{8,14},{9,15},{10,... | collective-permute-start | bytes 24584 | tf_op jit(solution)/shard_map/ppermute | solution.py:370
  56.6 3.7 %collective-permute-start.19 = (f32[16,128]{1,0:T(8,128)S(1)}, f32[16,128]{1,0:T(8,128)S(1)}, u32[]{:S(2)}, u32[]{:S(2)}) collective-permute-start(f32[16,128]{1,0:T(8,128)S(1)} %shard_map.114.refs_0_), channel_id=1, source_target_pairs={{0,4},{1,5},{2,6},{3,7},{4,0},{5,1},{6,2},{7,3},{8,12},{9,13},{10,... | collective-permute-start | bytes 24584 | tf_op jit(solution)/shard_map/ppermute | solution.py:370
  57.1 3.7 %collective-permute-start.18 = (f32[16,128]{1,0:T(8,128)S(1)}, f32[16,128]{1,0:T(8,128)S(1)}, u32[]{:S(2)}, u32[]{:S(2)}) collective-permute-start(f32[16,128]{1,0:T(8,128)S(1)} %shard_map.114.refs_0_), channel_id=1, source_target_pairs={{0,2},{1,3},{2,0},{3,1},{4,6},{5,7},{6,4},{7,5},{8,10},{9,11},{10,... | collective-permute-start | bytes 24584 | tf_op jit(solution)/shard_map/ppermute | solution.py:370
  61.2 5.5 %collective-permute-start.23 = (f32[24,128]{1,0:T(8,128)S(1)}, f32[24,128]{1,0:T(8,128)S(1)}, u32[]{:S(2)}, u32[]{:S(2)}) collective-permute-start(f32[24,128]{1,0:T(8,128)S(1)} %get-tuple-element.61.refs_1_), channel_id=1, source_target_pairs={{0,24},{8,16},{16,8},{24,0},{1,25},{9,17},{17,9},{25,1},{2,26},{10... | collective-permute-start | bytes 36872 | tf_op jit(solution)/shard_map/ppermute | solution.py:361
  63.7 4.6 %collective-permute-start.22 = (f32[24,128]{1,0:T(8,128)S(1)}, f32[24,128]{1,0:T(8,128)S(1)}, u32[]{:S(2)}, u32[]{:S(2)}) collective-permute-start(f32[24,128]{1,0:T(8,128)S(1)} %get-tuple-element.61.refs_1_), channel_id=1, source_target_pairs={{0,16},{8,24},{16,0},{24,8},{1,17},{9,25},{17,1},{25,9},{2,18},{10... | collective-permute-start | bytes 36872 | tf_op jit(solution)/shard_map/ppermute | solution.py:361
  64.6 3.8 %collective-permute-start.21 = (f32[24,128]{1,0:T(8,128)S(1)}, f32[24,128]{1,0:T(8,128)S(1)}, u32[]{:S(2)}, u32[]{:S(2)}) collective-permute-start(f32[24,128]{1,0:T(8,128)S(1)} %get-tuple-element.61.refs_1_), channel_id=1, source_target_pairs={{0,8},{8,0},{16,24},{24,16},{1,9},{9,1},{17,25},{25,17},{2,10},{10... | collective-permute-start | bytes 36872 | tf_op jit(solution)/shard_map/ppermute | solution.py:361
  70.0 1.2 %collective-permute-start.24 = (f32[8,128]{1,0:T(8,128)S(1)}, f32[8,128]{1,0:T(8,128)S(1)}, u32[]{:S(2)}, u32[]{:S(2)}) collective-permute-start(f32[8,128]{1,0:T(8,128)S(1)} %get-tuple-element.62.one_ref), channel_id=1, source_target_pairs={{0,1},{1,0},{2,3},{3,2},{4,5},{5,4},{6,7},{7,6},{8,9},{9,8},{10,11... | collective-permute-start | bytes 12296 | tf_op jit(solution)/shard_map/ppermute | solution.py:368
  71.2 4.5 %collective-permute-start.27 = (f32[8,128]{1,0:T(8,128)S(1)}, f32[8,128]{1,0:T(8,128)S(1)}, u32[]{:S(2)}, u32[]{:S(2)}) collective-permute-start(f32[8,128]{1,0:T(8,128)S(1)} %shard_map.117.refs_0_), channel_id=1, source_target_pairs={{0,6},{1,7},{2,4},{3,5},{4,2},{5,3},{6,0},{7,1},{8,14},{9,15},{10,... | collective-permute-start | bytes 12296 | tf_op jit(solution)/shard_map/ppermute | solution.py:370
  72.7 3.6 %collective-permute-start.26 = (f32[8,128]{1,0:T(8,128)S(1)}, f32[8,128]{1,0:T(8,128)S(1)}, u32[]{:S(2)}, u32[]{:S(2)}) collective-permute-start(f32[8,128]{1,0:T(8,128)S(1)} %shard_map.117.refs_0_), channel_id=1, source_target_pairs={{0,4},{1,5},{2,6},{3,7},{4,0},{5,1},{6,2},{7,3},{8,12},{9,13},{10,... | collective-permute-start | bytes 12296 | tf_op jit(solution)/shard_map/ppermute | solution.py:370
  74.0 3.6 %collective-permute-start.25 = (f32[8,128]{1,0:T(8,128)S(1)}, f32[8,128]{1,0:T(8,128)S(1)}, u32[]{:S(2)}, u32[]{:S(2)}) collective-permute-start(f32[8,128]{1,0:T(8,128)S(1)} %shard_map.117.refs_0_), channel_id=1, source_target_pairs={{0,2},{1,3},{2,0},{3,1},{4,6},{5,7},{6,4},{7,5},{8,10},{9,11},{10,... | collective-permute-start | bytes 12296 | tf_op jit(solution)/shard_map/ppermute | solution.py:370

commit v13 on v11

--- a/solution.py
+++ b/solution.py
@@ -11,12 +11,13 @@
 from jax.sharding import PartitionSpec as P
 
 CR = 2
-WAYS = 2
+WAYS = 4
 CHUNK = 16
 TERMS = 3
 STEPS = 3
 ROWS = 8
 VMEM = pl.BlockSpec(memory_space=pltpu.VMEM)
+SMEM = pl.BlockSpec(memory_space=pltpu.SMEM)
 ANY = pl.BlockSpec(memory_space=pl.ANY)
 F32 = jnp.float32
 BF16 = jnp.bfloat16
@@ -249,73 +250,56 @@
         out_ref[2 * s:2 * s + 2, :] = ref[at:at + ROWS, :][0:2].astype(jnp.int32)
 
 
-def widen(rows, pick_ref):
-    return lax.dot_general(split(rows), pick_ref[...], (((0,), (0,)), ((), ())), preferred_element_type=F32)
-
-
-def image_kernel(dims, no, first, last, ids_in, all_in, lat_ref, foot_ref, pick_ref, norm_ref, field_ref, *refs):
+def image_kernel(dims, no, first, last, ids_ref, all_ref, lat_ref, foot_ref, pick_ref, norm_ref, field_ref, *refs):
     nc, nb, modes, groups, band = dims
     if not first:
         prior_ref, refs = refs[0], refs[1:]
     ways = min(no, WAYS)
-    ids_ref, all_ref, sems = refs[-3:]
-    refs = refs[:-3]
-    copies = [
-        pltpu.make_async_copy(ids_in, ids_ref, sems.at[0]),
-        pltpu.make_async_copy(all_in, all_ref, sems.at[1]),
-    ]
-    for copy in copies:
-        copy.start()
-    kept = 7 + ways
+    kept = 6 + ways
     coef_refs, refs = refs[:-kept], refs[-kept:]
-    wide_ref, refs = refs[-1], refs[:-1]
     sum_refs, refs = refs[-ways:], refs[:-ways]
     if last:
         out_ref, row_ref, mine_ref, alpha_ref, next_ref, held_ref = refs
     else:
         out_ref, row_ref, next_ref, vector_ref, alpha_ref, held_ref = refs
     mine = nc * nb
-    chunks = mine // CHUNK
     periods = field_ref.shape[0]
     per_dev = row_ref.shape[0]
     subs = ROWS
     rows = sum(ref.shape[0] for ref in coef_refs) // no
     coef_refs = pieces(coef_refs, no, rows)
-    ahead = no <= 4
     for s in range(no):
-        if ahead:
-            for q in range(chunks):
-                wide_ref[s * chunks + q] = widen(coef_refs[s][q * CHUNK:(q + 1) * CHUNK, :], pick_ref)[:CR * modes]
-        else:
-            held_ref[s] = coef_refs[s][:mine, :]
+        held_ref[s] = coef_refs[s][:mine, :]
     for sum_ref in sum_refs:
         sum_ref[...] = jnp.zeros_like(sum_ref)
     gain = jnp.sum(tree_sum(ref[mine:mine + subs, :] for ref in coef_refs), keepdims=True)
     alpha_ref[...] = jnp.broadcast_to(1.0 + gain, alpha_ref.shape)
     norm = norm_ref[0:1, :]
     scale = 1.0 / norm
-    for copy in copies:
-        copy.wait()
     own = ids_ref[0, 3 * nb]
 
     def group(at, carry):
         found = [at * ways + i for i in range(ways)]
-        if permuted(no):
-            found = [own ^ at_i for at_i in found]
-        for q in range(chunks):
-            slots = [at_i * chunks + q for at_i in found] if ahead else range(ways)
-            if not ahead:
-                for at_i, slot in zip(found, slots):
-                    wide_ref[slot] = widen(held_ref[at_i, q * CHUNK:(q + 1) * CHUNK, :], pick_ref)[:CR * modes]
-            for at in range(CHUNK):
-                for at_i, slot, sum_ref in zip(found, slots, sum_refs):
-                    period = all_ref[2 * at_i, q * CHUNK + at]
-                    row = all_ref[2 * at_i + 1, q * CHUNK + at] * CR
-                    total = sum_ref[period]
-                    for r in range(CR):
-                        coef = wide_ref[slot, r * modes:(r + 1) * modes, at * 128:(at + 1) * 128]
-                        total += coef * lat_ref[row + r]
-                    sum_ref[period] = total
+        for chunk in range(0, mine, CHUNK):
+            left = [split(held_ref[s, chunk:chunk + CHUNK, :]) for s in found]
+            left = jnp.concatenate(left, axis=1)
+            for pair in range(0, CHUNK, 2):
+                wide = lax.dot_general(
+                    left,
+                    pick_ref[:, pair * 128:(pair + 2) * 128],
+                    (((0,), (0,)), ((), ())),
+                    preferred_element_type=F32,
+                )
+                for at_t in range(2):
+                    for i, s in enumerate(found):
+                        period = all_ref[2 * s, chunk + pair + at_t]
+                        row = all_ref[2 * s + 1, chunk + pair + at_t] * CR
+                        total = sum_refs[i][period]
+                        for r in range(CR):
+                            start = i * 128 + r * modes
+                            coef = wide[start:start + modes, at_t * 128:(at_t + 1) * 128]
+                            total += coef * lat_ref[row + r]
+                        sum_refs[i][period] = total
         return carry
 
     if no <= 4:
@@ -495,14 +479,11 @@
                 *([] if last else [field_shape]),
                 small,
             ),
-            [VMEM] * (7 + len(before) + len(coefs)),
+            [SMEM] * 2 + [VMEM] * (5 + len(before) + len(coefs)),
             ids, every, lat, foot, pick, norm, field, *before, *coefs,
             scratch=[pltpu.VMEM(field_shape.shape, F32)] * last
             + [pltpu.VMEM((no, mine, 128), F32)]
-            + [pltpu.VMEM(field_shape.shape, F32)] * ways
-            + [pltpu.VMEM((no * mine // CHUNK if no <= 4 else ways, CR * modes, CHUNK * 128), F32)]
-            + [pltpu.SMEM((nc, 128), jnp.int32), pltpu.SMEM((2 * no, 128), jnp.int32)]
-            + [pltpu.SemaphoreType.DMA((2,))],
+            + [pltpu.VMEM(field_shape.shape, F32)] * ways,
             limit=16,
         )
         vector = None if last else vector[0]

time: 78.8 us -> 78.1 us (level)
  no operation moved by 1% of the time
where the time goes in v13:
time: 78.1 us; the launch traced here: 77.7 us
  starting transfers between devices  37.4 us (48%)
  waiting for transfers between devices  24.9 us (32%)
  Pallas kernels  14 us (18%)
    ppermute x12, starting transfers between devices, share(): lax.ppermute(array, axis, [(d, d ^ s) for d in range(size)])  17.9 us
    pallas_call x15, Pallas kernels, call(): pl.pallas_call(kernel, out_shape=outs, in_specs=specs, out_specs=jax.tree...  14 us
    ppermute x12, starting transfers between devices, addends(): lax.ppermute(both, axis, [(d, d ^ s) for d in range(size)])  14 us
    ppermute x12, waiting for transfers between devices, addends(): lax.ppermute(both, axis, [(d, d ^ s) for d in range(size)])  11.6 us
    ppermute x12, waiting for transfers between devices, share(): lax.ppermute(array, axis, [(d, d ^ s) for d in range(size)])  8.61 us
    all_to_all x1, starting transfers between devices, swap(): return lax.all_to_all(array, axis, split_axis=0, concat_axis=0, tiled=True)  5.18 us
    ppermute x4, waiting for transfers between devices, addends(): other = lax.ppermute(array, axis, [(d, d ^ 1) for d in range(size)])  4.63 us
  transfers between devices with their start and end apart: 29, of which 25 were waited for; matrix products, arithmetic and copies ran while one was open for 0% of the time, Pallas kernels for 3%

profile of v13, /device:TPU:0, one launch (start us, length us, event | category | flops | bytes accessed | tf_op | source)
XLA Modules:
  0.0 77.7 jit_solution(5785610708721829544)
XLA Ops:
  0.6 2.7 %shard_map.104 = (bf16[8,208,128]{2,1,0:T(8,128)(2,1)}, f32[8,128]{1,0:T(8,128)}) custom-call(s32[1]{0:T(128)} %bitcast.1.place_any, bf16[384,384]{1,0:T(8,128)(2,1)} %constant.14.clone.high_any, bf16[384,384]{1,0:T(8,128)(2,1)} %constant.15.clone.low_any, bf16[2,128,768]{2,1,0:T(8,128)(2,1)} %foot_any.1, s32[2]{0:T(128)} %off_any.1, s32[2]{0:T(128)} %sub_any.1, ...), custom_call_target="tpu_custom_call" | custom-call | tf_op jit(solution)/shard_map/pallas_call | solution.py:41
  3.3 5.2 %all-to-all-start = ((bf16[8,208,128]{2,1,0:T(8,128)(2,1)}), bf16[8,208,128]{2,1,0:T(8,128)(2,1)}, u32[]{:S(2)}, u32[]{:S(2)}) async-start(bf16[8,208,128]{2,1,0:T(8,128)(2,1)} %get-tuple-element.39), calls=%async_computation | async-start | bytes 851968 | tf_op jit(solution)/shard_map/all_to_all | solution.py:370
  8.5 4.1 %collective-permute-start.2 = (f32[48,128]{1,0:T(8,128)}, f32[48,128]{1,0:T(8,128)S(1)}, u32[]{:S(2)}, u32[]{:S(2)}) collective-permute-start(f32[48,128]{1,0:T(8,128)} %bitcast.3), channel_id=1, source_target_pairs={{0,24},{8,16},{16,8},{24,0},{1,25},{9,17},{17,9},{25,1},{2,26},{10... | collective-permute-start | bytes 73736 | tf_op jit(solution)/shard_map/ppermute | solution.py:357
  12.6 0.6 collective-permute-start
  13.2 0.8 copy-done.1
  14.0 2.3 %shard_map.105 = (f32[128,48,128]{2,1,0:T(8,128)S(1)}, f32[48,128]{1,0:T(8,128)S(1)}, bf16[48,2048]{1,0:T(8,128)(2,1)S(1)}) custom-call(f32[48,128,128]{2,1,0:T(8,128)} %lat_any, f32[48,128]{1,0:T(8,128)S(1)} %bitcast.6), custom_call_target="tpu_custom_call" | custom-call | bytes 6340608 | tf_op jit(solution)/shard_map/pallas_call | solution.py:41
  16.3 1.2 %collective-permute-done.1.refs_2_ = f32[48,128]{1,0:T(8,128)S(1)} collective-permute-done((f32[48,128]{1,0:T(8,128)}, f32[48,128]{1,0:T(8,128)S(1)}, u32[]{:S(2)}, u32[]{:S(2)}) %collective-permute-start.1) | collective-permute-done | bytes 24608 | tf_op jit(solution)/shard_map/ppermute | solution.py:357
  17.5 1.9 %shard_map.106 = (f32[16,128]{1,0:T(8,128)S(1)}, f32[4,48,128]{2,1,0:T(8,128)S(1)}, bf16[8,192,128]{2,1,0:T(8,128)(2,1)S(1)}, s32[8,128]{1,0:T(8,128)S(1)}, bf16...) custom-call(f32[128,48,128]{2,1,0:T(8,128)S(1)} %get-tuple-element.38.lat_ref, bf16[8,208,128]{2,1,0:T(8,128)(2,1)} %all-to-all-done.came_ref, ...), custom_call_target="tpu_custom_call" | custom-call | tf_op jit(solution)/shard_map/pallas_call | solution.py:41
  19.5 1.2 %collective-permute-done.3.other_ref = f32[16,128]{1,0:T(8,128)S(1)} collective-permute-done((f32[16,128]{1,0:T(8,128)S(1)}, f32[16,128]{1,0:T(8,128)S(1)}, u32[]{:S(2)}, u32[]{:S(2)}) %collective-permute-start.3) | collective-permute-done | bytes 8224 | tf_op jit(solution)/shard_map/ppermute | solution.py:364
  20.7 2.8 %collective-permute-start.6 = (f32[16,128]{1,0:T(8,128)S(1)}, f32[16,128]{1,0:T(8,128)S(1)}, u32[]{:S(2)}, u32[]{:S(2)}) collective-permute-start(f32[16,128]{1,0:T(8,128)S(1)} %shard_map.107.refs_1_), channel_id=1, source_target_pairs={{0,6},{1,7},{2,4},{3,5},{4,2},{5,3},{6,0},{7,1},{8,14},{9,15},{10,... | collective-permute-start | bytes 24584 | tf_op jit(solution)/shard_map/ppermute | solution.py:366
  24.2 1.1 %collective-permute-done.6.refs_4_ = f32[16,128]{1,0:T(8,128)S(1)} collective-permute-done((f32[16,128]{1,0:T(8,128)S(1)}, f32[16,128]{1,0:T(8,128)S(1)}, u32[]{:S(2)}, u32[]{:S(2)}) %collective-permute-start.6) | collective-permute-done | bytes 8224 | tf_op jit(solution)/shard_map/ppermute | solution.py:366
  25.2 1.9 %collective-permute-done.5.refs_3_ = f32[16,128]{1,0:T(8,128)S(1)} collective-permute-done((f32[16,128]{1,0:T(8,128)S(1)}, f32[16,128]{1,0:T(8,128)S(1)}, u32[]{:S(2)}, u32[]{:S(2)}) %collective-permute-start.5) | collective-permute-done | bytes 8224 | tf_op jit(solution)/shard_map/ppermute | solution.py:366
  28.1 2.6 %collective-permute-start.9 = (f32[32,128]{1,0:T(8,128)S(1)}, f32[32,128]{1,0:T(8,128)S(1)}, u32[]{:S(2)}, u32[]{:S(2)}) collective-permute-start(f32[32,128]{1,0:T(8,128)S(1)} %get-tuple-element.46.refs_0_), channel_id=1, source_target_pairs={{0,24},{8,16},{16,8},{24,0},{1,25},{9,17},{17,9},{25,1},{2,26},{10... | collective-permute-start | bytes 49160 | tf_op jit(solution)/shard_map/ppermute | solution.py:357
  30.7 1.8 %collective-permute-start.7 = (f32[32,128]{1,0:T(8,128)S(1)}, f32[32,128]{1,0:T(8,128)S(1)}, u32[]{:S(2)}, u32[]{:S(2)}) collective-permute-start(f32[32,128]{1,0:T(8,128)S(1)} %get-tuple-element.46.refs_0_), channel_id=1, source_target_pairs={{0,8},{8,0},{16,24},{24,16},{1,9},{9,1},{17,25},{25,17},{2,10},{10... | collective-permute-start | bytes 49160 | tf_op jit(solution)/shard_map/ppermute | solution.py:357
  32.5 1.1 %collective-permute-done.9.refs_3_ = f32[32,128]{1,0:T(8,128)S(1)} collective-permute-done((f32[32,128]{1,0:T(8,128)S(1)}, f32[32,128]{1,0:T(8,128)S(1)}, u32[]{:S(2)}, u32[]{:S(2)}) %collective-permute-start.9) | collective-permute-done | bytes 16416 | tf_op jit(solution)/shard_map/ppermute | solution.py:357
  33.6 1.7 %collective-permute-done.8.refs_2_ = f32[32,128]{1,0:T(8,128)S(1)} collective-permute-done((f32[32,128]{1,0:T(8,128)S(1)}, f32[32,128]{1,0:T(8,128)S(1)}, u32[]{:S(2)}, u32[]{:S(2)}) %collective-permute-start.8) | collective-permute-done | bytes 16416 | tf_op jit(solution)/shard_map/ppermute | solution.py:357
  35.3 1.7 %shard_map.110 = (f32[16,128]{1,0:T(8,128)S(1)}, f32[1,48,128]{2,1,0:T(8,128)S(1)}, f32[4,48,128]{2,1,0:T(8,128)S(1)}, f32[4,48,128]{2,1,0:T(8,128)S(1)}, f32[8,128]{1,0:T(8,128)S(1)}) custom-call(s32[8,128]{1,0:T(8,128)S(1)} %get-tuple-element.41.ids_ref, s32[8,128]{1,0:T(8,128)S(1)} %shard_map.109.all_ref, f32[128,48,128]{2,1,0:T(8,128)S(1)} %get-tuple-element.38.lat_ref, ...), custom_call_target="tpu_custom_call" | custom-call | tf_op jit(solution)/shard_map/pallas_call | solution.py:41
  37.2 1.2 %collective-permute-done.10.other_ref = f32[16,128]{1,0:T(8,128)S(1)} collective-permute-done((f32[16,128]{1,0:T(8,128)S(1)}, f32[16,128]{1,0:T(8,128)S(1)}, u32[]{:S(2)}, u32[]{:S(2)}) %collective-permute-start.10) | collective-permute-done | bytes 8224 | tf_op jit(solution)/shard_map/ppermute | solution.py:364
  38.3 1.5 %collective-permute-start.13 = (f32[16,128]{1,0:T(8,128)S(1)}, f32[16,128]{1,0:T(8,128)S(1)}, u32[]{:S(2)}, u32[]{:S(2)}) collective-permute-start(f32[16,128]{1,0:T(8,128)S(1)} %shard_map.111.refs_0_), channel_id=1, source_target_pairs={{0,6},{1,7},{2,4},{3,5},{4,2},{5,3},{6,0},{7,1},{8,14},{9,15},{10,... | collective-permute-start | bytes 24584 | tf_op jit(solution)/shard_map/ppermute | solution.py:366
  39.8 1.3 %collective-permute-start.12 = (f32[16,128]{1,0:T(8,128)S(1)}, f32[16,128]{1,0:T(8,128)S(1)}, u32[]{:S(2)}, u32[]{:S(2)}) collective-permute-start(f32[16,128]{1,0:T(8,128)S(1)} %shard_map.111.refs_0_), channel_id=1, source_target_pairs={{0,4},{1,5},{2,6},{3,7},{4,0},{5,1},{6,2},{7,3},{8,12},{9,13},{10,... | collective-permute-start | bytes 24584 | tf_op jit(solution)/shard_map/ppermute | solution.py:366
  41.1 0.7 collective-permute-start.11
  41.8 1.1 %collective-permute-done.13.refs_3_ = f32[16,128]{1,0:T(8,128)S(1)} collective-permute-done((f32[16,128]{1,0:T(8,128)S(1)}, f32[16,128]{1,0:T(8,128)S(1)}, u32[]{:S(2)}, u32[]{:S(2)}) %collective-permute-start.13) | collective-permute-done | bytes 8224 | tf_op jit(solution)/shard_map/ppermute | solution.py:366
  42.9 0.6 collective-permute-done.12.refs_2_
  43.5 1.3 %collective-permute-done.11.refs_1_ = f32[16,128]{1,0:T(8,128)S(1)} collective-permute-done((f32[16,128]{1,0:T(8,128)S(1)}, f32[16,128]{1,0:T(8,128)S(1)}, u32[]{:S(2)}, u32[]{:S(2)}) %collective-permute-start.11) | collective-permute-done | bytes 8224 | tf_op jit(solution)/shard_map/ppermute | solution.py:366
  45.2 1.5 %collective-permute-start.16 = (f32[24,128]{1,0:T(8,128)S(1)}, f32[24,128]{1,0:T(8,128)S(1)}, u32[]{:S(2)}, u32[]{:S(2)}) collective-permute-start(f32[24,128]{1,0:T(8,128)S(1)} %get-tuple-element.54.refs_1_), channel_id=1, source_target_pairs={{0,24},{8,16},{16,8},{24,0},{1,25},{9,17},{17,9},{25,1},{2,26},{10... | collective-permute-start | bytes 36872 | tf_op jit(solution)/shard_map/ppermute | solution.py:357
  46.7 0.6 collective-permute-start.15
  47.3 2.3 %collective-permute-start.14 = (f32[24,128]{1,0:T(8,128)S(1)}, f32[24,128]{1,0:T(8,128)S(1)}, u32[]{:S(2)}, u32[]{:S(2)}) collective-permute-start(f32[24,128]{1,0:T(8,128)S(1)} %get-tuple-element.54.refs_1_), channel_id=1, source_target_pairs={{0,8},{8,0},{16,24},{24,16},{1,9},{9,1},{17,25},{25,17},{2,10},{10... | collective-permute-start | bytes 36872 | tf_op jit(solution)/shard_map/ppermute | solution.py:357
  49.6 1.1 %collective-permute-done.16.refs_4_ = f32[24,128]{1,0:T(8,128)S(1)} collective-permute-done((f32[24,128]{1,0:T(8,128)S(1)}, f32[24,128]{1,0:T(8,128)S(1)}, u32[]{:S(2)}, u32[]{:S(2)}) %collective-permute-start.16) | collective-permute-done | bytes 12320 | tf_op jit(solution)/shard_map/ppermute | solution.py:357
  51.4 1.7 %shard_map.113 = (f32[16,128]{1,0:T(8,128)S(1)}, f32[1,48,128]{2,1,0:T(8,128)S(1)}, f32[4,48,128]{2,1,0:T(8,128)S(1)}, f32[4,48,128]{2,1,0:T(8,128)S(1)}, f32[8,128]{1,0:T(8,128)S(1)}) custom-call(s32[8,128]{1,0:T(8,128)S(1)} %get-tuple-element.41.ids_ref, s32[8,128]{1,0:T(8,128)S(1)} %shard_map.109.all_ref, f32[128,48,128]{2,1,0:T(8,128)S(1)} %get-tuple-element.38.lat_ref, ...), custom_call_target="tpu_custom_call" | custom-call | tf_op jit(solution)/shard_map/pallas_call | solution.py:41
  53.2 1.2 %collective-permute-done.17.other_ref = f32[16,128]{1,0:T(8,128)S(1)} collective-permute-done((f32[16,128]{1,0:T(8,128)S(1)}, f32[16,128]{1,0:T(8,128)S(1)}, u32[]{:S(2)}, u32[]{:S(2)}) %collective-permute-start.17) | collective-permute-done | bytes 8224 | tf_op jit(solution)/shard_map/ppermute | solution.py:364
  54.4 1.7 %collective-permute-start.20 = (f32[16,128]{1,0:T(8,128)S(1)}, f32[16,128]{1,0:T(8,128)S(1)}, u32[]{:S(2)}, u32[]{:S(2)}) collective-permute-start(f32[16,128]{1,0:T(8,128)S(1)} %shard_map.114.refs_0_), channel_id=1, source_target_pairs={{0,6},{1,7},{2,4},{3,5},{4,2},{5,3},{6,0},{7,1},{8,14},{9,15},{10,... | collective-permute-start | bytes 24584 | tf_op jit(solution)/shard_map/ppermute | solution.py:366
  56.6 1.3 %collective-permute-start.18 = (f32[16,128]{1,0:T(8,128)S(1)}, f32[16,128]{1,0:T(8,128)S(1)}, u32[]{:S(2)}, u32[]{:S(2)}) collective-permute-start(f32[16,128]{1,0:T(8,128)S(1)} %shard_map.114.refs_0_), channel_id=1, source_target_pairs={{0,2},{1,3},{2,0},{3,1},{4,6},{5,7},{6,4},{7,5},{8,10},{9,11},{10,... | collective-permute-start | bytes 24584 | tf_op jit(solution)/shard_map/ppermute | solution.py:366
  57.9 1.1 %collective-permute-done.20.refs_3_ = f32[16,128]{1,0:T(8,128)S(1)} collective-permute-done((f32[16,128]{1,0:T(8,128)S(1)}, f32[16,128]{1,0:T(8,128)S(1)}, u32[]{:S(2)}, u32[]{:S(2)}) %collective-permute-start.20) | collective-permute-done | bytes 8224 | tf_op jit(solution)/shard_map/ppermute | solution.py:366
  58.9 0.8 collective-permute-done.19.refs_2_
  60.7 2.5 %collective-permute-start.23 = (f32[24,128]{1,0:T(8,128)S(1)}, f32[24,128]{1,0:T(8,128)S(1)}, u32[]{:S(2)}, u32[]{:S(2)}) collective-permute-start(f32[24,128]{1,0:T(8,128)S(1)} %get-tuple-element.59.refs_1_), channel_id=1, source_target_pairs={{0,24},{8,16},{16,8},{24,0},{1,25},{9,17},{17,9},{25,1},{2,26},{10... | collective-permute-start | bytes 36872 | tf_op jit(solution)/shard_map/ppermute | solution.py:357
  63.2 0.9 %collective-permute-start.22 = (f32[24,128]{1,0:T(8,128)S(1)}, f32[24,128]{1,0:T(8,128)S(1)}, u32[]{:S(2)}, u32[]{:S(2)}) collective-permute-start(f32[24,128]{1,0:T(8,128)S(1)} %get-tuple-element.59.refs_1_), channel_id=1, source_target_pairs={{0,16},{8,24},{16,0},{24,8},{1,17},{9,25},{17,1},{25,9},{2,18},{10... | collective-permute-start | bytes 36872 | tf_op jit(solution)/shard_map/ppermute | solution.py:357
  64.1 1.0 %collective-permute-start.21 = (f32[24,128]{1,0:T(8,128)S(1)}, f32[24,128]{1,0:T(8,128)S(1)}, u32[]{:S(2)}, u32[]{:S(2)}) collective-permute-start(f32[24,128]{1,0:T(8,128)S(1)} %get-tuple-element.59.refs_1_), channel_id=1, source_target_pairs={{0,8},{8,0},{16,24},{24,16},{1,9},{9,1},{17,25},{25,17},{2,10},{10... | collective-permute-start | bytes 36872 | tf_op jit(solution)/shard_map/ppermute | solution.py:357
  65.1 1.1 %collective-permute-done.23.refs_4_ = f32[24,128]{1,0:T(8,128)S(1)} collective-permute-done((f32[24,128]{1,0:T(8,128)S(1)}, f32[24,128]{1,0:T(8,128)S(1)}, u32[]{:S(2)}, u32[]{:S(2)}) %collective-permute-start.23) | collective-permute-done | bytes 12320 | tf_op jit(solution)/shard_map/ppermute | solution.py:357
  66.2 1.6 %collective-permute-done.22.refs_3_ = f32[24,128]{1,0:T(8,128)S(1)} collective-permute-done((f32[24,128]{1,0:T(8,128)S(1)}, f32[24,128]{1,0:T(8,128)S(1)}, u32[]{:S(2)}, u32[]{:S(2)}) %collective-permute-start.22) | collective-permute-done | bytes 12320 | tf_op jit(solution)/shard_map/ppermute | solution.py:357
  67.9 1.5 %shard_map.116 = (f32[8,128]{1,0:T(8,128)S(1)}, f32[1,48,128]{2,1,0:T(8,128)S(1)}, f32[1,48,128]{2,1,0:T(8,128)S(1)}, f32[8,128]{1,0:T(8,128)S(1)}) custom-call(s32[8,128]{1,0:T(8,128)S(1)} %get-tuple-element.41.ids_ref, s32[8,128]{1,0:T(8,128)S(1)} %shard_map.109.all_ref, f32[128,48,128]{2,1,0:T(8,128)S(1)} %get-tuple-element.38.lat_ref, ...), custom_call_target="tpu_custom_call" | custom-call | tf_op jit(solution)/shard_map/pallas_call | solution.py:41
  69.4 1.2 %collective-permute-done.24.other_ref = f32[8,128]{1,0:T(8,128)S(1)} collective-permute-done((f32[8,128]{1,0:T(8,128)S(1)}, f32[8,128]{1,0:T(8,128)S(1)}, u32[]{:S(2)}, u32[]{:S(2)}) %collective-permute-start.24) | collective-permute-done | bytes 4128 | tf_op jit(solution)/shard_map/ppermute | solution.py:364
  70.6 1.5 %collective-permute-start.27 = (f32[8,128]{1,0:T(8,128)S(1)}, f32[8,128]{1,0:T(8,128)S(1)}, u32[]{:S(2)}, u32[]{:S(2)}) collective-permute-start(f32[8,128]{1,0:T(8,128)S(1)} %shard_map.117.refs_0_), channel_id=1, source_target_pairs={{0,6},{1,7},{2,4},{3,5},{4,2},{5,3},{6,0},{7,1},{8,14},{9,15},{10,... | collective-permute-start | bytes 12296 | tf_op jit(solution)/shard_map/ppermute | solution.py:366
  72.1 1.3 %collective-permute-start.26 = (f32[8,128]{1,0:T(8,128)S(1)}, f32[8,128]{1,0:T(8,128)S(1)}, u32[]{:S(2)}, u32[]{:S(2)}) collective-permute-start(f32[8,128]{1,0:T(8,128)S(1)} %shard_map.117.refs_0_), channel_id=1, source_target_pairs={{0,4},{1,5},{2,6},{3,7},{4,0},{5,1},{6,2},{7,3},{8,12},{9,13},{10,... | collective-permute-start | bytes 12296 | tf_op jit(solution)/shard_map/ppermute | solution.py:366
  73.4 0.7 collective-permute-start.25
  74.1 1.0 %collective-permute-done.27.refs_3_ = f32[8,128]{1,0:T(8,128)S(1)} collective-permute-done((f32[8,128]{1,0:T(8,128)S(1)}, f32[8,128]{1,0:T(8,128)S(1)}, u32[]{:S(2)}, u32[]{:S(2)}) %collective-permute-start.27) | collective-permute-done | bytes 4128 | tf_op jit(solution)/shard_map/ppermute | solution.py:366
  75.1 0.6 collective-permute-done.26.refs_2_
  75.7 1.3 %collective-permute-done.25.refs_1_ = f32[8,128]{1,0:T(8,128)S(1)} collective-permute-done((f32[8,128]{1,0:T(8,128)S(1)}, f32[8,128]{1,0:T(8,128)S(1)}, u32[]{:S(2)}, u32[]{:S(2)}) %collective-permute-start.25) | collective-permute-done | bytes 4128 | tf_op jit(solution)/shard_map/ppermute | solution.py:366
  77.0 0.8 %shard_map.118 = (f32[4,1,48,128]{3,2,1,0:T(8,128)}, f32[2,3]{1,0:T(2,128)}) custom-call(f32[8,128]{1,0:T(8,128)S(1)} %shard_map.117.refs_0_, f32[8,128]{1,0:T(8,128)S(1)} %collective-permute-done.25.refs_1_, f32[8,128]{1,0:T(8,128)S(1)} %collective-permute-done.26.refs_2_, f32[8,128]{1,0:T(8,128)S(1)} %collective-permute-done.27.refs_3_, ...), custom_call_target="tpu_custom_call" | custom-call | tf_op jit(solution)/shard_map/pallas_call | solution.py:41
  (29 shorter events, 4.8 us)
Async XLA Ops:
  3.3 14.2 %all-to-all-start = ((bf16[8,208,128]{2,1,0:T(8,128)(2,1)}), bf16[8,208,128]{2,1,0:T(8,128)(2,1)}, u32[]{:S(2)}, u32[]{:S(2)}) async-start(bf16[8,208,128]{2,1,0:T(8,128)(2,1)} %get-tuple-element.39), calls=%async_computation | async-start | bytes 851968 | tf_op jit(solution)/shard_map/all_to_all | solution.py:370
  8.5 7.8 %collective-permute-start.2 = (f32[48,128]{1,0:T(8,128)}, f32[48,128]{1,0:T(8,128)S(1)}, u32[]{:S(2)}, u32[]{:S(2)}) collective-permute-start(f32[48,128]{1,0:T(8,128)} %bitcast.3), channel_id=1, source_target_pairs={{0,24},{8,16},{16,8},{24,0},{1,25},{9,17},{17,9},{25,1},{2,26},{10... | collective-permute-start | bytes 73736 | tf_op jit(solution)/shard_map/ppermute | solution.py:357
  12.5 4.9 %collective-permute-start.1 = (f32[48,128]{1,0:T(8,128)}, f32[48,128]{1,0:T(8,128)S(1)}, u32[]{:S(2)}, u32[]{:S(2)}) collective-permute-start(f32[48,128]{1,0:T(8,128)} %bitcast.4), channel_id=1, source_target_pairs={{0,16},{8,24},{16,0},{24,8},{1,17},{9,25},{17,1},{25,9},{2,18},{10... | collective-permute-start | bytes 73736 | tf_op jit(solution)/shard_map/ppermute | solution.py:357
  12.6 4.9 %collective-permute-start = (f32[48,128]{1,0:T(8,128)}, f32[48,128]{1,0:T(8,128)S(1)}, u32[]{:S(2)}, u32[]{:S(2)}) collective-permute-start(f32[48,128]{1,0:T(8,128)} %bitcast.5), channel_id=1, source_target_pairs={{0,8},{8,0},{16,24},{24,16},{1,9},{9,1},{17,25},{25,17},{2,10},{10... | collective-permute-start | bytes 73736 | tf_op jit(solution)/shard_map/ppermute | solution.py:357
  13.2 0.8 copy-start.1
  14.0 13.7 %copy-start = (f32[8,128]{1,0:T(8,128)S(1)}, f32[8,128]{1,0:T(8,128)}, u32[]{:S(2)}) copy-start(f32[8,128]{1,0:T(8,128)} %get-tuple-element.35.weight_ref) | copy-start | bytes 12292
  19.4 1.2 %collective-permute-start.3 = (f32[16,128]{1,0:T(8,128)S(1)}, f32[16,128]{1,0:T(8,128)S(1)}, u32[]{:S(2)}, u32[]{:S(2)}) collective-permute-start(f32[16,128]{1,0:T(8,128)S(1)} %get-tuple-element.45.one_ref), channel_id=1, source_target_pairs={{0,1},{1,0},{2,3},{3,2},{4,5},{5,4},{6,7},{7,6},{8,9},{9,8},{10,11... | collective-permute-start | bytes 24584 | tf_op jit(solution)/shard_map/ppermute | solution.py:364
  20.7 4.5 %collective-permute-start.6 = (f32[16,128]{1,0:T(8,128)S(1)}, f32[16,128]{1,0:T(8,128)S(1)}, u32[]{:S(2)}, u32[]{:S(2)}) collective-permute-start(f32[16,128]{1,0:T(8,128)S(1)} %shard_map.107.refs_1_), channel_id=1, source_target_pairs={{0,6},{1,7},{2,4},{3,5},{4,2},{5,3},{6,0},{7,1},{8,14},{9,15},{10,... | collective-permute-start | bytes 24584 | tf_op jit(solution)/shard_map/ppermute | solution.py:366
  23.4 3.7 %collective-permute-start.5 = (f32[16,128]{1,0:T(8,128)S(1)}, f32[16,128]{1,0:T(8,128)S(1)}, u32[]{:S(2)}, u32[]{:S(2)}) collective-permute-start(f32[16,128]{1,0:T(8,128)S(1)} %shard_map.107.refs_1_), channel_id=1, source_target_pairs={{0,4},{1,5},{2,6},{3,7},{4,0},{5,1},{6,2},{7,3},{8,12},{9,13},{10,... | collective-permute-start | bytes 24584 | tf_op jit(solution)/shard_map/ppermute | solution.py:366
  24.0 3.7 %collective-permute-start.4 = (f32[16,128]{1,0:T(8,128)S(1)}, f32[16,128]{1,0:T(8,128)S(1)}, u32[]{:S(2)}, u32[]{:S(2)}) collective-permute-start(f32[16,128]{1,0:T(8,128)S(1)} %shard_map.107.refs_1_), channel_id=1, source_target_pairs={{0,2},{1,3},{2,0},{3,1},{4,6},{5,7},{6,4},{7,5},{8,10},{9,11},{10,... | collective-permute-start | bytes 24584 | tf_op jit(solution)/shard_map/ppermute | solution.py:366
  28.1 5.6 %collective-permute-start.9 = (f32[32,128]{1,0:T(8,128)S(1)}, f32[32,128]{1,0:T(8,128)S(1)}, u32[]{:S(2)}, u32[]{:S(2)}) collective-permute-start(f32[32,128]{1,0:T(8,128)S(1)} %get-tuple-element.46.refs_0_), channel_id=1, source_target_pairs={{0,24},{8,16},{16,8},{24,0},{1,25},{9,17},{17,9},{25,1},{2,26},{10... | collective-permute-start | bytes 49160 | tf_op jit(solution)/shard_map/ppermute | solution.py:357
  30.7 4.6 %collective-permute-start.8 = (f32[32,128]{1,0:T(8,128)S(1)}, f32[32,128]{1,0:T(8,128)S(1)}, u32[]{:S(2)}, u32[]{:S(2)}) collective-permute-start(f32[32,128]{1,0:T(8,128)S(1)} %get-tuple-element.46.refs_0_), channel_id=1, source_target_pairs={{0,16},{8,24},{16,0},{24,8},{1,17},{9,25},{17,1},{25,9},{2,18},{10... | collective-permute-start | bytes 49160 | tf_op jit(solution)/shard_map/ppermute | solution.py:357
  30.7 4.6 %collective-permute-start.7 = (f32[32,128]{1,0:T(8,128)S(1)}, f32[32,128]{1,0:T(8,128)S(1)}, u32[]{:S(2)}, u32[]{:S(2)}) collective-permute-start(f32[32,128]{1,0:T(8,128)S(1)} %get-tuple-element.46.refs_0_), channel_id=1, source_target_pairs={{0,8},{8,0},{16,24},{24,16},{1,9},{9,1},{17,25},{25,17},{2,10},{10... | collective-permute-start | bytes 49160 | tf_op jit(solution)/shard_map/ppermute | solution.py:357
  37.1 1.2 %collective-permute-start.10 = (f32[16,128]{1,0:T(8,128)S(1)}, f32[16,128]{1,0:T(8,128)S(1)}, u32[]{:S(2)}, u32[]{:S(2)}) collective-permute-start(f32[16,128]{1,0:T(8,128)S(1)} %get-tuple-element.50.one_ref), channel_id=1, source_target_pairs={{0,1},{1,0},{2,3},{3,2},{4,5},{5,4},{6,7},{7,6},{8,9},{9,8},{10,11... | collective-permute-start | bytes 24584 | tf_op jit(solution)/shard_map/ppermute | solution.py:364
  38.3 4.5 %collective-permute-start.13 = (f32[16,128]{1,0:T(8,128)S(1)}, f32[16,128]{1,0:T(8,128)S(1)}, u32[]{:S(2)}, u32[]{:S(2)}) collective-permute-start(f32[16,128]{1,0:T(8,128)S(1)} %shard_map.111.refs_0_), channel_id=1, source_target_pairs={{0,6},{1,7},{2,4},{3,5},{4,2},{5,3},{6,0},{7,1},{8,14},{9,15},{10,... | collective-permute-start | bytes 24584 | tf_op jit(solution)/shard_map/ppermute | solution.py:366
  39.8 3.7 %collective-permute-start.12 = (f32[16,128]{1,0:T(8,128)S(1)}, f32[16,128]{1,0:T(8,128)S(1)}, u32[]{:S(2)}, u32[]{:S(2)}) collective-permute-start(f32[16,128]{1,0:T(8,128)S(1)} %shard_map.111.refs_0_), channel_id=1, source_target_pairs={{0,4},{1,5},{2,6},{3,7},{4,0},{5,1},{6,2},{7,3},{8,12},{9,13},{10,... | collective-permute-start | bytes 24584 | tf_op jit(solution)/shard_map/ppermute | solution.py:366
  41.1 3.7 %collective-permute-start.11 = (f32[16,128]{1,0:T(8,128)S(1)}, f32[16,128]{1,0:T(8,128)S(1)}, u32[]{:S(2)}, u32[]{:S(2)}) collective-permute-start(f32[16,128]{1,0:T(8,128)S(1)} %shard_map.111.refs_0_), channel_id=1, source_target_pairs={{0,2},{1,3},{2,0},{3,1},{4,6},{5,7},{6,4},{7,5},{8,10},{9,11},{10,... | collective-permute-start | bytes 24584 | tf_op jit(solution)/shard_map/ppermute | solution.py:366
  45.2 5.5 %collective-permute-start.16 = (f32[24,128]{1,0:T(8,128)S(1)}, f32[24,128]{1,0:T(8,128)S(1)}, u32[]{:S(2)}, u32[]{:S(2)}) collective-permute-start(f32[24,128]{1,0:T(8,128)S(1)} %get-tuple-element.54.refs_1_), channel_id=1, source_target_pairs={{0,24},{8,16},{16,8},{24,0},{1,25},{9,17},{17,9},{25,1},{2,26},{10... | collective-permute-start | bytes 36872 | tf_op jit(solution)/shard_map/ppermute | solution.py:357
  46.7 4.6 %collective-permute-start.15 = (f32[24,128]{1,0:T(8,128)S(1)}, f32[24,128]{1,0:T(8,128)S(1)}, u32[]{:S(2)}, u32[]{:S(2)}) collective-permute-start(f32[24,128]{1,0:T(8,128)S(1)} %get-tuple-element.54.refs_1_), channel_id=1, source_target_pairs={{0,16},{8,24},{16,0},{24,8},{1,17},{9,25},{17,1},{25,9},{2,18},{10... | collective-permute-start | bytes 36872 | tf_op jit(solution)/shard_map/ppermute | solution.py:357
  47.3 4.1 %collective-permute-start.14 = (f32[24,128]{1,0:T(8,128)S(1)}, f32[24,128]{1,0:T(8,128)S(1)}, u32[]{:S(2)}, u32[]{:S(2)}) collective-permute-start(f32[24,128]{1,0:T(8,128)S(1)} %get-tuple-element.54.refs_1_), channel_id=1, source_target_pairs={{0,8},{8,0},{16,24},{24,16},{1,9},{9,1},{17,25},{25,17},{2,10},{10... | collective-permute-start | bytes 36872 | tf_op jit(solution)/shard_map/ppermute | solution.py:357
  53.2 1.2 %collective-permute-start.17 = (f32[16,128]{1,0:T(8,128)S(1)}, f32[16,128]{1,0:T(8,128)S(1)}, u32[]{:S(2)}, u32[]{:S(2)}) collective-permute-start(f32[16,128]{1,0:T(8,128)S(1)} %get-tuple-element.55.one_ref), channel_id=1, source_target_pairs={{0,1},{1,0},{2,3},{3,2},{4,5},{5,4},{6,7},{7,6},{8,9},{9,8},{10,11... | collective-permute-start | bytes 24584 | tf_op jit(solution)/shard_map/ppermute | solution.py:364
  54.4 4.5 %collective-permute-start.20 = (f32[16,128]{1,0:T(8,128)S(1)}, f32[16,128]{1,0:T(8,128)S(1)}, u32[]{:S(2)}, u32[]{:S(2)}) collective-permute-start(f32[16,128]{1,0:T(8,128)S(1)} %shard_map.114.refs_0_), channel_id=1, source_target_pairs={{0,6},{1,7},{2,4},{3,5},{4,2},{5,3},{6,0},{7,1},{8,14},{9,15},{10,... | collective-permute-start | bytes 24584 | tf_op jit(solution)/shard_map/ppermute | solution.py:366
  56.0 3.7 %collective-permute-start.19 = (f32[16,128]{1,0:T(8,128)S(1)}, f32[16,128]{1,0:T(8,128)S(1)}, u32[]{:S(2)}, u32[]{:S(2)}) collective-permute-start(f32[16,128]{1,0:T(8,128)S(1)} %shard_map.114.refs_0_), channel_id=1, source_target_pairs={{0,4},{1,5},{2,6},{3,7},{4,0},{5,1},{6,2},{7,3},{8,12},{9,13},{10,... | collective-permute-start | bytes 24584 | tf_op jit(solution)/shard_map/ppermute | solution.py:366
  56.6 3.7 %collective-permute-start.18 = (f32[16,128]{1,0:T(8,128)S(1)}, f32[16,128]{1,0:T(8,128)S(1)}, u32[]{:S(2)}, u32[]{:S(2)}) collective-permute-start(f32[16,128]{1,0:T(8,128)S(1)} %shard_map.114.refs_0_), channel_id=1, source_target_pairs={{0,2},{1,3},{2,0},{3,1},{4,6},{5,7},{6,4},{7,5},{8,10},{9,11},{10,... | collective-permute-start | bytes 24584 | tf_op jit(solution)/shard_map/ppermute | solution.py:366
  60.7 5.5 %collective-permute-start.23 = (f32[24,128]{1,0:T(8,128)S(1)}, f32[24,128]{1,0:T(8,128)S(1)}, u32[]{:S(2)}, u32[]{:S(2)}) collective-permute-start(f32[24,128]{1,0:T(8,128)S(1)} %get-tuple-element.59.refs_1_), channel_id=1, source_target_pairs={{0,24},{8,16},{16,8},{24,0},{1,25},{9,17},{17,9},{25,1},{2,26},{10... | collective-permute-start | bytes 36872 | tf_op jit(solution)/shard_map/ppermute | solution.py:357
  63.2 4.6 %collective-permute-start.22 = (f32[24,128]{1,0:T(8,128)S(1)}, f32[24,128]{1,0:T(8,128)S(1)}, u32[]{:S(2)}, u32[]{:S(2)}) collective-permute-start(f32[24,128]{1,0:T(8,128)S(1)} %get-tuple-element.59.refs_1_), channel_id=1, source_target_pairs={{0,16},{8,24},{16,0},{24,8},{1,17},{9,25},{17,1},{25,9},{2,18},{10... | collective-permute-start | bytes 36872 | tf_op jit(solution)/shard_map/ppermute | solution.py:357
  64.1 3.8 %collective-permute-start.21 = (f32[24,128]{1,0:T(8,128)S(1)}, f32[24,128]{1,0:T(8,128)S(1)}, u32[]{:S(2)}, u32[]{:S(2)}) collective-permute-start(f32[24,128]{1,0:T(8,128)S(1)} %get-tuple-element.59.refs_1_), channel_id=1, source_target_pairs={{0,8},{8,0},{16,24},{24,16},{1,9},{9,1},{17,25},{25,17},{2,10},{10... | collective-permute-start | bytes 36872 | tf_op jit(solution)/shard_map/ppermute | solution.py:357
  69.4 1.2 %collective-permute-start.24 = (f32[8,128]{1,0:T(8,128)S(1)}, f32[8,128]{1,0:T(8,128)S(1)}, u32[]{:S(2)}, u32[]{:S(2)}) collective-permute-start(f32[8,128]{1,0:T(8,128)S(1)} %get-tuple-element.60.one_ref), channel_id=1, source_target_pairs={{0,1},{1,0},{2,3},{3,2},{4,5},{5,4},{6,7},{7,6},{8,9},{9,8},{10,11... | collective-permute-start | bytes 12296 | tf_op jit(solution)/shard_map/ppermute | solution.py:364
  70.6 4.5 %collective-permute-start.27 = (f32[8,128]{1,0:T(8,128)S(1)}, f32[8,128]{1,0:T(8,128)S(1)}, u32[]{:S(2)}, u32[]{:S(2)}) collective-permute-start(f32[8,128]{1,0:T(8,128)S(1)} %shard_map.117.refs_0_), channel_id=1, source_target_pairs={{0,6},{1,7},{2,4},{3,5},{4,2},{5,3},{6,0},{7,1},{8,14},{9,15},{10,... | collective-permute-start | bytes 12296 | tf_op jit(solution)/shard_map/ppermute | solution.py:366
  72.1 3.6 %collective-permute-start.26 = (f32[8,128]{1,0:T(8,128)S(1)}, f32[8,128]{1,0:T(8,128)S(1)}, u32[]{:S(2)}, u32[]{:S(2)}) collective-permute-start(f32[8,128]{1,0:T(8,128)S(1)} %shard_map.117.refs_0_), channel_id=1, source_target_pairs={{0,4},{1,5},{2,6},{3,7},{4,0},{5,1},{6,2},{7,3},{8,12},{9,13},{10,... | collective-permute-start | bytes 12296 | tf_op jit(solution)/shard_map/ppermute | solution.py:366
  73.4 3.6 %collective-permute-start.25 = (f32[8,128]{1,0:T(8,128)S(1)}, f32[8,128]{1,0:T(8,128)S(1)}, u32[]{:S(2)}, u32[]{:S(2)}) collective-permute-start(f32[8,128]{1,0:T(8,128)S(1)} %shard_map.117.refs_0_), channel_id=1, source_target_pairs={{0,2},{1,3},{2,0},{3,1},{4,6},{5,7},{6,4},{7,5},{8,10},{9,11},{10,... | collective-permute-start | bytes 12296 | tf_op jit(solution)/shard_map/ppermute | solution.py:366

commit v14 on v13

--- a/solution.py
+++ b/solution.py
@@ -12,6 +12,7 @@
 
 CR = 2
 WAYS = 4
+PARTS = 4
 CHUNK = 16
 TERMS = 3
 STEPS = 3
@@ -133,10 +134,12 @@
     return total
 
 
-def forward(dims, field_ref, lat_ref, foot_ref, ids_ref, sim_ref):
+def forward(dims, field_ref, lat_ref, foot_ref, ids_ref, part_refs, sim_ref):
     nc, nb, modes, groups, band = dims
     subs = sim_ref.shape[0] - ROWS
-    sim_ref[...] = jnp.zeros_like(sim_ref)
+    for part_ref in part_refs:
+        part_ref[...] = jnp.zeros_like(part_ref)
+    found = []
     for j in range(nc):
         for b in range(nb):
             period = ids_ref[j, b]
@@ -148,8 +151,14 @@
                 at = (b * CR + r) * modes
                 term = foot_ref[j, at:at + modes, :].astype(F32) * column
                 total = term if total is None else total + term
-            sim_ref[pl.ds(sub, 1), :] += jnp.sum(total, axis=0, keepdims=True)
+            found.append((sub, jnp.sum(total, axis=0, keepdims=True)))
     sim_ref[subs:, :] = fold(field_ref)
+    for at in range(0, len(found), len(part_refs)):
+        here = list(zip(part_refs, found[at:at + len(part_refs)]))
+        sums = [part_ref[pl.ds(sub, 1), :] + line for part_ref, (sub, line) in here]
+        for (part_ref, (sub, _)), line in zip(here, sums):
+            part_ref[pl.ds(sub, 1), :] = line
+    sim_ref[:subs, :] = tree_sum(part_ref[...] for part_ref in part_refs)
 
 
 def pieces(refs, size, rows):
@@ -170,6 +179,7 @@
 
 def first_kernel(dims, no, lat_ref, came_ref, *refs):
     nc, nb, modes, _, _ = dims
+    refs, part_refs = refs[:-PARTS], refs[-PARTS:]
     near_refs, refs = refs[:-8], refs[-8:]
     out_ref, field_ref, foot_ref, all_ref, choose_ref, tail_ref, ids_ref, sem = refs
     rows = nb * CR * modes
@@ -198,7 +208,7 @@
             tail = jnp.where(tail_lane == j * nb + b, value, tail)
     choose_ref[...] = jnp.where(lane % (choose_ref.shape[1] // TERMS) == subs, 1.0, 0.0).astype(BF16)
     tail_ref[...] = tail.astype(F32)
-    forward(dims, field_ref, lat_ref, foot_ref, ids_ref, out_ref)
+    forward(dims, field_ref, lat_ref, foot_ref, ids_ref, part_refs, out_ref)
 
 
 def split(values):
@@ -255,6 +265,7 @@
     if not first:
         prior_ref, refs = refs[0], refs[1:]
     ways = min(no, WAYS)
+    refs, part_refs = refs[:-PARTS], refs[-PARTS:]
     kept = 6 + ways
     coef_refs, refs = refs[:-kept], refs[-kept:]
     sum_refs, refs = refs[-ways:], refs[:-ways]
@@ -291,15 +302,18 @@
                     preferred_element_type=F32,
                 )
                 for at_t in range(2):
+                    at_block = chunk + pair + at_t
+                    totals = []
                     for i, s in enumerate(found):
-                        period = all_ref[2 * s, chunk + pair + at_t]
-                        row = all_ref[2 * s + 1, chunk + pair + at_t] * CR
-                        total = sum_refs[i][period]
+                        row = all_ref[2 * s + 1, at_block] * CR
+                        total = sum_refs[i][all_ref[2 * s, at_block]]
                         for r in range(CR):
                             start = i * 128 + r * modes
                             coef = wide[start:start + modes, at_t * 128:(at_t + 1) * 128]
                             total += coef * lat_ref[row + r]
-                        sum_refs[i][period] = total
+                        totals.append(total)
+                    for i, s in enumerate(found):
+                        sum_refs[i][all_ref[2 * s, at_block]] = totals[i]
         return carry
 
     if no <= 4:
@@ -322,7 +336,7 @@
         for l in range(per_dev):
             mine_ref[l] = next_ref[own * per_dev + l]
     else:
-        forward(dims, next_ref, lat_ref, foot_ref, ids_ref, out_ref)
+        forward(dims, next_ref, lat_ref, foot_ref, ids_ref, part_refs, out_ref)
 
 
 def finish_kernel(factor, sums, *refs):
@@ -445,7 +459,7 @@
         ),
         [VMEM] * (2 + len(near)),
         lat, came, *near,
-        scratch=[pltpu.SMEM((nc, 128), jnp.int32), pltpu.SemaphoreType.DMA],
+        scratch=[pltpu.SMEM((nc, 128), jnp.int32), pltpu.SemaphoreType.DMA] + [pltpu.VMEM((subs, ob), F32)] * PARTS,
     )
     ways = min(no, WAYS)
     rows, alphas, norms = [], [], []
@@ -483,7 +497,8 @@
             ids, every, lat, foot, pick, norm, field, *before, *coefs,
             scratch=[pltpu.VMEM(field_shape.shape, F32)] * last
             + [pltpu.VMEM((no, mine, 128), F32)]
-            + [pltpu.VMEM(field_shape.shape, F32)] * ways,
+            + [pltpu.VMEM(field_shape.shape, F32)] * ways
+            + [pltpu.VMEM((subs, ob), F32)] * PARTS,
             limit=16,
         )
         vector = None if last else vector[0]

time: 78.1 us -> 78.2 us (level)
  no operation moved by 1% of the time
where the time goes in v14:
time: 78.2 us; the launch traced here: 77.8 us
  starting transfers between devices  37.4 us (48%)
  waiting for transfers between devices  24.8 us (32%)
  Pallas kernels  14.1 us (18%)
    ppermute x12, starting transfers between devices, share(): lax.ppermute(array, axis, [(d, d ^ s) for d in range(size)])  17.9 us
    pallas_call x15, Pallas kernels, call(): pl.pallas_call(kernel, out_shape=outs, in_specs=specs, out_specs=jax.tree...  14.1 us
    ppermute x12, starting transfers between devices, addends(): lax.ppermute(both, axis, [(d, d ^ s) for d in range(size)])  14 us
    ppermute x12, waiting for transfers between devices, addends(): lax.ppermute(both, axis, [(d, d ^ s) for d in range(size)])  11.6 us
    ppermute x12, waiting for transfers between devices, share(): lax.ppermute(array, axis, [(d, d ^ s) for d in range(size)])  8.61 us
    all_to_all x1, starting transfers between devices, swap(): return lax.all_to_all(array, axis, split_axis=0, concat_axis=0, tiled=True)  5.18 us
    ppermute x4, waiting for transfers between devices, addends(): other = lax.ppermute(array, axis, [(d, d ^ 1) for d in range(size)])  4.63 us
  transfers between devices with their start and end apart: 29, of which 25 were waited for; matrix products, arithmetic and copies ran while one was open for 0% of the time, Pallas kernels for 3%

profile of v14, /device:TPU:0, one launch (start us, length us, event | category | flops | bytes accessed | tf_op | source)
XLA Modules:
  0.0 77.8 jit_solution(18440853761646100685)
XLA Ops:
  0.6 2.7 %shard_map.104 = (bf16[8,208,128]{2,1,0:T(8,128)(2,1)}, f32[8,128]{1,0:T(8,128)}) custom-call(s32[1]{0:T(128)} %bitcast.1.place_any, bf16[384,384]{1,0:T(8,128)(2,1)} %constant.14.clone.high_any, bf16[384,384]{1,0:T(8,128)(2,1)} %constant.15.clone.low_any, bf16[2,128,768]{2,1,0:T(8,128)(2,1)} %foot_any.1, s32[2]{0:T(128)} %off_any.1, s32[2]{0:T(128)} %sub_any.1, ...), custom_call_target="tpu_custom_call" | custom-call | tf_op jit(solution)/shard_map/pallas_call | solution.py:42
  3.3 5.2 %all-to-all-start = ((bf16[8,208,128]{2,1,0:T(8,128)(2,1)}), bf16[8,208,128]{2,1,0:T(8,128)(2,1)}, u32[]{:S(2)}, u32[]{:S(2)}) async-start(bf16[8,208,128]{2,1,0:T(8,128)(2,1)} %get-tuple-element.39), calls=%async_computation | async-start | bytes 851968 | tf_op jit(solution)/shard_map/all_to_all | solution.py:384
  8.5 4.1 %collective-permute-start.2 = (f32[48,128]{1,0:T(8,128)}, f32[48,128]{1,0:T(8,128)S(1)}, u32[]{:S(2)}, u32[]{:S(2)}) collective-permute-start(f32[48,128]{1,0:T(8,128)} %bitcast.3), channel_id=1, source_target_pairs={{0,24},{8,16},{16,8},{24,0},{1,25},{9,17},{17,9},{25,1},{2,26},{10... | collective-permute-start | bytes 73736 | tf_op jit(solution)/shard_map/ppermute | solution.py:371
  12.6 0.6 collective-permute-start
  13.2 0.8 copy-done.1
  14.0 2.3 %shard_map.105 = (f32[128,48,128]{2,1,0:T(8,128)S(1)}, f32[48,128]{1,0:T(8,128)S(1)}, bf16[48,2048]{1,0:T(8,128)(2,1)S(1)}) custom-call(f32[48,128,128]{2,1,0:T(8,128)} %lat_any, f32[48,128]{1,0:T(8,128)S(1)} %bitcast.6), custom_call_target="tpu_custom_call" | custom-call | bytes 6340608 | tf_op jit(solution)/shard_map/pallas_call | solution.py:42
  16.3 1.2 %collective-permute-done.1.refs_2_ = f32[48,128]{1,0:T(8,128)S(1)} collective-permute-done((f32[48,128]{1,0:T(8,128)}, f32[48,128]{1,0:T(8,128)S(1)}, u32[]{:S(2)}, u32[]{:S(2)}) %collective-permute-start.1) | collective-permute-done | bytes 24608 | tf_op jit(solution)/shard_map/ppermute | solution.py:371
  17.5 1.9 %shard_map.106 = (f32[16,128]{1,0:T(8,128)S(1)}, f32[4,48,128]{2,1,0:T(8,128)S(1)}, bf16[8,192,128]{2,1,0:T(8,128)(2,1)S(1)}, s32[8,128]{1,0:T(8,128)S(1)}, bf16...) custom-call(f32[128,48,128]{2,1,0:T(8,128)S(1)} %get-tuple-element.38.lat_ref, bf16[8,208,128]{2,1,0:T(8,128)(2,1)} %all-to-all-done.came_ref, ...), custom_call_target="tpu_custom_call" | custom-call | tf_op jit(solution)/shard_map/pallas_call | solution.py:42
  19.5 1.2 %collective-permute-done.3.other_ref = f32[16,128]{1,0:T(8,128)S(1)} collective-permute-done((f32[16,128]{1,0:T(8,128)S(1)}, f32[16,128]{1,0:T(8,128)S(1)}, u32[]{:S(2)}, u32[]{:S(2)}) %collective-permute-start.3) | collective-permute-done | bytes 8224 | tf_op jit(solution)/shard_map/ppermute | solution.py:378
  20.7 2.8 %collective-permute-start.6 = (f32[16,128]{1,0:T(8,128)S(1)}, f32[16,128]{1,0:T(8,128)S(1)}, u32[]{:S(2)}, u32[]{:S(2)}) collective-permute-start(f32[16,128]{1,0:T(8,128)S(1)} %shard_map.107.refs_1_), channel_id=1, source_target_pairs={{0,6},{1,7},{2,4},{3,5},{4,2},{5,3},{6,0},{7,1},{8,14},{9,15},{10,... | collective-permute-start | bytes 24584 | tf_op jit(solution)/shard_map/ppermute | solution.py:380
  24.2 1.1 %collective-permute-done.6.refs_4_ = f32[16,128]{1,0:T(8,128)S(1)} collective-permute-done((f32[16,128]{1,0:T(8,128)S(1)}, f32[16,128]{1,0:T(8,128)S(1)}, u32[]{:S(2)}, u32[]{:S(2)}) %collective-permute-start.6) | collective-permute-done | bytes 8224 | tf_op jit(solution)/shard_map/ppermute | solution.py:380
  25.2 1.9 %collective-permute-done.5.refs_3_ = f32[16,128]{1,0:T(8,128)S(1)} collective-permute-done((f32[16,128]{1,0:T(8,128)S(1)}, f32[16,128]{1,0:T(8,128)S(1)}, u32[]{:S(2)}, u32[]{:S(2)}) %collective-permute-start.5) | collective-permute-done | bytes 8224 | tf_op jit(solution)/shard_map/ppermute | solution.py:380
  28.1 2.6 %collective-permute-start.9 = (f32[32,128]{1,0:T(8,128)S(1)}, f32[32,128]{1,0:T(8,128)S(1)}, u32[]{:S(2)}, u32[]{:S(2)}) collective-permute-start(f32[32,128]{1,0:T(8,128)S(1)} %get-tuple-element.46.refs_0_), channel_id=1, source_target_pairs={{0,24},{8,16},{16,8},{24,0},{1,25},{9,17},{17,9},{25,1},{2,26},{10... | collective-permute-start | bytes 49160 | tf_op jit(solution)/shard_map/ppermute | solution.py:371
  30.7 1.8 %collective-permute-start.7 = (f32[32,128]{1,0:T(8,128)S(1)}, f32[32,128]{1,0:T(8,128)S(1)}, u32[]{:S(2)}, u32[]{:S(2)}) collective-permute-start(f32[32,128]{1,0:T(8,128)S(1)} %get-tuple-element.46.refs_0_), channel_id=1, source_target_pairs={{0,8},{8,0},{16,24},{24,16},{1,9},{9,1},{17,25},{25,17},{2,10},{10... | collective-permute-start | bytes 49160 | tf_op jit(solution)/shard_map/ppermute | solution.py:371
  32.5 1.1 %collective-permute-done.9.refs_3_ = f32[32,128]{1,0:T(8,128)S(1)} collective-permute-done((f32[32,128]{1,0:T(8,128)S(1)}, f32[32,128]{1,0:T(8,128)S(1)}, u32[]{:S(2)}, u32[]{:S(2)}) %collective-permute-start.9) | collective-permute-done | bytes 16416 | tf_op jit(solution)/shard_map/ppermute | solution.py:371
  33.7 1.7 %collective-permute-done.8.refs_2_ = f32[32,128]{1,0:T(8,128)S(1)} collective-permute-done((f32[32,128]{1,0:T(8,128)S(1)}, f32[32,128]{1,0:T(8,128)S(1)}, u32[]{:S(2)}, u32[]{:S(2)}) %collective-permute-start.8) | collective-permute-done | bytes 16416 | tf_op jit(solution)/shard_map/ppermute | solution.py:371
  35.4 1.7 %shard_map.110 = (f32[16,128]{1,0:T(8,128)S(1)}, f32[1,48,128]{2,1,0:T(8,128)S(1)}, f32[4,48,128]{2,1,0:T(8,128)S(1)}, f32[4,48,128]{2,1,0:T(8,128)S(1)}, f32[8,128]{1,0:T(8,128)S(1)}) custom-call(s32[8,128]{1,0:T(8,128)S(1)} %get-tuple-element.41.ids_ref, s32[8,128]{1,0:T(8,128)S(1)} %shard_map.109.all_ref, f32[128,48,128]{2,1,0:T(8,128)S(1)} %get-tuple-element.38.lat_ref, ...), custom_call_target="tpu_custom_call" | custom-call | tf_op jit(solution)/shard_map/pallas_call | solution.py:42
  37.2 1.2 %collective-permute-done.10.other_ref = f32[16,128]{1,0:T(8,128)S(1)} collective-permute-done((f32[16,128]{1,0:T(8,128)S(1)}, f32[16,128]{1,0:T(8,128)S(1)}, u32[]{:S(2)}, u32[]{:S(2)}) %collective-permute-start.10) | collective-permute-done | bytes 8224 | tf_op jit(solution)/shard_map/ppermute | solution.py:378
  38.3 1.5 %collective-permute-start.13 = (f32[16,128]{1,0:T(8,128)S(1)}, f32[16,128]{1,0:T(8,128)S(1)}, u32[]{:S(2)}, u32[]{:S(2)}) collective-permute-start(f32[16,128]{1,0:T(8,128)S(1)} %shard_map.111.refs_0_), channel_id=1, source_target_pairs={{0,6},{1,7},{2,4},{3,5},{4,2},{5,3},{6,0},{7,1},{8,14},{9,15},{10,... | collective-permute-start | bytes 24584 | tf_op jit(solution)/shard_map/ppermute | solution.py:380
  39.8 1.3 %collective-permute-start.12 = (f32[16,128]{1,0:T(8,128)S(1)}, f32[16,128]{1,0:T(8,128)S(1)}, u32[]{:S(2)}, u32[]{:S(2)}) collective-permute-start(f32[16,128]{1,0:T(8,128)S(1)} %shard_map.111.refs_0_), channel_id=1, source_target_pairs={{0,4},{1,5},{2,6},{3,7},{4,0},{5,1},{6,2},{7,3},{8,12},{9,13},{10,... | collective-permute-start | bytes 24584 | tf_op jit(solution)/shard_map/ppermute | solution.py:380
  41.1 0.7 collective-permute-start.11
  41.8 1.1 %collective-permute-done.13.refs_3_ = f32[16,128]{1,0:T(8,128)S(1)} collective-permute-done((f32[16,128]{1,0:T(8,128)S(1)}, f32[16,128]{1,0:T(8,128)S(1)}, u32[]{:S(2)}, u32[]{:S(2)}) %collective-permute-start.13) | collective-permute-done | bytes 8224 | tf_op jit(solution)/shard_map/ppermute | solution.py:380
  42.9 0.6 collective-permute-done.12.refs_2_
  43.5 1.3 %collective-permute-done.11.refs_1_ = f32[16,128]{1,0:T(8,128)S(1)} collective-permute-done((f32[16,128]{1,0:T(8,128)S(1)}, f32[16,128]{1,0:T(8,128)S(1)}, u32[]{:S(2)}, u32[]{:S(2)}) %collective-permute-start.11) | collective-permute-done | bytes 8224 | tf_op jit(solution)/shard_map/ppermute | solution.py:380
  45.2 1.5 %collective-permute-start.16 = (f32[24,128]{1,0:T(8,128)S(1)}, f32[24,128]{1,0:T(8,128)S(1)}, u32[]{:S(2)}, u32[]{:S(2)}) collective-permute-start(f32[24,128]{1,0:T(8,128)S(1)} %get-tuple-element.54.refs_1_), channel_id=1, source_target_pairs={{0,24},{8,16},{16,8},{24,0},{1,25},{9,17},{17,9},{25,1},{2,26},{10... | collective-permute-start | bytes 36872 | tf_op jit(solution)/shard_map/ppermute | solution.py:371
  46.7 0.6 collective-permute-start.15
  47.3 2.3 %collective-permute-start.14 = (f32[24,128]{1,0:T(8,128)S(1)}, f32[24,128]{1,0:T(8,128)S(1)}, u32[]{:S(2)}, u32[]{:S(2)}) collective-permute-start(f32[24,128]{1,0:T(8,128)S(1)} %get-tuple-element.54.refs_1_), channel_id=1, source_target_pairs={{0,8},{8,0},{16,24},{24,16},{1,9},{9,1},{17,25},{25,17},{2,10},{10... | collective-permute-start | bytes 36872 | tf_op jit(solution)/shard_map/ppermute | solution.py:371
  49.6 1.1 %collective-permute-done.16.refs_4_ = f32[24,128]{1,0:T(8,128)S(1)} collective-permute-done((f32[24,128]{1,0:T(8,128)S(1)}, f32[24,128]{1,0:T(8,128)S(1)}, u32[]{:S(2)}, u32[]{:S(2)}) %collective-permute-start.16) | collective-permute-done | bytes 12320 | tf_op jit(solution)/shard_map/ppermute | solution.py:371
  51.4 1.8 %shard_map.113 = (f32[16,128]{1,0:T(8,128)S(1)}, f32[1,48,128]{2,1,0:T(8,128)S(1)}, f32[4,48,128]{2,1,0:T(8,128)S(1)}, f32[4,48,128]{2,1,0:T(8,128)S(1)}, f32[8,128]{1,0:T(8,128)S(1)}) custom-call(s32[8,128]{1,0:T(8,128)S(1)} %get-tuple-element.41.ids_ref, s32[8,128]{1,0:T(8,128)S(1)} %shard_map.109.all_ref, f32[128,48,128]{2,1,0:T(8,128)S(1)} %get-tuple-element.38.lat_ref, ...), custom_call_target="tpu_custom_call" | custom-call | tf_op jit(solution)/shard_map/pallas_call | solution.py:42
  53.3 1.2 %collective-permute-done.17.other_ref = f32[16,128]{1,0:T(8,128)S(1)} collective-permute-done((f32[16,128]{1,0:T(8,128)S(1)}, f32[16,128]{1,0:T(8,128)S(1)}, u32[]{:S(2)}, u32[]{:S(2)}) %collective-permute-start.17) | collective-permute-done | bytes 8224 | tf_op jit(solution)/shard_map/ppermute | solution.py:378
  54.4 1.6 %collective-permute-start.20 = (f32[16,128]{1,0:T(8,128)S(1)}, f32[16,128]{1,0:T(8,128)S(1)}, u32[]{:S(2)}, u32[]{:S(2)}) collective-permute-start(f32[16,128]{1,0:T(8,128)S(1)} %shard_map.114.refs_0_), channel_id=1, source_target_pairs={{0,6},{1,7},{2,4},{3,5},{4,2},{5,3},{6,0},{7,1},{8,14},{9,15},{10,... | collective-permute-start | bytes 24584 | tf_op jit(solution)/shard_map/ppermute | solution.py:380
  56.6 1.3 %collective-permute-start.18 = (f32[16,128]{1,0:T(8,128)S(1)}, f32[16,128]{1,0:T(8,128)S(1)}, u32[]{:S(2)}, u32[]{:S(2)}) collective-permute-start(f32[16,128]{1,0:T(8,128)S(1)} %shard_map.114.refs_0_), channel_id=1, source_target_pairs={{0,2},{1,3},{2,0},{3,1},{4,6},{5,7},{6,4},{7,5},{8,10},{9,11},{10,... | collective-permute-start | bytes 24584 | tf_op jit(solution)/shard_map/ppermute | solution.py:380
  57.9 1.1 %collective-permute-done.20.refs_3_ = f32[16,128]{1,0:T(8,128)S(1)} collective-permute-done((f32[16,128]{1,0:T(8,128)S(1)}, f32[16,128]{1,0:T(8,128)S(1)}, u32[]{:S(2)}, u32[]{:S(2)}) %collective-permute-start.20) | collective-permute-done | bytes 8224 | tf_op jit(solution)/shard_map/ppermute | solution.py:380
  59.0 0.8 collective-permute-done.19.refs_2_
  60.7 2.5 %collective-permute-start.23 = (f32[24,128]{1,0:T(8,128)S(1)}, f32[24,128]{1,0:T(8,128)S(1)}, u32[]{:S(2)}, u32[]{:S(2)}) collective-permute-start(f32[24,128]{1,0:T(8,128)S(1)} %get-tuple-element.59.refs_1_), channel_id=1, source_target_pairs={{0,24},{8,16},{16,8},{24,0},{1,25},{9,17},{17,9},{25,1},{2,26},{10... | collective-permute-start | bytes 36872 | tf_op jit(solution)/shard_map/ppermute | solution.py:371
  63.2 0.9 %collective-permute-start.22 = (f32[24,128]{1,0:T(8,128)S(1)}, f32[24,128]{1,0:T(8,128)S(1)}, u32[]{:S(2)}, u32[]{:S(2)}) collective-permute-start(f32[24,128]{1,0:T(8,128)S(1)} %get-tuple-element.59.refs_1_), channel_id=1, source_target_pairs={{0,16},{8,24},{16,0},{24,8},{1,17},{9,25},{17,1},{25,9},{2,18},{10... | collective-permute-start | bytes 36872 | tf_op jit(solution)/shard_map/ppermute | solution.py:371
  64.1 1.0 %collective-permute-start.21 = (f32[24,128]{1,0:T(8,128)S(1)}, f32[24,128]{1,0:T(8,128)S(1)}, u32[]{:S(2)}, u32[]{:S(2)}) collective-permute-start(f32[24,128]{1,0:T(8,128)S(1)} %get-tuple-element.59.refs_1_), channel_id=1, source_target_pairs={{0,8},{8,0},{16,24},{24,16},{1,9},{9,1},{17,25},{25,17},{2,10},{10... | collective-permute-start | bytes 36872 | tf_op jit(solution)/shard_map/ppermute | solution.py:371
  65.1 1.1 %collective-permute-done.23.refs_4_ = f32[24,128]{1,0:T(8,128)S(1)} collective-permute-done((f32[24,128]{1,0:T(8,128)S(1)}, f32[24,128]{1,0:T(8,128)S(1)}, u32[]{:S(2)}, u32[]{:S(2)}) %collective-permute-start.23) | collective-permute-done | bytes 12320 | tf_op jit(solution)/shard_map/ppermute | solution.py:371
  66.2 1.6 %collective-permute-done.22.refs_3_ = f32[24,128]{1,0:T(8,128)S(1)} collective-permute-done((f32[24,128]{1,0:T(8,128)S(1)}, f32[24,128]{1,0:T(8,128)S(1)}, u32[]{:S(2)}, u32[]{:S(2)}) %collective-permute-start.22) | collective-permute-done | bytes 12320 | tf_op jit(solution)/shard_map/ppermute | solution.py:371
  67.9 1.5 %shard_map.116 = (f32[8,128]{1,0:T(8,128)S(1)}, f32[1,48,128]{2,1,0:T(8,128)S(1)}, f32[1,48,128]{2,1,0:T(8,128)S(1)}, f32[8,128]{1,0:T(8,128)S(1)}) custom-call(s32[8,128]{1,0:T(8,128)S(1)} %get-tuple-element.41.ids_ref, s32[8,128]{1,0:T(8,128)S(1)} %shard_map.109.all_ref, f32[128,48,128]{2,1,0:T(8,128)S(1)} %get-tuple-element.38.lat_ref, ...), custom_call_target="tpu_custom_call" | custom-call | tf_op jit(solution)/shard_map/pallas_call | solution.py:42
  69.5 1.2 %collective-permute-done.24.other_ref = f32[8,128]{1,0:T(8,128)S(1)} collective-permute-done((f32[8,128]{1,0:T(8,128)S(1)}, f32[8,128]{1,0:T(8,128)S(1)}, u32[]{:S(2)}, u32[]{:S(2)}) %collective-permute-start.24) | collective-permute-done | bytes 4128 | tf_op jit(solution)/shard_map/ppermute | solution.py:378
  70.6 1.5 %collective-permute-start.27 = (f32[8,128]{1,0:T(8,128)S(1)}, f32[8,128]{1,0:T(8,128)S(1)}, u32[]{:S(2)}, u32[]{:S(2)}) collective-permute-start(f32[8,128]{1,0:T(8,128)S(1)} %shard_map.117.refs_0_), channel_id=1, source_target_pairs={{0,6},{1,7},{2,4},{3,5},{4,2},{5,3},{6,0},{7,1},{8,14},{9,15},{10,... | collective-permute-start | bytes 12296 | tf_op jit(solution)/shard_map/ppermute | solution.py:380
  72.1 1.3 %collective-permute-start.26 = (f32[8,128]{1,0:T(8,128)S(1)}, f32[8,128]{1,0:T(8,128)S(1)}, u32[]{:S(2)}, u32[]{:S(2)}) collective-permute-start(f32[8,128]{1,0:T(8,128)S(1)} %shard_map.117.refs_0_), channel_id=1, source_target_pairs={{0,4},{1,5},{2,6},{3,7},{4,0},{5,1},{6,2},{7,3},{8,12},{9,13},{10,... | collective-permute-start | bytes 12296 | tf_op jit(solution)/shard_map/ppermute | solution.py:380
  73.4 0.7 collective-permute-start.25
  74.1 1.0 %collective-permute-done.27.refs_3_ = f32[8,128]{1,0:T(8,128)S(1)} collective-permute-done((f32[8,128]{1,0:T(8,128)S(1)}, f32[8,128]{1,0:T(8,128)S(1)}, u32[]{:S(2)}, u32[]{:S(2)}) %collective-permute-start.27) | collective-permute-done | bytes 4128 | tf_op jit(solution)/shard_map/ppermute | solution.py:380
  75.1 0.6 collective-permute-done.26.refs_2_
  75.7 1.3 %collective-permute-done.25.refs_1_ = f32[8,128]{1,0:T(8,128)S(1)} collective-permute-done((f32[8,128]{1,0:T(8,128)S(1)}, f32[8,128]{1,0:T(8,128)S(1)}, u32[]{:S(2)}, u32[]{:S(2)}) %collective-permute-start.25) | collective-permute-done | bytes 4128 | tf_op jit(solution)/shard_map/ppermute | solution.py:380
  77.0 0.8 %shard_map.118 = (f32[4,1,48,128]{3,2,1,0:T(8,128)}, f32[2,3]{1,0:T(2,128)}) custom-call(f32[8,128]{1,0:T(8,128)S(1)} %shard_map.117.refs_0_, f32[8,128]{1,0:T(8,128)S(1)} %collective-permute-done.25.refs_1_, f32[8,128]{1,0:T(8,128)S(1)} %collective-permute-done.26.refs_2_, f32[8,128]{1,0:T(8,128)S(1)} %collective-permute-done.27.refs_3_, ...), custom_call_target="tpu_custom_call" | custom-call | tf_op jit(solution)/shard_map/pallas_call | solution.py:42
  (29 shorter events, 4.8 us)
Async XLA Ops:
  3.3 14.2 %all-to-all-start = ((bf16[8,208,128]{2,1,0:T(8,128)(2,1)}), bf16[8,208,128]{2,1,0:T(8,128)(2,1)}, u32[]{:S(2)}, u32[]{:S(2)}) async-start(bf16[8,208,128]{2,1,0:T(8,128)(2,1)} %get-tuple-element.39), calls=%async_computation | async-start | bytes 851968 | tf_op jit(solution)/shard_map/all_to_all | solution.py:384
  8.5 7.8 %collective-permute-start.2 = (f32[48,128]{1,0:T(8,128)}, f32[48,128]{1,0:T(8,128)S(1)}, u32[]{:S(2)}, u32[]{:S(2)}) collective-permute-start(f32[48,128]{1,0:T(8,128)} %bitcast.3), channel_id=1, source_target_pairs={{0,24},{8,16},{16,8},{24,0},{1,25},{9,17},{17,9},{25,1},{2,26},{10... | collective-permute-start | bytes 73736 | tf_op jit(solution)/shard_map/ppermute | solution.py:371
  12.5 4.9 %collective-permute-start.1 = (f32[48,128]{1,0:T(8,128)}, f32[48,128]{1,0:T(8,128)S(1)}, u32[]{:S(2)}, u32[]{:S(2)}) collective-permute-start(f32[48,128]{1,0:T(8,128)} %bitcast.4), channel_id=1, source_target_pairs={{0,16},{8,24},{16,0},{24,8},{1,17},{9,25},{17,1},{25,9},{2,18},{10... | collective-permute-start | bytes 73736 | tf_op jit(solution)/shard_map/ppermute | solution.py:371
  12.6 4.9 %collective-permute-start = (f32[48,128]{1,0:T(8,128)}, f32[48,128]{1,0:T(8,128)S(1)}, u32[]{:S(2)}, u32[]{:S(2)}) collective-permute-start(f32[48,128]{1,0:T(8,128)} %bitcast.5), channel_id=1, source_target_pairs={{0,8},{8,0},{16,24},{24,16},{1,9},{9,1},{17,25},{25,17},{2,10},{10... | collective-permute-start | bytes 73736 | tf_op jit(solution)/shard_map/ppermute | solution.py:371
  13.2 0.8 copy-start.1
  14.0 13.7 %copy-start = (f32[8,128]{1,0:T(8,128)S(1)}, f32[8,128]{1,0:T(8,128)}, u32[]{:S(2)}) copy-start(f32[8,128]{1,0:T(8,128)} %get-tuple-element.35.weight_ref) | copy-start | bytes 12292
  19.4 1.2 %collective-permute-start.3 = (f32[16,128]{1,0:T(8,128)S(1)}, f32[16,128]{1,0:T(8,128)S(1)}, u32[]{:S(2)}, u32[]{:S(2)}) collective-permute-start(f32[16,128]{1,0:T(8,128)S(1)} %get-tuple-element.45.one_ref), channel_id=1, source_target_pairs={{0,1},{1,0},{2,3},{3,2},{4,5},{5,4},{6,7},{7,6},{8,9},{9,8},{10,11... | collective-permute-start | bytes 24584 | tf_op jit(solution)/shard_map/ppermute | solution.py:378
  20.7 4.5 %collective-permute-start.6 = (f32[16,128]{1,0:T(8,128)S(1)}, f32[16,128]{1,0:T(8,128)S(1)}, u32[]{:S(2)}, u32[]{:S(2)}) collective-permute-start(f32[16,128]{1,0:T(8,128)S(1)} %shard_map.107.refs_1_), channel_id=1, source_target_pairs={{0,6},{1,7},{2,4},{3,5},{4,2},{5,3},{6,0},{7,1},{8,14},{9,15},{10,... | collective-permute-start | bytes 24584 | tf_op jit(solution)/shard_map/ppermute | solution.py:380
  23.5 3.7 %collective-permute-start.5 = (f32[16,128]{1,0:T(8,128)S(1)}, f32[16,128]{1,0:T(8,128)S(1)}, u32[]{:S(2)}, u32[]{:S(2)}) collective-permute-start(f32[16,128]{1,0:T(8,128)S(1)} %shard_map.107.refs_1_), channel_id=1, source_target_pairs={{0,4},{1,5},{2,6},{3,7},{4,0},{5,1},{6,2},{7,3},{8,12},{9,13},{10,... | collective-permute-start | bytes 24584 | tf_op jit(solution)/shard_map/ppermute | solution.py:380
  24.0 3.7 %collective-permute-start.4 = (f32[16,128]{1,0:T(8,128)S(1)}, f32[16,128]{1,0:T(8,128)S(1)}, u32[]{:S(2)}, u32[]{:S(2)}) collective-permute-start(f32[16,128]{1,0:T(8,128)S(1)} %shard_map.107.refs_1_), channel_id=1, source_target_pairs={{0,2},{1,3},{2,0},{3,1},{4,6},{5,7},{6,4},{7,5},{8,10},{9,11},{10,... | collective-permute-start | bytes 24584 | tf_op jit(solution)/shard_map/ppermute | solution.py:380
  28.1 5.6 %collective-permute-start.9 = (f32[32,128]{1,0:T(8,128)S(1)}, f32[32,128]{1,0:T(8,128)S(1)}, u32[]{:S(2)}, u32[]{:S(2)}) collective-permute-start(f32[32,128]{1,0:T(8,128)S(1)} %get-tuple-element.46.refs_0_), channel_id=1, source_target_pairs={{0,24},{8,16},{16,8},{24,0},{1,25},{9,17},{17,9},{25,1},{2,26},{10... | collective-permute-start | bytes 49160 | tf_op jit(solution)/shard_map/ppermute | solution.py:371
  30.7 4.6 %collective-permute-start.8 = (f32[32,128]{1,0:T(8,128)S(1)}, f32[32,128]{1,0:T(8,128)S(1)}, u32[]{:S(2)}, u32[]{:S(2)}) collective-permute-start(f32[32,128]{1,0:T(8,128)S(1)} %get-tuple-element.46.refs_0_), channel_id=1, source_target_pairs={{0,16},{8,24},{16,0},{24,8},{1,17},{9,25},{17,1},{25,9},{2,18},{10... | collective-permute-start | bytes 49160 | tf_op jit(solution)/shard_map/ppermute | solution.py:371
  30.7 4.6 %collective-permute-start.7 = (f32[32,128]{1,0:T(8,128)S(1)}, f32[32,128]{1,0:T(8,128)S(1)}, u32[]{:S(2)}, u32[]{:S(2)}) collective-permute-start(f32[32,128]{1,0:T(8,128)S(1)} %get-tuple-element.46.refs_0_), channel_id=1, source_target_pairs={{0,8},{8,0},{16,24},{24,16},{1,9},{9,1},{17,25},{25,17},{2,10},{10... | collective-permute-start | bytes 49160 | tf_op jit(solution)/shard_map/ppermute | solution.py:371
  37.1 1.2 %collective-permute-start.10 = (f32[16,128]{1,0:T(8,128)S(1)}, f32[16,128]{1,0:T(8,128)S(1)}, u32[]{:S(2)}, u32[]{:S(2)}) collective-permute-start(f32[16,128]{1,0:T(8,128)S(1)} %get-tuple-element.50.one_ref), channel_id=1, source_target_pairs={{0,1},{1,0},{2,3},{3,2},{4,5},{5,4},{6,7},{7,6},{8,9},{9,8},{10,11... | collective-permute-start | bytes 24584 | tf_op jit(solution)/shard_map/ppermute | solution.py:378
  38.3 4.5 %collective-permute-start.13 = (f32[16,128]{1,0:T(8,128)S(1)}, f32[16,128]{1,0:T(8,128)S(1)}, u32[]{:S(2)}, u32[]{:S(2)}) collective-permute-start(f32[16,128]{1,0:T(8,128)S(1)} %shard_map.111.refs_0_), channel_id=1, source_target_pairs={{0,6},{1,7},{2,4},{3,5},{4,2},{5,3},{6,0},{7,1},{8,14},{9,15},{10,... | collective-permute-start | bytes 24584 | tf_op jit(solution)/shard_map/ppermute | solution.py:380
  39.8 3.7 %collective-permute-start.12 = (f32[16,128]{1,0:T(8,128)S(1)}, f32[16,128]{1,0:T(8,128)S(1)}, u32[]{:S(2)}, u32[]{:S(2)}) collective-permute-start(f32[16,128]{1,0:T(8,128)S(1)} %shard_map.111.refs_0_), channel_id=1, source_target_pairs={{0,4},{1,5},{2,6},{3,7},{4,0},{5,1},{6,2},{7,3},{8,12},{9,13},{10,... | collective-permute-start | bytes 24584 | tf_op jit(solution)/shard_map/ppermute | solution.py:380
  41.1 3.7 %collective-permute-start.11 = (f32[16,128]{1,0:T(8,128)S(1)}, f32[16,128]{1,0:T(8,128)S(1)}, u32[]{:S(2)}, u32[]{:S(2)}) collective-permute-start(f32[16,128]{1,0:T(8,128)S(1)} %shard_map.111.refs_0_), channel_id=1, source_target_pairs={{0,2},{1,3},{2,0},{3,1},{4,6},{5,7},{6,4},{7,5},{8,10},{9,11},{10,... | collective-permute-start | bytes 24584 | tf_op jit(solution)/shard_map/ppermute | solution.py:380
  45.2 5.5 %collective-permute-start.16 = (f32[24,128]{1,0:T(8,128)S(1)}, f32[24,128]{1,0:T(8,128)S(1)}, u32[]{:S(2)}, u32[]{:S(2)}) collective-permute-start(f32[24,128]{1,0:T(8,128)S(1)} %get-tuple-element.54.refs_1_), channel_id=1, source_target_pairs={{0,24},{8,16},{16,8},{24,0},{1,25},{9,17},{17,9},{25,1},{2,26},{10... | collective-permute-start | bytes 36872 | tf_op jit(solution)/shard_map/ppermute | solution.py:371
  46.7 4.6 %collective-permute-start.15 = (f32[24,128]{1,0:T(8,128)S(1)}, f32[24,128]{1,0:T(8,128)S(1)}, u32[]{:S(2)}, u32[]{:S(2)}) collective-permute-start(f32[24,128]{1,0:T(8,128)S(1)} %get-tuple-element.54.refs_1_), channel_id=1, source_target_pairs={{0,16},{8,24},{16,0},{24,8},{1,17},{9,25},{17,1},{25,9},{2,18},{10... | collective-permute-start | bytes 36872 | tf_op jit(solution)/shard_map/ppermute | solution.py:371
  47.3 4.1 %collective-permute-start.14 = (f32[24,128]{1,0:T(8,128)S(1)}, f32[24,128]{1,0:T(8,128)S(1)}, u32[]{:S(2)}, u32[]{:S(2)}) collective-permute-start(f32[24,128]{1,0:T(8,128)S(1)} %get-tuple-element.54.refs_1_), channel_id=1, source_target_pairs={{0,8},{8,0},{16,24},{24,16},{1,9},{9,1},{17,25},{25,17},{2,10},{10... | collective-permute-start | bytes 36872 | tf_op jit(solution)/shard_map/ppermute | solution.py:371
  53.2 1.2 %collective-permute-start.17 = (f32[16,128]{1,0:T(8,128)S(1)}, f32[16,128]{1,0:T(8,128)S(1)}, u32[]{:S(2)}, u32[]{:S(2)}) collective-permute-start(f32[16,128]{1,0:T(8,128)S(1)} %get-tuple-element.55.one_ref), channel_id=1, source_target_pairs={{0,1},{1,0},{2,3},{3,2},{4,5},{5,4},{6,7},{7,6},{8,9},{9,8},{10,11... | collective-permute-start | bytes 24584 | tf_op jit(solution)/shard_map/ppermute | solution.py:378
  54.4 4.5 %collective-permute-start.20 = (f32[16,128]{1,0:T(8,128)S(1)}, f32[16,128]{1,0:T(8,128)S(1)}, u32[]{:S(2)}, u32[]{:S(2)}) collective-permute-start(f32[16,128]{1,0:T(8,128)S(1)} %shard_map.114.refs_0_), channel_id=1, source_target_pairs={{0,6},{1,7},{2,4},{3,5},{4,2},{5,3},{6,0},{7,1},{8,14},{9,15},{10,... | collective-permute-start | bytes 24584 | tf_op jit(solution)/shard_map/ppermute | solution.py:380
  56.1 3.7 %collective-permute-start.19 = (f32[16,128]{1,0:T(8,128)S(1)}, f32[16,128]{1,0:T(8,128)S(1)}, u32[]{:S(2)}, u32[]{:S(2)}) collective-permute-start(f32[16,128]{1,0:T(8,128)S(1)} %shard_map.114.refs_0_), channel_id=1, source_target_pairs={{0,4},{1,5},{2,6},{3,7},{4,0},{5,1},{6,2},{7,3},{8,12},{9,13},{10,... | collective-permute-start | bytes 24584 | tf_op jit(solution)/shard_map/ppermute | solution.py:380
  56.6 3.7 %collective-permute-start.18 = (f32[16,128]{1,0:T(8,128)S(1)}, f32[16,128]{1,0:T(8,128)S(1)}, u32[]{:S(2)}, u32[]{:S(2)}) collective-permute-start(f32[16,128]{1,0:T(8,128)S(1)} %shard_map.114.refs_0_), channel_id=1, source_target_pairs={{0,2},{1,3},{2,0},{3,1},{4,6},{5,7},{6,4},{7,5},{8,10},{9,11},{10,... | collective-permute-start | bytes 24584 | tf_op jit(solution)/shard_map/ppermute | solution.py:380
  60.7 5.5 %collective-permute-start.23 = (f32[24,128]{1,0:T(8,128)S(1)}, f32[24,128]{1,0:T(8,128)S(1)}, u32[]{:S(2)}, u32[]{:S(2)}) collective-permute-start(f32[24,128]{1,0:T(8,128)S(1)} %get-tuple-element.59.refs_1_), channel_id=1, source_target_pairs={{0,24},{8,16},{16,8},{24,0},{1,25},{9,17},{17,9},{25,1},{2,26},{10... | collective-permute-start | bytes 36872 | tf_op jit(solution)/shard_map/ppermute | solution.py:371
  63.2 4.6 %collective-permute-start.22 = (f32[24,128]{1,0:T(8,128)S(1)}, f32[24,128]{1,0:T(8,128)S(1)}, u32[]{:S(2)}, u32[]{:S(2)}) collective-permute-start(f32[24,128]{1,0:T(8,128)S(1)} %get-tuple-element.59.refs_1_), channel_id=1, source_target_pairs={{0,16},{8,24},{16,0},{24,8},{1,17},{9,25},{17,1},{25,9},{2,18},{10... | collective-permute-start | bytes 36872 | tf_op jit(solution)/shard_map/ppermute | solution.py:371
  64.1 3.8 %collective-permute-start.21 = (f32[24,128]{1,0:T(8,128)S(1)}, f32[24,128]{1,0:T(8,128)S(1)}, u32[]{:S(2)}, u32[]{:S(2)}) collective-permute-start(f32[24,128]{1,0:T(8,128)S(1)} %get-tuple-element.59.refs_1_), channel_id=1, source_target_pairs={{0,8},{8,0},{16,24},{24,16},{1,9},{9,1},{17,25},{25,17},{2,10},{10... | collective-permute-start | bytes 36872 | tf_op jit(solution)/shard_map/ppermute | solution.py:371
  69.4 1.2 %collective-permute-start.24 = (f32[8,128]{1,0:T(8,128)S(1)}, f32[8,128]{1,0:T(8,128)S(1)}, u32[]{:S(2)}, u32[]{:S(2)}) collective-permute-start(f32[8,128]{1,0:T(8,128)S(1)} %get-tuple-element.60.one_ref), channel_id=1, source_target_pairs={{0,1},{1,0},{2,3},{3,2},{4,5},{5,4},{6,7},{7,6},{8,9},{9,8},{10,11... | collective-permute-start | bytes 12296 | tf_op jit(solution)/shard_map/ppermute | solution.py:378
  70.6 4.5 %collective-permute-start.27 = (f32[8,128]{1,0:T(8,128)S(1)}, f32[8,128]{1,0:T(8,128)S(1)}, u32[]{:S(2)}, u32[]{:S(2)}) collective-permute-start(f32[8,128]{1,0:T(8,128)S(1)} %shard_map.117.refs_0_), channel_id=1, source_target_pairs={{0,6},{1,7},{2,4},{3,5},{4,2},{5,3},{6,0},{7,1},{8,14},{9,15},{10,... | collective-permute-start | bytes 12296 | tf_op jit(solution)/shard_map/ppermute | solution.py:380
  72.1 3.6 %collective-permute-start.26 = (f32[8,128]{1,0:T(8,128)S(1)}, f32[8,128]{1,0:T(8,128)S(1)}, u32[]{:S(2)}, u32[]{:S(2)}) collective-permute-start(f32[8,128]{1,0:T(8,128)S(1)} %shard_map.117.refs_0_), channel_id=1, source_target_pairs={{0,4},{1,5},{2,6},{3,7},{4,0},{5,1},{6,2},{7,3},{8,12},{9,13},{10,... | collective-permute-start | bytes 12296 | tf_op jit(solution)/shard_map/ppermute | solution.py:380
  73.4 3.6 %collective-permute-start.25 = (f32[8,128]{1,0:T(8,128)S(1)}, f32[8,128]{1,0:T(8,128)S(1)}, u32[]{:S(2)}, u32[]{:S(2)}) collective-permute-start(f32[8,128]{1,0:T(8,128)S(1)} %shard_map.117.refs_0_), channel_id=1, source_target_pairs={{0,2},{1,3},{2,0},{3,1},{4,6},{5,7},{6,4},{7,5},{8,10},{9,11},{10,... | collective-permute-start | bytes 12296 | tf_op jit(solution)/shard_map/ppermute | solution.py:380

commit v15 on v14

--- a/solution.py
+++ b/solution.py
@@ -38,12 +38,12 @@
     return high, low
 
 
-def call(kernel, outs, specs, *args, scratch=(), limit=8, cost=None):
+def call(kernel, outs, specs, *args, scratch=(), limit=8, cost=None, out_specs=None):
     return pl.pallas_call(
         kernel,
         out_shape=outs,
         in_specs=specs,
-        out_specs=jax.tree.map(lambda _: VMEM, outs),
+        out_specs=out_specs or jax.tree.map(lambda _: VMEM, outs),
         scratch_shapes=scratch,
         cost_estimate=cost,
         compiler_params=pltpu.CompilerParams(vmem_limit_bytes=limit * 1024 * 1024),
@@ -57,9 +57,10 @@
     return parts[0]
 
 
-def transform_kernel(dims, place_any, high_any, low_any, foot_any, off_any, sub_any, count_any, rinv_any, *refs):
+def transform_kernel(dims, place_any, high_any, low_any, foot_any, off_any, sub_any, count_any, rinv_any, start_any, *refs):
     nc, nb, modes, groups, band = dims
-    out_ref, weight_ref, high_ref, low_ref, foot_ref, off_ref, sub_ref, count_ref, rinv_ref, place_ref, sems = refs
+    out_any, weight_ref, start_ref, *refs, sems, out_sems = refs
+    high_ref, low_ref, foot_ref, off_ref, sub_ref, count_ref, rinv_ref, place_ref, out_ref = refs
     copies = [
         pltpu.make_async_copy(source, target, sems.at[at])
         for at, (source, target) in enumerate(
@@ -72,6 +73,7 @@
                 (count_any, count_ref),
                 (rinv_any, rinv_ref),
                 (place_any, place_ref),
+                (start_any, start_ref),
             ]
         )
     ]
@@ -84,6 +86,16 @@
     ob = foot_ref.shape[1]
     lon = high_ref.shape[1]
     contract = (((1,), (1,)), ((), ()))
+    sent = []
+
+    def send(at, rows):
+        sent.append(
+            pltpu.make_async_copy(
+                out_ref.at[:, at:at + rows, :], out_any.at[:, at:at + rows, :], out_sems.at[len(sent)]
+            )
+        )
+        sent[-1].start()
+
     for r in range(CR):
         foot = foot_ref[:, :, r * lon:(r + 1) * lon].reshape(nb * ob, lon)
         hat = lax.dot_general(high_ref[...], foot, contract, preferred_element_type=F32)
@@ -93,6 +105,7 @@
             at = (b * CR + r) * modes
             for c in range(nc):
                 out_ref[c, at:at + modes, :] = hat[c * modes:(c + 1) * modes, b * ob:(b + 1) * ob]
+            send(at, modes)
     lane = lax.broadcasted_iota(jnp.int32, (16, ob), 1)
     ids = jnp.zeros((16, ob), F32)
     for b in range(nb):
@@ -103,18 +116,20 @@
     ids = jnp.where(lane == 3 * nb, obs.astype(F32), ids).astype(BF16)
     for c in range(nc):
         out_ref[c, nb * CR * modes:, :] = ids
+    send(nb * CR * modes, 16)
     row = lax.broadcasted_iota(jnp.int32, weight_ref.shape, 0)
     limit = jnp.zeros(weight_ref.shape, jnp.int32)
     for s in range(weight_ref.shape[0]):
         limit = jnp.where(row == s, count_ref[s], limit)
     lane = lax.broadcasted_iota(jnp.int32, weight_ref.shape, 1)
     weight_ref[...] = jnp.where(lane < limit, rinv_ref[...], 0.0)
-
-
-def fetch_kernel(lat_any, start_any, lat_ref, start_ref, pick_ref, sems):
+    for copy in sent:
+        copy.wait()
+
+
+def fetch_kernel(lat_any, lat_ref, pick_ref, sems):
     modes = lat_any.shape[0]
     copies = [pltpu.make_async_copy(lat_any.at[m], lat_ref.at[:, m, :], sems.at[m]) for m in range(modes)]
-    copies.append(pltpu.make_async_copy(start_any, start_ref, sems.at[modes]))
     for copy in copies:
         copy.start()
     line = lax.broadcasted_iota(jnp.int32, pick_ref.shape, 0)
@@ -408,11 +423,12 @@
     start = start.reshape(per_dev * modes, lat_rows)
     near = share(start, "obs")
     foot_rows = nb * CR * modes
-    hats, weights = call(
+    hats, weights, start = call(
         functools.partial(transform_kernel, dims),
-        (jax.ShapeDtypeStruct((nc, foot_rows + 16, ob), BF16), shape((subs, ob))),
-        [ANY] * 8,
-        place, jnp.asarray(high), jnp.asarray(low), footprints, blk_off, blk_sub, counts, rinv.reshape(subs, ob),
+        (jax.ShapeDtypeStruct((nc, foot_rows + 16, ob), BF16), shape((subs, ob)), shape(start.shape)),
+        [ANY] * 9,
+        place, jnp.asarray(high), jnp.asarray(low), footprints, blk_off, blk_sub, counts, rinv.reshape(subs, ob), start,
+        out_specs=(ANY, VMEM, VMEM),
         scratch=[
             pltpu.VMEM(high.shape, BF16),
             pltpu.VMEM(low.shape, BF16),
@@ -422,24 +438,25 @@
             pltpu.SMEM((subs,), jnp.int32),
             pltpu.VMEM((subs, ob), F32),
             pltpu.SMEM((1,), jnp.int32),
-            pltpu.SemaphoreType.DMA((8,)),
+            pltpu.VMEM((nc, foot_rows + 16, ob), BF16),
+            pltpu.SemaphoreType.DMA((9,)),
+            pltpu.SemaphoreType.DMA((nb * CR + 1,)),
         ],
         limit=60,
     )
     came = swap(hats, "cell")
-    lat, start, _ = lax.optimization_barrier((lat_mats, start, weights))
-    lat, start, pick = call(
+    lat, _ = lax.optimization_barrier((lat_mats, weights))
+    lat, pick = call(
         fetch_kernel,
         (
             shape((lat_rows, modes, lat_rows)),
-            shape(start.shape),
             jax.ShapeDtypeStruct((TERMS * CHUNK, CHUNK * 128), BF16),
         ),
-        [ANY] * 2,
-        lat, start,
-        scratch=[pltpu.SemaphoreType.DMA((modes + 1,))],
+        [ANY],
+        lat,
+        scratch=[pltpu.SemaphoreType.DMA((modes,))],
         limit=50,
-        cost=pl.CostEstimate(flops=0, transcendentals=0, bytes_accessed=8 * (lat.size + start.size)),
+        cost=pl.CostEstimate(flops=0, transcendentals=0, bytes_accessed=8 * lat.size),
     )
     if permuted(no):
         near[0] = start

time: 78.2 us -> 78.8 us (level)
  waiting for transfers between devices: 24.8 us -> 25.6 us
  transfers between devices with their start and end apart: 29 -> 29, of which waited for: 25 -> 24; matrix products, arithmetic and copies ran while one was open for 0% -> 0% of each run, Pallas kernels for 3% -> 3%
where the time goes in v15:
time: 78.8 us; the launch traced here: 78.5 us
  starting transfers between devices  37.4 us (47%)
  waiting for transfers between devices  25.6 us (32%)
  Pallas kernels  14.7 us (19%)
    ppermute x12, starting transfers between devices, share(): lax.ppermute(array, axis, [(d, d ^ s) for d in range(size)])  17.9 us
    pallas_call x15, Pallas kernels, call(): pl.pallas_call(kernel, out_shape=outs, in_specs=specs, out_specs=out_spec...  14.7 us
    ppermute x12, starting transfers between devices, addends(): lax.ppermute(both, axis, [(d, d ^ s) for d in range(size)])  14 us
    ppermute x12, waiting for transfers between devices, addends(): lax.ppermute(both, axis, [(d, d ^ s) for d in range(size)])  12 us
    ppermute x12, waiting for transfers between devices, share(): lax.ppermute(array, axis, [(d, d ^ s) for d in range(size)])  9.05 us
    all_to_all x1, starting transfers between devices, swap(): return lax.all_to_all(array, axis, split_axis=0, concat_axis=0, tiled=True)  5.18 us
    ppermute x4, waiting for transfers between devices, addends(): other = lax.ppermute(array, axis, [(d, d ^ 1) for d in range(size)])  4.63 us
  transfers between devices with their start and end apart: 29, of which 24 were waited for; matrix products, arithmetic and copies ran while one was open for 0% of the time, Pallas kernels for 3%

profile of v15, /device:TPU:0, one launch (start us, length us, event | category | flops | bytes accessed | tf_op | source)
XLA Modules:
  0.0 78.5 jit_solution(15040905758292185685)
XLA Ops:
  0.6 3.3 %shard_map.104 = (bf16[8,208,128]{2,1,0:T(8,128)(2,1)}, f32[8,128]{1,0:T(8,128)}, f32[48,128]{1,0:T(8,128)}) custom-call(s32[1]{0:T(128)} %bitcast.place_any, bf16[384,384]{1,0:T(8,128)(2,1)} %constant.14.clone.high_any, bf16[384,384]{1,0:T(8,128)(2,1)} %constant.15.clone.low_any, bf16[2,128,768]{2,1,0:T(8,128)(2,1)} %foot_any.1, s32[2]{0:T(128)} %off_any.1, ...), custom_call_target="tpu_custom_call" | custom-call | tf_op jit(solution)/shard_map/pallas_call | solution.py:42
  4.0 5.2 %all-to-all-start = ((bf16[8,208,128]{2,1,0:T(8,128)(2,1)}), bf16[8,208,128]{2,1,0:T(8,128)(2,1)}, u32[]{:S(2)}, u32[]{:S(2)}) async-start(bf16[8,208,128]{2,1,0:T(8,128)(2,1)} %get-tuple-element.37), calls=%async_computation | async-start | bytes 851968 | tf_op jit(solution)/shard_map/all_to_all | solution.py:399
  9.2 4.1 %collective-permute-start.2 = (f32[48,128]{1,0:T(8,128)}, f32[48,128]{1,0:T(8,128)S(1)}, u32[]{:S(2)}, u32[]{:S(2)}) collective-permute-start(f32[48,128]{1,0:T(8,128)} %bitcast.4), channel_id=1, source_target_pairs={{0,24},{8,16},{16,8},{24,0},{1,25},{9,17},{17,9},{25,1},{2,26},{10... | collective-permute-start | bytes 73736 | tf_op jit(solution)/shard_map/ppermute | solution.py:386
  13.2 0.6 collective-permute-start
  13.9 2.3 %shard_map.105 = (f32[128,48,128]{2,1,0:T(8,128)S(1)}, bf16[48,2048]{1,0:T(8,128)(2,1)S(1)}) custom-call(f32[48,128,128]{2,1,0:T(8,128)} %lat_any), custom_call_target="tpu_custom_call" | custom-call | bytes 6291456 | tf_op jit(solution)/shard_map/pallas_call | solution.py:42
  16.2 2.0 %collective-permute-done.1.refs_2_ = f32[48,128]{1,0:T(8,128)S(1)} collective-permute-done((f32[48,128]{1,0:T(8,128)}, f32[48,128]{1,0:T(8,128)S(1)}, u32[]{:S(2)}, u32[]{:S(2)}) %collective-permute-start.1) | collective-permute-done | bytes 24608 | tf_op jit(solution)/shard_map/ppermute | solution.py:386
  18.2 2.0 %shard_map.106 = (f32[16,128]{1,0:T(8,128)S(1)}, f32[4,48,128]{2,1,0:T(8,128)S(1)}, bf16[8,192,128]{2,1,0:T(8,128)(2,1)S(1)}, s32[8,128]{1,0:T(8,128)S(1)}, bf16...) custom-call(f32[128,48,128]{2,1,0:T(8,128)S(1)} %get-tuple-element.36.lat_ref, bf16[8,208,128]{2,1,0:T(8,128)(2,1)} %all-to-all-done.came_ref, ...), custom_call_target="tpu_custom_call" | custom-call | tf_op jit(solution)/shard_map/pallas_call | solution.py:42
  20.2 1.2 %collective-permute-done.3.other_ref = f32[16,128]{1,0:T(8,128)S(1)} collective-permute-done((f32[16,128]{1,0:T(8,128)S(1)}, f32[16,128]{1,0:T(8,128)S(1)}, u32[]{:S(2)}, u32[]{:S(2)}) %collective-permute-start.3) | collective-permute-done | bytes 8224 | tf_op jit(solution)/shard_map/ppermute | solution.py:393
  21.4 2.8 %collective-permute-start.6 = (f32[16,128]{1,0:T(8,128)S(1)}, f32[16,128]{1,0:T(8,128)S(1)}, u32[]{:S(2)}, u32[]{:S(2)}) collective-permute-start(f32[16,128]{1,0:T(8,128)S(1)} %shard_map.107.refs_1_), channel_id=1, source_target_pairs={{0,6},{1,7},{2,4},{3,5},{4,2},{5,3},{6,0},{7,1},{8,14},{9,15},{10,... | collective-permute-start | bytes 24584 | tf_op jit(solution)/shard_map/ppermute | solution.py:395
  24.9 1.1 %collective-permute-done.6.refs_4_ = f32[16,128]{1,0:T(8,128)S(1)} collective-permute-done((f32[16,128]{1,0:T(8,128)S(1)}, f32[16,128]{1,0:T(8,128)S(1)}, u32[]{:S(2)}, u32[]{:S(2)}) %collective-permute-start.6) | collective-permute-done | bytes 8224 | tf_op jit(solution)/shard_map/ppermute | solution.py:395
  25.9 1.9 %collective-permute-done.5.refs_3_ = f32[16,128]{1,0:T(8,128)S(1)} collective-permute-done((f32[16,128]{1,0:T(8,128)S(1)}, f32[16,128]{1,0:T(8,128)S(1)}, u32[]{:S(2)}, u32[]{:S(2)}) %collective-permute-start.5) | collective-permute-done | bytes 8224 | tf_op jit(solution)/shard_map/ppermute | solution.py:395
  28.8 2.4 %collective-permute-start.9 = (f32[32,128]{1,0:T(8,128)S(1)}, f32[32,128]{1,0:T(8,128)S(1)}, u32[]{:S(2)}, u32[]{:S(2)}) collective-permute-start(f32[32,128]{1,0:T(8,128)S(1)} %get-tuple-element.44.refs_0_), channel_id=1, source_target_pairs={{0,24},{8,16},{16,8},{24,0},{1,25},{9,17},{17,9},{25,1},{2,26},{10... | collective-permute-start | bytes 49160 | tf_op jit(solution)/shard_map/ppermute | solution.py:386
  31.2 2.0 %collective-permute-start.7 = (f32[32,128]{1,0:T(8,128)S(1)}, f32[32,128]{1,0:T(8,128)S(1)}, u32[]{:S(2)}, u32[]{:S(2)}) collective-permute-start(f32[32,128]{1,0:T(8,128)S(1)} %get-tuple-element.44.refs_0_), channel_id=1, source_target_pairs={{0,8},{8,0},{16,24},{24,16},{1,9},{9,1},{17,25},{25,17},{2,10},{10... | collective-permute-start | bytes 49160 | tf_op jit(solution)/shard_map/ppermute | solution.py:386
  33.2 1.1 %collective-permute-done.9.refs_3_ = f32[32,128]{1,0:T(8,128)S(1)} collective-permute-done((f32[32,128]{1,0:T(8,128)S(1)}, f32[32,128]{1,0:T(8,128)S(1)}, u32[]{:S(2)}, u32[]{:S(2)}) %collective-permute-start.9) | collective-permute-done | bytes 16416 | tf_op jit(solution)/shard_map/ppermute | solution.py:386
  34.3 1.5 %collective-permute-done.8.refs_2_ = f32[32,128]{1,0:T(8,128)S(1)} collective-permute-done((f32[32,128]{1,0:T(8,128)S(1)}, f32[32,128]{1,0:T(8,128)S(1)}, u32[]{:S(2)}, u32[]{:S(2)}) %collective-permute-start.8) | collective-permute-done | bytes 16416 | tf_op jit(solution)/shard_map/ppermute | solution.py:386
  35.9 1.8 %shard_map.110 = (f32[16,128]{1,0:T(8,128)S(1)}, f32[1,48,128]{2,1,0:T(8,128)S(1)}, f32[4,48,128]{2,1,0:T(8,128)S(1)}, f32[4,48,128]{2,1,0:T(8,128)S(1)}, f32[8,128]{1,0:T(8,128)S(1)}) custom-call(s32[8,128]{1,0:T(8,128)S(1)} %get-tuple-element.39.ids_ref, s32[8,128]{1,0:T(8,128)S(1)} %shard_map.109.all_ref, f32[128,48,128]{2,1,0:T(8,128)S(1)} %get-tuple-element.36.lat_ref, ...), custom_call_target="tpu_custom_call" | custom-call | tf_op jit(solution)/shard_map/pallas_call | solution.py:42
  37.7 1.2 %collective-permute-done.10.other_ref = f32[16,128]{1,0:T(8,128)S(1)} collective-permute-done((f32[16,128]{1,0:T(8,128)S(1)}, f32[16,128]{1,0:T(8,128)S(1)}, u32[]{:S(2)}, u32[]{:S(2)}) %collective-permute-start.10) | collective-permute-done | bytes 8224 | tf_op jit(solution)/shard_map/ppermute | solution.py:393
  38.8 1.4 %collective-permute-start.13 = (f32[16,128]{1,0:T(8,128)S(1)}, f32[16,128]{1,0:T(8,128)S(1)}, u32[]{:S(2)}, u32[]{:S(2)}) collective-permute-start(f32[16,128]{1,0:T(8,128)S(1)} %shard_map.111.refs_0_), channel_id=1, source_target_pairs={{0,6},{1,7},{2,4},{3,5},{4,2},{5,3},{6,0},{7,1},{8,14},{9,15},{10,... | collective-permute-start | bytes 24584 | tf_op jit(solution)/shard_map/ppermute | solution.py:395
  40.3 1.5 %collective-permute-start.12 = (f32[16,128]{1,0:T(8,128)S(1)}, f32[16,128]{1,0:T(8,128)S(1)}, u32[]{:S(2)}, u32[]{:S(2)}) collective-permute-start(f32[16,128]{1,0:T(8,128)S(1)} %shard_map.111.refs_0_), channel_id=1, source_target_pairs={{0,4},{1,5},{2,6},{3,7},{4,0},{5,1},{6,2},{7,3},{8,12},{9,13},{10,... | collective-permute-start | bytes 24584 | tf_op jit(solution)/shard_map/ppermute | solution.py:395
  41.8 0.6 collective-permute-start.11
  42.3 1.1 %collective-permute-done.13.refs_3_ = f32[16,128]{1,0:T(8,128)S(1)} collective-permute-done((f32[16,128]{1,0:T(8,128)S(1)}, f32[16,128]{1,0:T(8,128)S(1)}, u32[]{:S(2)}, u32[]{:S(2)}) %collective-permute-start.13) | collective-permute-done | bytes 8224 | tf_op jit(solution)/shard_map/ppermute | solution.py:395
  43.4 0.6 collective-permute-done.12.refs_2_
  43.9 1.5 %collective-permute-done.11.refs_1_ = f32[16,128]{1,0:T(8,128)S(1)} collective-permute-done((f32[16,128]{1,0:T(8,128)S(1)}, f32[16,128]{1,0:T(8,128)S(1)}, u32[]{:S(2)}, u32[]{:S(2)}) %collective-permute-start.11) | collective-permute-done | bytes 8224 | tf_op jit(solution)/shard_map/ppermute | solution.py:395
  45.9 1.5 %collective-permute-start.16 = (f32[24,128]{1,0:T(8,128)S(1)}, f32[24,128]{1,0:T(8,128)S(1)}, u32[]{:S(2)}, u32[]{:S(2)}) collective-permute-start(f32[24,128]{1,0:T(8,128)S(1)} %get-tuple-element.52.refs_1_), channel_id=1, source_target_pairs={{0,24},{8,16},{16,8},{24,0},{1,25},{9,17},{17,9},{25,1},{2,26},{10... | collective-permute-start | bytes 36872 | tf_op jit(solution)/shard_map/ppermute | solution.py:386
  47.4 0.6 collective-permute-start.15
  48.0 2.3 %collective-permute-start.14 = (f32[24,128]{1,0:T(8,128)S(1)}, f32[24,128]{1,0:T(8,128)S(1)}, u32[]{:S(2)}, u32[]{:S(2)}) collective-permute-start(f32[24,128]{1,0:T(8,128)S(1)} %get-tuple-element.52.refs_1_), channel_id=1, source_target_pairs={{0,8},{8,0},{16,24},{24,16},{1,9},{9,1},{17,25},{25,17},{2,10},{10... | collective-permute-start | bytes 36872 | tf_op jit(solution)/shard_map/ppermute | solution.py:386
  50.3 1.1 %collective-permute-done.16.refs_4_ = f32[24,128]{1,0:T(8,128)S(1)} collective-permute-done((f32[24,128]{1,0:T(8,128)S(1)}, f32[24,128]{1,0:T(8,128)S(1)}, u32[]{:S(2)}, u32[]{:S(2)}) %collective-permute-start.16) | collective-permute-done | bytes 12320 | tf_op jit(solution)/shard_map/ppermute | solution.py:386
  51.4 0.6 collective-permute-done.15.refs_3_
  52.1 1.8 %shard_map.113 = (f32[16,128]{1,0:T(8,128)S(1)}, f32[1,48,128]{2,1,0:T(8,128)S(1)}, f32[4,48,128]{2,1,0:T(8,128)S(1)}, f32[4,48,128]{2,1,0:T(8,128)S(1)}, f32[8,128]{1,0:T(8,128)S(1)}) custom-call(s32[8,128]{1,0:T(8,128)S(1)} %get-tuple-element.39.ids_ref, s32[8,128]{1,0:T(8,128)S(1)} %shard_map.109.all_ref, f32[128,48,128]{2,1,0:T(8,128)S(1)} %get-tuple-element.36.lat_ref, ...), custom_call_target="tpu_custom_call" | custom-call | tf_op jit(solution)/shard_map/pallas_call | solution.py:42
  53.9 1.2 %collective-permute-done.17.other_ref = f32[16,128]{1,0:T(8,128)S(1)} collective-permute-done((f32[16,128]{1,0:T(8,128)S(1)}, f32[16,128]{1,0:T(8,128)S(1)}, u32[]{:S(2)}, u32[]{:S(2)}) %collective-permute-start.17) | collective-permute-done | bytes 8224 | tf_op jit(solution)/shard_map/ppermute | solution.py:393
  55.1 1.7 %collective-permute-start.20 = (f32[16,128]{1,0:T(8,128)S(1)}, f32[16,128]{1,0:T(8,128)S(1)}, u32[]{:S(2)}, u32[]{:S(2)}) collective-permute-start(f32[16,128]{1,0:T(8,128)S(1)} %shard_map.114.refs_0_), channel_id=1, source_target_pairs={{0,6},{1,7},{2,4},{3,5},{4,2},{5,3},{6,0},{7,1},{8,14},{9,15},{10,... | collective-permute-start | bytes 24584 | tf_op jit(solution)/shard_map/ppermute | solution.py:395
  57.3 1.3 %collective-permute-start.18 = (f32[16,128]{1,0:T(8,128)S(1)}, f32[16,128]{1,0:T(8,128)S(1)}, u32[]{:S(2)}, u32[]{:S(2)}) collective-permute-start(f32[16,128]{1,0:T(8,128)S(1)} %shard_map.114.refs_0_), channel_id=1, source_target_pairs={{0,2},{1,3},{2,0},{3,1},{4,6},{5,7},{6,4},{7,5},{8,10},{9,11},{10,... | collective-permute-start | bytes 24584 | tf_op jit(solution)/shard_map/ppermute | solution.py:395
  58.6 1.1 %collective-permute-done.20.refs_3_ = f32[16,128]{1,0:T(8,128)S(1)} collective-permute-done((f32[16,128]{1,0:T(8,128)S(1)}, f32[16,128]{1,0:T(8,128)S(1)}, u32[]{:S(2)}, u32[]{:S(2)}) %collective-permute-start.20) | collective-permute-done | bytes 8224 | tf_op jit(solution)/shard_map/ppermute | solution.py:395
  59.7 0.8 collective-permute-done.19.refs_2_
  61.4 2.3 %collective-permute-start.23 = (f32[24,128]{1,0:T(8,128)S(1)}, f32[24,128]{1,0:T(8,128)S(1)}, u32[]{:S(2)}, u32[]{:S(2)}) collective-permute-start(f32[24,128]{1,0:T(8,128)S(1)} %get-tuple-element.57.refs_1_), channel_id=1, source_target_pairs={{0,24},{8,16},{16,8},{24,0},{1,25},{9,17},{17,9},{25,1},{2,26},{10... | collective-permute-start | bytes 36872 | tf_op jit(solution)/shard_map/ppermute | solution.py:386
  63.7 0.9 %collective-permute-start.22 = (f32[24,128]{1,0:T(8,128)S(1)}, f32[24,128]{1,0:T(8,128)S(1)}, u32[]{:S(2)}, u32[]{:S(2)}) collective-permute-start(f32[24,128]{1,0:T(8,128)S(1)} %get-tuple-element.57.refs_1_), channel_id=1, source_target_pairs={{0,16},{8,24},{16,0},{24,8},{1,17},{9,25},{17,1},{25,9},{2,18},{10... | collective-permute-start | bytes 36872 | tf_op jit(solution)/shard_map/ppermute | solution.py:386
  64.6 1.2 %collective-permute-start.21 = (f32[24,128]{1,0:T(8,128)S(1)}, f32[24,128]{1,0:T(8,128)S(1)}, u32[]{:S(2)}, u32[]{:S(2)}) collective-permute-start(f32[24,128]{1,0:T(8,128)S(1)} %get-tuple-element.57.refs_1_), channel_id=1, source_target_pairs={{0,8},{8,0},{16,24},{24,16},{1,9},{9,1},{17,25},{25,17},{2,10},{10... | collective-permute-start | bytes 36872 | tf_op jit(solution)/shard_map/ppermute | solution.py:386
  65.8 1.2 %collective-permute-done.23.refs_4_ = f32[24,128]{1,0:T(8,128)S(1)} collective-permute-done((f32[24,128]{1,0:T(8,128)S(1)}, f32[24,128]{1,0:T(8,128)S(1)}, u32[]{:S(2)}, u32[]{:S(2)}) %collective-permute-start.23) | collective-permute-done | bytes 12320 | tf_op jit(solution)/shard_map/ppermute | solution.py:386
  67.0 1.4 %collective-permute-done.22.refs_3_ = f32[24,128]{1,0:T(8,128)S(1)} collective-permute-done((f32[24,128]{1,0:T(8,128)S(1)}, f32[24,128]{1,0:T(8,128)S(1)}, u32[]{:S(2)}, u32[]{:S(2)}) %collective-permute-start.22) | collective-permute-done | bytes 12320 | tf_op jit(solution)/shard_map/ppermute | solution.py:386
  68.4 1.5 %shard_map.116 = (f32[8,128]{1,0:T(8,128)S(1)}, f32[1,48,128]{2,1,0:T(8,128)S(1)}, f32[1,48,128]{2,1,0:T(8,128)S(1)}, f32[8,128]{1,0:T(8,128)S(1)}) custom-call(s32[8,128]{1,0:T(8,128)S(1)} %get-tuple-element.39.ids_ref, s32[8,128]{1,0:T(8,128)S(1)} %shard_map.109.all_ref, f32[128,48,128]{2,1,0:T(8,128)S(1)} %get-tuple-element.36.lat_ref, ...), custom_call_target="tpu_custom_call" | custom-call | tf_op jit(solution)/shard_map/pallas_call | solution.py:42
  70.0 1.2 %collective-permute-done.24.other_ref = f32[8,128]{1,0:T(8,128)S(1)} collective-permute-done((f32[8,128]{1,0:T(8,128)S(1)}, f32[8,128]{1,0:T(8,128)S(1)}, u32[]{:S(2)}, u32[]{:S(2)}) %collective-permute-start.24) | collective-permute-done | bytes 4128 | tf_op jit(solution)/shard_map/ppermute | solution.py:393
  71.1 1.4 %collective-permute-start.27 = (f32[8,128]{1,0:T(8,128)S(1)}, f32[8,128]{1,0:T(8,128)S(1)}, u32[]{:S(2)}, u32[]{:S(2)}) collective-permute-start(f32[8,128]{1,0:T(8,128)S(1)} %shard_map.117.refs_0_), channel_id=1, source_target_pairs={{0,6},{1,7},{2,4},{3,5},{4,2},{5,3},{6,0},{7,1},{8,14},{9,15},{10,... | collective-permute-start | bytes 12296 | tf_op jit(solution)/shard_map/ppermute | solution.py:395
  72.6 1.5 %collective-permute-start.26 = (f32[8,128]{1,0:T(8,128)S(1)}, f32[8,128]{1,0:T(8,128)S(1)}, u32[]{:S(2)}, u32[]{:S(2)}) collective-permute-start(f32[8,128]{1,0:T(8,128)S(1)} %shard_map.117.refs_0_), channel_id=1, source_target_pairs={{0,4},{1,5},{2,6},{3,7},{4,0},{5,1},{6,2},{7,3},{8,12},{9,13},{10,... | collective-permute-start | bytes 12296 | tf_op jit(solution)/shard_map/ppermute | solution.py:395
  74.1 0.6 collective-permute-start.25
  74.6 1.0 %collective-permute-done.27.refs_3_ = f32[8,128]{1,0:T(8,128)S(1)} collective-permute-done((f32[8,128]{1,0:T(8,128)S(1)}, f32[8,128]{1,0:T(8,128)S(1)}, u32[]{:S(2)}, u32[]{:S(2)}) %collective-permute-start.27) | collective-permute-done | bytes 4128 | tf_op jit(solution)/shard_map/ppermute | solution.py:395
  75.6 0.5 collective-permute-done.26.refs_2_
  76.2 1.5 %collective-permute-done.25.refs_1_ = f32[8,128]{1,0:T(8,128)S(1)} collective-permute-done((f32[8,128]{1,0:T(8,128)S(1)}, f32[8,128]{1,0:T(8,128)S(1)}, u32[]{:S(2)}, u32[]{:S(2)}) %collective-permute-start.25) | collective-permute-done | bytes 4128 | tf_op jit(solution)/shard_map/ppermute | solution.py:395
  77.7 0.8 shard_map.118
  (29 shorter events, 4.2 us)
Async XLA Ops:
  4.0 14.2 %copy-start.1 = (f32[48,128]{1,0:T(8,128)S(1)}, f32[48,128]{1,0:T(8,128)}, u32[]{:S(2)}) copy-start(f32[48,128]{1,0:T(8,128)} %get-tuple-element.38.refs_0_) | copy-start | bytes 73732
  4.0 14.2 %all-to-all-start = ((bf16[8,208,128]{2,1,0:T(8,128)(2,1)}), bf16[8,208,128]{2,1,0:T(8,128)(2,1)}, u32[]{:S(2)}, u32[]{:S(2)}) async-start(bf16[8,208,128]{2,1,0:T(8,128)(2,1)} %get-tuple-element.37), calls=%async_computation | async-start | bytes 851968 | tf_op jit(solution)/shard_map/all_to_all | solution.py:399
  9.2 7.0 %collective-permute-start.2 = (f32[48,128]{1,0:T(8,128)}, f32[48,128]{1,0:T(8,128)S(1)}, u32[]{:S(2)}, u32[]{:S(2)}) collective-permute-start(f32[48,128]{1,0:T(8,128)} %bitcast.4), channel_id=1, source_target_pairs={{0,24},{8,16},{16,8},{24,0},{1,25},{9,17},{17,9},{25,1},{2,26},{10... | collective-permute-start | bytes 73736 | tf_op jit(solution)/shard_map/ppermute | solution.py:386
  13.2 4.9 %collective-permute-start.1 = (f32[48,128]{1,0:T(8,128)}, f32[48,128]{1,0:T(8,128)S(1)}, u32[]{:S(2)}, u32[]{:S(2)}) collective-permute-start(f32[48,128]{1,0:T(8,128)} %bitcast.5), channel_id=1, source_target_pairs={{0,16},{8,24},{16,0},{24,8},{1,17},{9,25},{17,1},{25,9},{2,18},{10... | collective-permute-start | bytes 73736 | tf_op jit(solution)/shard_map/ppermute | solution.py:386
  13.2 4.9 %collective-permute-start = (f32[48,128]{1,0:T(8,128)}, f32[48,128]{1,0:T(8,128)S(1)}, u32[]{:S(2)}, u32[]{:S(2)}) collective-permute-start(f32[48,128]{1,0:T(8,128)} %bitcast.6), channel_id=1, source_target_pairs={{0,8},{8,0},{16,24},{24,16},{1,9},{9,1},{17,25},{25,17},{2,10},{10... | collective-permute-start | bytes 73736 | tf_op jit(solution)/shard_map/ppermute | solution.py:386
  13.9 14.5 %copy-start = (f32[8,128]{1,0:T(8,128)S(1)}, f32[8,128]{1,0:T(8,128)}, u32[]{:S(2)}) copy-start(f32[8,128]{1,0:T(8,128)} %get-tuple-element.34.weight_ref) | copy-start | bytes 12292
  20.1 1.2 %collective-permute-start.3 = (f32[16,128]{1,0:T(8,128)S(1)}, f32[16,128]{1,0:T(8,128)S(1)}, u32[]{:S(2)}, u32[]{:S(2)}) collective-permute-start(f32[16,128]{1,0:T(8,128)S(1)} %get-tuple-element.43.one_ref), channel_id=1, source_target_pairs={{0,1},{1,0},{2,3},{3,2},{4,5},{5,4},{6,7},{7,6},{8,9},{9,8},{10,11... | collective-permute-start | bytes 24584 | tf_op jit(solution)/shard_map/ppermute | solution.py:393
  21.4 4.5 %collective-permute-start.6 = (f32[16,128]{1,0:T(8,128)S(1)}, f32[16,128]{1,0:T(8,128)S(1)}, u32[]{:S(2)}, u32[]{:S(2)}) collective-permute-start(f32[16,128]{1,0:T(8,128)S(1)} %shard_map.107.refs_1_), channel_id=1, source_target_pairs={{0,6},{1,7},{2,4},{3,5},{4,2},{5,3},{6,0},{7,1},{8,14},{9,15},{10,... | collective-permute-start | bytes 24584 | tf_op jit(solution)/shard_map/ppermute | solution.py:395
  24.1 3.7 %collective-permute-start.5 = (f32[16,128]{1,0:T(8,128)S(1)}, f32[16,128]{1,0:T(8,128)S(1)}, u32[]{:S(2)}, u32[]{:S(2)}) collective-permute-start(f32[16,128]{1,0:T(8,128)S(1)} %shard_map.107.refs_1_), channel_id=1, source_target_pairs={{0,4},{1,5},{2,6},{3,7},{4,0},{5,1},{6,2},{7,3},{8,12},{9,13},{10,... | collective-permute-start | bytes 24584 | tf_op jit(solution)/shard_map/ppermute | solution.py:395
  24.7 3.7 %collective-permute-start.4 = (f32[16,128]{1,0:T(8,128)S(1)}, f32[16,128]{1,0:T(8,128)S(1)}, u32[]{:S(2)}, u32[]{:S(2)}) collective-permute-start(f32[16,128]{1,0:T(8,128)S(1)} %shard_map.107.refs_1_), channel_id=1, source_target_pairs={{0,2},{1,3},{2,0},{3,1},{4,6},{5,7},{6,4},{7,5},{8,10},{9,11},{10,... | collective-permute-start | bytes 24584 | tf_op jit(solution)/shard_map/ppermute | solution.py:395
  28.8 5.6 %collective-permute-start.9 = (f32[32,128]{1,0:T(8,128)S(1)}, f32[32,128]{1,0:T(8,128)S(1)}, u32[]{:S(2)}, u32[]{:S(2)}) collective-permute-start(f32[32,128]{1,0:T(8,128)S(1)} %get-tuple-element.44.refs_0_), channel_id=1, source_target_pairs={{0,24},{8,16},{16,8},{24,0},{1,25},{9,17},{17,9},{25,1},{2,26},{10... | collective-permute-start | bytes 49160 | tf_op jit(solution)/shard_map/ppermute | solution.py:386
  31.2 4.6 %collective-permute-start.8 = (f32[32,128]{1,0:T(8,128)S(1)}, f32[32,128]{1,0:T(8,128)S(1)}, u32[]{:S(2)}, u32[]{:S(2)}) collective-permute-start(f32[32,128]{1,0:T(8,128)S(1)} %get-tuple-element.44.refs_0_), channel_id=1, source_target_pairs={{0,16},{8,24},{16,0},{24,8},{1,17},{9,25},{17,1},{25,9},{2,18},{10... | collective-permute-start | bytes 49160 | tf_op jit(solution)/shard_map/ppermute | solution.py:386
  31.2 4.6 %collective-permute-start.7 = (f32[32,128]{1,0:T(8,128)S(1)}, f32[32,128]{1,0:T(8,128)S(1)}, u32[]{:S(2)}, u32[]{:S(2)}) collective-permute-start(f32[32,128]{1,0:T(8,128)S(1)} %get-tuple-element.44.refs_0_), channel_id=1, source_target_pairs={{0,8},{8,0},{16,24},{24,16},{1,9},{9,1},{17,25},{25,17},{2,10},{10... | collective-permute-start | bytes 49160 | tf_op jit(solution)/shard_map/ppermute | solution.py:386
  37.6 1.2 %collective-permute-start.10 = (f32[16,128]{1,0:T(8,128)S(1)}, f32[16,128]{1,0:T(8,128)S(1)}, u32[]{:S(2)}, u32[]{:S(2)}) collective-permute-start(f32[16,128]{1,0:T(8,128)S(1)} %get-tuple-element.48.one_ref), channel_id=1, source_target_pairs={{0,1},{1,0},{2,3},{3,2},{4,5},{5,4},{6,7},{7,6},{8,9},{9,8},{10,11... | collective-permute-start | bytes 24584 | tf_op jit(solution)/shard_map/ppermute | solution.py:393
  38.8 4.5 %collective-permute-start.13 = (f32[16,128]{1,0:T(8,128)S(1)}, f32[16,128]{1,0:T(8,128)S(1)}, u32[]{:S(2)}, u32[]{:S(2)}) collective-permute-start(f32[16,128]{1,0:T(8,128)S(1)} %shard_map.111.refs_0_), channel_id=1, source_target_pairs={{0,6},{1,7},{2,4},{3,5},{4,2},{5,3},{6,0},{7,1},{8,14},{9,15},{10,... | collective-permute-start | bytes 24584 | tf_op jit(solution)/shard_map/ppermute | solution.py:395
  40.3 3.7 %collective-permute-start.12 = (f32[16,128]{1,0:T(8,128)S(1)}, f32[16,128]{1,0:T(8,128)S(1)}, u32[]{:S(2)}, u32[]{:S(2)}) collective-permute-start(f32[16,128]{1,0:T(8,128)S(1)} %shard_map.111.refs_0_), channel_id=1, source_target_pairs={{0,4},{1,5},{2,6},{3,7},{4,0},{5,1},{6,2},{7,3},{8,12},{9,13},{10,... | collective-permute-start | bytes 24584 | tf_op jit(solution)/shard_map/ppermute | solution.py:395
  41.8 3.7 %collective-permute-start.11 = (f32[16,128]{1,0:T(8,128)S(1)}, f32[16,128]{1,0:T(8,128)S(1)}, u32[]{:S(2)}, u32[]{:S(2)}) collective-permute-start(f32[16,128]{1,0:T(8,128)S(1)} %shard_map.111.refs_0_), channel_id=1, source_target_pairs={{0,2},{1,3},{2,0},{3,1},{4,6},{5,7},{6,4},{7,5},{8,10},{9,11},{10,... | collective-permute-start | bytes 24584 | tf_op jit(solution)/shard_map/ppermute | solution.py:395
  45.9 5.5 %collective-permute-start.16 = (f32[24,128]{1,0:T(8,128)S(1)}, f32[24,128]{1,0:T(8,128)S(1)}, u32[]{:S(2)}, u32[]{:S(2)}) collective-permute-start(f32[24,128]{1,0:T(8,128)S(1)} %get-tuple-element.52.refs_1_), channel_id=1, source_target_pairs={{0,24},{8,16},{16,8},{24,0},{1,25},{9,17},{17,9},{25,1},{2,26},{10... | collective-permute-start | bytes 36872 | tf_op jit(solution)/shard_map/ppermute | solution.py:386
  47.4 4.6 %collective-permute-start.15 = (f32[24,128]{1,0:T(8,128)S(1)}, f32[24,128]{1,0:T(8,128)S(1)}, u32[]{:S(2)}, u32[]{:S(2)}) collective-permute-start(f32[24,128]{1,0:T(8,128)S(1)} %get-tuple-element.52.refs_1_), channel_id=1, source_target_pairs={{0,16},{8,24},{16,0},{24,8},{1,17},{9,25},{17,1},{25,9},{2,18},{10... | collective-permute-start | bytes 36872 | tf_op jit(solution)/shard_map/ppermute | solution.py:386
  48.0 4.1 %collective-permute-start.14 = (f32[24,128]{1,0:T(8,128)S(1)}, f32[24,128]{1,0:T(8,128)S(1)}, u32[]{:S(2)}, u32[]{:S(2)}) collective-permute-start(f32[24,128]{1,0:T(8,128)S(1)} %get-tuple-element.52.refs_1_), channel_id=1, source_target_pairs={{0,8},{8,0},{16,24},{24,16},{1,9},{9,1},{17,25},{25,17},{2,10},{10... | collective-permute-start | bytes 36872 | tf_op jit(solution)/shard_map/ppermute | solution.py:386
  53.9 1.2 %collective-permute-start.17 = (f32[16,128]{1,0:T(8,128)S(1)}, f32[16,128]{1,0:T(8,128)S(1)}, u32[]{:S(2)}, u32[]{:S(2)}) collective-permute-start(f32[16,128]{1,0:T(8,128)S(1)} %get-tuple-element.53.one_ref), channel_id=1, source_target_pairs={{0,1},{1,0},{2,3},{3,2},{4,5},{5,4},{6,7},{7,6},{8,9},{9,8},{10,11... | collective-permute-start | bytes 24584 | tf_op jit(solution)/shard_map/ppermute | solution.py:393
  55.1 4.5 %collective-permute-start.20 = (f32[16,128]{1,0:T(8,128)S(1)}, f32[16,128]{1,0:T(8,128)S(1)}, u32[]{:S(2)}, u32[]{:S(2)}) collective-permute-start(f32[16,128]{1,0:T(8,128)S(1)} %shard_map.114.refs_0_), channel_id=1, source_target_pairs={{0,6},{1,7},{2,4},{3,5},{4,2},{5,3},{6,0},{7,1},{8,14},{9,15},{10,... | collective-permute-start | bytes 24584 | tf_op jit(solution)/shard_map/ppermute | solution.py:395
  56.8 3.7 %collective-permute-start.19 = (f32[16,128]{1,0:T(8,128)S(1)}, f32[16,128]{1,0:T(8,128)S(1)}, u32[]{:S(2)}, u32[]{:S(2)}) collective-permute-start(f32[16,128]{1,0:T(8,128)S(1)} %shard_map.114.refs_0_), channel_id=1, source_target_pairs={{0,4},{1,5},{2,6},{3,7},{4,0},{5,1},{6,2},{7,3},{8,12},{9,13},{10,... | collective-permute-start | bytes 24584 | tf_op jit(solution)/shard_map/ppermute | solution.py:395
  57.3 3.7 %collective-permute-start.18 = (f32[16,128]{1,0:T(8,128)S(1)}, f32[16,128]{1,0:T(8,128)S(1)}, u32[]{:S(2)}, u32[]{:S(2)}) collective-permute-start(f32[16,128]{1,0:T(8,128)S(1)} %shard_map.114.refs_0_), channel_id=1, source_target_pairs={{0,2},{1,3},{2,0},{3,1},{4,6},{5,7},{6,4},{7,5},{8,10},{9,11},{10,... | collective-permute-start | bytes 24584 | tf_op jit(solution)/shard_map/ppermute | solution.py:395
  61.4 5.6 %collective-permute-start.23 = (f32[24,128]{1,0:T(8,128)S(1)}, f32[24,128]{1,0:T(8,128)S(1)}, u32[]{:S(2)}, u32[]{:S(2)}) collective-permute-start(f32[24,128]{1,0:T(8,128)S(1)} %get-tuple-element.57.refs_1_), channel_id=1, source_target_pairs={{0,24},{8,16},{16,8},{24,0},{1,25},{9,17},{17,9},{25,1},{2,26},{10... | collective-permute-start | bytes 36872 | tf_op jit(solution)/shard_map/ppermute | solution.py:386
  63.7 4.7 %collective-permute-start.22 = (f32[24,128]{1,0:T(8,128)S(1)}, f32[24,128]{1,0:T(8,128)S(1)}, u32[]{:S(2)}, u32[]{:S(2)}) collective-permute-start(f32[24,128]{1,0:T(8,128)S(1)} %get-tuple-element.57.refs_1_), channel_id=1, source_target_pairs={{0,16},{8,24},{16,0},{24,8},{1,17},{9,25},{17,1},{25,9},{2,18},{10... | collective-permute-start | bytes 36872 | tf_op jit(solution)/shard_map/ppermute | solution.py:386
  64.6 3.8 %collective-permute-start.21 = (f32[24,128]{1,0:T(8,128)S(1)}, f32[24,128]{1,0:T(8,128)S(1)}, u32[]{:S(2)}, u32[]{:S(2)}) collective-permute-start(f32[24,128]{1,0:T(8,128)S(1)} %get-tuple-element.57.refs_1_), channel_id=1, source_target_pairs={{0,8},{8,0},{16,24},{24,16},{1,9},{9,1},{17,25},{25,17},{2,10},{10... | collective-permute-start | bytes 36872 | tf_op jit(solution)/shard_map/ppermute | solution.py:386
  69.9 1.2 %collective-permute-start.24 = (f32[8,128]{1,0:T(8,128)S(1)}, f32[8,128]{1,0:T(8,128)S(1)}, u32[]{:S(2)}, u32[]{:S(2)}) collective-permute-start(f32[8,128]{1,0:T(8,128)S(1)} %get-tuple-element.58.one_ref), channel_id=1, source_target_pairs={{0,1},{1,0},{2,3},{3,2},{4,5},{5,4},{6,7},{7,6},{8,9},{9,8},{10,11... | collective-permute-start | bytes 12296 | tf_op jit(solution)/shard_map/ppermute | solution.py:393
  71.1 4.5 %collective-permute-start.27 = (f32[8,128]{1,0:T(8,128)S(1)}, f32[8,128]{1,0:T(8,128)S(1)}, u32[]{:S(2)}, u32[]{:S(2)}) collective-permute-start(f32[8,128]{1,0:T(8,128)S(1)} %shard_map.117.refs_0_), channel_id=1, source_target_pairs={{0,6},{1,7},{2,4},{3,5},{4,2},{5,3},{6,0},{7,1},{8,14},{9,15},{10,... | collective-permute-start | bytes 12296 | tf_op jit(solution)/shard_map/ppermute | solution.py:395
  72.6 3.6 %collective-permute-start.26 = (f32[8,128]{1,0:T(8,128)S(1)}, f32[8,128]{1,0:T(8,128)S(1)}, u32[]{:S(2)}, u32[]{:S(2)}) collective-permute-start(f32[8,128]{1,0:T(8,128)S(1)} %shard_map.117.refs_0_), channel_id=1, source_target_pairs={{0,4},{1,5},{2,6},{3,7},{4,0},{5,1},{6,2},{7,3},{8,12},{9,13},{10,... | collective-permute-start | bytes 12296 | tf_op jit(solution)/shard_map/ppermute | solution.py:395
  74.1 3.6 %collective-permute-start.25 = (f32[8,128]{1,0:T(8,128)S(1)}, f32[8,128]{1,0:T(8,128)S(1)}, u32[]{:S(2)}, u32[]{:S(2)}) collective-permute-start(f32[8,128]{1,0:T(8,128)S(1)} %shard_map.117.refs_0_), channel_id=1, source_target_pairs={{0,2},{1,3},{2,0},{3,1},{4,6},{5,7},{6,4},{7,5},{8,10},{9,11},{10,... | collective-permute-start | bytes 12296 | tf_op jit(solution)/shard_map/ppermute | solution.py:395

commit v16 on v14

--- a/solution.py
+++ b/solution.py
@@ -77,22 +77,25 @@
     ]
     for copy in copies:
         copy.start()
-    for copy in copies:
-        copy.wait()
-    cell = place_ref[0] % nc
-    obs = place_ref[0] // nc
     ob = foot_ref.shape[1]
     lon = high_ref.shape[1]
     contract = (((1,), (1,)), ((), ()))
+    copies[0].wait()
+    copies[1].wait()
+    feet = [foot_ref[:, :, r * lon:(r + 1) * lon].reshape(nb * ob, lon) for r in range(CR)]
+    hats = [lax.dot_general(high_ref[...], foot, contract, preferred_element_type=F32) for foot in feet]
+    copies[2].wait()
     for r in range(CR):
-        foot = foot_ref[:, :, r * lon:(r + 1) * lon].reshape(nb * ob, lon)
-        hat = lax.dot_general(high_ref[...], foot, contract, preferred_element_type=F32)
-        hat += lax.dot_general(low_ref[...], foot, contract, preferred_element_type=F32)
+        hat = hats[r] + lax.dot_general(low_ref[...], feet[r], contract, preferred_element_type=F32)
         hat = hat.astype(BF16)
         for b in range(nb):
             at = (b * CR + r) * modes
             for c in range(nc):
                 out_ref[c, at:at + modes, :] = hat[c * modes:(c + 1) * modes, b * ob:(b + 1) * ob]
+    for copy in copies[3:]:
+        copy.wait()
+    cell = place_ref[0] % nc
+    obs = place_ref[0] // nc
     lane = lax.broadcasted_iota(jnp.int32, (16, ob), 1)
     ids = jnp.zeros((16, ob), F32)
     for b in range(nb):

time: 78.2 us -> 78.2 us (level)
  no operation moved by 1% of the time
where the time goes in v16:
time: 78.2 us; the launch traced here: 77.8 us
  starting transfers between devices  37.4 us (48%)
  waiting for transfers between devices  24.8 us (32%)
  Pallas kernels  14.1 us (18%)
    ppermute x12, starting transfers between devices, share(): lax.ppermute(array, axis, [(d, d ^ s) for d in range(size)])  17.9 us
    pallas_call x15, Pallas kernels, call(): pl.pallas_call(kernel, out_shape=outs, in_specs=specs, out_specs=jax.tree...  14.1 us
    ppermute x12, starting transfers between devices, addends(): lax.ppermute(both, axis, [(d, d ^ s) for d in range(size)])  14 us
    ppermute x12, waiting for transfers between devices, addends(): lax.ppermute(both, axis, [(d, d ^ s) for d in range(size)])  11.6 us
    ppermute x12, waiting for transfers between devices, share(): lax.ppermute(array, axis, [(d, d ^ s) for d in range(size)])  8.6 us
    all_to_all x1, starting transfers between devices, swap(): return lax.all_to_all(array, axis, split_axis=0, concat_axis=0, tiled=True)  5.18 us
    ppermute x4, waiting for transfers between devices, addends(): other = lax.ppermute(array, axis, [(d, d ^ 1) for d in range(size)])  4.63 us
  transfers between devices with their start and end apart: 29, of which 25 were waited for; matrix products, arithmetic and copies ran while one was open for 0% of the time, Pallas kernels for 3%

profile of v16, /device:TPU:0, one launch (start us, length us, event | category | flops | bytes accessed | tf_op | source)
XLA Modules:
  0.0 77.8 jit_solution(7893003884477928858)
XLA Ops:
  0.6 2.7 %shard_map.104 = (bf16[8,208,128]{2,1,0:T(8,128)(2,1)}, f32[8,128]{1,0:T(8,128)}) custom-call(s32[1]{0:T(128)} %bitcast.1.place_any, bf16[384,384]{1,0:T(8,128)(2,1)} %constant.14.clone.high_any, bf16[384,384]{1,0:T(8,128)(2,1)} %constant.15.clone.low_any, bf16[2,128,768]{2,1,0:T(8,128)(2,1)} %foot_any.1, s32[2]{0:T(128)} %off_any.1, s32[2]{0:T(128)} %sub_any.1, ...), custom_call_target="tpu_custom_call" | custom-call | tf_op jit(solution)/shard_map/pallas_call | solution.py:42
  3.3 5.2 %all-to-all-start = ((bf16[8,208,128]{2,1,0:T(8,128)(2,1)}), bf16[8,208,128]{2,1,0:T(8,128)(2,1)}, u32[]{:S(2)}, u32[]{:S(2)}) async-start(bf16[8,208,128]{2,1,0:T(8,128)(2,1)} %get-tuple-element.39), calls=%async_computation | async-start | bytes 851968 | tf_op jit(solution)/shard_map/all_to_all | solution.py:387
  8.5 4.1 %collective-permute-start.2 = (f32[48,128]{1,0:T(8,128)}, f32[48,128]{1,0:T(8,128)S(1)}, u32[]{:S(2)}, u32[]{:S(2)}) collective-permute-start(f32[48,128]{1,0:T(8,128)} %bitcast.3), channel_id=1, source_target_pairs={{0,24},{8,16},{16,8},{24,0},{1,25},{9,17},{17,9},{25,1},{2,26},{10... | collective-permute-start | bytes 73736 | tf_op jit(solution)/shard_map/ppermute | solution.py:374
  12.6 0.6 collective-permute-start
  13.2 0.8 copy-done.1
  14.0 2.3 %shard_map.105 = (f32[128,48,128]{2,1,0:T(8,128)S(1)}, f32[48,128]{1,0:T(8,128)S(1)}, bf16[48,2048]{1,0:T(8,128)(2,1)S(1)}) custom-call(f32[48,128,128]{2,1,0:T(8,128)} %lat_any, f32[48,128]{1,0:T(8,128)S(1)} %bitcast.6), custom_call_target="tpu_custom_call" | custom-call | bytes 6340608 | tf_op jit(solution)/shard_map/pallas_call | solution.py:42
  16.3 1.2 %collective-permute-done.1.refs_2_ = f32[48,128]{1,0:T(8,128)S(1)} collective-permute-done((f32[48,128]{1,0:T(8,128)}, f32[48,128]{1,0:T(8,128)S(1)}, u32[]{:S(2)}, u32[]{:S(2)}) %collective-permute-start.1) | collective-permute-done | bytes 24608 | tf_op jit(solution)/shard_map/ppermute | solution.py:374
  17.5 2.0 %shard_map.106 = (f32[16,128]{1,0:T(8,128)S(1)}, f32[4,48,128]{2,1,0:T(8,128)S(1)}, bf16[8,192,128]{2,1,0:T(8,128)(2,1)S(1)}, s32[8,128]{1,0:T(8,128)S(1)}, bf16...) custom-call(f32[128,48,128]{2,1,0:T(8,128)S(1)} %get-tuple-element.38.lat_ref, bf16[8,208,128]{2,1,0:T(8,128)(2,1)} %all-to-all-done.came_ref, ...), custom_call_target="tpu_custom_call" | custom-call | tf_op jit(solution)/shard_map/pallas_call | solution.py:42
  19.6 1.2 %collective-permute-done.3.other_ref = f32[16,128]{1,0:T(8,128)S(1)} collective-permute-done((f32[16,128]{1,0:T(8,128)S(1)}, f32[16,128]{1,0:T(8,128)S(1)}, u32[]{:S(2)}, u32[]{:S(2)}) %collective-permute-start.3) | collective-permute-done | bytes 8224 | tf_op jit(solution)/shard_map/ppermute | solution.py:381
  20.7 2.8 %collective-permute-start.6 = (f32[16,128]{1,0:T(8,128)S(1)}, f32[16,128]{1,0:T(8,128)S(1)}, u32[]{:S(2)}, u32[]{:S(2)}) collective-permute-start(f32[16,128]{1,0:T(8,128)S(1)} %shard_map.107.refs_1_), channel_id=1, source_target_pairs={{0,6},{1,7},{2,4},{3,5},{4,2},{5,3},{6,0},{7,1},{8,14},{9,15},{10,... | collective-permute-start | bytes 24584 | tf_op jit(solution)/shard_map/ppermute | solution.py:383
  24.2 1.1 %collective-permute-done.6.refs_4_ = f32[16,128]{1,0:T(8,128)S(1)} collective-permute-done((f32[16,128]{1,0:T(8,128)S(1)}, f32[16,128]{1,0:T(8,128)S(1)}, u32[]{:S(2)}, u32[]{:S(2)}) %collective-permute-start.6) | collective-permute-done | bytes 8224 | tf_op jit(solution)/shard_map/ppermute | solution.py:383
  25.3 1.9 %collective-permute-done.5.refs_3_ = f32[16,128]{1,0:T(8,128)S(1)} collective-permute-done((f32[16,128]{1,0:T(8,128)S(1)}, f32[16,128]{1,0:T(8,128)S(1)}, u32[]{:S(2)}, u32[]{:S(2)}) %collective-permute-start.5) | collective-permute-done | bytes 8224 | tf_op jit(solution)/shard_map/ppermute | solution.py:383
  28.1 2.6 %collective-permute-start.9 = (f32[32,128]{1,0:T(8,128)S(1)}, f32[32,128]{1,0:T(8,128)S(1)}, u32[]{:S(2)}, u32[]{:S(2)}) collective-permute-start(f32[32,128]{1,0:T(8,128)S(1)} %get-tuple-element.46.refs_0_), channel_id=1, source_target_pairs={{0,24},{8,16},{16,8},{24,0},{1,25},{9,17},{17,9},{25,1},{2,26},{10... | collective-permute-start | bytes 49160 | tf_op jit(solution)/shard_map/ppermute | solution.py:374
  30.7 1.8 %collective-permute-start.7 = (f32[32,128]{1,0:T(8,128)S(1)}, f32[32,128]{1,0:T(8,128)S(1)}, u32[]{:S(2)}, u32[]{:S(2)}) collective-permute-start(f32[32,128]{1,0:T(8,128)S(1)} %get-tuple-element.46.refs_0_), channel_id=1, source_target_pairs={{0,8},{8,0},{16,24},{24,16},{1,9},{9,1},{17,25},{25,17},{2,10},{10... | collective-permute-start | bytes 49160 | tf_op jit(solution)/shard_map/ppermute | solution.py:374
  32.5 1.1 %collective-permute-done.9.refs_3_ = f32[32,128]{1,0:T(8,128)S(1)} collective-permute-done((f32[32,128]{1,0:T(8,128)S(1)}, f32[32,128]{1,0:T(8,128)S(1)}, u32[]{:S(2)}, u32[]{:S(2)}) %collective-permute-start.9) | collective-permute-done | bytes 16416 | tf_op jit(solution)/shard_map/ppermute | solution.py:374
  33.7 1.7 %collective-permute-done.8.refs_2_ = f32[32,128]{1,0:T(8,128)S(1)} collective-permute-done((f32[32,128]{1,0:T(8,128)S(1)}, f32[32,128]{1,0:T(8,128)S(1)}, u32[]{:S(2)}, u32[]{:S(2)}) %collective-permute-start.8) | collective-permute-done | bytes 16416 | tf_op jit(solution)/shard_map/ppermute | solution.py:374
  35.4 1.7 %shard_map.110 = (f32[16,128]{1,0:T(8,128)S(1)}, f32[1,48,128]{2,1,0:T(8,128)S(1)}, f32[4,48,128]{2,1,0:T(8,128)S(1)}, f32[4,48,128]{2,1,0:T(8,128)S(1)}, f32[8,128]{1,0:T(8,128)S(1)}) custom-call(s32[8,128]{1,0:T(8,128)S(1)} %get-tuple-element.41.ids_ref, s32[8,128]{1,0:T(8,128)S(1)} %shard_map.109.all_ref, f32[128,48,128]{2,1,0:T(8,128)S(1)} %get-tuple-element.38.lat_ref, ...), custom_call_target="tpu_custom_call" | custom-call | tf_op jit(solution)/shard_map/pallas_call | solution.py:42
  37.2 1.2 %collective-permute-done.10.other_ref = f32[16,128]{1,0:T(8,128)S(1)} collective-permute-done((f32[16,128]{1,0:T(8,128)S(1)}, f32[16,128]{1,0:T(8,128)S(1)}, u32[]{:S(2)}, u32[]{:S(2)}) %collective-permute-start.10) | collective-permute-done | bytes 8224 | tf_op jit(solution)/shard_map/ppermute | solution.py:381
  38.4 1.5 %collective-permute-start.13 = (f32[16,128]{1,0:T(8,128)S(1)}, f32[16,128]{1,0:T(8,128)S(1)}, u32[]{:S(2)}, u32[]{:S(2)}) collective-permute-start(f32[16,128]{1,0:T(8,128)S(1)} %shard_map.111.refs_0_), channel_id=1, source_target_pairs={{0,6},{1,7},{2,4},{3,5},{4,2},{5,3},{6,0},{7,1},{8,14},{9,15},{10,... | collective-permute-start | bytes 24584 | tf_op jit(solution)/shard_map/ppermute | solution.py:383
  39.9 1.3 %collective-permute-start.12 = (f32[16,128]{1,0:T(8,128)S(1)}, f32[16,128]{1,0:T(8,128)S(1)}, u32[]{:S(2)}, u32[]{:S(2)}) collective-permute-start(f32[16,128]{1,0:T(8,128)S(1)} %shard_map.111.refs_0_), channel_id=1, source_target_pairs={{0,4},{1,5},{2,6},{3,7},{4,0},{5,1},{6,2},{7,3},{8,12},{9,13},{10,... | collective-permute-start | bytes 24584 | tf_op jit(solution)/shard_map/ppermute | solution.py:383
  41.1 0.7 collective-permute-start.11
  41.9 1.1 %collective-permute-done.13.refs_3_ = f32[16,128]{1,0:T(8,128)S(1)} collective-permute-done((f32[16,128]{1,0:T(8,128)S(1)}, f32[16,128]{1,0:T(8,128)S(1)}, u32[]{:S(2)}, u32[]{:S(2)}) %collective-permute-start.13) | collective-permute-done | bytes 8224 | tf_op jit(solution)/shard_map/ppermute | solution.py:383
  42.9 0.6 collective-permute-done.12.refs_2_
  43.5 1.3 %collective-permute-done.11.refs_1_ = f32[16,128]{1,0:T(8,128)S(1)} collective-permute-done((f32[16,128]{1,0:T(8,128)S(1)}, f32[16,128]{1,0:T(8,128)S(1)}, u32[]{:S(2)}, u32[]{:S(2)}) %collective-permute-start.11) | collective-permute-done | bytes 8224 | tf_op jit(solution)/shard_map/ppermute | solution.py:383
  45.2 1.5 %collective-permute-start.16 = (f32[24,128]{1,0:T(8,128)S(1)}, f32[24,128]{1,0:T(8,128)S(1)}, u32[]{:S(2)}, u32[]{:S(2)}) collective-permute-start(f32[24,128]{1,0:T(8,128)S(1)} %get-tuple-element.54.refs_1_), channel_id=1, source_target_pairs={{0,24},{8,16},{16,8},{24,0},{1,25},{9,17},{17,9},{25,1},{2,26},{10... | collective-permute-start | bytes 36872 | tf_op jit(solution)/shard_map/ppermute | solution.py:374
  46.7 0.6 collective-permute-start.15
  47.4 2.3 %collective-permute-start.14 = (f32[24,128]{1,0:T(8,128)S(1)}, f32[24,128]{1,0:T(8,128)S(1)}, u32[]{:S(2)}, u32[]{:S(2)}) collective-permute-start(f32[24,128]{1,0:T(8,128)S(1)} %get-tuple-element.54.refs_1_), channel_id=1, source_target_pairs={{0,8},{8,0},{16,24},{24,16},{1,9},{9,1},{17,25},{25,17},{2,10},{10... | collective-permute-start | bytes 36872 | tf_op jit(solution)/shard_map/ppermute | solution.py:374
  49.7 1.1 %collective-permute-done.16.refs_4_ = f32[24,128]{1,0:T(8,128)S(1)} collective-permute-done((f32[24,128]{1,0:T(8,128)S(1)}, f32[24,128]{1,0:T(8,128)S(1)}, u32[]{:S(2)}, u32[]{:S(2)}) %collective-permute-start.16) | collective-permute-done | bytes 12320 | tf_op jit(solution)/shard_map/ppermute | solution.py:374
  51.5 1.8 %shard_map.113 = (f32[16,128]{1,0:T(8,128)S(1)}, f32[1,48,128]{2,1,0:T(8,128)S(1)}, f32[4,48,128]{2,1,0:T(8,128)S(1)}, f32[4,48,128]{2,1,0:T(8,128)S(1)}, f32[8,128]{1,0:T(8,128)S(1)}) custom-call(s32[8,128]{1,0:T(8,128)S(1)} %get-tuple-element.41.ids_ref, s32[8,128]{1,0:T(8,128)S(1)} %shard_map.109.all_ref, f32[128,48,128]{2,1,0:T(8,128)S(1)} %get-tuple-element.38.lat_ref, ...), custom_call_target="tpu_custom_call" | custom-call | tf_op jit(solution)/shard_map/pallas_call | solution.py:42
  53.3 1.2 %collective-permute-done.17.other_ref = f32[16,128]{1,0:T(8,128)S(1)} collective-permute-done((f32[16,128]{1,0:T(8,128)S(1)}, f32[16,128]{1,0:T(8,128)S(1)}, u32[]{:S(2)}, u32[]{:S(2)}) %collective-permute-start.17) | collective-permute-done | bytes 8224 | tf_op jit(solution)/shard_map/ppermute | solution.py:381
  54.5 1.7 %collective-permute-start.20 = (f32[16,128]{1,0:T(8,128)S(1)}, f32[16,128]{1,0:T(8,128)S(1)}, u32[]{:S(2)}, u32[]{:S(2)}) collective-permute-start(f32[16,128]{1,0:T(8,128)S(1)} %shard_map.114.refs_0_), channel_id=1, source_target_pairs={{0,6},{1,7},{2,4},{3,5},{4,2},{5,3},{6,0},{7,1},{8,14},{9,15},{10,... | collective-permute-start | bytes 24584 | tf_op jit(solution)/shard_map/ppermute | solution.py:383
  56.6 1.3 %collective-permute-start.18 = (f32[16,128]{1,0:T(8,128)S(1)}, f32[16,128]{1,0:T(8,128)S(1)}, u32[]{:S(2)}, u32[]{:S(2)}) collective-permute-start(f32[16,128]{1,0:T(8,128)S(1)} %shard_map.114.refs_0_), channel_id=1, source_target_pairs={{0,2},{1,3},{2,0},{3,1},{4,6},{5,7},{6,4},{7,5},{8,10},{9,11},{10,... | collective-permute-start | bytes 24584 | tf_op jit(solution)/shard_map/ppermute | solution.py:383
  57.9 1.1 %collective-permute-done.20.refs_3_ = f32[16,128]{1,0:T(8,128)S(1)} collective-permute-done((f32[16,128]{1,0:T(8,128)S(1)}, f32[16,128]{1,0:T(8,128)S(1)}, u32[]{:S(2)}, u32[]{:S(2)}) %collective-permute-start.20) | collective-permute-done | bytes 8224 | tf_op jit(solution)/shard_map/ppermute | solution.py:383
  59.0 0.8 collective-permute-done.19.refs_2_
  60.8 2.5 %collective-permute-start.23 = (f32[24,128]{1,0:T(8,128)S(1)}, f32[24,128]{1,0:T(8,128)S(1)}, u32[]{:S(2)}, u32[]{:S(2)}) collective-permute-start(f32[24,128]{1,0:T(8,128)S(1)} %get-tuple-element.59.refs_1_), channel_id=1, source_target_pairs={{0,24},{8,16},{16,8},{24,0},{1,25},{9,17},{17,9},{25,1},{2,26},{10... | collective-permute-start | bytes 36872 | tf_op jit(solution)/shard_map/ppermute | solution.py:374
  63.2 0.9 %collective-permute-start.22 = (f32[24,128]{1,0:T(8,128)S(1)}, f32[24,128]{1,0:T(8,128)S(1)}, u32[]{:S(2)}, u32[]{:S(2)}) collective-permute-start(f32[24,128]{1,0:T(8,128)S(1)} %get-tuple-element.59.refs_1_), channel_id=1, source_target_pairs={{0,16},{8,24},{16,0},{24,8},{1,17},{9,25},{17,1},{25,9},{2,18},{10... | collective-permute-start | bytes 36872 | tf_op jit(solution)/shard_map/ppermute | solution.py:374
  64.1 1.0 %collective-permute-start.21 = (f32[24,128]{1,0:T(8,128)S(1)}, f32[24,128]{1,0:T(8,128)S(1)}, u32[]{:S(2)}, u32[]{:S(2)}) collective-permute-start(f32[24,128]{1,0:T(8,128)S(1)} %get-tuple-element.59.refs_1_), channel_id=1, source_target_pairs={{0,8},{8,0},{16,24},{24,16},{1,9},{9,1},{17,25},{25,17},{2,10},{10... | collective-permute-start | bytes 36872 | tf_op jit(solution)/shard_map/ppermute | solution.py:374
  65.2 1.1 %collective-permute-done.23.refs_4_ = f32[24,128]{1,0:T(8,128)S(1)} collective-permute-done((f32[24,128]{1,0:T(8,128)S(1)}, f32[24,128]{1,0:T(8,128)S(1)}, u32[]{:S(2)}, u32[]{:S(2)}) %collective-permute-start.23) | collective-permute-done | bytes 12320 | tf_op jit(solution)/shard_map/ppermute | solution.py:374
  66.3 1.6 %collective-permute-done.22.refs_3_ = f32[24,128]{1,0:T(8,128)S(1)} collective-permute-done((f32[24,128]{1,0:T(8,128)S(1)}, f32[24,128]{1,0:T(8,128)S(1)}, u32[]{:S(2)}, u32[]{:S(2)}) %collective-permute-start.22) | collective-permute-done | bytes 12320 | tf_op jit(solution)/shard_map/ppermute | solution.py:374
  68.0 1.5 %shard_map.116 = (f32[8,128]{1,0:T(8,128)S(1)}, f32[1,48,128]{2,1,0:T(8,128)S(1)}, f32[1,48,128]{2,1,0:T(8,128)S(1)}, f32[8,128]{1,0:T(8,128)S(1)}) custom-call(s32[8,128]{1,0:T(8,128)S(1)} %get-tuple-element.41.ids_ref, s32[8,128]{1,0:T(8,128)S(1)} %shard_map.109.all_ref, f32[128,48,128]{2,1,0:T(8,128)S(1)} %get-tuple-element.38.lat_ref, ...), custom_call_target="tpu_custom_call" | custom-call | tf_op jit(solution)/shard_map/pallas_call | solution.py:42
  69.5 1.2 %collective-permute-done.24.other_ref = f32[8,128]{1,0:T(8,128)S(1)} collective-permute-done((f32[8,128]{1,0:T(8,128)S(1)}, f32[8,128]{1,0:T(8,128)S(1)}, u32[]{:S(2)}, u32[]{:S(2)}) %collective-permute-start.24) | collective-permute-done | bytes 4128 | tf_op jit(solution)/shard_map/ppermute | solution.py:381
  70.7 1.5 %collective-permute-start.27 = (f32[8,128]{1,0:T(8,128)S(1)}, f32[8,128]{1,0:T(8,128)S(1)}, u32[]{:S(2)}, u32[]{:S(2)}) collective-permute-start(f32[8,128]{1,0:T(8,128)S(1)} %shard_map.117.refs_0_), channel_id=1, source_target_pairs={{0,6},{1,7},{2,4},{3,5},{4,2},{5,3},{6,0},{7,1},{8,14},{9,15},{10,... | collective-permute-start | bytes 12296 | tf_op jit(solution)/shard_map/ppermute | solution.py:383
  72.1 1.3 %collective-permute-start.26 = (f32[8,128]{1,0:T(8,128)S(1)}, f32[8,128]{1,0:T(8,128)S(1)}, u32[]{:S(2)}, u32[]{:S(2)}) collective-permute-start(f32[8,128]{1,0:T(8,128)S(1)} %shard_map.117.refs_0_), channel_id=1, source_target_pairs={{0,4},{1,5},{2,6},{3,7},{4,0},{5,1},{6,2},{7,3},{8,12},{9,13},{10,... | collective-permute-start | bytes 12296 | tf_op jit(solution)/shard_map/ppermute | solution.py:383
  73.4 0.7 collective-permute-start.25
  74.1 1.0 %collective-permute-done.27.refs_3_ = f32[8,128]{1,0:T(8,128)S(1)} collective-permute-done((f32[8,128]{1,0:T(8,128)S(1)}, f32[8,128]{1,0:T(8,128)S(1)}, u32[]{:S(2)}, u32[]{:S(2)}) %collective-permute-start.27) | collective-permute-done | bytes 4128 | tf_op jit(solution)/shard_map/ppermute | solution.py:383
  75.2 0.6 collective-permute-done.26.refs_2_
  75.7 1.3 %collective-permute-done.25.refs_1_ = f32[8,128]{1,0:T(8,128)S(1)} collective-permute-done((f32[8,128]{1,0:T(8,128)S(1)}, f32[8,128]{1,0:T(8,128)S(1)}, u32[]{:S(2)}, u32[]{:S(2)}) %collective-permute-start.25) | collective-permute-done | bytes 4128 | tf_op jit(solution)/shard_map/ppermute | solution.py:383
  77.0 0.8 %shard_map.118 = (f32[4,1,48,128]{3,2,1,0:T(8,128)}, f32[2,3]{1,0:T(2,128)}) custom-call(f32[8,128]{1,0:T(8,128)S(1)} %shard_map.117.refs_0_, f32[8,128]{1,0:T(8,128)S(1)} %collective-permute-done.25.refs_1_, f32[8,128]{1,0:T(8,128)S(1)} %collective-permute-done.26.refs_2_, f32[8,128]{1,0:T(8,128)S(1)} %collective-permute-done.27.refs_3_, ...), custom_call_target="tpu_custom_call" | custom-call | tf_op jit(solution)/shard_map/pallas_call | solution.py:42
  (29 shorter events, 4.8 us)
Async XLA Ops:
  3.3 14.2 %all-to-all-start = ((bf16[8,208,128]{2,1,0:T(8,128)(2,1)}), bf16[8,208,128]{2,1,0:T(8,128)(2,1)}, u32[]{:S(2)}, u32[]{:S(2)}) async-start(bf16[8,208,128]{2,1,0:T(8,128)(2,1)} %get-tuple-element.39), calls=%async_computation | async-start | bytes 851968 | tf_op jit(solution)/shard_map/all_to_all | solution.py:387
  8.5 7.8 %collective-permute-start.2 = (f32[48,128]{1,0:T(8,128)}, f32[48,128]{1,0:T(8,128)S(1)}, u32[]{:S(2)}, u32[]{:S(2)}) collective-permute-start(f32[48,128]{1,0:T(8,128)} %bitcast.3), channel_id=1, source_target_pairs={{0,24},{8,16},{16,8},{24,0},{1,25},{9,17},{17,9},{25,1},{2,26},{10... | collective-permute-start | bytes 73736 | tf_op jit(solution)/shard_map/ppermute | solution.py:374
  12.6 4.9 %collective-permute-start.1 = (f32[48,128]{1,0:T(8,128)}, f32[48,128]{1,0:T(8,128)S(1)}, u32[]{:S(2)}, u32[]{:S(2)}) collective-permute-start(f32[48,128]{1,0:T(8,128)} %bitcast.4), channel_id=1, source_target_pairs={{0,16},{8,24},{16,0},{24,8},{1,17},{9,25},{17,1},{25,9},{2,18},{10... | collective-permute-start | bytes 73736 | tf_op jit(solution)/shard_map/ppermute | solution.py:374
  12.6 4.9 %collective-permute-start = (f32[48,128]{1,0:T(8,128)}, f32[48,128]{1,0:T(8,128)S(1)}, u32[]{:S(2)}, u32[]{:S(2)}) collective-permute-start(f32[48,128]{1,0:T(8,128)} %bitcast.5), channel_id=1, source_target_pairs={{0,8},{8,0},{16,24},{24,16},{1,9},{9,1},{17,25},{25,17},{2,10},{10... | collective-permute-start | bytes 73736 | tf_op jit(solution)/shard_map/ppermute | solution.py:374
  13.2 0.8 copy-start.1
  14.0 13.7 %copy-start = (f32[8,128]{1,0:T(8,128)S(1)}, f32[8,128]{1,0:T(8,128)}, u32[]{:S(2)}) copy-start(f32[8,128]{1,0:T(8,128)} %get-tuple-element.35.weight_ref) | copy-start | bytes 12292
  19.5 1.2 %collective-permute-start.3 = (f32[16,128]{1,0:T(8,128)S(1)}, f32[16,128]{1,0:T(8,128)S(1)}, u32[]{:S(2)}, u32[]{:S(2)}) collective-permute-start(f32[16,128]{1,0:T(8,128)S(1)} %get-tuple-element.45.one_ref), channel_id=1, source_target_pairs={{0,1},{1,0},{2,3},{3,2},{4,5},{5,4},{6,7},{7,6},{8,9},{9,8},{10,11... | collective-permute-start | bytes 24584 | tf_op jit(solution)/shard_map/ppermute | solution.py:381
  20.7 4.5 %collective-permute-start.6 = (f32[16,128]{1,0:T(8,128)S(1)}, f32[16,128]{1,0:T(8,128)S(1)}, u32[]{:S(2)}, u32[]{:S(2)}) collective-permute-start(f32[16,128]{1,0:T(8,128)S(1)} %shard_map.107.refs_1_), channel_id=1, source_target_pairs={{0,6},{1,7},{2,4},{3,5},{4,2},{5,3},{6,0},{7,1},{8,14},{9,15},{10,... | collective-permute-start | bytes 24584 | tf_op jit(solution)/shard_map/ppermute | solution.py:383
  23.5 3.7 %collective-permute-start.5 = (f32[16,128]{1,0:T(8,128)S(1)}, f32[16,128]{1,0:T(8,128)S(1)}, u32[]{:S(2)}, u32[]{:S(2)}) collective-permute-start(f32[16,128]{1,0:T(8,128)S(1)} %shard_map.107.refs_1_), channel_id=1, source_target_pairs={{0,4},{1,5},{2,6},{3,7},{4,0},{5,1},{6,2},{7,3},{8,12},{9,13},{10,... | collective-permute-start | bytes 24584 | tf_op jit(solution)/shard_map/ppermute | solution.py:383
  24.0 3.7 %collective-permute-start.4 = (f32[16,128]{1,0:T(8,128)S(1)}, f32[16,128]{1,0:T(8,128)S(1)}, u32[]{:S(2)}, u32[]{:S(2)}) collective-permute-start(f32[16,128]{1,0:T(8,128)S(1)} %shard_map.107.refs_1_), channel_id=1, source_target_pairs={{0,2},{1,3},{2,0},{3,1},{4,6},{5,7},{6,4},{7,5},{8,10},{9,11},{10,... | collective-permute-start | bytes 24584 | tf_op jit(solution)/shard_map/ppermute | solution.py:383
  28.1 5.6 %collective-permute-start.9 = (f32[32,128]{1,0:T(8,128)S(1)}, f32[32,128]{1,0:T(8,128)S(1)}, u32[]{:S(2)}, u32[]{:S(2)}) collective-permute-start(f32[32,128]{1,0:T(8,128)S(1)} %get-tuple-element.46.refs_0_), channel_id=1, source_target_pairs={{0,24},{8,16},{16,8},{24,0},{1,25},{9,17},{17,9},{25,1},{2,26},{10... | collective-permute-start | bytes 49160 | tf_op jit(solution)/shard_map/ppermute | solution.py:374
  30.7 4.6 %collective-permute-start.8 = (f32[32,128]{1,0:T(8,128)S(1)}, f32[32,128]{1,0:T(8,128)S(1)}, u32[]{:S(2)}, u32[]{:S(2)}) collective-permute-start(f32[32,128]{1,0:T(8,128)S(1)} %get-tuple-element.46.refs_0_), channel_id=1, source_target_pairs={{0,16},{8,24},{16,0},{24,8},{1,17},{9,25},{17,1},{25,9},{2,18},{10... | collective-permute-start | bytes 49160 | tf_op jit(solution)/shard_map/ppermute | solution.py:374
  30.7 4.6 %collective-permute-start.7 = (f32[32,128]{1,0:T(8,128)S(1)}, f32[32,128]{1,0:T(8,128)S(1)}, u32[]{:S(2)}, u32[]{:S(2)}) collective-permute-start(f32[32,128]{1,0:T(8,128)S(1)} %get-tuple-element.46.refs_0_), channel_id=1, source_target_pairs={{0,8},{8,0},{16,24},{24,16},{1,9},{9,1},{17,25},{25,17},{2,10},{10... | collective-permute-start | bytes 49160 | tf_op jit(solution)/shard_map/ppermute | solution.py:374
  37.1 1.2 %collective-permute-start.10 = (f32[16,128]{1,0:T(8,128)S(1)}, f32[16,128]{1,0:T(8,128)S(1)}, u32[]{:S(2)}, u32[]{:S(2)}) collective-permute-start(f32[16,128]{1,0:T(8,128)S(1)} %get-tuple-element.50.one_ref), channel_id=1, source_target_pairs={{0,1},{1,0},{2,3},{3,2},{4,5},{5,4},{6,7},{7,6},{8,9},{9,8},{10,11... | collective-permute-start | bytes 24584 | tf_op jit(solution)/shard_map/ppermute | solution.py:381
  38.4 4.5 %collective-permute-start.13 = (f32[16,128]{1,0:T(8,128)S(1)}, f32[16,128]{1,0:T(8,128)S(1)}, u32[]{:S(2)}, u32[]{:S(2)}) collective-permute-start(f32[16,128]{1,0:T(8,128)S(1)} %shard_map.111.refs_0_), channel_id=1, source_target_pairs={{0,6},{1,7},{2,4},{3,5},{4,2},{5,3},{6,0},{7,1},{8,14},{9,15},{10,... | collective-permute-start | bytes 24584 | tf_op jit(solution)/shard_map/ppermute | solution.py:383
  39.9 3.7 %collective-permute-start.12 = (f32[16,128]{1,0:T(8,128)S(1)}, f32[16,128]{1,0:T(8,128)S(1)}, u32[]{:S(2)}, u32[]{:S(2)}) collective-permute-start(f32[16,128]{1,0:T(8,128)S(1)} %shard_map.111.refs_0_), channel_id=1, source_target_pairs={{0,4},{1,5},{2,6},{3,7},{4,0},{5,1},{6,2},{7,3},{8,12},{9,13},{10,... | collective-permute-start | bytes 24584 | tf_op jit(solution)/shard_map/ppermute | solution.py:383
  41.1 3.7 %collective-permute-start.11 = (f32[16,128]{1,0:T(8,128)S(1)}, f32[16,128]{1,0:T(8,128)S(1)}, u32[]{:S(2)}, u32[]{:S(2)}) collective-permute-start(f32[16,128]{1,0:T(8,128)S(1)} %shard_map.111.refs_0_), channel_id=1, source_target_pairs={{0,2},{1,3},{2,0},{3,1},{4,6},{5,7},{6,4},{7,5},{8,10},{9,11},{10,... | collective-permute-start | bytes 24584 | tf_op jit(solution)/shard_map/ppermute | solution.py:383
  45.2 5.5 %collective-permute-start.16 = (f32[24,128]{1,0:T(8,128)S(1)}, f32[24,128]{1,0:T(8,128)S(1)}, u32[]{:S(2)}, u32[]{:S(2)}) collective-permute-start(f32[24,128]{1,0:T(8,128)S(1)} %get-tuple-element.54.refs_1_), channel_id=1, source_target_pairs={{0,24},{8,16},{16,8},{24,0},{1,25},{9,17},{17,9},{25,1},{2,26},{10... | collective-permute-start | bytes 36872 | tf_op jit(solution)/shard_map/ppermute | solution.py:374
  46.7 4.6 %collective-permute-start.15 = (f32[24,128]{1,0:T(8,128)S(1)}, f32[24,128]{1,0:T(8,128)S(1)}, u32[]{:S(2)}, u32[]{:S(2)}) collective-permute-start(f32[24,128]{1,0:T(8,128)S(1)} %get-tuple-element.54.refs_1_), channel_id=1, source_target_pairs={{0,16},{8,24},{16,0},{24,8},{1,17},{9,25},{17,1},{25,9},{2,18},{10... | collective-permute-start | bytes 36872 | tf_op jit(solution)/shard_map/ppermute | solution.py:374
  47.4 4.1 %collective-permute-start.14 = (f32[24,128]{1,0:T(8,128)S(1)}, f32[24,128]{1,0:T(8,128)S(1)}, u32[]{:S(2)}, u32[]{:S(2)}) collective-permute-start(f32[24,128]{1,0:T(8,128)S(1)} %get-tuple-element.54.refs_1_), channel_id=1, source_target_pairs={{0,8},{8,0},{16,24},{24,16},{1,9},{9,1},{17,25},{25,17},{2,10},{10... | collective-permute-start | bytes 36872 | tf_op jit(solution)/shard_map/ppermute | solution.py:374
  53.2 1.2 %collective-permute-start.17 = (f32[16,128]{1,0:T(8,128)S(1)}, f32[16,128]{1,0:T(8,128)S(1)}, u32[]{:S(2)}, u32[]{:S(2)}) collective-permute-start(f32[16,128]{1,0:T(8,128)S(1)} %get-tuple-element.55.one_ref), channel_id=1, source_target_pairs={{0,1},{1,0},{2,3},{3,2},{4,5},{5,4},{6,7},{7,6},{8,9},{9,8},{10,11... | collective-permute-start | bytes 24584 | tf_op jit(solution)/shard_map/ppermute | solution.py:381
  54.5 4.5 %collective-permute-start.20 = (f32[16,128]{1,0:T(8,128)S(1)}, f32[16,128]{1,0:T(8,128)S(1)}, u32[]{:S(2)}, u32[]{:S(2)}) collective-permute-start(f32[16,128]{1,0:T(8,128)S(1)} %shard_map.114.refs_0_), channel_id=1, source_target_pairs={{0,6},{1,7},{2,4},{3,5},{4,2},{5,3},{6,0},{7,1},{8,14},{9,15},{10,... | collective-permute-start | bytes 24584 | tf_op jit(solution)/shard_map/ppermute | solution.py:383
  56.1 3.7 %collective-permute-start.19 = (f32[16,128]{1,0:T(8,128)S(1)}, f32[16,128]{1,0:T(8,128)S(1)}, u32[]{:S(2)}, u32[]{:S(2)}) collective-permute-start(f32[16,128]{1,0:T(8,128)S(1)} %shard_map.114.refs_0_), channel_id=1, source_target_pairs={{0,4},{1,5},{2,6},{3,7},{4,0},{5,1},{6,2},{7,3},{8,12},{9,13},{10,... | collective-permute-start | bytes 24584 | tf_op jit(solution)/shard_map/ppermute | solution.py:383
  56.6 3.7 %collective-permute-start.18 = (f32[16,128]{1,0:T(8,128)S(1)}, f32[16,128]{1,0:T(8,128)S(1)}, u32[]{:S(2)}, u32[]{:S(2)}) collective-permute-start(f32[16,128]{1,0:T(8,128)S(1)} %shard_map.114.refs_0_), channel_id=1, source_target_pairs={{0,2},{1,3},{2,0},{3,1},{4,6},{5,7},{6,4},{7,5},{8,10},{9,11},{10,... | collective-permute-start | bytes 24584 | tf_op jit(solution)/shard_map/ppermute | solution.py:383
  60.8 5.5 %collective-permute-start.23 = (f32[24,128]{1,0:T(8,128)S(1)}, f32[24,128]{1,0:T(8,128)S(1)}, u32[]{:S(2)}, u32[]{:S(2)}) collective-permute-start(f32[24,128]{1,0:T(8,128)S(1)} %get-tuple-element.59.refs_1_), channel_id=1, source_target_pairs={{0,24},{8,16},{16,8},{24,0},{1,25},{9,17},{17,9},{25,1},{2,26},{10... | collective-permute-start | bytes 36872 | tf_op jit(solution)/shard_map/ppermute | solution.py:374
  63.2 4.6 %collective-permute-start.22 = (f32[24,128]{1,0:T(8,128)S(1)}, f32[24,128]{1,0:T(8,128)S(1)}, u32[]{:S(2)}, u32[]{:S(2)}) collective-permute-start(f32[24,128]{1,0:T(8,128)S(1)} %get-tuple-element.59.refs_1_), channel_id=1, source_target_pairs={{0,16},{8,24},{16,0},{24,8},{1,17},{9,25},{17,1},{25,9},{2,18},{10... | collective-permute-start | bytes 36872 | tf_op jit(solution)/shard_map/ppermute | solution.py:374
  64.1 3.8 %collective-permute-start.21 = (f32[24,128]{1,0:T(8,128)S(1)}, f32[24,128]{1,0:T(8,128)S(1)}, u32[]{:S(2)}, u32[]{:S(2)}) collective-permute-start(f32[24,128]{1,0:T(8,128)S(1)} %get-tuple-element.59.refs_1_), channel_id=1, source_target_pairs={{0,8},{8,0},{16,24},{24,16},{1,9},{9,1},{17,25},{25,17},{2,10},{10... | collective-permute-start | bytes 36872 | tf_op jit(solution)/shard_map/ppermute | solution.py:374
  69.4 1.2 %collective-permute-start.24 = (f32[8,128]{1,0:T(8,128)S(1)}, f32[8,128]{1,0:T(8,128)S(1)}, u32[]{:S(2)}, u32[]{:S(2)}) collective-permute-start(f32[8,128]{1,0:T(8,128)S(1)} %get-tuple-element.60.one_ref), channel_id=1, source_target_pairs={{0,1},{1,0},{2,3},{3,2},{4,5},{5,4},{6,7},{7,6},{8,9},{9,8},{10,11... | collective-permute-start | bytes 12296 | tf_op jit(solution)/shard_map/ppermute | solution.py:381
  70.7 4.5 %collective-permute-start.27 = (f32[8,128]{1,0:T(8,128)S(1)}, f32[8,128]{1,0:T(8,128)S(1)}, u32[]{:S(2)}, u32[]{:S(2)}) collective-permute-start(f32[8,128]{1,0:T(8,128)S(1)} %shard_map.117.refs_0_), channel_id=1, source_target_pairs={{0,6},{1,7},{2,4},{3,5},{4,2},{5,3},{6,0},{7,1},{8,14},{9,15},{10,... | collective-permute-start | bytes 12296 | tf_op jit(solution)/shard_map/ppermute | solution.py:383
  72.1 3.6 %collective-permute-start.26 = (f32[8,128]{1,0:T(8,128)S(1)}, f32[8,128]{1,0:T(8,128)S(1)}, u32[]{:S(2)}, u32[]{:S(2)}) collective-permute-start(f32[8,128]{1,0:T(8,128)S(1)} %shard_map.117.refs_0_), channel_id=1, source_target_pairs={{0,4},{1,5},{2,6},{3,7},{4,0},{5,1},{6,2},{7,3},{8,12},{9,13},{10,... | collective-permute-start | bytes 12296 | tf_op jit(solution)/shard_map/ppermute | solution.py:383
  73.4 3.6 %collective-permute-start.25 = (f32[8,128]{1,0:T(8,128)S(1)}, f32[8,128]{1,0:T(8,128)S(1)}, u32[]{:S(2)}, u32[]{:S(2)}) collective-permute-start(f32[8,128]{1,0:T(8,128)S(1)} %shard_map.117.refs_0_), channel_id=1, source_target_pairs={{0,2},{1,3},{2,0},{3,1},{4,6},{5,7},{6,4},{7,5},{8,10},{9,11},{10,... | collective-permute-start | bytes 12296 | tf_op jit(solution)/shard_map/ppermute | solution.py:383

commit v17 on v16

--- a/solution.py
+++ b/solution.py
@@ -371,7 +371,8 @@
     size = lax.axis_size(axis)
     if not permuted(size):
         return [swap(jnp.broadcast_to(array[None], (size,) + array.shape), axis).reshape(-1, array.shape[1])]
-    return [array] + [lax.ppermute(array, axis, [(d, d ^ s) for d in range(size)]) for s in range(1, size)]
+    came = [lax.ppermute(array, axis, [(d, d ^ s) for d in range(size)]) for s in range(size - 1, 0, -1)]
+    return [array] + came[::-1]
 
 
 def addends(array, axis):
@@ -380,7 +381,7 @@
         return [swap(jnp.broadcast_to(array[None], (size,) + array.shape), axis).reshape(-1, array.shape[1])]
     other = lax.ppermute(array, axis, [(d, d ^ 1) for d in range(size)])
     both = call(add_kernel, jax.ShapeDtypeStruct(array.shape, F32), [VMEM] * 2, array, other)
-    return [both] + [lax.ppermute(both, axis, [(d, d ^ s) for d in range(size)]) for s in (2, 4, 6)]
+    return [both] + [lax.ppermute(both, axis, [(d, d ^ s) for d in range(size)]) for s in (6, 4, 2)][::-1]
 
 
 def swap(array, axis):

time: 78.2 us -> 78.2 us (level)
  no operation moved by 1% of the time
where the time goes in v17:
time: 78.2 us; the launch traced here: 77.8 us
  starting transfers between devices  37.4 us (48%)
  waiting for transfers between devices  24.8 us (32%)
  Pallas kernels  14.1 us (18%)
    ppermute x12, starting transfers between devices, share(): lax.ppermute(array, axis, [(d, d ^ s) for d in range(size)])  17.9 us
    pallas_call x15, Pallas kernels, call(): pl.pallas_call(kernel, out_shape=outs, in_specs=specs, out_specs=jax.tree...  14.1 us
    ppermute x12, starting transfers between devices, addends(): lax.ppermute(both, axis, [(d, d ^ s) for d in range(size)])  14 us
    ppermute x12, waiting for transfers between devices, addends(): lax.ppermute(both, axis, [(d, d ^ s) for d in range(size)])  11.6 us
    ppermute x12, waiting for transfers between devices, share(): lax.ppermute(array, axis, [(d, d ^ s) for d in range(size)])  8.59 us
    all_to_all x1, starting transfers between devices, swap(): return lax.all_to_all(array, axis, split_axis=0, concat_axis=0, tiled=True)  5.18 us
    ppermute x4, waiting for transfers between devices, addends(): other = lax.ppermute(array, axis, [(d, d ^ 1) for d in range(size)])  4.63 us
  transfers between devices with their start and end apart: 29, of which 25 were waited for; matrix products, arithmetic and copies ran while one was open for 0% of the time, Pallas kernels for 3%

profile of v17, /device:TPU:0, one launch (start us, length us, event | category | flops | bytes accessed | tf_op | source)
XLA Modules:
  0.0 77.8 jit_solution(7893003884477928858)
XLA Ops:
  0.6 2.7 %shard_map.104 = (bf16[8,208,128]{2,1,0:T(8,128)(2,1)}, f32[8,128]{1,0:T(8,128)}) custom-call(s32[1]{0:T(128)} %bitcast.1.place_any, bf16[384,384]{1,0:T(8,128)(2,1)} %constant.14.clone.high_any, bf16[384,384]{1,0:T(8,128)(2,1)} %constant.15.clone.low_any, bf16[2,128,768]{2,1,0:T(8,128)(2,1)} %foot_any.1, s32[2]{0:T(128)} %off_any.1, s32[2]{0:T(128)} %sub_any.1, ...), custom_call_target="tpu_custom_call" | custom-call | tf_op jit(solution)/shard_map/pallas_call | solution.py:42
  3.3 5.2 %all-to-all-start = ((bf16[8,208,128]{2,1,0:T(8,128)(2,1)}), bf16[8,208,128]{2,1,0:T(8,128)(2,1)}, u32[]{:S(2)}, u32[]{:S(2)}) async-start(bf16[8,208,128]{2,1,0:T(8,128)(2,1)} %get-tuple-element.39), calls=%async_computation | async-start | bytes 851968 | tf_op jit(solution)/shard_map/all_to_all | solution.py:388
  8.5 4.1 %collective-permute-start.2 = (f32[48,128]{1,0:T(8,128)}, f32[48,128]{1,0:T(8,128)S(1)}, u32[]{:S(2)}, u32[]{:S(2)}) collective-permute-start(f32[48,128]{1,0:T(8,128)} %bitcast.3), channel_id=1, source_target_pairs={{0,24},{8,16},{16,8},{24,0},{1,25},{9,17},{17,9},{25,1},{2,26},{10... | collective-permute-start | bytes 73736 | tf_op jit(solution)/shard_map/ppermute | solution.py:374
  12.6 0.6 collective-permute-start
  13.2 0.8 copy-done.1
  14.0 2.3 %shard_map.105 = (f32[128,48,128]{2,1,0:T(8,128)S(1)}, f32[48,128]{1,0:T(8,128)S(1)}, bf16[48,2048]{1,0:T(8,128)(2,1)S(1)}) custom-call(f32[48,128,128]{2,1,0:T(8,128)} %lat_any, f32[48,128]{1,0:T(8,128)S(1)} %bitcast.6), custom_call_target="tpu_custom_call" | custom-call | bytes 6340608 | tf_op jit(solution)/shard_map/pallas_call | solution.py:42
  16.3 1.2 %collective-permute-done.1.refs_2_ = f32[48,128]{1,0:T(8,128)S(1)} collective-permute-done((f32[48,128]{1,0:T(8,128)}, f32[48,128]{1,0:T(8,128)S(1)}, u32[]{:S(2)}, u32[]{:S(2)}) %collective-permute-start.1) | collective-permute-done | bytes 24608 | tf_op jit(solution)/shard_map/ppermute | solution.py:374
  17.5 2.0 %shard_map.106 = (f32[16,128]{1,0:T(8,128)S(1)}, f32[4,48,128]{2,1,0:T(8,128)S(1)}, bf16[8,192,128]{2,1,0:T(8,128)(2,1)S(1)}, s32[8,128]{1,0:T(8,128)S(1)}, bf16...) custom-call(f32[128,48,128]{2,1,0:T(8,128)S(1)} %get-tuple-element.38.lat_ref, bf16[8,208,128]{2,1,0:T(8,128)(2,1)} %all-to-all-done.came_ref, ...), custom_call_target="tpu_custom_call" | custom-call | tf_op jit(solution)/shard_map/pallas_call | solution.py:42
  19.6 1.2 %collective-permute-done.3.other_ref = f32[16,128]{1,0:T(8,128)S(1)} collective-permute-done((f32[16,128]{1,0:T(8,128)S(1)}, f32[16,128]{1,0:T(8,128)S(1)}, u32[]{:S(2)}, u32[]{:S(2)}) %collective-permute-start.3) | collective-permute-done | bytes 8224 | tf_op jit(solution)/shard_map/ppermute | solution.py:382
  20.7 2.8 %collective-permute-start.6 = (f32[16,128]{1,0:T(8,128)S(1)}, f32[16,128]{1,0:T(8,128)S(1)}, u32[]{:S(2)}, u32[]{:S(2)}) collective-permute-start(f32[16,128]{1,0:T(8,128)S(1)} %shard_map.107.refs_1_), channel_id=1, source_target_pairs={{0,6},{1,7},{2,4},{3,5},{4,2},{5,3},{6,0},{7,1},{8,14},{9,15},{10,... | collective-permute-start | bytes 24584 | tf_op jit(solution)/shard_map/ppermute | solution.py:384
  24.2 1.1 %collective-permute-done.6.refs_4_ = f32[16,128]{1,0:T(8,128)S(1)} collective-permute-done((f32[16,128]{1,0:T(8,128)S(1)}, f32[16,128]{1,0:T(8,128)S(1)}, u32[]{:S(2)}, u32[]{:S(2)}) %collective-permute-start.6) | collective-permute-done | bytes 8224 | tf_op jit(solution)/shard_map/ppermute | solution.py:384
  25.3 1.9 %collective-permute-done.5.refs_3_ = f32[16,128]{1,0:T(8,128)S(1)} collective-permute-done((f32[16,128]{1,0:T(8,128)S(1)}, f32[16,128]{1,0:T(8,128)S(1)}, u32[]{:S(2)}, u32[]{:S(2)}) %collective-permute-start.5) | collective-permute-done | bytes 8224 | tf_op jit(solution)/shard_map/ppermute | solution.py:384
  28.1 2.6 %collective-permute-start.9 = (f32[32,128]{1,0:T(8,128)S(1)}, f32[32,128]{1,0:T(8,128)S(1)}, u32[]{:S(2)}, u32[]{:S(2)}) collective-permute-start(f32[32,128]{1,0:T(8,128)S(1)} %get-tuple-element.46.refs_0_), channel_id=1, source_target_pairs={{0,24},{8,16},{16,8},{24,0},{1,25},{9,17},{17,9},{25,1},{2,26},{10... | collective-permute-start | bytes 49160 | tf_op jit(solution)/shard_map/ppermute | solution.py:374
  30.7 1.8 %collective-permute-start.7 = (f32[32,128]{1,0:T(8,128)S(1)}, f32[32,128]{1,0:T(8,128)S(1)}, u32[]{:S(2)}, u32[]{:S(2)}) collective-permute-start(f32[32,128]{1,0:T(8,128)S(1)} %get-tuple-element.46.refs_0_), channel_id=1, source_target_pairs={{0,8},{8,0},{16,24},{24,16},{1,9},{9,1},{17,25},{25,17},{2,10},{10... | collective-permute-start | bytes 49160 | tf_op jit(solution)/shard_map/ppermute | solution.py:374
  32.5 1.1 %collective-permute-done.9.refs_3_ = f32[32,128]{1,0:T(8,128)S(1)} collective-permute-done((f32[32,128]{1,0:T(8,128)S(1)}, f32[32,128]{1,0:T(8,128)S(1)}, u32[]{:S(2)}, u32[]{:S(2)}) %collective-permute-start.9) | collective-permute-done | bytes 16416 | tf_op jit(solution)/shard_map/ppermute | solution.py:374
  33.7 1.7 %collective-permute-done.8.refs_2_ = f32[32,128]{1,0:T(8,128)S(1)} collective-permute-done((f32[32,128]{1,0:T(8,128)S(1)}, f32[32,128]{1,0:T(8,128)S(1)}, u32[]{:S(2)}, u32[]{:S(2)}) %collective-permute-start.8) | collective-permute-done | bytes 16416 | tf_op jit(solution)/shard_map/ppermute | solution.py:374
  35.4 1.7 %shard_map.110 = (f32[16,128]{1,0:T(8,128)S(1)}, f32[1,48,128]{2,1,0:T(8,128)S(1)}, f32[4,48,128]{2,1,0:T(8,128)S(1)}, f32[4,48,128]{2,1,0:T(8,128)S(1)}, f32[8,128]{1,0:T(8,128)S(1)}) custom-call(s32[8,128]{1,0:T(8,128)S(1)} %get-tuple-element.41.ids_ref, s32[8,128]{1,0:T(8,128)S(1)} %shard_map.109.all_ref, f32[128,48,128]{2,1,0:T(8,128)S(1)} %get-tuple-element.38.lat_ref, ...), custom_call_target="tpu_custom_call" | custom-call | tf_op jit(solution)/shard_map/pallas_call | solution.py:42
  37.2 1.2 %collective-permute-done.10.other_ref = f32[16,128]{1,0:T(8,128)S(1)} collective-permute-done((f32[16,128]{1,0:T(8,128)S(1)}, f32[16,128]{1,0:T(8,128)S(1)}, u32[]{:S(2)}, u32[]{:S(2)}) %collective-permute-start.10) | collective-permute-done | bytes 8224 | tf_op jit(solution)/shard_map/ppermute | solution.py:382
  38.4 1.5 %collective-permute-start.13 = (f32[16,128]{1,0:T(8,128)S(1)}, f32[16,128]{1,0:T(8,128)S(1)}, u32[]{:S(2)}, u32[]{:S(2)}) collective-permute-start(f32[16,128]{1,0:T(8,128)S(1)} %shard_map.111.refs_0_), channel_id=1, source_target_pairs={{0,6},{1,7},{2,4},{3,5},{4,2},{5,3},{6,0},{7,1},{8,14},{9,15},{10,... | collective-permute-start | bytes 24584 | tf_op jit(solution)/shard_map/ppermute | solution.py:384
  39.9 1.3 %collective-permute-start.12 = (f32[16,128]{1,0:T(8,128)S(1)}, f32[16,128]{1,0:T(8,128)S(1)}, u32[]{:S(2)}, u32[]{:S(2)}) collective-permute-start(f32[16,128]{1,0:T(8,128)S(1)} %shard_map.111.refs_0_), channel_id=1, source_target_pairs={{0,4},{1,5},{2,6},{3,7},{4,0},{5,1},{6,2},{7,3},{8,12},{9,13},{10,... | collective-permute-start | bytes 24584 | tf_op jit(solution)/shard_map/ppermute | solution.py:384
  41.1 0.7 collective-permute-start.11
  41.9 1.1 %collective-permute-done.13.refs_3_ = f32[16,128]{1,0:T(8,128)S(1)} collective-permute-done((f32[16,128]{1,0:T(8,128)S(1)}, f32[16,128]{1,0:T(8,128)S(1)}, u32[]{:S(2)}, u32[]{:S(2)}) %collective-permute-start.13) | collective-permute-done | bytes 8224 | tf_op jit(solution)/shard_map/ppermute | solution.py:384
  42.9 0.6 collective-permute-done.12.refs_2_
  43.5 1.3 %collective-permute-done.11.refs_1_ = f32[16,128]{1,0:T(8,128)S(1)} collective-permute-done((f32[16,128]{1,0:T(8,128)S(1)}, f32[16,128]{1,0:T(8,128)S(1)}, u32[]{:S(2)}, u32[]{:S(2)}) %collective-permute-start.11) | collective-permute-done | bytes 8224 | tf_op jit(solution)/shard_map/ppermute | solution.py:384
  45.2 1.5 %collective-permute-start.16 = (f32[24,128]{1,0:T(8,128)S(1)}, f32[24,128]{1,0:T(8,128)S(1)}, u32[]{:S(2)}, u32[]{:S(2)}) collective-permute-start(f32[24,128]{1,0:T(8,128)S(1)} %get-tuple-element.54.refs_1_), channel_id=1, source_target_pairs={{0,24},{8,16},{16,8},{24,0},{1,25},{9,17},{17,9},{25,1},{2,26},{10... | collective-permute-start | bytes 36872 | tf_op jit(solution)/shard_map/ppermute | solution.py:374
  46.7 0.6 collective-permute-start.15
  47.4 2.3 %collective-permute-start.14 = (f32[24,128]{1,0:T(8,128)S(1)}, f32[24,128]{1,0:T(8,128)S(1)}, u32[]{:S(2)}, u32[]{:S(2)}) collective-permute-start(f32[24,128]{1,0:T(8,128)S(1)} %get-tuple-element.54.refs_1_), channel_id=1, source_target_pairs={{0,8},{8,0},{16,24},{24,16},{1,9},{9,1},{17,25},{25,17},{2,10},{10... | collective-permute-start | bytes 36872 | tf_op jit(solution)/shard_map/ppermute | solution.py:374
  49.7 1.1 %collective-permute-done.16.refs_4_ = f32[24,128]{1,0:T(8,128)S(1)} collective-permute-done((f32[24,128]{1,0:T(8,128)S(1)}, f32[24,128]{1,0:T(8,128)S(1)}, u32[]{:S(2)}, u32[]{:S(2)}) %collective-permute-start.16) | collective-permute-done | bytes 12320 | tf_op jit(solution)/shard_map/ppermute | solution.py:374
  51.4 1.8 %shard_map.113 = (f32[16,128]{1,0:T(8,128)S(1)}, f32[1,48,128]{2,1,0:T(8,128)S(1)}, f32[4,48,128]{2,1,0:T(8,128)S(1)}, f32[4,48,128]{2,1,0:T(8,128)S(1)}, f32[8,128]{1,0:T(8,128)S(1)}) custom-call(s32[8,128]{1,0:T(8,128)S(1)} %get-tuple-element.41.ids_ref, s32[8,128]{1,0:T(8,128)S(1)} %shard_map.109.all_ref, f32[128,48,128]{2,1,0:T(8,128)S(1)} %get-tuple-element.38.lat_ref, ...), custom_call_target="tpu_custom_call" | custom-call | tf_op jit(solution)/shard_map/pallas_call | solution.py:42
  53.3 1.2 %collective-permute-done.17.other_ref = f32[16,128]{1,0:T(8,128)S(1)} collective-permute-done((f32[16,128]{1,0:T(8,128)S(1)}, f32[16,128]{1,0:T(8,128)S(1)}, u32[]{:S(2)}, u32[]{:S(2)}) %collective-permute-start.17) | collective-permute-done | bytes 8224 | tf_op jit(solution)/shard_map/ppermute | solution.py:382
  54.4 1.7 %collective-permute-start.20 = (f32[16,128]{1,0:T(8,128)S(1)}, f32[16,128]{1,0:T(8,128)S(1)}, u32[]{:S(2)}, u32[]{:S(2)}) collective-permute-start(f32[16,128]{1,0:T(8,128)S(1)} %shard_map.114.refs_0_), channel_id=1, source_target_pairs={{0,6},{1,7},{2,4},{3,5},{4,2},{5,3},{6,0},{7,1},{8,14},{9,15},{10,... | collective-permute-start | bytes 24584 | tf_op jit(solution)/shard_map/ppermute | solution.py:384
  56.6 1.3 %collective-permute-start.18 = (f32[16,128]{1,0:T(8,128)S(1)}, f32[16,128]{1,0:T(8,128)S(1)}, u32[]{:S(2)}, u32[]{:S(2)}) collective-permute-start(f32[16,128]{1,0:T(8,128)S(1)} %shard_map.114.refs_0_), channel_id=1, source_target_pairs={{0,2},{1,3},{2,0},{3,1},{4,6},{5,7},{6,4},{7,5},{8,10},{9,11},{10,... | collective-permute-start | bytes 24584 | tf_op jit(solution)/shard_map/ppermute | solution.py:384
  57.9 1.1 %collective-permute-done.20.refs_3_ = f32[16,128]{1,0:T(8,128)S(1)} collective-permute-done((f32[16,128]{1,0:T(8,128)S(1)}, f32[16,128]{1,0:T(8,128)S(1)}, u32[]{:S(2)}, u32[]{:S(2)}) %collective-permute-start.20) | collective-permute-done | bytes 8224 | tf_op jit(solution)/shard_map/ppermute | solution.py:384
  59.0 0.8 collective-permute-done.19.refs_2_
  60.8 2.5 %collective-permute-start.23 = (f32[24,128]{1,0:T(8,128)S(1)}, f32[24,128]{1,0:T(8,128)S(1)}, u32[]{:S(2)}, u32[]{:S(2)}) collective-permute-start(f32[24,128]{1,0:T(8,128)S(1)} %get-tuple-element.59.refs_1_), channel_id=1, source_target_pairs={{0,24},{8,16},{16,8},{24,0},{1,25},{9,17},{17,9},{25,1},{2,26},{10... | collective-permute-start | bytes 36872 | tf_op jit(solution)/shard_map/ppermute | solution.py:374
  63.2 0.9 %collective-permute-start.22 = (f32[24,128]{1,0:T(8,128)S(1)}, f32[24,128]{1,0:T(8,128)S(1)}, u32[]{:S(2)}, u32[]{:S(2)}) collective-permute-start(f32[24,128]{1,0:T(8,128)S(1)} %get-tuple-element.59.refs_1_), channel_id=1, source_target_pairs={{0,16},{8,24},{16,0},{24,8},{1,17},{9,25},{17,1},{25,9},{2,18},{10... | collective-permute-start | bytes 36872 | tf_op jit(solution)/shard_map/ppermute | solution.py:374
  64.1 1.0 %collective-permute-start.21 = (f32[24,128]{1,0:T(8,128)S(1)}, f32[24,128]{1,0:T(8,128)S(1)}, u32[]{:S(2)}, u32[]{:S(2)}) collective-permute-start(f32[24,128]{1,0:T(8,128)S(1)} %get-tuple-element.59.refs_1_), channel_id=1, source_target_pairs={{0,8},{8,0},{16,24},{24,16},{1,9},{9,1},{17,25},{25,17},{2,10},{10... | collective-permute-start | bytes 36872 | tf_op jit(solution)/shard_map/ppermute | solution.py:374
  65.2 1.1 %collective-permute-done.23.refs_4_ = f32[24,128]{1,0:T(8,128)S(1)} collective-permute-done((f32[24,128]{1,0:T(8,128)S(1)}, f32[24,128]{1,0:T(8,128)S(1)}, u32[]{:S(2)}, u32[]{:S(2)}) %collective-permute-start.23) | collective-permute-done | bytes 12320 | tf_op jit(solution)/shard_map/ppermute | solution.py:374
  66.3 1.6 %collective-permute-done.22.refs_3_ = f32[24,128]{1,0:T(8,128)S(1)} collective-permute-done((f32[24,128]{1,0:T(8,128)S(1)}, f32[24,128]{1,0:T(8,128)S(1)}, u32[]{:S(2)}, u32[]{:S(2)}) %collective-permute-start.22) | collective-permute-done | bytes 12320 | tf_op jit(solution)/shard_map/ppermute | solution.py:374
  68.0 1.5 %shard_map.116 = (f32[8,128]{1,0:T(8,128)S(1)}, f32[1,48,128]{2,1,0:T(8,128)S(1)}, f32[1,48,128]{2,1,0:T(8,128)S(1)}, f32[8,128]{1,0:T(8,128)S(1)}) custom-call(s32[8,128]{1,0:T(8,128)S(1)} %get-tuple-element.41.ids_ref, s32[8,128]{1,0:T(8,128)S(1)} %shard_map.109.all_ref, f32[128,48,128]{2,1,0:T(8,128)S(1)} %get-tuple-element.38.lat_ref, ...), custom_call_target="tpu_custom_call" | custom-call | tf_op jit(solution)/shard_map/pallas_call | solution.py:42
  69.5 1.2 %collective-permute-done.24.other_ref = f32[8,128]{1,0:T(8,128)S(1)} collective-permute-done((f32[8,128]{1,0:T(8,128)S(1)}, f32[8,128]{1,0:T(8,128)S(1)}, u32[]{:S(2)}, u32[]{:S(2)}) %collective-permute-start.24) | collective-permute-done | bytes 4128 | tf_op jit(solution)/shard_map/ppermute | solution.py:382
  70.7 1.5 %collective-permute-start.27 = (f32[8,128]{1,0:T(8,128)S(1)}, f32[8,128]{1,0:T(8,128)S(1)}, u32[]{:S(2)}, u32[]{:S(2)}) collective-permute-start(f32[8,128]{1,0:T(8,128)S(1)} %shard_map.117.refs_0_), channel_id=1, source_target_pairs={{0,6},{1,7},{2,4},{3,5},{4,2},{5,3},{6,0},{7,1},{8,14},{9,15},{10,... | collective-permute-start | bytes 12296 | tf_op jit(solution)/shard_map/ppermute | solution.py:384
  72.1 1.3 %collective-permute-start.26 = (f32[8,128]{1,0:T(8,128)S(1)}, f32[8,128]{1,0:T(8,128)S(1)}, u32[]{:S(2)}, u32[]{:S(2)}) collective-permute-start(f32[8,128]{1,0:T(8,128)S(1)} %shard_map.117.refs_0_), channel_id=1, source_target_pairs={{0,4},{1,5},{2,6},{3,7},{4,0},{5,1},{6,2},{7,3},{8,12},{9,13},{10,... | collective-permute-start | bytes 12296 | tf_op jit(solution)/shard_map/ppermute | solution.py:384
  73.4 0.7 collective-permute-start.25
  74.1 1.0 %collective-permute-done.27.refs_3_ = f32[8,128]{1,0:T(8,128)S(1)} collective-permute-done((f32[8,128]{1,0:T(8,128)S(1)}, f32[8,128]{1,0:T(8,128)S(1)}, u32[]{:S(2)}, u32[]{:S(2)}) %collective-permute-start.27) | collective-permute-done | bytes 4128 | tf_op jit(solution)/shard_map/ppermute | solution.py:384
  75.2 0.6 collective-permute-done.26.refs_2_
  75.7 1.3 %collective-permute-done.25.refs_1_ = f32[8,128]{1,0:T(8,128)S(1)} collective-permute-done((f32[8,128]{1,0:T(8,128)S(1)}, f32[8,128]{1,0:T(8,128)S(1)}, u32[]{:S(2)}, u32[]{:S(2)}) %collective-permute-start.25) | collective-permute-done | bytes 4128 | tf_op jit(solution)/shard_map/ppermute | solution.py:384
  77.0 0.8 %shard_map.118 = (f32[4,1,48,128]{3,2,1,0:T(8,128)}, f32[2,3]{1,0:T(2,128)}) custom-call(f32[8,128]{1,0:T(8,128)S(1)} %shard_map.117.refs_0_, f32[8,128]{1,0:T(8,128)S(1)} %collective-permute-done.25.refs_1_, f32[8,128]{1,0:T(8,128)S(1)} %collective-permute-done.26.refs_2_, f32[8,128]{1,0:T(8,128)S(1)} %collective-permute-done.27.refs_3_, ...), custom_call_target="tpu_custom_call" | custom-call | tf_op jit(solution)/shard_map/pallas_call | solution.py:42
  (29 shorter events, 4.8 us)
Async XLA Ops:
  3.3 14.2 %all-to-all-start = ((bf16[8,208,128]{2,1,0:T(8,128)(2,1)}), bf16[8,208,128]{2,1,0:T(8,128)(2,1)}, u32[]{:S(2)}, u32[]{:S(2)}) async-start(bf16[8,208,128]{2,1,0:T(8,128)(2,1)} %get-tuple-element.39), calls=%async_computation | async-start | bytes 851968 | tf_op jit(solution)/shard_map/all_to_all | solution.py:388
  8.5 7.8 %collective-permute-start.2 = (f32[48,128]{1,0:T(8,128)}, f32[48,128]{1,0:T(8,128)S(1)}, u32[]{:S(2)}, u32[]{:S(2)}) collective-permute-start(f32[48,128]{1,0:T(8,128)} %bitcast.3), channel_id=1, source_target_pairs={{0,24},{8,16},{16,8},{24,0},{1,25},{9,17},{17,9},{25,1},{2,26},{10... | collective-permute-start | bytes 73736 | tf_op jit(solution)/shard_map/ppermute | solution.py:374
  12.6 4.9 %collective-permute-start.1 = (f32[48,128]{1,0:T(8,128)}, f32[48,128]{1,0:T(8,128)S(1)}, u32[]{:S(2)}, u32[]{:S(2)}) collective-permute-start(f32[48,128]{1,0:T(8,128)} %bitcast.4), channel_id=1, source_target_pairs={{0,16},{8,24},{16,0},{24,8},{1,17},{9,25},{17,1},{25,9},{2,18},{10... | collective-permute-start | bytes 73736 | tf_op jit(solution)/shard_map/ppermute | solution.py:374
  12.6 4.9 %collective-permute-start = (f32[48,128]{1,0:T(8,128)}, f32[48,128]{1,0:T(8,128)S(1)}, u32[]{:S(2)}, u32[]{:S(2)}) collective-permute-start(f32[48,128]{1,0:T(8,128)} %bitcast.5), channel_id=1, source_target_pairs={{0,8},{8,0},{16,24},{24,16},{1,9},{9,1},{17,25},{25,17},{2,10},{10... | collective-permute-start | bytes 73736 | tf_op jit(solution)/shard_map/ppermute | solution.py:374
  13.2 0.8 copy-start.1
  14.0 13.7 %copy-start = (f32[8,128]{1,0:T(8,128)S(1)}, f32[8,128]{1,0:T(8,128)}, u32[]{:S(2)}) copy-start(f32[8,128]{1,0:T(8,128)} %get-tuple-element.35.weight_ref) | copy-start | bytes 12292
  19.5 1.2 %collective-permute-start.3 = (f32[16,128]{1,0:T(8,128)S(1)}, f32[16,128]{1,0:T(8,128)S(1)}, u32[]{:S(2)}, u32[]{:S(2)}) collective-permute-start(f32[16,128]{1,0:T(8,128)S(1)} %get-tuple-element.45.one_ref), channel_id=1, source_target_pairs={{0,1},{1,0},{2,3},{3,2},{4,5},{5,4},{6,7},{7,6},{8,9},{9,8},{10,11... | collective-permute-start | bytes 24584 | tf_op jit(solution)/shard_map/ppermute | solution.py:382
  20.7 4.5 %collective-permute-start.6 = (f32[16,128]{1,0:T(8,128)S(1)}, f32[16,128]{1,0:T(8,128)S(1)}, u32[]{:S(2)}, u32[]{:S(2)}) collective-permute-start(f32[16,128]{1,0:T(8,128)S(1)} %shard_map.107.refs_1_), channel_id=1, source_target_pairs={{0,6},{1,7},{2,4},{3,5},{4,2},{5,3},{6,0},{7,1},{8,14},{9,15},{10,... | collective-permute-start | bytes 24584 | tf_op jit(solution)/shard_map/ppermute | solution.py:384
  23.5 3.7 %collective-permute-start.5 = (f32[16,128]{1,0:T(8,128)S(1)}, f32[16,128]{1,0:T(8,128)S(1)}, u32[]{:S(2)}, u32[]{:S(2)}) collective-permute-start(f32[16,128]{1,0:T(8,128)S(1)} %shard_map.107.refs_1_), channel_id=1, source_target_pairs={{0,4},{1,5},{2,6},{3,7},{4,0},{5,1},{6,2},{7,3},{8,12},{9,13},{10,... | collective-permute-start | bytes 24584 | tf_op jit(solution)/shard_map/ppermute | solution.py:384
  24.0 3.7 %collective-permute-start.4 = (f32[16,128]{1,0:T(8,128)S(1)}, f32[16,128]{1,0:T(8,128)S(1)}, u32[]{:S(2)}, u32[]{:S(2)}) collective-permute-start(f32[16,128]{1,0:T(8,128)S(1)} %shard_map.107.refs_1_), channel_id=1, source_target_pairs={{0,2},{1,3},{2,0},{3,1},{4,6},{5,7},{6,4},{7,5},{8,10},{9,11},{10,... | collective-permute-start | bytes 24584 | tf_op jit(solution)/shard_map/ppermute | solution.py:384
  28.1 5.6 %collective-permute-start.9 = (f32[32,128]{1,0:T(8,128)S(1)}, f32[32,128]{1,0:T(8,128)S(1)}, u32[]{:S(2)}, u32[]{:S(2)}) collective-permute-start(f32[32,128]{1,0:T(8,128)S(1)} %get-tuple-element.46.refs_0_), channel_id=1, source_target_pairs={{0,24},{8,16},{16,8},{24,0},{1,25},{9,17},{17,9},{25,1},{2,26},{10... | collective-permute-start | bytes 49160 | tf_op jit(solution)/shard_map/ppermute | solution.py:374
  30.7 4.6 %collective-permute-start.8 = (f32[32,128]{1,0:T(8,128)S(1)}, f32[32,128]{1,0:T(8,128)S(1)}, u32[]{:S(2)}, u32[]{:S(2)}) collective-permute-start(f32[32,128]{1,0:T(8,128)S(1)} %get-tuple-element.46.refs_0_), channel_id=1, source_target_pairs={{0,16},{8,24},{16,0},{24,8},{1,17},{9,25},{17,1},{25,9},{2,18},{10... | collective-permute-start | bytes 49160 | tf_op jit(solution)/shard_map/ppermute | solution.py:374
  30.7 4.6 %collective-permute-start.7 = (f32[32,128]{1,0:T(8,128)S(1)}, f32[32,128]{1,0:T(8,128)S(1)}, u32[]{:S(2)}, u32[]{:S(2)}) collective-permute-start(f32[32,128]{1,0:T(8,128)S(1)} %get-tuple-element.46.refs_0_), channel_id=1, source_target_pairs={{0,8},{8,0},{16,24},{24,16},{1,9},{9,1},{17,25},{25,17},{2,10},{10... | collective-permute-start | bytes 49160 | tf_op jit(solution)/shard_map/ppermute | solution.py:374
  37.1 1.2 %collective-permute-start.10 = (f32[16,128]{1,0:T(8,128)S(1)}, f32[16,128]{1,0:T(8,128)S(1)}, u32[]{:S(2)}, u32[]{:S(2)}) collective-permute-start(f32[16,128]{1,0:T(8,128)S(1)} %get-tuple-element.50.one_ref), channel_id=1, source_target_pairs={{0,1},{1,0},{2,3},{3,2},{4,5},{5,4},{6,7},{7,6},{8,9},{9,8},{10,11... | collective-permute-start | bytes 24584 | tf_op jit(solution)/shard_map/ppermute | solution.py:382
  38.4 4.5 %collective-permute-start.13 = (f32[16,128]{1,0:T(8,128)S(1)}, f32[16,128]{1,0:T(8,128)S(1)}, u32[]{:S(2)}, u32[]{:S(2)}) collective-permute-start(f32[16,128]{1,0:T(8,128)S(1)} %shard_map.111.refs_0_), channel_id=1, source_target_pairs={{0,6},{1,7},{2,4},{3,5},{4,2},{5,3},{6,0},{7,1},{8,14},{9,15},{10,... | collective-permute-start | bytes 24584 | tf_op jit(solution)/shard_map/ppermute | solution.py:384
  39.9 3.7 %collective-permute-start.12 = (f32[16,128]{1,0:T(8,128)S(1)}, f32[16,128]{1,0:T(8,128)S(1)}, u32[]{:S(2)}, u32[]{:S(2)}) collective-permute-start(f32[16,128]{1,0:T(8,128)S(1)} %shard_map.111.refs_0_), channel_id=1, source_target_pairs={{0,4},{1,5},{2,6},{3,7},{4,0},{5,1},{6,2},{7,3},{8,12},{9,13},{10,... | collective-permute-start | bytes 24584 | tf_op jit(solution)/shard_map/ppermute | solution.py:384
  41.1 3.7 %collective-permute-start.11 = (f32[16,128]{1,0:T(8,128)S(1)}, f32[16,128]{1,0:T(8,128)S(1)}, u32[]{:S(2)}, u32[]{:S(2)}) collective-permute-start(f32[16,128]{1,0:T(8,128)S(1)} %shard_map.111.refs_0_), channel_id=1, source_target_pairs={{0,2},{1,3},{2,0},{3,1},{4,6},{5,7},{6,4},{7,5},{8,10},{9,11},{10,... | collective-permute-start | bytes 24584 | tf_op jit(solution)/shard_map/ppermute | solution.py:384
  45.2 5.5 %collective-permute-start.16 = (f32[24,128]{1,0:T(8,128)S(1)}, f32[24,128]{1,0:T(8,128)S(1)}, u32[]{:S(2)}, u32[]{:S(2)}) collective-permute-start(f32[24,128]{1,0:T(8,128)S(1)} %get-tuple-element.54.refs_1_), channel_id=1, source_target_pairs={{0,24},{8,16},{16,8},{24,0},{1,25},{9,17},{17,9},{25,1},{2,26},{10... | collective-permute-start | bytes 36872 | tf_op jit(solution)/shard_map/ppermute | solution.py:374
  46.7 4.6 %collective-permute-start.15 = (f32[24,128]{1,0:T(8,128)S(1)}, f32[24,128]{1,0:T(8,128)S(1)}, u32[]{:S(2)}, u32[]{:S(2)}) collective-permute-start(f32[24,128]{1,0:T(8,128)S(1)} %get-tuple-element.54.refs_1_), channel_id=1, source_target_pairs={{0,16},{8,24},{16,0},{24,8},{1,17},{9,25},{17,1},{25,9},{2,18},{10... | collective-permute-start | bytes 36872 | tf_op jit(solution)/shard_map/ppermute | solution.py:374
  47.4 4.1 %collective-permute-start.14 = (f32[24,128]{1,0:T(8,128)S(1)}, f32[24,128]{1,0:T(8,128)S(1)}, u32[]{:S(2)}, u32[]{:S(2)}) collective-permute-start(f32[24,128]{1,0:T(8,128)S(1)} %get-tuple-element.54.refs_1_), channel_id=1, source_target_pairs={{0,8},{8,0},{16,24},{24,16},{1,9},{9,1},{17,25},{25,17},{2,10},{10... | collective-permute-start | bytes 36872 | tf_op jit(solution)/shard_map/ppermute | solution.py:374
  53.2 1.2 %collective-permute-start.17 = (f32[16,128]{1,0:T(8,128)S(1)}, f32[16,128]{1,0:T(8,128)S(1)}, u32[]{:S(2)}, u32[]{:S(2)}) collective-permute-start(f32[16,128]{1,0:T(8,128)S(1)} %get-tuple-element.55.one_ref), channel_id=1, source_target_pairs={{0,1},{1,0},{2,3},{3,2},{4,5},{5,4},{6,7},{7,6},{8,9},{9,8},{10,11... | collective-permute-start | bytes 24584 | tf_op jit(solution)/shard_map/ppermute | solution.py:382
  54.4 4.5 %collective-permute-start.20 = (f32[16,128]{1,0:T(8,128)S(1)}, f32[16,128]{1,0:T(8,128)S(1)}, u32[]{:S(2)}, u32[]{:S(2)}) collective-permute-start(f32[16,128]{1,0:T(8,128)S(1)} %shard_map.114.refs_0_), channel_id=1, source_target_pairs={{0,6},{1,7},{2,4},{3,5},{4,2},{5,3},{6,0},{7,1},{8,14},{9,15},{10,... | collective-permute-start | bytes 24584 | tf_op jit(solution)/shard_map/ppermute | solution.py:384
  56.1 3.7 %collective-permute-start.19 = (f32[16,128]{1,0:T(8,128)S(1)}, f32[16,128]{1,0:T(8,128)S(1)}, u32[]{:S(2)}, u32[]{:S(2)}) collective-permute-start(f32[16,128]{1,0:T(8,128)S(1)} %shard_map.114.refs_0_), channel_id=1, source_target_pairs={{0,4},{1,5},{2,6},{3,7},{4,0},{5,1},{6,2},{7,3},{8,12},{9,13},{10,... | collective-permute-start | bytes 24584 | tf_op jit(solution)/shard_map/ppermute | solution.py:384
  56.6 3.7 %collective-permute-start.18 = (f32[16,128]{1,0:T(8,128)S(1)}, f32[16,128]{1,0:T(8,128)S(1)}, u32[]{:S(2)}, u32[]{:S(2)}) collective-permute-start(f32[16,128]{1,0:T(8,128)S(1)} %shard_map.114.refs_0_), channel_id=1, source_target_pairs={{0,2},{1,3},{2,0},{3,1},{4,6},{5,7},{6,4},{7,5},{8,10},{9,11},{10,... | collective-permute-start | bytes 24584 | tf_op jit(solution)/shard_map/ppermute | solution.py:384
  60.8 5.5 %collective-permute-start.23 = (f32[24,128]{1,0:T(8,128)S(1)}, f32[24,128]{1,0:T(8,128)S(1)}, u32[]{:S(2)}, u32[]{:S(2)}) collective-permute-start(f32[24,128]{1,0:T(8,128)S(1)} %get-tuple-element.59.refs_1_), channel_id=1, source_target_pairs={{0,24},{8,16},{16,8},{24,0},{1,25},{9,17},{17,9},{25,1},{2,26},{10... | collective-permute-start | bytes 36872 | tf_op jit(solution)/shard_map/ppermute | solution.py:374
  63.2 4.6 %collective-permute-start.22 = (f32[24,128]{1,0:T(8,128)S(1)}, f32[24,128]{1,0:T(8,128)S(1)}, u32[]{:S(2)}, u32[]{:S(2)}) collective-permute-start(f32[24,128]{1,0:T(8,128)S(1)} %get-tuple-element.59.refs_1_), channel_id=1, source_target_pairs={{0,16},{8,24},{16,0},{24,8},{1,17},{9,25},{17,1},{25,9},{2,18},{10... | collective-permute-start | bytes 36872 | tf_op jit(solution)/shard_map/ppermute | solution.py:374
  64.1 3.8 %collective-permute-start.21 = (f32[24,128]{1,0:T(8,128)S(1)}, f32[24,128]{1,0:T(8,128)S(1)}, u32[]{:S(2)}, u32[]{:S(2)}) collective-permute-start(f32[24,128]{1,0:T(8,128)S(1)} %get-tuple-element.59.refs_1_), channel_id=1, source_target_pairs={{0,8},{8,0},{16,24},{24,16},{1,9},{9,1},{17,25},{25,17},{2,10},{10... | collective-permute-start | bytes 36872 | tf_op jit(solution)/shard_map/ppermute | solution.py:374
  69.4 1.2 %collective-permute-start.24 = (f32[8,128]{1,0:T(8,128)S(1)}, f32[8,128]{1,0:T(8,128)S(1)}, u32[]{:S(2)}, u32[]{:S(2)}) collective-permute-start(f32[8,128]{1,0:T(8,128)S(1)} %get-tuple-element.60.one_ref), channel_id=1, source_target_pairs={{0,1},{1,0},{2,3},{3,2},{4,5},{5,4},{6,7},{7,6},{8,9},{9,8},{10,11... | collective-permute-start | bytes 12296 | tf_op jit(solution)/shard_map/ppermute | solution.py:382
  70.7 4.5 %collective-permute-start.27 = (f32[8,128]{1,0:T(8,128)S(1)}, f32[8,128]{1,0:T(8,128)S(1)}, u32[]{:S(2)}, u32[]{:S(2)}) collective-permute-start(f32[8,128]{1,0:T(8,128)S(1)} %shard_map.117.refs_0_), channel_id=1, source_target_pairs={{0,6},{1,7},{2,4},{3,5},{4,2},{5,3},{6,0},{7,1},{8,14},{9,15},{10,... | collective-permute-start | bytes 12296 | tf_op jit(solution)/shard_map/ppermute | solution.py:384
  72.1 3.6 %collective-permute-start.26 = (f32[8,128]{1,0:T(8,128)S(1)}, f32[8,128]{1,0:T(8,128)S(1)}, u32[]{:S(2)}, u32[]{:S(2)}) collective-permute-start(f32[8,128]{1,0:T(8,128)S(1)} %shard_map.117.refs_0_), channel_id=1, source_target_pairs={{0,4},{1,5},{2,6},{3,7},{4,0},{5,1},{6,2},{7,3},{8,12},{9,13},{10,... | collective-permute-start | bytes 12296 | tf_op jit(solution)/shard_map/ppermute | solution.py:384
  73.4 3.6 %collective-permute-start.25 = (f32[8,128]{1,0:T(8,128)S(1)}, f32[8,128]{1,0:T(8,128)S(1)}, u32[]{:S(2)}, u32[]{:S(2)}) collective-permute-start(f32[8,128]{1,0:T(8,128)S(1)} %shard_map.117.refs_0_), channel_id=1, source_target_pairs={{0,2},{1,3},{2,0},{3,1},{4,6},{5,7},{6,4},{7,5},{8,10},{9,11},{10,... | collective-permute-start | bytes 12296 | tf_op jit(solution)/shard_map/ppermute | solution.py:384
